TPU v7x, 128 devices: a whole 4x4x4 slice. The times are simulated.
128 devices in a mesh: grp: 16 (over x, y_lo, core), ctx: 8 (over y_hi, z).
Axes of the slice: x: 4, y: 4 (y_hi: 2, y_lo: 2; y = y_hi * 2 + y_lo), z: 4, core: 2. Of those that a mesh axis runs over, the one named last changes fastest.
Arguments:
- inputs: bfloat16 [16, 1536, 1024], P('grp', 'ctx'), may hold values from -6 to 6
- cotangent: bfloat16 [16, 1536, 1024], P('grp', 'ctx'), may hold values from -6 to 6
- segments: int32 [16, 1536], P('grp'), may hold values from 0 to 2, as said below
- norm_one_gain: bfloat16 [2, 1024], P(None, 'ctx'), may hold values from 0.5 to 1.5
- norm_one_bias: bfloat16 [2, 1024], P(None, 'ctx'), may hold values from -1.25 to 1.25
- input_weight: bfloat16 [2, 1024, 3072], P(None, 'ctx'), may hold values from -1 to 1
- input_bias: bfloat16 [2, 2048], P(None, 'ctx'), may hold values from -2 to 2
- project_weight: bfloat16 [2, 1024, 1024], P(None, 'ctx'), may hold values from -0.75 to 0.75
- project_bias: bfloat16 [2, 1024], P(None, 'ctx'), may hold values from -1.25 to 1.25
- norm_two_gain: bfloat16 [2, 1024], P(None, 'ctx'), may hold values from 0.5 to 1.5
- norm_two_bias: bfloat16 [2, 1024], P(None, 'ctx'), may hold values from -1.25 to 1.25
- up_weight: bfloat16 [2, 1024, 4096], P(None, 'ctx'), may hold values from -0.1875 to 0.1875
- up_bias: bfloat16 [2, 4096], P(None, 'ctx'), may hold values from -1.75 to 1.75
- down_weight: bfloat16 [2, 4096, 1024], P(None, 'ctx'), may hold values from -0.09375 to 0.09375
- down_bias: bfloat16 [2, 1024], P(None, 'ctx'), may hold values from -1.25 to 1.25
Outputs:
- block_output: float32 [16, 1536, 1024], P('grp', 'ctx')
- grad_inputs: float32 [16, 1536, 1024], P('grp', 'ctx')
- grad_norm_one_gain: float32 [2, 1024], P(None, 'ctx')
- grad_norm_one_bias: float32 [2, 1024], P(None, 'ctx')
- grad_input_weight: float32 [2, 1024, 3072], P(None, 'ctx')
- grad_input_bias: float32 [2, 2048], P(None, 'ctx')
- grad_project_weight: float32 [2, 1024, 1024], P(None, 'ctx')
- grad_project_bias: float32 [2, 1024], P(None, 'ctx')
- grad_norm_two_gain: float32 [2, 1024], P(None, 'ctx')
- grad_norm_two_bias: float32 [2, 1024], P(None, 'ctx')
- grad_up_weight: float32 [2, 1024, 4096], P(None, 'ctx')
- grad_up_bias: float32 [2, 4096], P(None, 'ctx')
- grad_down_weight: float32 [2, 4096, 1024], P(None, 'ctx')
- grad_down_bias: float32 [2, 1024], P(None, 'ctx')
Inputs may be any that keep to these rules, and one draw needn't show every extreme that they name: `segments`: in every group the first 1024 tokens have segment 0, then come the tokens of continuation 1 and then those of continuation 2, each continuation one token or more.
All inputs are finite; a program needn't handle non-finite values.
Results may differ from a plain program's by a relative error of at most 0.03.
Values may be sent and summed in bfloat16 or wider, within the bound.
No kernel may reach another device: no remote copies, remote signals or barrier semaphores. Data moves between devices by JAX's collectives and lax.ppermute only.
A program may use at most 192 MiB of HBM per device.

v0:
```python
import math

import jax
import jax.numpy as jnp
from jax import lax
from jax.sharding import Mesh
from jax.sharding import PartitionSpec as P

D = 1024
HEADS = 16
HEAD_DIM = 64
FF = 4096
NCONT = 2
PROMPT = 1024
CTX = ("ctx_0", "ctx_1")


masked_value = -1e30


def joined_along(blocks, dim):
    dims = list(blocks.shape[1:])
    dims[dim] *= blocks.shape[0]
    return jnp.moveaxis(blocks, 0, dim).reshape(dims)


def gather_in_order(shard, axes, order):
    blocks = shard
    for k in order:
        blocks = lax.all_gather(blocks, axes[k])
    done = order[::-1]
    back = [done.index(k) for k in range(len(axes))]
    blocks = blocks.transpose(*back, *range(len(axes), blocks.ndim))
    return blocks.reshape(-1, *shard.shape)


def gather_axes(shard, axes, order, dim):
    return joined_along(gather_in_order(shard, axes, order), dim)


def in_one_piece(arrays, axis, split_dim, concat_dim, along):
    widths = [a.shape[along] for a in arrays]
    both = jnp.concatenate(arrays, axis=along)
    filled = lax.all_to_all(both, axis, split_axis=split_dim, concat_axis=concat_dim, tiled=True)
    return tuple(jnp.split(filled, [sum(widths[:k]) for k in range(1, len(widths))], axis=along))


def layer_norm(values, gain, offset):
    average = jnp.mean(values, axis=-1, keepdims=True)
    centered = values - average
    variance = jnp.mean(centered * centered, axis=-1, keepdims=True)
    return centered * lax.rsqrt(variance + 1e-05) * gain + offset


def gelu_tanh(values):
    return jax.nn.gelu(values, approximate=True)


def token_places(segment_ids):
    length = segment_ids.shape[0]
    token_index = jnp.arange(length, dtype=jnp.int32)
    numbers = jnp.arange(NCONT + 1, dtype=jnp.int32)
    member = segment_ids[None, :] == numbers[:, None]
    starts = jnp.min(jnp.where(member, token_index[None, :], length), axis=1)
    seg_start = jnp.sum(jnp.where(member, starts[:, None], 0), axis=0)
    prompt_shift = jnp.where(segment_ids > 0, PROMPT, 0).astype(jnp.int32)
    return token_index - seg_start + prompt_shift


def outer_sum(left, right):
    return lax.dot_general(
        left, right, (((0,), (0,)), ((), ())), preferred_element_type=jnp.float32
    )


def back_dot(grad_rows, weight):
    return lax.dot_general(
        grad_rows, weight, (((1,), (1,)), ((), ())), preferred_element_type=jnp.float32
    )


def column_sums(rows_low):
    return jnp.sum(rows_low.astype(jnp.float32), axis=0)


def local_fold(fold_fn, blocks, start):
    total = jax.tree.leaves(blocks)[0].shape[0]
    size = math.gcd(total, 512)

    def step(index, running):
        offset = (index * size).astype(jnp.int32)
        piece = jax.tree.map(lambda whole: lax.dynamic_slice_in_dim(whole, offset, size, 0), blocks)
        return fold_fn(running, piece, offset)

    return lax.fori_loop(0, total // size, step, start)


def mask_block(layout, offset, key_count):
    segment_ids, places, query_ids, query_places, query_index, row_order = layout
    key_index = lax.dynamic_slice_in_dim(row_order, offset, key_count)
    key_ids = lax.dynamic_slice_in_dim(segment_ids, offset, key_count)
    key_places = lax.dynamic_slice_in_dim(places, offset, key_count)
    visible = (key_index[None, :] <= query_index[:, None]) & (
        (key_ids[None, :] == 0) | (key_ids[None, :] == query_ids[:, None])
    )
    distance = (key_places[None, :] - query_places[:, None]).astype(jnp.float32)
    return (visible, distance)


def block_scores(query_heads, key_block, visible, distance, slopes):
    key_count = key_block.shape[0]
    heads = query_heads.shape[1]
    key_heads = key_block.reshape(key_count, heads, HEAD_DIM)
    raw_scores = jnp.einsum(
        "qhd,khd->hqk", query_heads, key_heads, preferred_element_type=jnp.float32
    )
    scores = raw_scores * HEAD_DIM ** (-0.5) + slopes[:, None, None] * distance[None]
    return jnp.where(visible[None], scores, masked_value)


def attend(query_rows, key_rows, value_rows, layout, slopes):
    row_count = query_rows.shape[0]
    heads = query_rows.shape[1] // HEAD_DIM
    query_heads = query_rows.reshape(row_count, heads, HEAD_DIM)

    def fold_stats(running, key_block, offset):
        visible, distance = mask_block(layout, offset, key_block.shape[0])

        def block_work(current):
            row_top, row_total = current
            scores = block_scores(query_heads, key_block, visible, distance, slopes)
            new_top = jnp.maximum(row_top, jnp.max(scores, axis=2))
            exponent = jnp.where(visible[None], jnp.exp(scores - new_top[:, :, None]), 0.0)
            return (new_top, row_total * jnp.exp(row_top - new_top) + jnp.sum(exponent, axis=2))

        return block_work(running)

    start_stats = (
        jnp.full((heads, row_count), masked_value, jnp.float32),
        jnp.zeros((heads, row_count), jnp.float32),
    )
    row_top, row_total = local_fold(fold_stats, key_rows, start_stats)
    logsum = row_top + jnp.log(row_total)

    def fold_values(running, pair_block, offset):
        key_block, value_block = pair_block
        key_count = key_block.shape[0]
        visible, distance = mask_block(layout, offset, key_count)

        def block_work(current):
            weighted, remainder = current
            scores = block_scores(query_heads, key_block, visible, distance, slopes)
            weights = jnp.where(visible[None], jnp.exp(scores - logsum[:, :, None]), 0.0)
            weights_low = weights.astype(jnp.bfloat16)
            leftover = (weights - weights_low.astype(jnp.float32)).astype(jnp.bfloat16)
            value_heads = value_block.reshape(key_count, heads, HEAD_DIM)
            weighted = weighted + jnp.einsum(
                "hqk,khd->qhd", weights_low, value_heads, preferred_element_type=jnp.float32
            )
            remainder = remainder + jnp.einsum(
                "hqk,khd->qhd", leftover, value_heads, preferred_element_type=jnp.float32
            )
            return (weighted, remainder)

        return block_work(running)

    start_values = (
        jnp.zeros((row_count, heads, HEAD_DIM), jnp.float32),
        jnp.zeros((row_count, heads, HEAD_DIM), jnp.float32),
    )
    weighted, remainder = local_fold(fold_values, (key_rows, value_rows), start_values)
    unrounded = weighted + remainder
    return (weighted.reshape(row_count, heads * HEAD_DIM), unrounded, logsum)


def attend_back(query_rows, key_rows, value_rows, d_context, unrounded, logsum, layout, slopes):
    row_count = query_rows.shape[0]
    total_rows = layout[0].shape[0]
    width = query_rows.shape[1]
    heads = width // HEAD_DIM
    query_heads = query_rows.reshape(row_count, heads, HEAD_DIM)
    grad_heads = d_context.reshape(row_count, heads, HEAD_DIM)
    correction = jnp.sum(grad_heads.astype(jnp.float32) * unrounded, axis=2).T

    def fold_back(running, pair_block, offset):
        key_block, value_block = pair_block
        key_count = key_block.shape[0]
        visible, distance = mask_block(layout, offset, key_count)

        def block_work(current):
            d_query, key_grads, value_grads = current
            scores = block_scores(query_heads, key_block, visible, distance, slopes)
            weights = jnp.where(visible[None], jnp.exp(scores - logsum[:, :, None]), 0.0)
            key_heads = key_block.reshape(key_count, heads, HEAD_DIM)
            value_heads = value_block.reshape(key_count, heads, HEAD_DIM)
            d_weights = jnp.einsum(
                "qhd,khd->hqk", grad_heads, value_heads, preferred_element_type=jnp.float32
            )
            d_scores = (weights * (d_weights - correction[:, :, None])).astype(jnp.bfloat16)
            d_query = d_query + jnp.einsum(
                "hqk,khd->qhd", d_scores, key_heads, preferred_element_type=jnp.float32
            ) * HEAD_DIM ** (-0.5)
            key_part = jnp.einsum(
                "hqk,qhd->khd", d_scores, query_heads, preferred_element_type=jnp.float32
            ).reshape(key_count, width) * HEAD_DIM ** (-0.5)
            value_part = jnp.einsum(
                "hqk,qhd->khd",
                weights.astype(jnp.bfloat16),
                grad_heads,
                preferred_element_type=jnp.float32,
            ).reshape(key_count, width)
            key_grads = lax.dynamic_update_slice_in_dim(
                key_grads,
                lax.dynamic_slice_in_dim(key_grads, offset, key_count, 0) + key_part,
                offset,
                0,
            )
            value_grads = lax.dynamic_update_slice_in_dim(
                value_grads,
                lax.dynamic_slice_in_dim(value_grads, offset, key_count, 0) + value_part,
                offset,
                0,
            )
            return (d_query, key_grads, value_grads)

        return block_work(running)

    start_back = (
        jnp.zeros((row_count, heads, HEAD_DIM), jnp.float32),
        jnp.zeros((total_rows, width), jnp.float32),
        jnp.zeros((total_rows, width), jnp.float32),
    )
    d_query, key_grads, value_grads = local_fold(fold_back, (key_rows, value_rows), start_back)
    d_query = d_query.reshape(row_count, width).astype(jnp.bfloat16)
    return (d_query, key_grads.astype(jnp.bfloat16), value_grads.astype(jnp.bfloat16))


def gather_rows(rows_low):
    return gather_axes(rows_low, CTX, (0, 1), 0)


def scatter_rows(partial_value):
    return lax.psum_scatter(
        partial_value.astype(jnp.bfloat16), CTX, scatter_dimension=0, tiled=True
    ).astype(jnp.float32)


def forward_tensor(hidden, params, layout, slopes, place):
    (
        norm_one_gain,
        norm_one_bias,
        input_weight,
        input_bias,
        project_weight,
        project_bias,
        norm_two_gain,
        norm_two_bias,
        up_weight,
        up_bias,
        down_weight,
        down_bias,
    ) = params
    local_width = input_weight.shape[1] // 3
    local_units = up_weight.shape[1]
    bias_full = input_bias.astype(jnp.float32)
    query_bias = lax.dynamic_slice_in_dim(bias_full, place * local_width, local_width)
    value_bias = lax.dynamic_slice_in_dim(bias_full, D + place * local_width, local_width)
    normed = layer_norm(
        hidden, norm_one_gain.astype(jnp.float32), norm_one_bias.astype(jnp.float32)
    ).astype(jnp.bfloat16)
    normed_all = gather_rows(normed)
    projected = jnp.dot(normed_all, input_weight, preferred_element_type=jnp.float32)
    query_rows = (projected[:, :local_width] + query_bias).astype(jnp.bfloat16)
    key_rows = projected[:, local_width : 2 * local_width].astype(jnp.bfloat16)
    value_rows = (projected[:, 2 * local_width :] + value_bias).astype(jnp.bfloat16)
    context, unrounded, logsum = attend(query_rows, key_rows, value_rows, layout, slopes)
    context_low = context.astype(jnp.bfloat16)
    middle = (
        hidden
        + scatter_rows(jnp.dot(context_low, project_weight, preferred_element_type=jnp.float32))
        + project_bias.astype(jnp.float32)
    )
    normed_two = layer_norm(
        middle, norm_two_gain.astype(jnp.float32), norm_two_bias.astype(jnp.float32)
    ).astype(jnp.bfloat16)
    normed_two_all = gather_rows(normed_two)
    unit_bias = lax.dynamic_slice_in_dim(
        up_bias.astype(jnp.float32), place * local_units, local_units
    )
    before = jnp.dot(normed_two_all, up_weight, preferred_element_type=jnp.float32) + unit_bias
    activated = gelu_tanh(before).astype(jnp.bfloat16)
    result = (
        middle
        + scatter_rows(jnp.dot(activated, down_weight, preferred_element_type=jnp.float32))
        + down_bias.astype(jnp.float32)
    )
    kept_state = (
        hidden,
        normed_all,
        query_rows,
        key_rows,
        value_rows,
        context_low,
        unrounded,
        logsum,
        middle,
        normed_two_all,
        before,
        activated,
    )
    return (result, kept_state)


def backward_tensor(gradient, params, kept_state, layout, slopes, place):
    (
        norm_one_gain,
        norm_one_bias,
        input_weight,
        input_bias,
        project_weight,
        project_bias,
        norm_two_gain,
        norm_two_bias,
        up_weight,
        up_bias,
        down_weight,
        down_bias,
    ) = params
    (
        hidden,
        normed_all,
        query_rows,
        key_rows,
        value_rows,
        context_low,
        unrounded,
        logsum,
        middle,
        normed_two_all,
        before,
        activated,
    ) = kept_state
    local_width = input_weight.shape[1] // 3
    local_units = up_weight.shape[1]
    grad_down_rows = gradient.astype(jnp.bfloat16)
    grad_down = gather_rows(grad_down_rows)
    grad_down_weight = outer_sum(activated, grad_down)
    grad_down_bias = column_sums(grad_down_rows)
    ignored, gelu_back = jax.vjp(gelu_tanh, before)
    d_before = gelu_back(back_dot(grad_down, down_weight))[0].astype(jnp.bfloat16)
    grad_up_weight = outer_sum(normed_two_all, d_before)
    grad_up_bias = lax.dynamic_update_slice_in_dim(
        jnp.zeros((FF,), jnp.float32), column_sums(d_before), place * local_units, 0
    )
    ignored, norm_back_two = jax.vjp(
        layer_norm, middle, norm_two_gain.astype(jnp.float32), norm_two_bias.astype(jnp.float32)
    )
    d_middle, grad_two_gain, grad_two_bias = norm_back_two(
        scatter_rows(back_dot(d_before, up_weight))
    )
    d_middle = d_middle + gradient
    grad_out = d_middle.astype(jnp.bfloat16)
    grad_out_all = gather_rows(grad_out)
    grad_project_weight = outer_sum(context_low, grad_out_all)
    grad_project_bias = column_sums(grad_out)
    d_context = back_dot(grad_out_all, project_weight).astype(jnp.bfloat16)
    d_query, d_key, d_value = attend_back(
        query_rows, key_rows, value_rows, d_context, unrounded, logsum, layout, slopes
    )
    d_joined = jnp.concatenate([d_query, d_key, d_value], axis=1)
    grad_input_weight = outer_sum(normed_all, d_joined)
    grad_input_bias = jnp.zeros((2 * D,), jnp.float32)
    grad_input_bias = lax.dynamic_update_slice_in_dim(
        grad_input_bias, column_sums(d_query), place * local_width, 0
    )
    grad_input_bias = lax.dynamic_update_slice_in_dim(
        grad_input_bias, column_sums(d_value), D + place * local_width, 0
    )
    ignored, norm_back_one = jax.vjp(
        layer_norm, hidden, norm_one_gain.astype(jnp.float32), norm_one_bias.astype(jnp.float32)
    )
    d_hidden, grad_one_gain, grad_one_bias = norm_back_one(
        scatter_rows(back_dot(d_joined, input_weight))
    )
    layer_grads = (
        grad_one_gain,
        grad_one_bias,
        grad_input_weight,
        grad_input_bias,
        grad_project_weight,
        grad_project_bias,
        grad_two_gain,
        grad_two_bias,
        grad_up_weight,
        grad_up_bias,
        grad_down_weight,
        grad_down_bias,
    )
    return (d_middle + d_hidden, layer_grads)


def reduce_tensor(layer_grads, cycle_size):
    (
        grad_one_gain,
        grad_one_bias,
        grad_input_weight,
        grad_input_bias,
        grad_project_weight,
        grad_project_bias,
        grad_two_gain,
        grad_two_bias,
        grad_up_weight,
        grad_up_bias,
        grad_down_weight,
        grad_down_bias,
    ) = layer_grads
    full_rows = grad_input_weight.shape[0]
    local_width = grad_input_weight.shape[1] // 3
    local_units = grad_up_weight.shape[1]

    def split_vector(vector):
        return vector.reshape(cycle_size, 1, 1, vector.shape[0] // cycle_size)

    moved = (
        lax.all_to_all(
            grad_input_weight.reshape(full_rows, 3, 1, local_width).astype(jnp.bfloat16),
            CTX,
            split_axis=0,
            concat_axis=2,
            tiled=True,
        ).astype(jnp.float32),
        lax.all_to_all(
            grad_up_weight.reshape(full_rows, 1, 1, local_units).astype(jnp.bfloat16),
            CTX,
            split_axis=0,
            concat_axis=2,
            tiled=True,
        ).astype(jnp.float32),
        *tuple(
            (
                part.astype(jnp.float32)
                for part in in_one_piece(
                    (
                        split_vector(grad_one_gain).astype(jnp.bfloat16),
                        split_vector(grad_one_bias).astype(jnp.bfloat16),
                        split_vector(grad_input_bias).astype(jnp.bfloat16),
                        split_vector(grad_project_bias).astype(jnp.bfloat16),
                        split_vector(grad_two_gain).astype(jnp.bfloat16),
                        split_vector(grad_two_bias).astype(jnp.bfloat16),
                        split_vector(grad_up_bias).astype(jnp.bfloat16),
                        split_vector(grad_down_bias).astype(jnp.bfloat16),
                    ),
                    CTX,
                    0,
                    2,
                    3,
                )
            )
        ),
    )
    input_rows = moved[0].reshape(full_rows // cycle_size, 3 * full_rows)
    up_rows = moved[1].reshape(full_rows // cycle_size, cycle_size * local_units)
    small = [jnp.sum(piece, axis=2).reshape(-1) for piece in moved[2:]]
    return (
        lax.psum(small[0].astype(jnp.bfloat16), "grp").astype(jnp.float32),
        lax.psum(small[1].astype(jnp.bfloat16), "grp").astype(jnp.float32),
        lax.psum(input_rows.astype(jnp.bfloat16), "grp").astype(jnp.float32),
        lax.psum(small[2].astype(jnp.bfloat16), "grp").astype(jnp.float32),
        lax.psum(grad_project_weight.astype(jnp.bfloat16), "grp").astype(jnp.float32),
        lax.psum(small[3].astype(jnp.bfloat16), "grp").astype(jnp.float32),
        lax.psum(small[4].astype(jnp.bfloat16), "grp").astype(jnp.float32),
        lax.psum(small[5].astype(jnp.bfloat16), "grp").astype(jnp.float32),
        lax.psum(up_rows.astype(jnp.bfloat16), "grp").astype(jnp.float32),
        lax.psum(small[6].astype(jnp.bfloat16), "grp").astype(jnp.float32),
        lax.psum(grad_down_weight.astype(jnp.bfloat16), "grp").astype(jnp.float32),
        lax.psum(small[7].astype(jnp.bfloat16), "grp").astype(jnp.float32),
    )


def on_device(
    inputs,
    cotangent,
    segments,
    norm_one_gain,
    norm_one_bias,
    input_weight,
    input_bias,
    project_weight,
    project_bias,
    norm_two_gain,
    norm_two_bias,
    up_weight,
    up_bias,
    down_weight,
    down_bias,
):
    cycle_size = lax.axis_size(CTX)
    cycle_place = lax.axis_index(CTX)
    segment_ids = segments[0]
    total_rows = segment_ids.shape[0]
    places = token_places(segment_ids)
    spots = jnp.arange(total_rows, dtype=jnp.int32)
    hidden_rows = inputs[0]
    cot_rows = cotangent[0]
    layer_count = input_weight.shape[0]
    hidden = hidden_rows.astype(jnp.float32)
    gradient = cot_rows.astype(jnp.float32)
    per_layer = [None] * layer_count
    layout = (segment_ids, places, segment_ids, places, spots, spots)
    local_heads = HEADS // cycle_size
    head_index = (cycle_place * local_heads + jnp.arange(local_heads, dtype=jnp.int32)).astype(
        jnp.float32
    )
    slopes = jnp.exp2(-8.0 * (head_index + 1.0) / HEADS)
    row_width = input_weight.shape[1]

    def tiles(vector):
        return jnp.tile(vector[:, None, None, None, :], (1, 1, 1, cycle_size, 1))

    moved = (
        lax.all_to_all(
            input_weight.reshape(layer_count, row_width, 3, cycle_size, row_width),
            CTX,
            split_axis=3,
            concat_axis=1,
            tiled=True,
        ),
        lax.all_to_all(
            up_weight.reshape(layer_count, row_width, 1, cycle_size, FF // cycle_size),
            CTX,
            split_axis=3,
            concat_axis=1,
            tiled=True,
        ),
        *in_one_piece(
            (
                tiles(norm_one_gain),
                tiles(norm_one_bias),
                tiles(input_bias),
                tiles(project_bias),
                tiles(norm_two_gain),
                tiles(norm_two_bias),
                tiles(up_bias),
                tiles(down_bias),
            ),
            CTX,
            3,
            1,
            4,
        ),
    )
    column_input = moved[0].reshape(layer_count, D, 3 * row_width)
    column_up = moved[1].reshape(layer_count, D, FF // cycle_size)
    full_small = [piece.reshape(layer_count, -1) for piece in moved[2:]]
    kept_layers = []
    for layer_num in range(layer_count):
        params = (
            full_small[0][layer_num],
            full_small[1][layer_num],
            column_input[layer_num],
            full_small[2][layer_num],
            project_weight[layer_num],
            full_small[3][layer_num],
            full_small[4][layer_num],
            full_small[5][layer_num],
            column_up[layer_num],
            full_small[6][layer_num],
            down_weight[layer_num],
            full_small[7][layer_num],
        )
        hidden, kept_state = forward_tensor(hidden, params, layout, slopes, cycle_place)
        kept_layers.append((params, kept_state))
    for layer_num in range(layer_count - 1, -1, -1):
        params, kept_state = kept_layers[layer_num]
        gradient, layer_grads = backward_tensor(
            gradient, params, kept_state, layout, slopes, cycle_place
        )
        per_layer[layer_num] = reduce_tensor(layer_grads, cycle_size)
    stacked = tuple(
        (
            jnp.stack([per_layer[layer_num][member] for layer_num in range(layer_count)])
            for member in range(12)
        )
    )
    return (
        hidden[None],
        gradient[None],
        stacked[0],
        stacked[1],
        stacked[2],
        stacked[3],
        stacked[4],
        stacked[5],
        stacked[6],
        stacked[7],
        stacked[8],
        stacked[9],
        stacked[10],
        stacked[11],
    )


def solution(mesh):
    split = Mesh(mesh.devices.reshape(mesh.shape["grp"], 2, 4), ("grp", "ctx_0", "ctx_1"))
    return jax.shard_map(
        on_device,
        mesh=split,
        in_specs=(
            P("grp", CTX, None),
            P("grp", CTX, None),
            P("grp", None),
            P(None, CTX),
            P(None, CTX),
            P(None, CTX, None),
            P(None, CTX),
            P(None, CTX, None),
            P(None, CTX),
            P(None, CTX),
            P(None, CTX),
            P(None, CTX, None),
            P(None, CTX),
            P(None, CTX, None),
            P(None, CTX),
        ),
        out_specs=(
            P("grp", CTX, None),
            P("grp", CTX, None),
            P(None, CTX),
            P(None, CTX),
            P(None, CTX, None),
            P(None, CTX),
            P(None, CTX, None),
            P(None, CTX),
            P(None, CTX),
            P(None, CTX),
            P(None, CTX, None),
            P(None, CTX),
            P(None, CTX, None),
            P(None, CTX),
        ),
        check_vma=False,
    )
```

profile of v0, /device:TPU:1, one launch (start us, length us, event | category | flops | bytes accessed | tf_op | source)
XLA Modules:
  0.0 1609.5 jit_solution(11933636477443957225)
XLA Ops:
  17.4 8.5 all-to-all-start
  28.3 4.2 all-to-all-done
  34.4 10.8 all_gather.92
  47.4 3.6 all-to-all-start.1
  52.0 16.7 %all-to-all-done.1 = bf16[2,128,3,8,128]{1,4,2,0,3:T(8,128)(2,1)S(1)} async-done(((bf16[2,128,3,8,128]{1,4,2,0,3:T(8,128)(2,1)}), bf16[2,128,3,8,128]{1,4,2,0,3:T(8,128)(2,1)S(1)}, u32[]{:S(2)}, u32[]{:S(2)}) %all-to-all-start.1) | async-done | bytes 1572896 | tf_op jit(solution)/shard_map/all_to_all | solution.py:521
  70.3 27.3 %all-gather.23.cloned.1.call-done = bf16[8,192,1024]{2,1,0:T(8,128)(2,1)} async-done(((bf16[2,192,1024]{2,1,0:T(8,128)(2,1)}), bf16[8,192,1024]{2,1,0:T(8,128)(2,1)}) %all-gather.23.cloned.1.call-update) | async-done | bytes 3145744 | tf_op jit(solution)/shard_map/all_gather | solution.py:30
  101.6 17.7 %while.106 = (s32[]{:T(128)}, f32[2,1536]{1,0:T(2,128)S(1)}, f32[2,1536]{1,0:T(2,128)S(1)}, s32[1536]{0:T(1024)S(1)}, s32[1536]{0:T(1024)S(1)}, /*index=5*/s32[1...) while((s32[]{:T(128)}, f32[2,1536]{1,0:T(2,128)S(1)}, ...), condition=%wide.region_7.8_spmd.clone.clone, body=%wide.region_4.7_spmd.clone.clone.sunk | while | flops 224935440 | bytes 25375988 | solution.py:95
  119.3 17.2 %while.107 = (s32[]{:T(128)}, f32[1536,2,64]{0,2,1:T(8,128)S(1)}, f32[1536,2,64]{0,2,1:T(8,128)S(1)}, bf16[1536,128]{0,1:T(8,128)(2,1)S(1)}, s32[1536]{0:T(1024)...) while((s32[]{:T(128)}, f32[1536,2,64]{0,2,1:T(8,128)S(1)}, ...), condition=%wide.region_9.10_spmd.clone.clone, body=%wide.region_8.9_spmd.clone.clone.sunk | while | flops 626786816 | bytes 31257852 | solution.py:95
  137.9 3.9 convolution_convert_fusion.1
  142.2 77.4 %reduce-scatter.9.cloned.1.call-done = bf16[192,1024]{1,0:T(8,128)(2,1)} async-done(((bf16[1536,1024]{1,0:T(8,128)(2,1)}), bf16[192,1024]{1,0:T(8,128)(2,1)}) %reduce-scatter.9.cloned.1.call-update) | async-done | bytes 393232 | tf_op jit(solution)/shard_map/reduce_scatter | solution.py:243
  223.4 11.1 all-gather.1
  234.5 4.1 copy.255
  241.7 4.4 all-to-all-start.2
  246.8 32.2 %all-to-all-done.2 = bf16[2,128,1,8,512]{1,4,0,2,3:T(8,128)(2,1)} async-done(((bf16[2,128,1,8,512]{1,4,0,2,3:T(8,128)(2,1)}), bf16[2,128,1,8,512]{1,4,0,2,3:T(8,128)(2,1)}, u32[]{:S(2)}, u32[]{:S(2)}) %all-to-all-start.2) | async-done | bytes 2097184 | tf_op jit(solution)/shard_map/all_to_all | solution.py:528
  279.0 3.9 copy.257
  285.7 11.7 all-gather.25.cloned.1.call-done
  303.1 3.8 convolution_convert_fusion.7
  307.1 78.4 %reduce-scatter.11.cloned.1.call-done = bf16[192,1024]{1,0:T(8,128)(2,1)} async-done(((bf16[1536,1024]{1,0:T(8,128)(2,1)}), bf16[192,1024]{1,0:T(8,128)(2,1)}) %reduce-scatter.11.cloned.1.call-update) | async-done | bytes 393232 | tf_op jit(solution)/shard_map/reduce_scatter | solution.py:243
  387.3 11.1 all-gather.3
  399.9 38.9 %all-gather.27.cloned.1.call-done = bf16[8,192,1024]{2,1,0:T(8,128)(2,1)} async-done(((bf16[2,192,1024]{2,1,0:T(8,128)(2,1)}), bf16[8,192,1024]{2,1,0:T(8,128)(2,1)}) %all-gather.27.cloned.1.call-update) | async-done | bytes 3145744 | tf_op jit(solution)/shard_map/all_gather | solution.py:30
  443.6 36.3 %while.108 = (s32[]{:T(128)}, f32[2,1536]{1,0:T(2,128)}, f32[2,1536]{1,0:T(2,128)}, s32[1536]{0:T(1024)}, s32[1536]{0:T(1024)}, /*index=5*/s32[1,1536]{1,0:T(1,1...) while((s32[]{:T(128)}, f32[2,1536]{1,0:T(2,128)}, ...), condition=%wide.region_19.20_spmd.clone.clone, body=%wide.region_16.19_spmd.clone.clone.sunk | while | flops 224935440 | bytes 25523588 | solution.py:95
  481.9 34.1 %while.109 = (s32[]{:T(128)}, f32[1536,2,64]{0,2,1:T(8,128)S(1)}, f32[1536,2,64]{0,2,1:T(8,128)S(1)}, bf16[1536,128]{0,1:T(8,128)(2,1)S(1)}, s32[1536]{0:T(1024)...) while((s32[]{:T(128)}, f32[1536,2,64]{0,2,1:T(8,128)S(1)}, ...), condition=%wide.region_21.22_spmd.clone.clone, body=%wide.region_20.21_spmd.clone.clone.sunk | while | flops 626786816 | bytes 31307092 | solution.py:95
  516.9 3.6 convolution_convert_fusion
  520.6 19.5 %all_gather.107 = bf16[2,192,1024]{2,1,0:T(8,128)(2,1)} all-gather(bf16[1,192,1024]{2,1,0:T(8,128)(2,1)} %param.28), channel_id=1, replica_groups=mesh['grp'=16,'ctx_0'=2,'ctx_1'=4] {'ctx_0'}, dimensions={0}, use_global_device_ids=true | all-gather | bytes 1179648 | tf_op jit(solution)/shard_map/all_gather | solution.py:30
  540.3 61.3 %reduce-scatter.13.cloned.1.call-done = bf16[192,1024]{1,0:T(8,128)(2,1)} async-done(((bf16[1536,1024]{1,0:T(8,128)(2,1)}), bf16[192,1024]{1,0:T(8,128)(2,1)}) %reduce-scatter.13.cloned.1.call-update) | async-done | bytes 393232 | tf_op jit(solution)/shard_map/reduce_scatter | solution.py:243
  604.5 11.1 all-gather.5
  617.0 25.9 %all-gather.31.cloned.1.call-done = bf16[8,192,1024]{2,1,0:T(8,128)(2,1)} async-done(((bf16[2,192,1024]{2,1,0:T(8,128)(2,1)}), bf16[8,192,1024]{2,1,0:T(8,128)(2,1)}) %all-gather.31.cloned.1.call-update) | async-done | bytes 3145744 | tf_op jit(solution)/shard_map/all_gather | solution.py:30
  643.0 3.9 copy.261
  646.8 37.6 %all-gather.29.cloned.1.call-done = bf16[8,192,1024]{2,1,0:T(8,128)(2,1)} async-done(((bf16[2,192,1024]{2,1,0:T(8,128)(2,1)}), bf16[8,192,1024]{2,1,0:T(8,128)(2,1)}) %all-gather.29.cloned.1.call-update) | async-done | bytes 3145744 | tf_op jit(solution)/shard_map/all_gather | solution.py:30
  691.6 4.4 convert_reduce_fusion
  700.8 5.9 convolution_convert_fusion.6
  706.8 72.5 %reduce-scatter.17.cloned.1.call-done = bf16[192,1024]{1,0:T(8,128)(2,1)} async-done(((bf16[1536,1024]{1,0:T(8,128)(2,1)}), bf16[192,1024]{1,0:T(8,128)(2,1)}) %reduce-scatter.17.cloned.1.call-update) | async-done | bytes 393232 | tf_op jit(solution)/shard_map/reduce_scatter | solution.py:243
  782.5 78.7 %reduce-scatter.15.cloned.1.call-done = bf16[192,1024]{1,0:T(8,128)(2,1)} async-done(((bf16[1536,1024]{1,0:T(8,128)(2,1)}), bf16[192,1024]{1,0:T(8,128)(2,1)}) %reduce-scatter.15.cloned.1.call-update) | async-done | bytes 393232 | tf_op jit(solution)/shard_map/reduce_scatter | solution.py:243
  865.4 11.1 all-gather.8
  876.9 39.9 %all-gather.33.cloned.1.call-done = bf16[8,192,1024]{2,1,0:T(8,128)(2,1)} async-done(((bf16[2,192,1024]{2,1,0:T(8,128)(2,1)}), bf16[8,192,1024]{2,1,0:T(8,128)(2,1)}) %all-gather.33.cloned.1.call-update) | async-done | bytes 3145744 | tf_op jit(solution)/shard_map/all_gather | solution.py:30
  922.7 38.2 %while.110 = (s32[]{:T(128)}, f32[1536,2,64]{0,2,1:T(8,128)}, f32[1536,128]{0,1:T(8,128)}, f32[1536,128]{0,1:T(8,128)}, bf16[1536,128]{0,1:T(8,128)(2,1)}, /*ind...) while((s32[]{:T(128)}, f32[1536,2,64]{0,2,1:T(8,128)}, ...), condition=%wide.region_31.32_spmd.clone.clone, body=%wide.region_30.31_spmd.clone.clone.sunk | while | flops 1027867136 | bytes 61285828 | solution.py:95
  970.5 78.5 %reduce-scatter.19.cloned.1.call-done = bf16[192,1024]{1,0:T(8,128)(2,1)} async-done(((bf16[1536,1024]{1,0:T(8,128)(2,1)}), bf16[192,1024]{1,0:T(8,128)(2,1)}) %reduce-scatter.19.cloned.1.call-update) | async-done | bytes 393232 | tf_op jit(solution)/shard_map/reduce_scatter | solution.py:243
  1054.6 11.1 all-gather.10
  1065.7 40.4 %all-gather.35.cloned.1.call-done = bf16[8,192,1024]{2,1,0:T(8,128)(2,1)} async-done(((bf16[2,192,1024]{2,1,0:T(8,128)(2,1)}), bf16[8,192,1024]{2,1,0:T(8,128)(2,1)}) %all-gather.35.cloned.1.call-update) | async-done | bytes 3145744 | tf_op jit(solution)/shard_map/all_gather | solution.py:30
  1109.9 4.4 convert_reduce_fusion.1
  1115.4 3.5 convolution_convert_fusion.3
  1119.0 78.4 %reduce-scatter.21.cloned.1.call-done = bf16[192,1024]{1,0:T(8,128)(2,1)} async-done(((bf16[1536,1024]{1,0:T(8,128)(2,1)}), bf16[192,1024]{1,0:T(8,128)(2,1)}) %reduce-scatter.21.cloned.1.call-update) | async-done | bytes 393232 | tf_op jit(solution)/shard_map/reduce_scatter | solution.py:243
  1203.2 11.1 all-gather.12
  1214.6 40.2 %all-gather.37.cloned.1.call-done = bf16[8,192,1024]{2,1,0:T(8,128)(2,1)} async-done(((bf16[2,192,1024]{2,1,0:T(8,128)(2,1)}), bf16[8,192,1024]{2,1,0:T(8,128)(2,1)}) %all-gather.37.cloned.1.call-update) | async-done | bytes 3145744 | tf_op jit(solution)/shard_map/all_gather | solution.py:30
  1259.8 46.8 %while.111 = (s32[]{:T(128)}, f32[1536,2,64]{0,2,1:T(8,128)S(1)}, f32[1536,128]{0,1:T(8,128)S(1)}, f32[1536,128]{0,1:T(8,128)S(1)}, bf16[1536,128]{0,1:T(8,128)(...) while((s32[]{:T(128)}, f32[1536,2,64]{0,2,1:T(8,128)S(1)}, ...), condition=%wide.region_40.41_spmd.clone.clone, body=%wide.region_39.40_spmd.clone.clone.sunk | while | flops 1027867136 | bytes 42509712 | solution.py:95
  1313.3 4.2 fusion.73
  1322.4 5.6 all-to-all-start.8
  1329.1 3.8 fusion.77
  1334.5 10.7 all-to-all-done.8
  1345.2 7.0 all-to-all-start.6
  1352.3 5.9 fusion.75
  1360.8 5.2 fusion.72
  1366.0 3.6 reduce.54
  1372.2 6.6 all-to-all-start.7
  1384.7 3.7 fusion.76
  1393.2 8.4 all-to-all-start.5
  1401.7 4.9 fusion.74
  1406.6 5.8 reshape.1519
  1426.2 13.0 all_to_all.138
  1451.5 3.9 all-to-all-done.3
  1455.5 55.5 %all-reduce = (bf16[1,128]{1,0:T(2,128)(2,1)S(1)}, bf16[1,128]{1,0:T(2,128)(2,1)S(1)}, bf16[1,128]{1,0:T(2,128)(2,1)S(1)}, bf16[1,128]{1,0:T(2,128)(2,1)S(1)}, b...) all-reduce(bf16[1,128]{1,0:T(2,128)(2,1)S(1)} %bitcast.721, ...), channel_id=1, replica_groups=mesh['grp'=16,'ctx_0'=2,'ctx_1'=4] {'grp'}, use_global_device_ids=true, to_apply=%region_65.66 | all-reduce | flops 3072 | bytes 12288 | tf_op jit(solution)/shard_map/psum | solution.py:465
  1515.5 72.1 %all-reduce.4.cloned.1.call-done = (bf16[1,128,3072]{2,1,0:T(8,128)(2,1)}, bf16[1,128,3072]{2,1,0:T(8,128)(2,1)}, bf16[1,128,1024]{2,1,0:T(8,128)(2,1)}, bf16[1,...) async-done(((bf16[1,128,3072]{2,1,0:T(8,128)(2,1)}, ...) | async-done | bytes 6291472 | tf_op jit(solution)/shard_map/psum | solution.py:467
  1587.7 3.8 maximum_convert_fusion
  1591.5 5.8 copy.277
  (832 shorter events, 367.3 us)
Async XLA Ops:
  7.2 38.1 %copy-start.48 = (bf16[2,128,3072]{2,1,0:T(8,128)(2,1)S(1)}, bf16[2,128,3072]{2,1,0:T(8,128)(2,1)}, u32[]{:S(2)}) copy-start(bf16[2,128,3072]{2,1,0:T(8,128)(2,1)} %param.32) | copy-start | bytes 4718596
  17.4 15.2 all-to-all-start
  25.9 71.7 %all-gather.23.cloned.1.call-start = ((), (), s32[]{:S(2)}) async-start(), calls=%async_computation.25 | async-start | bytes 3932160 | tf_op jit(solution)/shard_map/all_gather | solution.py:30
  33.2 188.9 %copy-start.76 = (f32[1024]{0:T(1024)}, f32[1024]{0:T(1024)S(1)}, u32[]{:S(2)}) copy-start(f32[1024]{0:T(1024)S(1)} %get-tuple-element.2007) | copy-start | bytes 12292
  33.2 188.9 %copy-start.82 = (f32[1024]{0:T(1024)}, f32[1024]{0:T(1024)S(1)}, u32[]{:S(2)}) copy-start(f32[1024]{0:T(1024)S(1)} %get-tuple-element.2006) | copy-start | bytes 12292
  47.4 21.3 %all-to-all-start.1 = ((bf16[2,128,3,8,128]{1,4,2,0,3:T(8,128)(2,1)}), bf16[2,128,3,8,128]{1,4,2,0,3:T(8,128)(2,1)S(1)}, u32[]{:S(2)}, u32[]{:S(2)}) async-start(bf16[2,128,3,8,128]{1,4,2,0,3:T(8,128)(2,1)} %copy.252), calls=%async_computation.1 | async-start | bytes 3145728 | tf_op jit(solution)/shard_map/all_to_all | solution.py:521
  51.0 168.5 %reduce-scatter.9.cloned.1.call-start = ((), (), s32[]{:S(2)}) async-start(), calls=%async_computation.17 | async-start | bytes 3538944 | tf_op jit(solution)/shard_map/reduce_scatter | solution.py:243
  70.2 29.6 %copy-start.69 = (bf16[1,8,128,3,1,128]{2,1,5,3,4,0:T(8,128)(2,1)}, bf16[1,8,128,3,1,128]{2,1,5,3,4,0:T(8,128)(2,1)S(1)}, u32[]{:S(2)}) copy-start(bf16[1,8,128,3,1,128]{2,1,5,3,4,0:T(8,128)(2,1)S(1)} %copy.253) | copy-start | bytes 2359300
  137.9 81.7 %copy-start.2 = (bf16[1,192,1024]{2,1,0:T(8,128)(2,1)S(1)}, bf16[1,192,1024]{2,1,0:T(8,128)(2,1)}, u32[]{:S(2)}) copy-start(bf16[1,192,1024]{2,1,0:T(8,128)(2,1)} %param.27) | copy-start | bytes 1179652
  141.8 155.6 %all-gather.25.cloned.1.call-start = ((), (), s32[]{:S(2)}) async-start(), calls=%async_computation.26 | async-start | bytes 3932160 | tf_op jit(solution)/shard_map/all_gather | solution.py:30
  241.7 37.3 %all-to-all-start.2 = ((bf16[2,128,1,8,512]{1,4,0,2,3:T(8,128)(2,1)}), bf16[2,128,1,8,512]{1,4,0,2,3:T(8,128)(2,1)}, u32[]{:S(2)}, u32[]{:S(2)}) async-start(bf16[2,128,1,8,512]{1,4,0,2,3:T(8,128)(2,1)} %copy.256), calls=%async_computation.3 | async-start | bytes 4194304 | tf_op jit(solution)/shard_map/all_to_all | solution.py:528
  246.0 139.5 %reduce-scatter.11.cloned.1.call-start = ((), (), s32[]{:S(2)}) async-start(), calls=%async_computation.18 | async-start | bytes 3538944 | tf_op jit(solution)/shard_map/reduce_scatter | solution.py:243
  306.9 78.5 %copy-start.14 = (bf16[192,1024]{1,0:T(8,128)(2,1)S(1)}, bf16[192,1024]{1,0:T(8,128)(2,1)}, u32[]{:S(2)}) copy-start(bf16[192,1024]{1,0:T(8,128)(2,1)} %reduce-scatter.9.cloned.1.call-done) | copy-start | bytes 1179652
  306.9 78.5 %copy-start.77 = (f32[1024]{0:T(1024)S(1)}, f32[1024]{0:T(1024)}, u32[]{:S(2)}) copy-start(f32[1024]{0:T(1024)} %copy-done.76) | copy-start | bytes 12292
  307.0 78.5 %copy-start.108 = (f32[1024]{0:T(1024)S(1)}, f32[1024]{0:T(1024)}, u32[]{:S(2)}) copy-start(f32[1024]{0:T(1024)} %get-tuple-element.2004) | copy-start | bytes 12292
  307.0 80.1 %copy-start.87 = (f32[1024]{0:T(1024)S(1)}, f32[1024]{0:T(1024)}, u32[]{:S(2)}) copy-start(f32[1024]{0:T(1024)} %get-tuple-element.2003) | copy-start | bytes 12292
  307.0 80.1 %copy-start.107 = (f32[1024]{0:T(1024)S(1)}, f32[1024]{0:T(1024)}, u32[]{:S(2)}) copy-start(f32[1024]{0:T(1024)} %get-tuple-element.2002) | copy-start | bytes 12292
  307.0 91.5 %copy-start.45 = (bf16[1,8,128,3,1,128]{2,5,3,0,1,4:T(8,128)(2,1)S(1)}, bf16[1,8,128,3,1,128]{2,5,3,0,1,4:T(8,128)(2,1)}, u32[]{:S(2)}) copy-start(bf16[1,8,128,3,1,128]{2,5,3,0,1,4:T(8,128)(2,1)} %get-tuple-element.1993) | copy-start | bytes 2359300
  307.0 131.8 %all-gather.27.cloned.1.call-start = ((), (), s32[]{:S(2)}) async-start(), calls=%async_computation.27 | async-start | bytes 3932160 | tf_op jit(solution)/shard_map/all_gather | solution.py:30
  398.4 203.2 %reduce-scatter.13.cloned.1.call-start = ((), (), s32[]{:S(2)}) async-start(), calls=%async_computation.19 | async-start | bytes 3538944 | tf_op jit(solution)/shard_map/reduce_scatter | solution.py:243
  520.6 122.4 %all-gather.31.cloned.1.call-start = ((), (), s32[]{:S(2)}) async-start(), calls=%async_computation.29 | async-start | bytes 3932160 | tf_op jit(solution)/shard_map/all_gather | solution.py:30
  540.1 144.4 %all-gather.29.cloned.1.call-start = ((), (), s32[]{:S(2)}) async-start(), calls=%async_computation.28 | async-start | bytes 3932160 | tf_op jit(solution)/shard_map/all_gather | solution.py:30
  615.6 163.7 %reduce-scatter.17.cloned.1.call-start = ((), (), s32[]{:S(2)}) async-start(), calls=%async_computation.21 | async-start | bytes 3538944 | tf_op jit(solution)/shard_map/reduce_scatter | solution.py:243
  700.7 160.5 %reduce-scatter.15.cloned.1.call-start = ((), (), s32[]{:S(2)}) async-start(), calls=%async_computation.20 | async-start | bytes 3538944 | tf_op jit(solution)/shard_map/reduce_scatter | solution.py:243
  706.7 210.2 %all-gather.33.cloned.1.call-start = ((), (), s32[]{:S(2)}) async-start(), calls=%async_computation.30 | async-start | bytes 3932160 | tf_op jit(solution)/shard_map/all_gather | solution.py:30
  876.5 172.5 %reduce-scatter.19.cloned.1.call-start = ((), (), s32[]{:S(2)}) async-start(), calls=%async_computation.22 | async-start | bytes 3538944 | tf_op jit(solution)/shard_map/reduce_scatter | solution.py:243
  970.4 78.6 %copy-start.88 = (f32[1024]{0:T(1024)S(1)}, f32[1024]{0:T(1024)}, u32[]{:S(2)}) copy-start(f32[1024]{0:T(1024)} %get-tuple-element.2003) | copy-start | bytes 12292
  970.4 78.6 %copy-start.96 = (f32[192]{0:T(256)S(1)}, f32[192]{0:T(256)}, u32[]{:S(2)}) copy-start(f32[192]{0:T(256)} %copy-done.95) | copy-start | bytes 2308
  970.4 79.9 %copy-start.121 = (f32[192]{0:T(256)S(1)}, f32[192]{0:T(256)}, u32[]{:S(2)}) copy-start(f32[192]{0:T(256)} %copy-done.120) | copy-start | bytes 2308
  970.4 79.9 %copy-start.106 = (f32[192]{0:T(256)S(1)}, f32[192]{0:T(256)}, u32[]{:S(2)}) copy-start(f32[192]{0:T(256)} %copy-done.105) | copy-start | bytes 2308
  970.4 81.9 %copy-start.28 = (f32[192,1024]{1,0:T(8,128)S(1)}, f32[192,1024]{1,0:T(8,128)}, u32[]{:S(2)}) copy-start(f32[192,1024]{1,0:T(8,128)} %copy-done.27) | copy-start | bytes 2359300
  970.4 81.9 %copy-start.30 = (bf16[1,192,1024]{2,1,0:T(8,128)(2,1)S(1)}, bf16[1,192,1024]{2,1,0:T(8,128)(2,1)}, u32[]{:S(2)}) copy-start(bf16[1,192,1024]{2,1,0:T(8,128)(2,1)} %param.28) | copy-start | bytes 1179652
  970.5 135.6 %all-gather.35.cloned.1.call-start = ((), (), s32[]{:S(2)}) async-start(), calls=%async_computation.31 | async-start | bytes 3932160 | tf_op jit(solution)/shard_map/all_gather | solution.py:30
  1054.6 146.5 %copy-start.25 = (f32[192,1024]{1,0:T(8,128)}, f32[192,1024]{1,0:T(8,128)S(1)}, u32[]{:S(2)}) copy-start(f32[192,1024]{1,0:T(8,128)S(1)} %get-tuple-element.1956) | copy-start | bytes 2359300
  1065.7 131.8 %reduce-scatter.21.cloned.1.call-start = ((), (), s32[]{:S(2)}) async-start(), calls=%async_computation.23 | async-start | bytes 3538944 | tf_op jit(solution)/shard_map/reduce_scatter | solution.py:243
  1118.9 78.6 %copy-start.3 = (bf16[1,192,1024]{2,1,0:T(8,128)(2,1)S(1)}, bf16[1,192,1024]{2,1,0:T(8,128)(2,1)}, u32[]{:S(2)}) copy-start(bf16[1,192,1024]{2,1,0:T(8,128)(2,1)} %param.27) | copy-start | bytes 1179652
  1118.9 78.6 %copy-start.15 = (bf16[192,1024]{1,0:T(8,128)(2,1)S(1)}, bf16[192,1024]{1,0:T(8,128)(2,1)}, u32[]{:S(2)}) copy-start(bf16[192,1024]{1,0:T(8,128)(2,1)} %reduce-scatter.9.cloned.1.call-done) | copy-start | bytes 1179652
  1118.9 78.6 %copy-start.78 = (f32[1024]{0:T(1024)S(1)}, f32[1024]{0:T(1024)}, u32[]{:S(2)}) copy-start(f32[1024]{0:T(1024)} %copy-done.76) | copy-start | bytes 12292
  1118.9 78.6 %copy-start.83 = (f32[1024]{0:T(1024)S(1)}, f32[1024]{0:T(1024)}, u32[]{:S(2)}) copy-start(f32[1024]{0:T(1024)} %copy-done.82) | copy-start | bytes 12292
  1118.9 78.6 %copy-start.91 = (f32[192]{0:T(256)S(1)}, f32[192]{0:T(256)}, u32[]{:S(2)}) copy-start(f32[192]{0:T(256)} %copy-done.90) | copy-start | bytes 2308
  1118.9 79.9 %copy-start.119 = (f32[192]{0:T(256)S(1)}, f32[192]{0:T(256)}, u32[]{:S(2)}) copy-start(f32[192]{0:T(256)} %copy-done.118) | copy-start | bytes 2308
  1118.9 79.9 %copy-start.98 = (f32[192]{0:T(256)S(1)}, f32[192]{0:T(256)}, u32[]{:S(2)}) copy-start(f32[192]{0:T(256)} %copy-done.97) | copy-start | bytes 2308
  1119.0 135.8 %all-gather.37.cloned.1.call-start = ((), (), s32[]{:S(2)}) async-start(), calls=%async_computation.32 | async-start | bytes 3932160 | tf_op jit(solution)/shard_map/all_gather | solution.py:30
  1198.9 55.9 %copy-start.101 = (f32[192]{0:T(256)}, f32[192]{0:T(256)S(1)}, u32[]{:S(2)}) copy-start(f32[192]{0:T(256)S(1)} %multiply_multiply_fusion.5) | copy-start | bytes 2308
  1201.0 53.7 %copy-start.114 = (f32[192]{0:T(256)}, f32[192]{0:T(256)S(1)}, u32[]{:S(2)}) copy-start(f32[192]{0:T(256)S(1)} %negate_multiply_fusion.1) | copy-start | bytes 2308
  1214.3 225.8 %reduce-scatter.23.cloned.1.call-start = ((), (), s32[]{:S(2)}) async-start(), calls=%async_computation.24 | async-start | bytes 3538944 | tf_op jit(solution)/shard_map/reduce_scatter | solution.py:243
  1322.4 22.8 %all-to-all-start.8 = ((bf16[8,2,32768]{2,1,0:T(2,128)(2,1)}), bf16[8,2,32768]{2,1,0:T(2,128)(2,1)S(1)}, u32[]{:S(2)}, u32[]{:S(2)}) async-start(bf16[8,2,32768]{2,1,0:T(2,128)(2,1)} %reshape.1516), calls=%async_computation.16 | async-start | bytes 2097152 | tf_op jit(solution)/shard_map/all_to_all | solution.py:432
  1345.2 27.0 %all-to-all-start.6 = ((bf16[1024,3,1,128]{3,1,2,0:T(4,128)(2,1)}), bf16[1024,3,1,128]{3,1,2,0:T(4,128)(2,1)}, u32[]{:S(2)}, u32[]{:S(2)}) async-start(bf16[1024,3,1,128]{3,1,2,0:T(4,128)(2,1)} %copy.271), calls=%async_computation.14 | async-start | bytes 2097152 | tf_op jit(solution)/shard_map/all_to_all | solution.py:425
  1372.2 21.1 %all-to-all-start.7 = ((bf16[8,2,32768]{2,1,0:T(2,128)(2,1)}), bf16[8,2,32768]{2,1,0:T(2,128)(2,1)}, u32[]{:S(2)}, u32[]{:S(2)}) async-start(bf16[8,2,32768]{2,1,0:T(2,128)(2,1)} %reshape.1518), calls=%async_computation.15 | async-start | bytes 2097152 | tf_op jit(solution)/shard_map/all_to_all | solution.py:432
  1393.2 26.7 %all-to-all-start.5 = ((bf16[1024,3,1,128]{3,1,2,0:T(4,128)(2,1)}), bf16[1024,3,1,128]{3,1,2,0:T(4,128)(2,1)}, u32[]{:S(2)}, u32[]{:S(2)}) async-start(bf16[1024,3,1,128]{3,1,2,0:T(4,128)(2,1)} %copy.268), calls=%async_computation.13 | async-start | bytes 2097152 | tf_op jit(solution)/shard_map/all_to_all | solution.py:425
  1401.6 186.1 %all-reduce.4.cloned.1.call-start = ((), (), s32[]{:S(2)}) async-start(), calls=%async_computation.33 | async-start | bytes 12582912 | tf_op jit(solution)/shard_map/psum | solution.py:467
  1424.3 19.8 %copy-start.126 = (bf16[1024]{0:T(1024)(128)(2,1)S(1)}, bf16[1024]{0:T(1024)(128)(2,1)}, u32[]{:S(2)}) copy-start(bf16[1024]{0:T(1024)(128)(2,1)} %get-tuple-element.1750) | copy-start | bytes 6148
  1424.3 19.8 %copy-start.127 = (bf16[1024]{0:T(1024)(128)(2,1)S(1)}, bf16[1024]{0:T(1024)(128)(2,1)}, u32[]{:S(2)}) copy-start(bf16[1024]{0:T(1024)(128)(2,1)} %get-tuple-element.1996) | copy-start | bytes 6148
  1424.3 19.9 %copy-start.125 = (bf16[1024]{0:T(1024)(128)(2,1)S(1)}, bf16[1024]{0:T(1024)(128)(2,1)}, u32[]{:S(2)}) copy-start(bf16[1024]{0:T(1024)(128)(2,1)} %get-tuple-element.1954) | copy-start | bytes 6148
  1424.3 24.5 %copy-start.16 = (bf16[192,1024]{1,0:T(8,128)(2,1)S(1)}, bf16[192,1024]{1,0:T(8,128)(2,1)}, u32[]{:S(2)}) copy-start(bf16[192,1024]{1,0:T(8,128)(2,1)} %reduce-scatter.9.cloned.1.call-done) | copy-start | bytes 1179652
  1424.3 24.5 %copy-start.26 = (f32[192,1024]{1,0:T(8,128)S(1)}, f32[192,1024]{1,0:T(8,128)}, u32[]{:S(2)}) copy-start(f32[192,1024]{1,0:T(8,128)} %copy-done.25) | copy-start | bytes 2359300
  1424.3 24.5 %copy-start.32 = (bf16[192,1024]{1,0:T(8,128)(2,1)S(1)}, bf16[192,1024]{1,0:T(8,128)(2,1)}, u32[]{:S(2)}) copy-start(bf16[192,1024]{1,0:T(8,128)(2,1)} %reduce-scatter.21.cloned.1.call-done) | copy-start | bytes 1179652
  1424.4 24.5 %copy-start.79 = (f32[1024]{0:T(1024)S(1)}, f32[1024]{0:T(1024)}, u32[]{:S(2)}) copy-start(f32[1024]{0:T(1024)} %copy-done.76) | copy-start | bytes 12292
  1424.4 24.5 %copy-start.84 = (f32[1024]{0:T(1024)S(1)}, f32[1024]{0:T(1024)}, u32[]{:S(2)}) copy-start(f32[1024]{0:T(1024)} %copy-done.82) | copy-start | bytes 12292
  1424.4 24.5 %copy-start.92 = (f32[192]{0:T(256)S(1)}, f32[192]{0:T(256)}, u32[]{:S(2)}) copy-start(f32[192]{0:T(256)} %copy-done.90) | copy-start | bytes 2308
  1424.4 24.5 %copy-start.99 = (f32[192]{0:T(256)S(1)}, f32[192]{0:T(256)}, u32[]{:S(2)}) copy-start(f32[192]{0:T(256)} %copy-done.97) | copy-start | bytes 2308
  1424.4 24.5 %copy-start.102 = (f32[192]{0:T(256)S(1)}, f32[192]{0:T(256)}, u32[]{:S(2)}) copy-start(f32[192]{0:T(256)} %copy-done.101) | copy-start | bytes 2308
  1424.4 24.5 %copy-start.115 = (f32[192]{0:T(256)S(1)}, f32[192]{0:T(256)}, u32[]{:S(2)}) copy-start(f32[192]{0:T(256)} %copy-done.114) | copy-start | bytes 2308
  1445.5 9.9 all-to-all-start.3
  (139 other events, 642.1 us)
Sparse Core Ops, SparseCore 0:
  45.4 52.1 all-gather.22
  141.9 77.6 reduce-scatter.8
  234.6 62.7 all-gather.24
  307.1 78.3 reduce-scatter.10
  398.5 40.2 all-gather.26
  520.7 80.8 reduce-scatter.12
  603.2 39.6 all-gather.30
  644.6 39.7 all-gather.28
  700.8 78.4 reduce-scatter.16
  783.0 78.1 reduce-scatter.14
  876.6 40.2 all-gather.32
  970.6 78.3 reduce-scatter.18
  1065.8 40.2 all-gather.34
  1119.1 78.3 reduce-scatter.20
  1214.5 40.2 all-gather.36
  1311.6 94.6 reduce-scatter.22
  1423.6 164.0 all-reduce.3
where the time goes:
time: 1620 us; the launch traced here: 1610 us
  waiting for transfers between devices  931 us (57%)
  blocking collectives  165 us (10%)
  matrix products  156 us (10%)
  local copies, waits for them, and re-layouts  147 us (9%)
  other arithmetic  144 us (9%)
  starting transfers between devices  49.2 us (3%)
  between operations  16.3 us (1%)
    reduce_scatter x8, waiting for transfers between devices, scatter_rows(): lax.psum_scatter(partial_value.astype(jnp.bfloat16), CTX, scatter_dimensi...  525 us
    all_gather x8, waiting for transfers between devices, gather_in_order(): blocks = lax.all_gather(blocks, axes[k])  262 us
    all_gather x8, blocking collectives, gather_in_order(): blocks = lax.all_gather(blocks, axes[k])  96.7 us
    psum x1, waiting for transfers between devices, reduce_tensor(): lax.psum(input_rows.astype(jnp.bfloat16), 'grp').astype(jnp.float32)  72.1 us
    psum x1, blocking collectives, reduce_tensor(): lax.psum(small[0].astype(jnp.bfloat16), 'grp').astype(jnp.float32)  55.5 us
    unnamed x306, local copies, waits for them, and re-layouts  53.1 us
    dot_general x18, matrix products, block_scores(): jnp.einsum('qhd,khd->hqk', query_heads, key_heads, preferred_element_type...  41.6 us
  transfers between devices with their start and end apart: 25, of which 22 were waited for; matrix products, arithmetic and copies ran while one was open for 8% of the time, Pallas kernels for 0%

commit v1 on v0

v1 whole, which is shorter than its diff:
```python
import functools

import jax
import jax.numpy as jnp
from jax import lax
from jax.experimental import pallas as pl
from jax.experimental.pallas import tpu as pltpu
from jax.sharding import Mesh
from jax.sharding import PartitionSpec as P

D = 1024
HEADS = 16
HEAD_DIM = 64
FF = 4096
PROMPT = 1024
TOKENS = 1536
PIECE = 192
LAYERS = 2
TILE = 256
HALF = 4 * PIECE
SCALE = HEAD_DIM ** (-0.5)
masked_value = -1e30

GRP = ("x", "y_lo", "core")
CTX = ("y_hi", "z")
bf16 = jnp.bfloat16
f32 = jnp.float32


def shift_z(value, step):
    return lax.ppermute(value, "z", [(i, (i + step) % 4) for i in range(4)])


def shift_x(value, step):
    return lax.ppermute(value, "x", [(i, (i + step) % 4) for i in range(4)])


def swap(value, axis):
    return lax.ppermute(value, axis, [(0, 1), (1, 0)])


def gather_z(rows):
    return jnp.concatenate([rows] + [shift_z(rows, k) for k in (1, 2, 3)], axis=0)


def scatter_z(own, others):
    total = own
    for k in (1, 2, 3):
        block = others[(k - 1) * PIECE : k * PIECE]
        total = total + shift_z(block, -k).astype(f32)
    return total


def dot(left, right):
    return jnp.dot(left, right, preferred_element_type=f32)


def dot_t(left, right):
    return lax.dot_general(left, right, (((1,), (1,)), ((), ())), preferred_element_type=f32)


def outer(left, right):
    return lax.dot_general(left, right, (((0,), (0,)), ((), ())), preferred_element_type=f32)


def dot_scatter(left, weight, product):
    others = product(left[PIECE:], weight).astype(bf16)
    own = product(left[:PIECE], weight)
    return scatter_z(own, others)


def tile_mask(block, low, high, cut):
    keys = lax.broadcasted_iota(jnp.int32, (high - low, TILE), 0) + low
    queries = lax.broadcasted_iota(jnp.int32, (high - low, TILE), 1) + block * TILE
    visible = keys <= queries
    if block * TILE >= PROMPT:
        visible = visible & ((keys >= cut) | (queries < cut))
    return visible


def fill_bias(bias, slopes, cut):
    keys = lax.broadcasted_iota(jnp.int32, (TOKENS, 128), 0)
    places = jnp.where(keys >= cut, keys - cut + PROMPT, keys).astype(f32)
    for h in range(2):
        bias[h] = places * slopes[h]


def scores_t(keys, queries, bias, block, high, cut):
    low = min(block * TILE, PROMPT)
    scores = dot_t(keys, queries)
    scores = scores + jnp.concatenate([bias[0:high], bias[0:high]], axis=1)
    tail = jnp.where(tile_mask(block, low, high, cut), scores[low:high], masked_value)
    if low == 0:
        return tail
    return jnp.concatenate([scores[:low], tail], axis=0)


def piece_places(info):
    y, z = info[0], info[1]
    out = []
    for side in range(2):
        y_of = y if side == 0 else 1 - y
        for k in range(4):
            out.append(pl.multiple_of((y_of * 4 + ((z - k) & 3)) * PIECE, 64))
    return out


def attend_kernel(info, slopes, mine, other, ctx_mine, ctx_other, logsum, rows, ctx, vt, bias):
    spots = piece_places(info)
    cut = info[2]
    for k in range(4):
        span = slice(k * PIECE, (k + 1) * PIECE)
        rows[pl.ds(spots[k], PIECE), :] = mine[span, :]
        rows[pl.ds(spots[4 + k], PIECE), :] = other[span, :]
    fill_bias(bias, slopes, cut)
    vt[...] = rows[:, 256:384].astype(f32).T.astype(bf16)
    for block in range(TOKENS // TILE):
        high = (block + 1) * TILE
        span = slice(block * TILE, high)
        parts = []
        for h in range(2):
            lanes = slice(h * HEAD_DIM, (h + 1) * HEAD_DIM)
            key_lanes = slice(128 + h * HEAD_DIM, 128 + (h + 1) * HEAD_DIM)
            queries = rows[span, lanes] * jnp.asarray(SCALE, bf16)
            scores = scores_t(rows[0:high, key_lanes], queries, bias[h], block, high, cut)
            top = jnp.max(scores, axis=0, keepdims=True)
            weights = jnp.exp(scores - top)
            total = jnp.sum(weights, axis=0, keepdims=True)
            found = dot(vt[lanes, 0:high], weights.astype(bf16))
            parts.append(found * (1.0 / total))
            logsum[h : h + 1, span] = top + jnp.log(total)
        ctx[span, :] = jnp.concatenate(parts, axis=0).T.astype(bf16)
    for k in range(4):
        span = slice(k * PIECE, (k + 1) * PIECE)
        ctx_mine[span, :] = ctx[pl.ds(spots[k], PIECE), :]
        ctx_other[span, :] = ctx[pl.ds(spots[4 + k], PIECE), :]


def attend_back_kernel(
    info, slopes, rows, mine, other, logsum, out_mine, out_other, sums, grad, kt, bias, dq, dk, dv, out
):
    spots = piece_places(info)
    cut = info[2]
    for k in range(4):
        span = slice(k * PIECE, (k + 1) * PIECE)
        grad[pl.ds(spots[k], PIECE), :] = mine[span, :]
        grad[pl.ds(spots[4 + k], PIECE), :] = other[span, :]
    fill_bias(bias, slopes, cut)
    kt[...] = rows[:, 128:256].astype(f32).T.astype(bf16)
    dk[...] = jnp.zeros_like(dk)
    dv[...] = jnp.zeros_like(dv)
    for block in range(TOKENS // TILE):
        high = (block + 1) * TILE
        span = slice(block * TILE, high)
        parts = []
        for h in range(2):
            lanes = slice(h * HEAD_DIM, (h + 1) * HEAD_DIM)
            key_lanes = slice(128 + h * HEAD_DIM, 128 + (h + 1) * HEAD_DIM)
            value_lanes = slice(256 + h * HEAD_DIM, 256 + (h + 1) * HEAD_DIM)
            queries = rows[span, lanes] * jnp.asarray(SCALE, bf16)
            grads = grad[span, lanes]
            scores = scores_t(rows[0:high, key_lanes], queries, bias[h], block, high, cut)
            weights = jnp.exp(scores - logsum[h : h + 1, span])
            d_weights = dot_t(rows[0:high, value_lanes], grads)
            correction = jnp.sum(weights * d_weights, axis=0, keepdims=True)
            d_scores = (weights * (d_weights - correction)).astype(bf16)
            dv[h, 0:high, :] += dot(weights.astype(bf16), grads)
            dk[h, 0:high, :] += dot(d_scores, queries)
            parts.append(dot(kt[lanes, 0:high], d_scores))
        dq[span, :] = (jnp.concatenate(parts, axis=0) * SCALE).T
    out[:, 0:128] = dq[...].astype(bf16)
    out[:, 128:256] = jnp.concatenate([dk[0], dk[1]], axis=1).astype(bf16)
    out[:, 256:384] = jnp.concatenate([dv[0], dv[1]], axis=1).astype(bf16)
    sums[...] = jnp.sum(out[...].astype(f32), axis=0, keepdims=True)
    for k in range(4):
        span = slice(k * PIECE, (k + 1) * PIECE)
        out_mine[span, :] = out[pl.ds(spots[k], PIECE), :]
        out_other[span, :] = out[pl.ds(spots[4 + k], PIECE), :]


smem = pl.BlockSpec(memory_space=pltpu.SMEM)
vmem = pl.BlockSpec(memory_space=pltpu.VMEM)
LIMIT = 40 * 2**20


def attend(info, slopes, mine, other):
    return pl.pallas_call(
        attend_kernel,
        out_shape=(
            jax.ShapeDtypeStruct((HALF, 128), bf16),
            jax.ShapeDtypeStruct((HALF, 128), bf16),
            jax.ShapeDtypeStruct((2, TOKENS), f32),
            jax.ShapeDtypeStruct((TOKENS, 384), bf16),
        ),
        in_specs=[smem, smem, vmem, vmem],
        out_specs=(vmem, vmem, vmem, vmem),
        scratch_shapes=[
            pltpu.VMEM((TOKENS, 128), bf16),
            pltpu.VMEM((128, TOKENS), bf16),
            pltpu.VMEM((2, TOKENS, 128), f32),
        ],
        compiler_params=pltpu.CompilerParams(vmem_limit_bytes=LIMIT),
        cost_estimate=pl.CostEstimate(
            flops=4 * 2 * 1400000 * 64, bytes_accessed=3000000, transcendentals=2800000
        ),
        name="attend",
    )(info, slopes, mine, other)


def attend_back(info, slopes, rows, mine, other, logsum):
    return pl.pallas_call(
        attend_back_kernel,
        out_shape=(
            jax.ShapeDtypeStruct((HALF, 384), bf16),
            jax.ShapeDtypeStruct((HALF, 384), bf16),
            jax.ShapeDtypeStruct((1, 384), f32),
        ),
        in_specs=[smem, smem, vmem, vmem, vmem, vmem],
        out_specs=(vmem, vmem, vmem),
        scratch_shapes=[
            pltpu.VMEM((TOKENS, 128), bf16),
            pltpu.VMEM((128, TOKENS), bf16),
            pltpu.VMEM((2, TOKENS, 128), f32),
            pltpu.VMEM((TOKENS, 128), f32),
            pltpu.VMEM((2, TOKENS, HEAD_DIM), f32),
            pltpu.VMEM((2, TOKENS, HEAD_DIM), f32),
            pltpu.VMEM((TOKENS, 384), bf16),
        ],
        compiler_params=pltpu.CompilerParams(vmem_limit_bytes=LIMIT),
        cost_estimate=pl.CostEstimate(
            flops=10 * 2 * 1400000 * 64, bytes_accessed=5000000, transcendentals=2800000
        ),
        name="attend_back",
    )(info, slopes, rows, mine, other, logsum)


def norm_parts(values):
    average = jnp.mean(values, axis=-1, keepdims=True)
    centered = values - average
    variance = jnp.mean(centered * centered, axis=-1, keepdims=True)
    scale = lax.rsqrt(variance + 1e-05)
    return centered * scale, scale


def norm(values, gain, offset):
    return norm_parts(values)[0] * gain + offset


def norm_back(values, gain, grads):
    unit, scale = norm_parts(values)
    weighted = grads * gain
    mean_one = jnp.mean(weighted, axis=-1, keepdims=True)
    mean_two = jnp.mean(weighted * unit, axis=-1, keepdims=True)
    d_values = scale * (weighted - mean_one - unit * mean_two)
    return d_values, jnp.sum(grads * unit, axis=0), jnp.sum(grads, axis=0)


def gelu(values):
    return jax.nn.gelu(values, approximate=True)


def core_join(half, core):
    other = swap(half, "core")
    return jnp.where(
        core == 0, jnp.stack([half, other], axis=1), jnp.stack([other, half], axis=1)
    )


def columns_for_all(weight, parts):
    rows = weight.shape[0]
    split = weight.reshape(rows, parts, 8, -1)
    out = []
    for place in range(8):
        own = split[:, :, place].reshape(rows, -1)
        other = split[:, :, (place + 4) % 8].reshape(rows, -1)
        out.append(jnp.concatenate([own, other], axis=1))
    return jnp.stack(out)


def to_ctx(value):
    return lax.all_to_all(value, CTX, split_axis=0, concat_axis=0, tiled=True)


def core_half(value, core, axis):
    size = value.shape[axis] // 2
    return lax.dynamic_slice_in_dim(value, core * size, size, axis)


def gather_columns(blocks, core):
    got = to_ctx(core_half(blocks, core, 1))
    return core_join(got, core).reshape(D, -1)


def gather_rows(rows, core):
    got = swap(core_half(rows, core, 0), "y_hi")
    return core_join(got[None], core).reshape(rows.shape)


def forward(hidden, normed_all, params, info, slopes):
    (_, _, w_own, w_other, bias_own, bias_other, project, project_bias) = params[:8]
    (gain_two, offset_two, up, up_bias, down, down_bias) = params[8:]
    other = (dot(normed_all, w_other) + bias_other).astype(bf16)
    received = swap(other, "y_hi")
    mine = (dot(normed_all, w_own) + bias_own).astype(bf16)
    ctx_mine, ctx_other, logsum, rows = attend(info, slopes, mine, received)
    context = jnp.concatenate([ctx_mine, swap(ctx_other, "y_hi")], axis=1)
    middle = hidden + dot_scatter(context, project, dot) + project_bias
    normed_two = gather_z(norm(middle, gain_two, offset_two).astype(bf16))
    before = dot(normed_two, up) + up_bias
    activated = gelu(before).astype(bf16)
    result = middle + dot_scatter(activated, down, dot) + down_bias
    kept = (hidden, normed_all, logsum, rows, context, middle, normed_two, before, activated)
    return result, kept


def backward(gradient, params, kept, info, slopes):
    (gain_one, _, w_own, w_other, _, _, project, _) = params[:8]
    (gain_two, _, up, _, down, _) = params[8:]
    hidden, normed_all, logsum, rows, context, middle, normed_two, before, activated = kept
    grad_low = gradient.astype(bf16)
    grad_down = gather_z(grad_low)
    sum_down = jnp.sum(grad_low.astype(f32), axis=0)
    d_act = dot_t(grad_down, down)
    d_before = jax.vjp(gelu, before)[1](d_act)[0].astype(bf16)
    sum_up = jnp.sum(d_before.astype(f32), axis=0)
    d_normed = dot_scatter(d_before, up, dot_t)
    g_down = outer(activated, grad_down)
    g_up = outer(normed_two, d_before)
    d_values, sum_gain_two, sum_offset_two = norm_back(middle, gain_two, d_normed)
    d_middle = gradient + d_values
    grad_out = d_middle.astype(bf16)
    grad_out_all = gather_z(grad_out)
    sum_project = jnp.sum(grad_out.astype(f32), axis=0)
    ctx_other = dot_t(grad_out_all, project[128:]).astype(bf16)
    received = swap(ctx_other, "y_hi")
    ctx_mine = dot_t(grad_out_all, project[:128]).astype(bf16)
    g_project = outer(context, grad_out_all)
    d_mine, d_other, sums = attend_back(info, slopes, rows, ctx_mine, received, logsum)
    d_received = swap(d_other, "y_hi")
    d_joined = jnp.concatenate([d_mine, d_received], axis=1)
    w_both = jnp.concatenate([w_own, w_other], axis=1)
    d_normed_one = dot_scatter(d_joined, w_both, dot_t)
    g_input = outer(normed_all, d_joined)
    d_hidden, sum_gain_one, sum_offset_one = norm_back(hidden, gain_one, d_normed_one)
    big = (g_down, g_up, g_project, g_input)
    small = (
        sum_gain_one,
        sum_offset_one,
        sum_project,
        sum_gain_two,
        sum_offset_two,
        sum_down,
        sums,
        sum_up,
    )
    return d_middle + d_hidden, big, small


def other_half_first(value, width):
    return jnp.concatenate([value[..., width:], value[..., :width]], axis=-1)


def finish(down, up, project, inputs, y_hi, z):
    if down is not None:
        down = down[0].astype(f32) + swap(down[1], "y_hi").astype(f32)
        project = project[0].astype(f32) + swap(project[1], "y_hi").astype(f32)
    both = inputs if up is None else jnp.concatenate([up, inputs], axis=-1)
    return down, project, both


def spread_rows(both, widths, y_hi):
    keep = lax.dynamic_slice_in_dim(both, y_hi * 4, 4, 0).astype(f32)
    send = lax.dynamic_slice_in_dim(both, (1 - y_hi) * 4, 4, 0)
    got = swap(send, "y_hi")
    at = 0
    pieces = []
    for width in widths:
        pieces.append(other_half_first(got[..., at : at + width], width // 2))
        at += width
    total = (keep + jnp.concatenate(pieces, axis=-1).astype(f32)).astype(bf16)
    return lax.all_to_all(total, "z", split_axis=0, concat_axis=0, tiled=True)


def order_columns(rows, parts, y_hi):
    *lead, four, count, width = rows.shape
    split = rows.reshape(*lead, four, count, 2, parts, width // (2 * parts))
    split = jnp.where(y_hi == 0, split, split[..., ::-1, :, :])
    return split


def reduce_grp(pack):
    return lax.psum_scatter(pack, GRP, scatter_dimension=0, tiled=True)


def rows_by_group(value):
    return value.reshape(8, 16, 8, -1).transpose(1, 0, 2, 3).reshape(16, 64, -1)


def pack_big(g_down, g_up, g_project, g_input):
    pieces = [
        g_down.reshape(2, 16, 32, D).transpose(1, 0, 2, 3).reshape(16, 64, D),
        rows_by_group(g_up),
        g_project.reshape(2, 16, 8, 4, 256).transpose(1, 0, 2, 3, 4).reshape(16, 64, 256),
    ]
    if g_input is not None:
        pieces.append(rows_by_group(g_input))
    return jnp.concatenate([piece.astype(bf16) for piece in pieces], axis=-1)


def reduce_big(g_down, g_up, g_project, g_input, y_hi):
    packed = reduce_grp(pack_big(g_down, g_up, g_project, g_input)).reshape(64, -1)
    rows = jnp.concatenate([packed[:, :D], packed[:, 2 * D : 2 * D + 256]], axis=1)
    rows = rows.reshape(2, 32, D + 256)
    rows = rows[0].astype(f32) + swap(rows[1], "y_hi").astype(f32)
    widths = [D]
    both = packed[:, D : 2 * D]
    if g_input is not None:
        both = jnp.concatenate([both, packed[:, 2 * D + 256 :]], axis=1)
        widths.append(768)
    columns = spread_rows(both.reshape(8, 8, -1), widths, y_hi)
    full = jnp.concatenate([rows.astype(bf16), columns.reshape(32, -1)], axis=1)
    full = lax.all_gather(full, GRP, axis=0, tiled=False).astype(f32)
    down = full[:, :, :D].reshape(512, D)
    project = full[:, :, D : D + 256].reshape(16 * 8, D)
    up = input_columns(full[:, :, D + 256 : 2 * D + 256], 1, y_hi)
    inputs = None
    if g_input is not None:
        inputs = input_columns(full[:, :, 2 * D + 256 :], 3, y_hi)
    return down, up, project, inputs


def input_columns(rows, parts, y_hi):
    split = rows.reshape(16, 4, 8, 2, parts, -1)
    split = jnp.where(y_hi == 0, split, split[:, :, :, ::-1])
    return split.transpose(0, 2, 4, 3, 1, 5).reshape(128, -1)


def reduce_input(g_input, y_hi, x, y_lo, core):
    low = g_input.astype(bf16).reshape(8, 4, 2, 2, 8, 768)
    take = lambda value, at, axis: lax.dynamic_index_in_dim(value, at, axis, keepdims=False)
    total = take(low, core, 3).astype(f32) + swap(take(low, 1 - core, 3), "core").astype(f32)
    low = total.astype(bf16)
    total = take(total, x, 1)
    for k in (1, 2, 3):
        total = total + shift_x(take(low, (x + k) % 4, 1), k).astype(f32)
    low = total.astype(bf16)
    total = take(total, y_lo, 1) + swap(take(low, 1 - y_lo, 1), "y_lo").astype(f32)
    columns = spread_rows(total.astype(bf16), [768], y_hi).reshape(32, 768)
    full = lax.all_gather(columns, GRP, axis=0, tiled=False).astype(f32)
    return input_columns(full, 3, y_hi)


def pack_small(small, place):
    (gain_one, offset_one, project, gain_two, offset_two, down, sums, up) = small
    vectors = [
        v.reshape(8, 128) for v in (gain_one, offset_one, project, gain_two, offset_two, down)
    ]
    sums = sums.reshape(-1)
    inputs = lax.dynamic_update_slice_in_dim(jnp.zeros((2 * D,), f32), sums[:128], place * 128, 0)
    inputs = lax.dynamic_update_slice_in_dim(inputs, sums[256:], D + place * 128, 0)
    units = jnp.zeros((8, 512), f32)
    units = lax.dynamic_update_slice_in_dim(units, up[None, :512], place, 0)
    units = lax.dynamic_update_slice_in_dim(units, up[None, 512:], (place + 4) % 8, 0)
    return jnp.concatenate(vectors + [inputs.reshape(8, 256), units], axis=1)


def on_device(
    inputs,
    cotangent,
    segments,
    norm_one_gain,
    norm_one_bias,
    input_weight,
    input_bias,
    project_weight,
    project_bias,
    norm_two_gain,
    norm_two_bias,
    up_weight,
    up_bias,
    down_weight,
    down_bias,
):
    y_hi, z = lax.axis_index("y_hi"), lax.axis_index("z")
    x, y_lo, core = lax.axis_index("x"), lax.axis_index("y_lo"), lax.axis_index("core")
    place = y_hi * 4 + z
    cut = jnp.sum((segments[0] < 2).astype(jnp.int32))
    info = jnp.stack([y_hi, z, cut]).astype(jnp.int32)
    heads = (place * 2 + jnp.arange(2, dtype=jnp.int32)).astype(f32)
    slopes = jnp.exp2(-8.0 * (heads + 1.0) / HEADS)

    raw_all = gather_z(inputs[0])
    small = jnp.concatenate(
        [
            norm_one_gain,
            norm_one_bias,
            project_bias,
            norm_two_gain,
            norm_two_bias,
            down_bias,
            input_bias,
            up_bias,
        ],
        axis=1,
    )
    small = jnp.concatenate([small.reshape(4, 768), jnp.zeros((12, 768), bf16)], axis=0)
    first = core_half(columns_for_all(input_weight[0], 3), core, 1)
    first = jnp.concatenate([first, jnp.broadcast_to(small[None], (8, 16, 768))], axis=1)
    first = to_ctx(first)
    small = first[:, 64:68].reshape(8, LAYERS, -1).transpose(1, 0, 2).astype(f32)
    w_first = core_join(first[:, :64], core).reshape(D, 768)
    up_first = gather_columns(columns_for_all(up_weight[0], 1), core)
    second = gather_columns(
        jnp.concatenate(
            [columns_for_all(input_weight[1], 3), columns_for_all(up_weight[1], 1)], axis=2
        ),
        core,
    )
    w_all = (w_first, second[:, :768])
    up_all = (up_first, second[:, 768:])

    layers = []
    for layer in range(LAYERS):
        rows = jnp.concatenate([down_weight[layer], project_weight[layer]], axis=0)
        rows_other = gather_rows(rows, core)
        down = jnp.concatenate([rows[:512], rows_other[:512]], axis=0)
        project = jnp.concatenate([rows[512:], rows_other[512:]], axis=0)
        vectors = [small[layer, :, i * 128 : (i + 1) * 128].reshape(D) for i in range(6)]
        in_bias = small[layer, :, 768:1024].reshape(2 * D)
        unit_bias = small[layer, :, 1024:1536]

        def bias_of(at):
            query = lax.dynamic_slice_in_dim(in_bias, at * 128, 128)
            value = lax.dynamic_slice_in_dim(in_bias, D + at * 128, 128)
            return jnp.concatenate([query, jnp.zeros((128,), f32), value])

        partner = (place + 4) % 8
        unit = jnp.concatenate(
            [
                lax.dynamic_index_in_dim(unit_bias, place, 0, keepdims=False),
                lax.dynamic_index_in_dim(unit_bias, partner, 0, keepdims=False),
            ]
        )
        layers.append(
            (
                vectors[0],
                vectors[1],
                w_all[layer][:, :384],
                w_all[layer][:, 384:],
                bias_of(place),
                bias_of(partner),
                project,
                vectors[2],
                vectors[3],
                vectors[4],
                up_all[layer],
                unit,
                down,
                vectors[5],
            )
        )

    hidden = inputs[0].astype(f32)
    kept = []
    for layer in range(LAYERS):
        params = layers[layer]
        if layer == 0:
            normed_all = norm(raw_all.astype(f32), params[0], params[1]).astype(bf16)
        else:
            normed_all = gather_z(norm(hidden, params[0], params[1]).astype(bf16))
        hidden, state = forward(hidden, normed_all, params, info, slopes)
        kept.append(state)
    gradient = cotangent[0].astype(f32)
    bigs = [None] * LAYERS
    smalls = [None] * LAYERS
    for layer in (1, 0):
        gradient, big, smalls[layer] = backward(gradient, layers[layer], kept[layer], info, slopes)
        if layer == 1:
            bigs[1] = reduce_big(*big, y_hi)
        else:
            down, up, project, _ = reduce_big(*big[:3], None, y_hi)
            bigs[0] = (down, up, project, reduce_input(big[3], y_hi, x, y_lo, core))
    packed = jnp.concatenate([pack_small(s, place) for s in smalls], axis=1)
    vector = jnp.sum(to_ctx(packed), axis=0)
    vector = jnp.sum(lax.all_gather(vector.reshape(8, -1), GRP, axis=0, tiled=False), axis=0)
    vector = vector.reshape(LAYERS, -1)
    parts = [vector[:, i * 128 : (i + 1) * 128] for i in range(6)]
    both = [jnp.stack([bigs[0][i], bigs[1][i]]) for i in range(4)]
    return (
        hidden[None],
        gradient[None],
        parts[0],
        parts[1],
        both[3],
        vector[:, 768:1024],
        both[2],
        parts[2],
        parts[3],
        parts[4],
        both[1],
        vector[:, 1024:1536],
        both[0],
        parts[5],
    )


def solution(mesh):
    split = Mesh(mesh.devices.reshape(4, 2, 2, 2, 4), GRP + CTX)
    rows = P(GRP, CTX, None)
    vector = P(None, CTX)
    matrix = P(None, CTX, None)
    weights = (
        vector,
        vector,
        matrix,
        vector,
        matrix,
        vector,
        vector,
        vector,
        matrix,
        vector,
        matrix,
        vector,
    )
    return jax.shard_map(
        on_device,
        mesh=split,
        in_specs=(rows, rows, P(GRP, None)) + weights,
        out_specs=(rows, rows) + weights,
        check_vma=False,
    )
```

time: 1620 us -> 809 us (0.50)
  waiting for transfers between devices: 931 us -> 352 us
  blocking collectives: 165 us -> 39.6 us
  starting transfers between devices: 49.2 us -> 157 us
  matrix products: 156 us -> 60.9 us
  local copies, waits for them, and re-layouts: 147 us -> 64.6 us
  other arithmetic: 144 us -> 71.2 us
  Pallas kernels: 0 us -> 37.9 us
    reduce_scatter x8 -> x2, waiting for transfers between devices: 525 us -> 20.4 us  [reduce_grp(): return lax.psum_scatter(pack, GRP, scatter_dimension=0, tiled=True)]
    ppermute x0 -> x73, waiting for transfers between devices: none -> 312 us  [the longest x48 215 us: shift_z(): return lax.ppermute(value, 'z', [(i, (i + step) % 4) for i in range(4)])]
    all_gather x8 -> x2, waiting for transfers between devices: 262 us -> 0.01 us  [reduce_big(): full = lax.all_gather(full, GRP, axis=0, tiled=False).astype(f32)]
    ppermute x0 -> x73, starting transfers between devices: none -> 129 us  [the longest x48 62.2 us: shift_z(): return lax.ppermute(value, 'z', [(i, (i + step) % 4) for i in range(4)])]
    dot_general x78 -> x36, matrix products: 156 us -> 60.9 us  [the longest x14 23.6 us: dot(): return jnp.dot(left, right, preferred_element_type=f32)]
    psum x1 -> x0, waiting for transfers between devices: 72.1 us -> none  [reduce_tensor(): lax.psum(input_rows.astype(jnp.bfloat16), 'grp').astype(jnp.float32)]
    all_gather x8 -> x2, blocking collectives: 96.7 us -> 39.6 us  [the longest x1 21.4 us: reduce_input(): full = lax.all_gather(columns, GRP, axis=0, tiled=False).astype(f32)]
    psum x1 -> x0, blocking collectives: 55.5 us -> none  [reduce_tensor(): lax.psum(small[0].astype(jnp.bfloat16), 'grp').astype(jnp.float32)]
  transfers between devices with their start and end apart: 25 -> 84, of which waited for: 22 -> 49; matrix products, arithmetic and copies ran while one was open for 8% -> 18% of each run, Pallas kernels for 0% -> 3%
where the time goes in v1:
time: 809 us; the launch traced here: 800 us
  waiting for transfers between devices  352 us (44%)
  starting transfers between devices  157 us (19%)
  other arithmetic  71.2 us (9%)
  local copies, waits for them, and re-layouts  64.6 us (8%)
  matrix products  60.9 us (8%)
  blocking collectives  39.6 us (5%)
  Pallas kernels  37.9 us (5%)
  between operations  16.2 us (2%)
    ppermute x48, waiting for transfers between devices, shift_z(): return lax.ppermute(value, 'z', [(i, (i + step) % 4) for i in range(4)])  215 us
    ppermute x22, waiting for transfers between devices, swap(): return lax.ppermute(value, axis, [(0, 1), (1, 0)])  85.6 us
    ppermute x48, starting transfers between devices, shift_z(): return lax.ppermute(value, 'z', [(i, (i + step) % 4) for i in range(4)])  62.2 us
    ppermute x22, starting transfers between devices, swap(): return lax.ppermute(value, axis, [(0, 1), (1, 0)])  58.9 us
    dot_general x14, matrix products, dot(): return jnp.dot(left, right, preferred_element_type=f32)  23.6 us
    dot_general x14, matrix products, dot_t(): lax.dot_general(left, right, (((1,), (1,)), ((), ())), preferred_element_...  23.1 us
    all_gather x1, blocking collectives, reduce_input(): full = lax.all_gather(columns, GRP, axis=0, tiled=False).astype(f32)  21.4 us
    pallas_call x2, Pallas kernels, attend_back(): pl.pallas_call(attend_back_kernel, out_shape=(jax.ShapeDtypeStruct((HALF,...  21.3 us
  transfers between devices with their start and end apart: 84, of which 49 were waited for; matrix products, arithmetic and copies ran while one was open for 18% of the time, Pallas kernels for 3%

profile of v1, /device:TPU:1, one launch (start us, length us, event | category | flops | bytes accessed | tf_op | source)
XLA Modules:
  0.0 799.7 jit_solution(481009364716740710)
XLA Ops:
  9.7 3.3 collective-permute-start.1
  20.6 4.6 all-to-all-start
  63.9 4.2 all-to-all-start.1
  76.0 3.3 collective-permute-start.4
  82.5 13.3 %collective-permute-done.4.other = bf16[768,384]{1,0:T(8,128)(2,1)S(1)} collective-permute-done((bf16[768,384]{1,0:T(8,128)(2,1)S(1)}, bf16[768,384]{1,0:T(8,128)(2,1)S(1)}, u32[]{:S(2)}, u32[]{:S(2)}) %collective-permute-start.4) | collective-permute-done | bytes 589856 | tf_op jit(solution)/shard_map/ppermute | solution.py:39
  95.8 8.3 %attend.2 = (bf16[768,128]{1,0:T(8,128)(2,1)S(1)}, bf16[768,128]{1,0:T(8,128)(2,1)S(1)}, f32[2,1536]{1,0:T(2,128)S(1)}, bf16[1536,384]{1,0:T(8,128)(2,1)S(1)}) custom-call(s32[3]{0:T(128)S(1)} %pad_add_fusion.info, f32[2]{0:T(128)S(1)} %multiply_exponential_fusion.slopes, bf16[768,384]{1,0:T(8,128)(2,1)S(1)} %fusion.34.mine, ...), custom_call_target="tpu_custom_call" | custom-call | flops 716800000 | bytes 3000000 | tf_op jit(solution)/shard_map/attend/pallas_call | solution.py:187
  106.5 4.6 collective-permute-done.5
  117.1 4.9 dynamic-slice_maximum_fusion
  122.0 4.5 copy.110
  126.6 4.5 all-to-all-start.2
  143.4 8.9 %all-to-all-done.2 = bf16[8,64,1792]{2,1,0:T(8,128)(2,1)} async-done(((bf16[8,64,1792]{2,1,0:T(8,128)(2,1)}), bf16[8,64,1792]{2,1,0:T(8,128)(2,1)}, u32[]{:S(2)}, u32[]{:S(2)}) %all-to-all-start.2) | async-done | bytes 1835040 | tf_op jit(solution)/shard_map/all_to_all | solution.py:281
  152.4 9.4 %collective-permute-start.21 = (bf16[8,64,1792]{2,1,0:T(8,128)(2,1)}, bf16[8,64,1792]{2,1,0:T(8,128)(2,1)S(1)}, u32[]{:S(2)}, u32[]{:S(2)}) collective-permute-start(bf16[8,64,1792]{2,1,0:T(8,128)(2,1)} %all-to-all-done.2), channel_id=1, source_target_pairs={{0,8},{8,0},{1,9},{9,1},{2,10},{10,2},{3,11},{11,3},{4,12},{12,4},... | collective-permute-start | bytes 5505032 | tf_op jit(solution)/shard_map/ppermute | solution.py:39
  164.4 4.4 collective-permute-done.12
  168.8 3.5 multiply_convert_fusion.1
  177.6 4.5 collective-permute-start.24
  186.3 11.1 %collective-permute-done.17 = bf16[192,1024]{1,0:T(8,128)(2,1)S(1)} collective-permute-done((bf16[192,1024]{1,0:T(8,128)(2,1)S(1)}, bf16[192,1024]{1,0:T(8,128)(2,1)S(1)}, u32[]{:S(2)}, u32[]{:S(2)}) %collective-permute-start.17) | collective-permute-done | bytes 393248 | tf_op jit(solution)/shard_map/ppermute | solution.py:31
  204.6 14.1 %collective-permute-done.18 = bf16[192,1024]{1,0:T(8,128)(2,1)S(1)} collective-permute-done((bf16[192,1024]{1,0:T(8,128)(2,1)S(1)}, bf16[192,1024]{1,0:T(8,128)(2,1)S(1)}, u32[]{:S(2)}, u32[]{:S(2)}) %collective-permute-start.18) | collective-permute-done | bytes 393248 | tf_op jit(solution)/shard_map/ppermute | solution.py:31
  225.2 9.6 %collective-permute-done.22.other = bf16[768,384]{1,0:T(8,128)(2,1)S(1)} collective-permute-done((bf16[768,384]{1,0:T(8,128)(2,1)S(1)}, bf16[768,384]{1,0:T(8,128)(2,1)S(1)}, u32[]{:S(2)}, u32[]{:S(2)}) %collective-permute-start.22) | collective-permute-done | bytes 589856 | tf_op jit(solution)/shard_map/ppermute | solution.py:39
  234.9 8.3 %attend.3 = (bf16[768,128]{1,0:T(8,128)(2,1)S(1)}, bf16[768,128]{1,0:T(8,128)(2,1)S(1)}, f32[2,1536]{1,0:T(2,128)S(1)}, bf16[1536,384]{1,0:T(8,128)(2,1)S(1)}) custom-call(s32[3]{0:T(128)S(1)} %pad_add_fusion.info, f32[2]{0:T(128)S(1)} %multiply_exponential_fusion.slopes, bf16[768,384]{1,0:T(8,128)(2,1)S(1)} %fusion.36.mine, ...), custom_call_target="tpu_custom_call" | custom-call | flops 716800000 | bytes 3000000 | tf_op jit(solution)/shard_map/attend/pallas_call | solution.py:187
  245.8 3.5 collective-permute-done.23
  249.9 5.2 collective-permute-start.26
  255.9 7.6 collective-permute-done.26
  264.7 11.0 %collective-permute-done.28 = bf16[192,1024]{1,0:T(8,128)(2,1)S(1)} collective-permute-done((bf16[192,1024]{1,0:T(8,128)(2,1)S(1)}, bf16[192,1024]{1,0:T(8,128)(2,1)S(1)}, u32[]{:S(2)}, u32[]{:S(2)}) %collective-permute-start.28) | collective-permute-done | bytes 393248 | tf_op jit(solution)/shard_map/ppermute | solution.py:31
  282.0 13.3 %collective-permute-done.29 = bf16[192,1024]{1,0:T(8,128)(2,1)S(1)} collective-permute-done((bf16[192,1024]{1,0:T(8,128)(2,1)S(1)}, bf16[192,1024]{1,0:T(8,128)(2,1)S(1)}, u32[]{:S(2)}, u32[]{:S(2)}) %collective-permute-start.29) | collective-permute-done | bytes 393248 | tf_op jit(solution)/shard_map/ppermute | solution.py:31
  296.9 3.6 multiply_convert_fusion
  300.4 12.9 %collective-permute-done.35 = bf16[192,1024]{1,0:T(8,128)(2,1)S(1)} collective-permute-done((bf16[192,1024]{1,0:T(8,128)(2,1)S(1)}, bf16[192,1024]{1,0:T(8,128)(2,1)S(1)}, u32[]{:S(2)}, u32[]{:S(2)}) %collective-permute-start.35) | collective-permute-done | bytes 393248 | tf_op jit(solution)/shard_map/ppermute | solution.py:31
  313.8 3.7 convert_reduce_fusion.1
  322.6 9.0 %collective-permute-done.38 = bf16[192,1024]{1,0:T(8,128)(2,1)S(1)} collective-permute-done((bf16[192,1024]{1,0:T(8,128)(2,1)S(1)}, bf16[192,1024]{1,0:T(8,128)(2,1)S(1)}, u32[]{:S(2)}, u32[]{:S(2)}) %collective-permute-start.38) | collective-permute-done | bytes 393248 | tf_op jit(solution)/shard_map/ppermute | solution.py:31
  333.0 9.5 %collective-permute-done.40 = bf16[192,1024]{1,0:T(8,128)(2,1)S(1)} collective-permute-done((bf16[192,1024]{1,0:T(8,128)(2,1)S(1)}, bf16[192,1024]{1,0:T(8,128)(2,1)S(1)}, u32[]{:S(2)}, u32[]{:S(2)}) %collective-permute-start.40) | collective-permute-done | bytes 393248 | tf_op jit(solution)/shard_map/ppermute | solution.py:31
  347.3 16.9 %collective-permute-done.41 = bf16[192,1024]{1,0:T(8,128)(2,1)S(1)} collective-permute-done((bf16[192,1024]{1,0:T(8,128)(2,1)S(1)}, bf16[192,1024]{1,0:T(8,128)(2,1)S(1)}, u32[]{:S(2)}, u32[]{:S(2)}) %collective-permute-start.41) | collective-permute-done | bytes 393248 | tf_op jit(solution)/shard_map/ppermute | solution.py:31
  371.2 10.7 %attend_back.2 = (bf16[768,384]{1,0:T(8,128)(2,1)S(1)}, bf16[768,384]{1,0:T(8,128)(2,1)S(1)}, f32[1,384]{1,0:T(1,128)S(1)}) custom-call(s32[3]{0:T(128)S(1)} %pad_add_fusion.info, f32[2]{0:T(128)S(1)} %multiply_exponential_fusion.slopes, bf16[1536,384]{1,0:T(8,128)(2,1)S(1)} %get-tuple-element.32.rows, bf16[768,128]{1,0:T(8,128)(2,1)S(1)} %convolution_convert_fusion.18.mine, ...), custom_call_target="tpu_custom_call" | custom-call | flops 1792000000 | bytes 5000000 | tf_op jit(solution)/shard_map/attend_back/pallas_call | solution.py:211
  384.5 11.0 %collective-permute-done.45 = bf16[768,384]{1,0:T(8,128)(2,1)S(1)} collective-permute-done((bf16[768,384]{1,0:T(8,128)(2,1)S(1)}, bf16[768,384]{1,0:T(8,128)(2,1)S(1)}, u32[]{:S(2)}, u32[]{:S(2)}) %collective-permute-start.45) | collective-permute-done | bytes 589856 | tf_op jit(solution)/shard_map/ppermute | solution.py:39
  396.8 5.5 collective-permute-start.46
  403.1 5.4 collective-permute-done.46
  411.5 11.7 %collective-permute-done.48 = bf16[192,1024]{1,0:T(8,128)(2,1)S(1)} collective-permute-done((bf16[192,1024]{1,0:T(8,128)(2,1)S(1)}, bf16[192,1024]{1,0:T(8,128)(2,1)S(1)}, u32[]{:S(2)}, u32[]{:S(2)}) %collective-permute-start.48) | collective-permute-done | bytes 393248 | tf_op jit(solution)/shard_map/ppermute | solution.py:31
  427.6 16.9 %collective-permute-done.49 = bf16[192,1024]{1,0:T(8,128)(2,1)S(1)} collective-permute-done((bf16[192,1024]{1,0:T(8,128)(2,1)S(1)}, bf16[192,1024]{1,0:T(8,128)(2,1)S(1)}, u32[]{:S(2)}, u32[]{:S(2)}) %collective-permute-start.49) | collective-permute-done | bytes 393248 | tf_op jit(solution)/shard_map/ppermute | solution.py:31
  444.9 3.7 convert_reduce_fusion.2
  450.1 3.4 collective-permute-start.52
  456.2 13.5 %collective-permute-done.52 = bf16[192,1024]{1,0:T(8,128)(2,1)S(1)} collective-permute-done((bf16[192,1024]{1,0:T(8,128)(2,1)S(1)}, bf16[192,1024]{1,0:T(8,128)(2,1)S(1)}, u32[]{:S(2)}, u32[]{:S(2)}) %collective-permute-start.52) | collective-permute-done | bytes 393248 | tf_op jit(solution)/shard_map/ppermute | solution.py:31
  469.7 4.1 collective-permute-done.54
  482.7 13.6 %collective-permute-done.55 = bf16[192,1024]{1,0:T(8,128)(2,1)S(1)} collective-permute-done((bf16[192,1024]{1,0:T(8,128)(2,1)S(1)}, bf16[192,1024]{1,0:T(8,128)(2,1)S(1)}, u32[]{:S(2)}, u32[]{:S(2)}) %collective-permute-start.55) | collective-permute-done | bytes 393248 | tf_op jit(solution)/shard_map/ppermute | solution.py:31
  501.4 3.5 convolution_convert_fusion.2
  514.0 5.7 pad_maximum_fusion
  520.1 3.3 convolution_convert_fusion.9
  528.3 15.4 %collective-permute-done.32 = bf16[192,1024]{1,0:T(8,128)(2,1)} collective-permute-done((bf16[192,1024]{1,0:T(8,128)(2,1)}, bf16[192,1024]{1,0:T(8,128)(2,1)}, u32[]{:S(2)}, u32[]{:S(2)}) %collective-permute-start.32) | collective-permute-done | bytes 393248 | tf_op jit(solution)/shard_map/ppermute | solution.py:31
  543.6 4.4 collective-permute-done.34
  548.0 3.7 add_bitcast_fusion
  557.2 10.8 %collective-permute-done.58.other = bf16[768,128]{1,0:T(8,128)(2,1)S(1)} collective-permute-done((bf16[768,128]{1,0:T(8,128)(2,1)S(1)}, bf16[768,128]{1,0:T(8,128)(2,1)S(1)}, u32[]{:S(2)}, u32[]{:S(2)}) %collective-permute-start.58) | collective-permute-done | bytes 196640 | tf_op jit(solution)/shard_map/ppermute | solution.py:39
  568.0 10.6 %attend_back.3 = (bf16[768,384]{1,0:T(8,128)(2,1)S(1)}, bf16[768,384]{1,0:T(8,128)(2,1)S(1)}, f32[1,384]{1,0:T(1,128)S(1)}) custom-call(s32[3]{0:T(128)S(1)} %pad_add_fusion.info, f32[2]{0:T(128)S(1)} %multiply_exponential_fusion.slopes, bf16[1536,384]{1,0:T(8,128)(2,1)S(1)} %get-tuple-element.36.rows, bf16[768,128]{1,0:T(8,128)(2,1)S(1)} %convolution_convert_fusion.16.mine, ...), custom_call_target="tpu_custom_call" | custom-call | flops 1792000000 | bytes 5000000 | tf_op jit(solution)/shard_map/attend_back/pallas_call | solution.py:211
  580.4 22.1 %collective-permute-done.59 = bf16[768,384]{1,0:T(8,128)(2,1)S(1)} collective-permute-done((bf16[768,384]{1,0:T(8,128)(2,1)S(1)}, bf16[768,384]{1,0:T(8,128)(2,1)S(1)}, u32[]{:S(2)}, u32[]{:S(2)}) %collective-permute-start.59) | collective-permute-done | bytes 589856 | tf_op jit(solution)/shard_map/ppermute | solution.py:39
  615.3 3.3 all-to-all-start.6
  619.5 3.9 all-to-all-done.6
  627.5 8.0 %collective-permute-start.63 = (bf16[8,4,2,8,768]{4,3,2,1,0:T(8,128)(2,1)S(1)}, bf16[8,4,2,8,768]{4,3,2,1,0:T(8,128)(2,1)}, u32[]{:S(2)}, u32[]{:S(2)}) collective-permute-start(bf16[8,4,2,8,768]{4,3,2,1,0:T(8,128)(2,1)S(1)} %dynamic-slice_bitcast_fusion), channel_id=1, source_target_pairs={{0,8},{8,0},{1,9},{9,1},{2,10},{10,2},{3,11},{11,3},{4,12},{12,4},... | collective-permute-start | bytes 2359304 | tf_op jit(solution)/shard_map/ppermute | solution.py:39
  635.6 6.9 collective-permute-done.62
  644.3 20.3 %reduce-scatter.3.cloned.1.call-done = bf16[1,64,3072]{2,1,0:T(8,128)(2,1)} async-done(((bf16[16,64,3072]{2,1,0:T(8,128)(2,1)}), bf16[1,64,3072]{2,1,0:T(8,128)(2,1)}) %reduce-scatter.3.cloned.1.call-update) | async-done | bytes 393232 | tf_op jit(solution)/shard_map/reduce_scatter | solution.py:392
  673.3 3.7 all-to-all-start.5
  677.0 4.7 all-to-all-done.5
  683.3 3.4 all-to-all-start.3
  690.4 5.6 collective-permute-start.65
  698.6 8.6 %collective-permute-done.65 = bf16[8,2,8,768]{3,2,1,0:T(8,128)(2,1)S(1)} collective-permute-done((bf16[8,2,8,768]{3,2,1,0:T(8,128)(2,1)S(1)}, bf16[8,2,8,768]{3,2,1,0:T(8,128)(2,1)S(1)}, u32[]{:S(2)}, u32[]{:S(2)}) %collective-permute-start.65) | collective-permute-done | bytes 196640 | tf_op jit(solution)/shard_map/ppermute | solution.py:35
  714.3 18.2 %all_gather.18 = f32[16,8,384]{2,1,0:T(8,128)S(1)} all-gather(f32[1,8,384]{2,1,0:T(8,128)S(1)} %all_gather_reshape.6), channel_id=1, replica_groups=mesh['x'=4,'y_lo'=2,'core'=2,'y_hi'=2,'z'=4] {'x','y_lo','core'}, dimensions={0}, use_global_device_ids=true | all-gather | bytes 208896 | tf_op jit(solution)/shard_map/all_gather | solution.py:585
  733.2 3.9 all-to-all-start.4
  741.5 21.4 %all_gather.19 = bf16[16,32,768]{2,1,0:T(8,128)(2,1)S(1)} all-gather(bf16[1,32,768]{2,1,0:T(8,128)(2,1)S(1)} %bitcast.505), channel_id=1, replica_groups=mesh['x'=4,'y_lo'=2,'core'=2,'y_hi'=2,'z'=4] {'x','y_lo','core'}, dimensions={0}, use_global_device_ids=true | all-gather | bytes 835584 | tf_op jit(solution)/shard_map/all_gather | solution.py:449
  771.6 3.4 fusion.170
  (595 shorter events, 263.6 us)
Async XLA Ops:
  7.2 50.9 %collective-permute-start = (bf16[192,1024]{1,0:T(8,128)(2,1)}, bf16[192,1024]{1,0:T(8,128)(2,1)}, u32[]{:S(2)}, u32[]{:S(2)}) collective-permute-start(bf16[192,1024]{1,0:T(8,128)(2,1)} %bitcast.392), channel_id=1, source_target_pairs={{0,1},{1,2},{2,3},{3,0},{4,5},{5,6},{6,7},{7,4},{8,9},{9,10},{10,1... | collective-permute-start | bytes 1179656 | tf_op jit(solution)/shard_map/ppermute | solution.py:31
  9.7 48.4 %collective-permute-start.1 = (bf16[192,1024]{1,0:T(8,128)(2,1)}, bf16[192,1024]{1,0:T(8,128)(2,1)}, u32[]{:S(2)}, u32[]{:S(2)}) collective-permute-start(bf16[192,1024]{1,0:T(8,128)(2,1)} %bitcast.393), channel_id=1, source_target_pairs={{0,2},{1,3},{2,0},{3,1},{4,6},{5,7},{6,4},{7,5},{8,10},{9,11},{10,... | collective-permute-start | bytes 1179656 | tf_op jit(solution)/shard_map/ppermute | solution.py:31
  13.0 45.1 %collective-permute-start.2 = (bf16[192,1024]{1,0:T(8,128)(2,1)}, bf16[192,1024]{1,0:T(8,128)(2,1)}, u32[]{:S(2)}, u32[]{:S(2)}) collective-permute-start(bf16[192,1024]{1,0:T(8,128)(2,1)} %bitcast.394), channel_id=1, source_target_pairs={{0,3},{1,0},{2,1},{3,2},{4,7},{5,4},{6,5},{7,6},{8,11},{9,8},{10,9... | collective-permute-start | bytes 1179656 | tf_op jit(solution)/shard_map/ppermute | solution.py:31
  20.6 43.3 %all-to-all-start = ((bf16[8,80,768]{2,1,0:T(8,128)(2,1)}), bf16[8,80,768]{2,1,0:T(8,128)(2,1)}, u32[]{:S(2)}, u32[]{:S(2)}) async-start(bf16[8,80,768]{2,1,0:T(8,128)(2,1)} %copy.99), calls=%async_computation | async-start | bytes 1966080 | tf_op jit(solution)/shard_map/all_to_all | solution.py:281
  29.4 32.1 %collective-permute-start.6 = (bf16[320,1024]{1,0:T(8,128)(2,1)}, bf16[320,1024]{1,0:T(8,128)(2,1)}, u32[]{:S(2)}, u32[]{:S(2)}) collective-permute-start(bf16[320,1024]{1,0:T(8,128)(2,1)} %fusion.89), channel_id=1, source_target_pairs={{0,4},{4,0},{1,5},{5,1},{2,6},{6,2},{3,7},{7,3},{8,12},{12,8},{9,1... | collective-permute-start | bytes 1966088 | tf_op jit(solution)/shard_map/ppermute | solution.py:39
  61.5 43.0 %collective-permute-start.7 = (bf16[1,320,1024]{2,1,0:T(8,128)(2,1)}, bf16[1,320,1024]{2,1,0:T(8,128)(2,1)}, u32[]{:S(2)}, u32[]{:S(2)}) collective-permute-start(bf16[1,320,1024]{2,1,0:T(8,128)(2,1)} %bitcast.31), channel_id=1, source_target_pairs={{0,8},{8,0},{1,9},{9,1},{2,10},{10,2},{3,11},{11,3},{4,12},{12,4},... | collective-permute-start | bytes 1966088 | tf_op jit(solution)/shard_map/ppermute | solution.py:39
  63.9 62.7 %all-to-all-start.1 = ((bf16[8,64,1024]{2,1,0:T(8,128)(2,1)}), bf16[8,64,1024]{2,1,0:T(8,128)(2,1)}, u32[]{:S(2)}, u32[]{:S(2)}) async-start(bf16[8,64,1024]{2,1,0:T(8,128)(2,1)} %copy.104), calls=%async_computation.1 | async-start | bytes 2097152 | tf_op jit(solution)/shard_map/all_to_all | solution.py:281
  76.0 19.8 %collective-permute-start.4 = (bf16[768,384]{1,0:T(8,128)(2,1)S(1)}, bf16[768,384]{1,0:T(8,128)(2,1)S(1)}, u32[]{:S(2)}, u32[]{:S(2)}) collective-permute-start(bf16[768,384]{1,0:T(8,128)(2,1)S(1)} %fusion.35), channel_id=1, source_target_pairs={{0,4},{4,0},{1,5},{5,1},{2,6},{6,2},{3,7},{7,3},{8,12},{12,8},{9,1... | collective-permute-start | bytes 1769480 | tf_op jit(solution)/shard_map/ppermute | solution.py:39
  112.6 21.4 %collective-permute-start.10 = (bf16[192,1024]{1,0:T(8,128)(2,1)}, bf16[192,1024]{1,0:T(8,128)(2,1)S(1)}, u32[]{:S(2)}, u32[]{:S(2)}) collective-permute-start(bf16[192,1024]{1,0:T(8,128)(2,1)} %get-tuple-element.101), channel_id=1, source_target_pairs={{0,1},{1,2},{2,3},{3,0},{4,5},{5,6},{6,7},{7,4},{8,9},{9,10},{10,1... | collective-permute-start | bytes 1179656 | tf_op jit(solution)/shard_map/ppermute | solution.py:31
  113.9 20.2 %collective-permute-start.8 = (bf16[192,1024]{1,0:T(8,128)(2,1)}, bf16[192,1024]{1,0:T(8,128)(2,1)}, u32[]{:S(2)}, u32[]{:S(2)}) collective-permute-start(bf16[192,1024]{1,0:T(8,128)(2,1)} %get-tuple-element.100), channel_id=1, source_target_pairs={{0,3},{1,0},{2,1},{3,2},{4,7},{5,4},{6,5},{7,6},{8,11},{9,8},{10,9... | collective-permute-start | bytes 1179656 | tf_op jit(solution)/shard_map/ppermute | solution.py:31
  115.4 18.7 %collective-permute-start.9 = (bf16[192,1024]{1,0:T(8,128)(2,1)S(1)}, bf16[192,1024]{1,0:T(8,128)(2,1)}, u32[]{:S(2)}, u32[]{:S(2)}) collective-permute-start(bf16[192,1024]{1,0:T(8,128)(2,1)S(1)} %get-tuple-element.102), channel_id=1, source_target_pairs={{0,2},{1,3},{2,0},{3,1},{4,6},{5,7},{6,4},{7,5},{8,10},{9,11},{10,... | collective-permute-start | bytes 1179656 | tf_op jit(solution)/shard_map/ppermute | solution.py:31
  126.6 25.8 %all-to-all-start.2 = ((bf16[8,64,1792]{2,1,0:T(8,128)(2,1)}), bf16[8,64,1792]{2,1,0:T(8,128)(2,1)}, u32[]{:S(2)}, u32[]{:S(2)}) async-start(bf16[8,64,1792]{2,1,0:T(8,128)(2,1)} %copy.110), calls=%async_computation.2 | async-start | bytes 3670016 | tf_op jit(solution)/shard_map/all_to_all | solution.py:281
  131.1 475.1 %reduce-scatter.5.cloned.1.call-start = ((), (), s32[]{:S(2)}) async-start(), calls=%async_computation.10 | async-start | bytes 5013504 | tf_op jit(solution)/shard_map/reduce_scatter | solution.py:392
  131.2 30.5 %collective-permute-start.14 = (bf16[8,64,1024]{2,1,0:T(8,128)(2,1)}, bf16[8,64,1024]{2,1,0:T(8,128)(2,1)}, u32[]{:S(2)}, u32[]{:S(2)}) collective-permute-start(bf16[8,64,1024]{2,1,0:T(8,128)(2,1)} %all-to-all-done.1), channel_id=1, source_target_pairs={{0,8},{8,0},{1,9},{9,1},{2,10},{10,2},{3,11},{11,3},{4,12},{12,4},... | collective-permute-start | bytes 3145736 | tf_op jit(solution)/shard_map/ppermute | solution.py:39
  137.2 27.3 %collective-permute-start.11 = (bf16[192,1024]{1,0:T(8,128)(2,1)S(1)}, bf16[192,1024]{1,0:T(8,128)(2,1)S(1)}, u32[]{:S(2)}, u32[]{:S(2)}) collective-permute-start(bf16[192,1024]{1,0:T(8,128)(2,1)S(1)} %add_convert_fusion.2), channel_id=1, source_target_pairs={{0,1},{1,2},{2,3},{3,0},{4,5},{5,6},{6,7},{7,4},{8,9},{9,10},{10,1... | collective-permute-start | bytes 1179656 | tf_op jit(solution)/shard_map/ppermute | solution.py:31
  138.8 30.0 %collective-permute-start.12 = (bf16[192,1024]{1,0:T(8,128)(2,1)S(1)}, bf16[192,1024]{1,0:T(8,128)(2,1)}, u32[]{:S(2)}, u32[]{:S(2)}) collective-permute-start(bf16[192,1024]{1,0:T(8,128)(2,1)S(1)} %add_convert_fusion.2), channel_id=1, source_target_pairs={{0,2},{1,3},{2,0},{3,1},{4,6},{5,7},{6,4},{7,5},{8,10},{9,11},{10,... | collective-permute-start | bytes 1179656 | tf_op jit(solution)/shard_map/ppermute | solution.py:31
  141.2 27.6 %collective-permute-start.13 = (bf16[192,1024]{1,0:T(8,128)(2,1)S(1)}, bf16[192,1024]{1,0:T(8,128)(2,1)}, u32[]{:S(2)}, u32[]{:S(2)}) collective-permute-start(bf16[192,1024]{1,0:T(8,128)(2,1)S(1)} %add_convert_fusion.2), channel_id=1, source_target_pairs={{0,3},{1,0},{2,1},{3,2},{4,7},{5,4},{6,5},{7,6},{8,11},{9,8},{10,9... | collective-permute-start | bytes 1179656 | tf_op jit(solution)/shard_map/ppermute | solution.py:31
  152.4 49.5 %collective-permute-start.21 = (bf16[8,64,1792]{2,1,0:T(8,128)(2,1)}, bf16[8,64,1792]{2,1,0:T(8,128)(2,1)S(1)}, u32[]{:S(2)}, u32[]{:S(2)}) collective-permute-start(bf16[8,64,1792]{2,1,0:T(8,128)(2,1)} %all-to-all-done.2), channel_id=1, source_target_pairs={{0,8},{8,0},{1,9},{9,1},{2,10},{10,2},{3,11},{11,3},{4,12},{12,4},... | collective-permute-start | bytes 5505032 | tf_op jit(solution)/shard_map/ppermute | solution.py:39
  173.9 11.4 %collective-permute-start.15 = (bf16[192,1024]{1,0:T(8,128)(2,1)S(1)}, bf16[192,1024]{1,0:T(8,128)(2,1)S(1)}, u32[]{:S(2)}, u32[]{:S(2)}) collective-permute-start(bf16[192,1024]{1,0:T(8,128)(2,1)S(1)} %get-tuple-element.97), channel_id=1, source_target_pairs={{0,3},{1,0},{2,1},{3,2},{4,7},{5,4},{6,5},{7,6},{8,11},{9,8},{10,9... | collective-permute-start | bytes 1179656 | tf_op jit(solution)/shard_map/ppermute | solution.py:31
  176.8 20.6 %collective-permute-start.17 = (bf16[192,1024]{1,0:T(8,128)(2,1)S(1)}, bf16[192,1024]{1,0:T(8,128)(2,1)S(1)}, u32[]{:S(2)}, u32[]{:S(2)}) collective-permute-start(bf16[192,1024]{1,0:T(8,128)(2,1)S(1)} %get-tuple-element.98), channel_id=1, source_target_pairs={{0,1},{1,2},{2,3},{3,0},{4,5},{5,6},{6,7},{7,4},{8,9},{9,10},{10,1... | collective-permute-start | bytes 1179656 | tf_op jit(solution)/shard_map/ppermute | solution.py:31
  177.6 44.8 %collective-permute-start.24 = (bf16[320,1024]{1,0:T(8,128)(2,1)S(1)}, bf16[320,1024]{1,0:T(8,128)(2,1)S(1)}, u32[]{:S(2)}, u32[]{:S(2)}) collective-permute-start(bf16[320,1024]{1,0:T(8,128)(2,1)S(1)} %fusion.88), channel_id=1, source_target_pairs={{0,4},{4,0},{1,5},{5,1},{2,6},{6,2},{3,7},{7,3},{8,12},{12,8},{9,1... | collective-permute-start | bytes 1966088 | tf_op jit(solution)/shard_map/ppermute | solution.py:39
  198.7 19.9 %collective-permute-start.18 = (bf16[192,1024]{1,0:T(8,128)(2,1)S(1)}, bf16[192,1024]{1,0:T(8,128)(2,1)S(1)}, u32[]{:S(2)}, u32[]{:S(2)}) collective-permute-start(bf16[192,1024]{1,0:T(8,128)(2,1)S(1)} %add_convert_fusion.1), channel_id=1, source_target_pairs={{0,1},{1,2},{2,3},{3,0},{4,5},{5,6},{6,7},{7,4},{8,9},{9,10},{10,1... | collective-permute-start | bytes 1179656 | tf_op jit(solution)/shard_map/ppermute | solution.py:31
  198.8 19.8 %collective-permute-start.19 = (bf16[192,1024]{1,0:T(8,128)(2,1)S(1)}, bf16[192,1024]{1,0:T(8,128)(2,1)S(1)}, u32[]{:S(2)}, u32[]{:S(2)}) collective-permute-start(bf16[192,1024]{1,0:T(8,128)(2,1)S(1)} %add_convert_fusion.1), channel_id=1, source_target_pairs={{0,2},{1,3},{2,0},{3,1},{4,6},{5,7},{6,4},{7,5},{8,10},{9,11},{10,... | collective-permute-start | bytes 1179656 | tf_op jit(solution)/shard_map/ppermute | solution.py:31
  199.3 19.8 %collective-permute-start.20 = (bf16[192,1024]{1,0:T(8,128)(2,1)S(1)}, bf16[192,1024]{1,0:T(8,128)(2,1)S(1)}, u32[]{:S(2)}, u32[]{:S(2)}) collective-permute-start(bf16[192,1024]{1,0:T(8,128)(2,1)S(1)} %add_convert_fusion.1), channel_id=1, source_target_pairs={{0,3},{1,0},{2,1},{3,2},{4,7},{5,4},{6,5},{7,6},{8,11},{9,8},{10,9... | collective-permute-start | bytes 1179656 | tf_op jit(solution)/shard_map/ppermute | solution.py:31
  220.0 14.8 %collective-permute-start.22 = (bf16[768,384]{1,0:T(8,128)(2,1)S(1)}, bf16[768,384]{1,0:T(8,128)(2,1)S(1)}, u32[]{:S(2)}, u32[]{:S(2)}) collective-permute-start(bf16[768,384]{1,0:T(8,128)(2,1)S(1)} %fusion.37), channel_id=1, source_target_pairs={{0,4},{4,0},{1,5},{5,1},{2,6},{6,2},{3,7},{7,3},{8,12},{12,8},{9,1... | collective-permute-start | bytes 1769480 | tf_op jit(solution)/shard_map/ppermute | solution.py:39
  222.4 23.1 %collective-permute-start.25 = (bf16[1,320,1024]{2,1,0:T(8,128)(2,1)S(1)}, bf16[1,320,1024]{2,1,0:T(8,128)(2,1)S(1)}, u32[]{:S(2)}, u32[]{:S(2)}) collective-permute-start(bf16[1,320,1024]{2,1,0:T(8,128)(2,1)S(1)} %bitcast.485), channel_id=1, source_target_pairs={{0,8},{8,0},{1,9},{9,1},{2,10},{10,2},{3,11},{11,3},{4,12},{12,4},... | collective-permute-start | bytes 1966088 | tf_op jit(solution)/shard_map/ppermute | solution.py:39
  249.9 13.6 %collective-permute-start.26 = (bf16[192,1024]{1,0:T(8,128)(2,1)S(1)}, bf16[192,1024]{1,0:T(8,128)(2,1)S(1)}, u32[]{:S(2)}, u32[]{:S(2)}) collective-permute-start(bf16[192,1024]{1,0:T(8,128)(2,1)S(1)} %get-tuple-element.94), channel_id=1, source_target_pairs={{0,3},{1,0},{2,1},{3,2},{4,7},{5,4},{6,5},{7,6},{8,11},{9,8},{10,9... | collective-permute-start | bytes 1179656 | tf_op jit(solution)/shard_map/ppermute | solution.py:31
  255.1 20.7 %collective-permute-start.28 = (bf16[192,1024]{1,0:T(8,128)(2,1)S(1)}, bf16[192,1024]{1,0:T(8,128)(2,1)S(1)}, u32[]{:S(2)}, u32[]{:S(2)}) collective-permute-start(bf16[192,1024]{1,0:T(8,128)(2,1)S(1)} %get-tuple-element.95), channel_id=1, source_target_pairs={{0,1},{1,2},{2,3},{3,0},{4,5},{5,6},{6,7},{7,4},{8,9},{9,10},{10,1... | collective-permute-start | bytes 1179656 | tf_op jit(solution)/shard_map/ppermute | solution.py:31
  276.8 18.5 %collective-permute-start.29 = (bf16[192,1024]{1,0:T(8,128)(2,1)S(1)}, bf16[192,1024]{1,0:T(8,128)(2,1)S(1)}, u32[]{:S(2)}, u32[]{:S(2)}) collective-permute-start(bf16[192,1024]{1,0:T(8,128)(2,1)S(1)} %add_convert_fusion), channel_id=1, source_target_pairs={{0,1},{1,2},{2,3},{3,0},{4,5},{5,6},{6,7},{7,4},{8,9},{9,10},{10,1... | collective-permute-start | bytes 1179656 | tf_op jit(solution)/shard_map/ppermute | solution.py:31
  276.9 18.4 %collective-permute-start.30 = (bf16[192,1024]{1,0:T(8,128)(2,1)S(1)}, bf16[192,1024]{1,0:T(8,128)(2,1)S(1)}, u32[]{:S(2)}, u32[]{:S(2)}) collective-permute-start(bf16[192,1024]{1,0:T(8,128)(2,1)S(1)} %add_convert_fusion), channel_id=1, source_target_pairs={{0,2},{1,3},{2,0},{3,1},{4,6},{5,7},{6,4},{7,5},{8,10},{9,11},{10,... | collective-permute-start | bytes 1179656 | tf_op jit(solution)/shard_map/ppermute | solution.py:31
  277.3 19.6 %collective-permute-start.31 = (bf16[192,1024]{1,0:T(8,128)(2,1)S(1)}, bf16[192,1024]{1,0:T(8,128)(2,1)S(1)}, u32[]{:S(2)}, u32[]{:S(2)}) collective-permute-start(bf16[192,1024]{1,0:T(8,128)(2,1)S(1)} %add_convert_fusion), channel_id=1, source_target_pairs={{0,3},{1,0},{2,1},{3,2},{4,7},{5,4},{6,5},{7,6},{8,11},{9,8},{10,9... | collective-permute-start | bytes 1179656 | tf_op jit(solution)/shard_map/ppermute | solution.py:31
  279.5 33.8 %collective-permute-start.35 = (bf16[192,1024]{1,0:T(8,128)(2,1)S(1)}, bf16[192,1024]{1,0:T(8,128)(2,1)S(1)}, u32[]{:S(2)}, u32[]{:S(2)}) collective-permute-start(bf16[192,1024]{1,0:T(8,128)(2,1)S(1)} %bitcast.491), channel_id=1, source_target_pairs={{0,1},{1,2},{2,3},{3,0},{4,5},{5,6},{6,7},{7,4},{8,9},{9,10},{10,1... | collective-permute-start | bytes 1179656 | tf_op jit(solution)/shard_map/ppermute | solution.py:31
  280.1 33.3 %collective-permute-start.36 = (bf16[192,1024]{1,0:T(8,128)(2,1)S(1)}, bf16[192,1024]{1,0:T(8,128)(2,1)S(1)}, u32[]{:S(2)}, u32[]{:S(2)}) collective-permute-start(bf16[192,1024]{1,0:T(8,128)(2,1)S(1)} %bitcast.492), channel_id=1, source_target_pairs={{0,2},{1,3},{2,0},{3,1},{4,6},{5,7},{6,4},{7,5},{8,10},{9,11},{10,... | collective-permute-start | bytes 1179656 | tf_op jit(solution)/shard_map/ppermute | solution.py:31
  295.2 18.5 %collective-permute-start.37 = (bf16[192,1024]{1,0:T(8,128)(2,1)S(1)}, bf16[192,1024]{1,0:T(8,128)(2,1)S(1)}, u32[]{:S(2)}, u32[]{:S(2)}) collective-permute-start(bf16[192,1024]{1,0:T(8,128)(2,1)S(1)} %bitcast.493), channel_id=1, source_target_pairs={{0,3},{1,0},{2,1},{3,2},{4,7},{5,4},{6,5},{7,6},{8,11},{9,8},{10,9... | collective-permute-start | bytes 1179656 | tf_op jit(solution)/shard_map/ppermute | solution.py:31
  319.0 12.6 %collective-permute-start.38 = (bf16[192,1024]{1,0:T(8,128)(2,1)S(1)}, bf16[192,1024]{1,0:T(8,128)(2,1)S(1)}, u32[]{:S(2)}, u32[]{:S(2)}) collective-permute-start(bf16[192,1024]{1,0:T(8,128)(2,1)S(1)} %get-tuple-element.88), channel_id=1, source_target_pairs={{0,3},{1,0},{2,1},{3,2},{4,7},{5,4},{6,5},{7,6},{8,11},{9,8},{10,9... | collective-permute-start | bytes 1179656 | tf_op jit(solution)/shard_map/ppermute | solution.py:31
  322.1 20.5 %collective-permute-start.40 = (bf16[192,1024]{1,0:T(8,128)(2,1)S(1)}, bf16[192,1024]{1,0:T(8,128)(2,1)S(1)}, u32[]{:S(2)}, u32[]{:S(2)}) collective-permute-start(bf16[192,1024]{1,0:T(8,128)(2,1)S(1)} %get-tuple-element.89), channel_id=1, source_target_pairs={{0,1},{1,2},{2,3},{3,0},{4,5},{5,6},{6,7},{7,4},{8,9},{9,10},{10,1... | collective-permute-start | bytes 1179656 | tf_op jit(solution)/shard_map/ppermute | solution.py:31
  344.1 20.1 %collective-permute-start.41 = (bf16[192,1024]{1,0:T(8,128)(2,1)S(1)}, bf16[192,1024]{1,0:T(8,128)(2,1)S(1)}, u32[]{:S(2)}, u32[]{:S(2)}) collective-permute-start(bf16[192,1024]{1,0:T(8,128)(2,1)S(1)} %get-tuple-element.61), channel_id=1, source_target_pairs={{0,1},{1,2},{2,3},{3,0},{4,5},{5,6},{6,7},{7,4},{8,9},{9,10},{10,1... | collective-permute-start | bytes 1179656 | tf_op jit(solution)/shard_map/ppermute | solution.py:31
  344.6 19.6 %collective-permute-start.42 = (bf16[192,1024]{1,0:T(8,128)(2,1)S(1)}, bf16[192,1024]{1,0:T(8,128)(2,1)S(1)}, u32[]{:S(2)}, u32[]{:S(2)}) collective-permute-start(bf16[192,1024]{1,0:T(8,128)(2,1)S(1)} %get-tuple-element.61), channel_id=1, source_target_pairs={{0,2},{1,3},{2,0},{3,1},{4,6},{5,7},{6,4},{7,5},{8,10},{9,11},{10,... | collective-permute-start | bytes 1179656 | tf_op jit(solution)/shard_map/ppermute | solution.py:31
  345.2 19.3 %collective-permute-start.43 = (bf16[192,1024]{1,0:T(8,128)(2,1)S(1)}, bf16[192,1024]{1,0:T(8,128)(2,1)S(1)}, u32[]{:S(2)}, u32[]{:S(2)}) collective-permute-start(bf16[192,1024]{1,0:T(8,128)(2,1)S(1)} %get-tuple-element.61), channel_id=1, source_target_pairs={{0,3},{1,0},{2,1},{3,2},{4,7},{5,4},{6,5},{7,6},{8,11},{9,8},{10,9... | collective-permute-start | bytes 1179656 | tf_op jit(solution)/shard_map/ppermute | solution.py:31
  381.9 13.6 %collective-permute-start.45 = (bf16[768,384]{1,0:T(8,128)(2,1)S(1)}, bf16[768,384]{1,0:T(8,128)(2,1)S(1)}, u32[]{:S(2)}, u32[]{:S(2)}) collective-permute-start(bf16[768,384]{1,0:T(8,128)(2,1)S(1)} %get-tuple-element.35), channel_id=1, source_target_pairs={{0,4},{4,0},{1,5},{5,1},{2,6},{6,2},{3,7},{7,3},{8,12},{12,8},{9,1... | collective-permute-start | bytes 1769480 | tf_op jit(solution)/shard_map/ppermute | solution.py:39
  396.8 11.7 %collective-permute-start.46 = (bf16[192,1024]{1,0:T(8,128)(2,1)S(1)}, bf16[192,1024]{1,0:T(8,128)(2,1)S(1)}, u32[]{:S(2)}, u32[]{:S(2)}) collective-permute-start(bf16[192,1024]{1,0:T(8,128)(2,1)S(1)} %get-tuple-element.85), channel_id=1, source_target_pairs={{0,3},{1,0},{2,1},{3,2},{4,7},{5,4},{6,5},{7,6},{8,11},{9,8},{10,9... | collective-permute-start | bytes 1179656 | tf_op jit(solution)/shard_map/ppermute | solution.py:31
  403.1 20.1 %collective-permute-start.48 = (bf16[192,1024]{1,0:T(8,128)(2,1)S(1)}, bf16[192,1024]{1,0:T(8,128)(2,1)S(1)}, u32[]{:S(2)}, u32[]{:S(2)}) collective-permute-start(bf16[192,1024]{1,0:T(8,128)(2,1)S(1)} %get-tuple-element.86), channel_id=1, source_target_pairs={{0,1},{1,2},{2,3},{3,0},{4,5},{5,6},{6,7},{7,4},{8,9},{9,10},{10,1... | collective-permute-start | bytes 1179656 | tf_op jit(solution)/shard_map/ppermute | solution.py:31
  424.6 19.9 %collective-permute-start.49 = (bf16[192,1024]{1,0:T(8,128)(2,1)S(1)}, bf16[192,1024]{1,0:T(8,128)(2,1)S(1)}, u32[]{:S(2)}, u32[]{:S(2)}) collective-permute-start(bf16[192,1024]{1,0:T(8,128)(2,1)S(1)} %get-tuple-element.64), channel_id=1, source_target_pairs={{0,1},{1,2},{2,3},{3,0},{4,5},{5,6},{6,7},{7,4},{8,9},{9,10},{10,1... | collective-permute-start | bytes 1179656 | tf_op jit(solution)/shard_map/ppermute | solution.py:31
  424.7 19.8 %collective-permute-start.50 = (bf16[192,1024]{1,0:T(8,128)(2,1)S(1)}, bf16[192,1024]{1,0:T(8,128)(2,1)S(1)}, u32[]{:S(2)}, u32[]{:S(2)}) collective-permute-start(bf16[192,1024]{1,0:T(8,128)(2,1)S(1)} %get-tuple-element.64), channel_id=1, source_target_pairs={{0,2},{1,3},{2,0},{3,1},{4,6},{5,7},{6,4},{7,5},{8,10},{9,11},{10,... | collective-permute-start | bytes 1179656 | tf_op jit(solution)/shard_map/ppermute | solution.py:31
  425.6 19.2 %collective-permute-start.51 = (bf16[192,1024]{1,0:T(8,128)(2,1)S(1)}, bf16[192,1024]{1,0:T(8,128)(2,1)S(1)}, u32[]{:S(2)}, u32[]{:S(2)}) collective-permute-start(bf16[192,1024]{1,0:T(8,128)(2,1)S(1)} %get-tuple-element.64), channel_id=1, source_target_pairs={{0,3},{1,0},{2,1},{3,2},{4,7},{5,4},{6,5},{7,6},{8,11},{9,8},{10,9... | collective-permute-start | bytes 1179656 | tf_op jit(solution)/shard_map/ppermute | solution.py:31
  450.1 19.6 %collective-permute-start.52 = (bf16[192,1024]{1,0:T(8,128)(2,1)S(1)}, bf16[192,1024]{1,0:T(8,128)(2,1)S(1)}, u32[]{:S(2)}, u32[]{:S(2)}) collective-permute-start(bf16[192,1024]{1,0:T(8,128)(2,1)S(1)} %get-tuple-element.82), channel_id=1, source_target_pairs={{0,3},{1,0},{2,1},{3,2},{4,7},{5,4},{6,5},{7,6},{8,11},{9,8},{10,9... | collective-permute-start | bytes 1179656 | tf_op jit(solution)/shard_map/ppermute | solution.py:31
  453.5 16.2 %collective-permute-start.53 = (bf16[192,1024]{1,0:T(8,128)(2,1)S(1)}, bf16[192,1024]{1,0:T(8,128)(2,1)S(1)}, u32[]{:S(2)}, u32[]{:S(2)}) collective-permute-start(bf16[192,1024]{1,0:T(8,128)(2,1)S(1)} %get-tuple-element.84), channel_id=1, source_target_pairs={{0,2},{1,3},{2,0},{3,1},{4,6},{5,7},{6,4},{7,5},{8,10},{9,11},{10,... | collective-permute-start | bytes 1179656 | tf_op jit(solution)/shard_map/ppermute | solution.py:31
  453.5 20.3 %collective-permute-start.54 = (bf16[192,1024]{1,0:T(8,128)(2,1)S(1)}, bf16[192,1024]{1,0:T(8,128)(2,1)S(1)}, u32[]{:S(2)}, u32[]{:S(2)}) collective-permute-start(bf16[192,1024]{1,0:T(8,128)(2,1)S(1)} %get-tuple-element.83), channel_id=1, source_target_pairs={{0,1},{1,2},{2,3},{3,0},{4,5},{5,6},{6,7},{7,4},{8,9},{9,10},{10,1... | collective-permute-start | bytes 1179656 | tf_op jit(solution)/shard_map/ppermute | solution.py:31
  476.8 19.4 %collective-permute-start.55 = (bf16[192,1024]{1,0:T(8,128)(2,1)S(1)}, bf16[192,1024]{1,0:T(8,128)(2,1)S(1)}, u32[]{:S(2)}, u32[]{:S(2)}) collective-permute-start(bf16[192,1024]{1,0:T(8,128)(2,1)S(1)} %get-tuple-element.67), channel_id=1, source_target_pairs={{0,1},{1,2},{2,3},{3,0},{4,5},{5,6},{6,7},{7,4},{8,9},{9,10},{10,1... | collective-permute-start | bytes 1179656 | tf_op jit(solution)/shard_map/ppermute | solution.py:31
  476.8 19.4 %collective-permute-start.56 = (bf16[192,1024]{1,0:T(8,128)(2,1)S(1)}, bf16[192,1024]{1,0:T(8,128)(2,1)S(1)}, u32[]{:S(2)}, u32[]{:S(2)}) collective-permute-start(bf16[192,1024]{1,0:T(8,128)(2,1)S(1)} %get-tuple-element.67), channel_id=1, source_target_pairs={{0,2},{1,3},{2,0},{3,1},{4,6},{5,7},{6,4},{7,5},{8,10},{9,11},{10,... | collective-permute-start | bytes 1179656 | tf_op jit(solution)/shard_map/ppermute | solution.py:31
  477.8 18.9 %collective-permute-start.57 = (bf16[192,1024]{1,0:T(8,128)(2,1)S(1)}, bf16[192,1024]{1,0:T(8,128)(2,1)S(1)}, u32[]{:S(2)}, u32[]{:S(2)}) collective-permute-start(bf16[192,1024]{1,0:T(8,128)(2,1)S(1)} %get-tuple-element.67), channel_id=1, source_target_pairs={{0,3},{1,0},{2,1},{3,2},{4,7},{5,4},{6,5},{7,6},{8,11},{9,8},{10,9... | collective-permute-start | bytes 1179656 | tf_op jit(solution)/shard_map/ppermute | solution.py:31
  500.3 164.3 %reduce-scatter.3.cloned.1.call-start = ((), (), s32[]{:S(2)}) async-start(), calls=%async_computation.9 | async-start | bytes 6684672 | tf_op jit(solution)/shard_map/reduce_scatter | solution.py:392
  524.3 19.3 %collective-permute-start.32 = (bf16[192,1024]{1,0:T(8,128)(2,1)}, bf16[192,1024]{1,0:T(8,128)(2,1)}, u32[]{:S(2)}, u32[]{:S(2)}) collective-permute-start(bf16[192,1024]{1,0:T(8,128)(2,1)} %get-tuple-element.91), channel_id=1, source_target_pairs={{0,3},{1,0},{2,1},{3,2},{4,7},{5,4},{6,5},{7,6},{8,11},{9,8},{10,9... | collective-permute-start | bytes 1179656 | tf_op jit(solution)/shard_map/ppermute | solution.py:31
  527.5 16.1 %collective-permute-start.33 = (bf16[192,1024]{1,0:T(8,128)(2,1)S(1)}, bf16[192,1024]{1,0:T(8,128)(2,1)}, u32[]{:S(2)}, u32[]{:S(2)}) collective-permute-start(bf16[192,1024]{1,0:T(8,128)(2,1)S(1)} %get-tuple-element.93), channel_id=1, source_target_pairs={{0,2},{1,3},{2,0},{3,1},{4,6},{5,7},{6,4},{7,5},{8,10},{9,11},{10,... | collective-permute-start | bytes 1179656 | tf_op jit(solution)/shard_map/ppermute | solution.py:31
  527.6 20.5 %collective-permute-start.34 = (bf16[192,1024]{1,0:T(8,128)(2,1)S(1)}, bf16[192,1024]{1,0:T(8,128)(2,1)}, u32[]{:S(2)}, u32[]{:S(2)}) collective-permute-start(bf16[192,1024]{1,0:T(8,128)(2,1)S(1)} %get-tuple-element.92), channel_id=1, source_target_pairs={{0,1},{1,2},{2,3},{3,0},{4,5},{5,6},{6,7},{7,4},{8,9},{9,10},{10,1... | collective-permute-start | bytes 1179656 | tf_op jit(solution)/shard_map/ppermute | solution.py:31
  553.9 14.1 %collective-permute-start.58 = (bf16[768,128]{1,0:T(8,128)(2,1)S(1)}, bf16[768,128]{1,0:T(8,128)(2,1)S(1)}, u32[]{:S(2)}, u32[]{:S(2)}) collective-permute-start(bf16[768,128]{1,0:T(8,128)(2,1)S(1)} %convolution_convert_fusion.15), channel_id=1, source_target_pairs={{0,4},{4,0},{1,5},{5,1},{2,6},{6,2},{3,7},{7,3},{8,12},{12,8},{9,1... | collective-permute-start | bytes 589832 | tf_op jit(solution)/shard_map/ppermute | solution.py:39
  578.6 23.9 %collective-permute-start.59 = (bf16[768,384]{1,0:T(8,128)(2,1)S(1)}, bf16[768,384]{1,0:T(8,128)(2,1)S(1)}, u32[]{:S(2)}, u32[]{:S(2)}) collective-permute-start(bf16[768,384]{1,0:T(8,128)(2,1)S(1)} %get-tuple-element.39), channel_id=1, source_target_pairs={{0,4},{4,0},{1,5},{5,1},{2,6},{6,2},{3,7},{7,3},{8,12},{12,8},{9,1... | collective-permute-start | bytes 1769480 | tf_op jit(solution)/shard_map/ppermute | solution.py:39
  618.6 146.0 %all-gather.7.cloned.1.call-start = ((), (), s32[]{:S(2)}) async-start(), calls=%async_computation.12 | async-start | bytes 2506752 | tf_op jit(solution)/shard_map/all_gather | solution.py:422
  626.0 16.6 %collective-permute-start.62 = (bf16[192,1024]{1,0:T(8,128)(2,1)S(1)}, bf16[192,1024]{1,0:T(8,128)(2,1)S(1)}, u32[]{:S(2)}, u32[]{:S(2)}) collective-permute-start(bf16[192,1024]{1,0:T(8,128)(2,1)S(1)} %get-tuple-element.80), channel_id=1, source_target_pairs={{0,1},{1,2},{2,3},{3,0},{4,5},{5,6},{6,7},{7,4},{8,9},{9,10},{10,1... | collective-permute-start | bytes 1179656 | tf_op jit(solution)/shard_map/ppermute | solution.py:31
  627.5 59.2 %collective-permute-start.63 = (bf16[8,4,2,8,768]{4,3,2,1,0:T(8,128)(2,1)S(1)}, bf16[8,4,2,8,768]{4,3,2,1,0:T(8,128)(2,1)}, u32[]{:S(2)}, u32[]{:S(2)}) collective-permute-start(bf16[8,4,2,8,768]{4,3,2,1,0:T(8,128)(2,1)S(1)} %dynamic-slice_bitcast_fusion), channel_id=1, source_target_pairs={{0,8},{8,0},{1,9},{9,1},{2,10},{10,2},{3,11},{11,3},{4,12},{12,4},... | collective-permute-start | bytes 2359304 | tf_op jit(solution)/shard_map/ppermute | solution.py:39
  677.0 94.6 %all-gather.5.cloned.1.call-start = ((), (), s32[]{:S(2)}) async-start(), calls=%async_computation.11 | async-start | bytes 3342336 | tf_op jit(solution)/shard_map/all_gather | solution.py:422
  683.3 25.4 %all-to-all-start.3 = ((f32[8,1,3072]{2,1,0:T(1,128)}), f32[8,1,3072]{2,1,0:T(1,128)S(1)}, u32[]{:S(2)}, u32[]{:S(2)}) async-start(f32[8,1,3072]{2,1,0:T(1,128)} %all_to_all.27), calls=%async_computation.3 | async-start | bytes 196608 | tf_op jit(solution)/shard_map/all_to_all | solution.py:281
  690.4 16.8 %collective-permute-start.65 = (bf16[8,2,8,768]{3,2,1,0:T(8,128)(2,1)S(1)}, bf16[8,2,8,768]{3,2,1,0:T(8,128)(2,1)S(1)}, u32[]{:S(2)}, u32[]{:S(2)}) collective-permute-start(bf16[8,2,8,768]{3,2,1,0:T(8,128)(2,1)S(1)} %get-tuple-element.123), channel_id=1, source_target_pairs={{0,64},{32,96},{64,0},{96,32},{1,65},{33,97},{65,1},{97,33},{2,66}... | collective-permute-start | bytes 589832 | tf_op jit(solution)/shard_map/ppermute | solution.py:35
  711.4 21.2 %collective-permute-start.68 = (bf16[4,8,768]{2,1,0:T(8,128)(2,1)S(1)}, bf16[4,8,768]{2,1,0:T(8,128)(2,1)S(1)}, u32[]{:S(2)}, u32[]{:S(2)}) collective-permute-start(bf16[4,8,768]{2,1,0:T(8,128)(2,1)S(1)} %constant_dynamic-slice_fusion.2), channel_id=1, source_target_pairs={{0,4},{4,0},{1,5},{5,1},{2,6},{6,2},{3,7},{7,3},{8,12},{12,8},{9,1... | collective-permute-start | bytes 147464 | tf_op jit(solution)/shard_map/ppermute | solution.py:39
  (124 other events, 904.2 us)
Sparse Core Ops, SparseCore 0:
  500.4 71.8 reduce-scatter.4
  574.7 89.9 reduce-scatter.2
  666.9 38.7 all-gather.6
  707.9 35.9 all-gather.4

commit v2 on v1

--- a/solution.py
+++ b/solution.py
@@ -39,6 +39,15 @@
     return lax.ppermute(value, axis, [(0, 1), (1, 0)])
 
 
+def regroup(value, core, y_hi):
+    got = lax.ppermute(value, ("core", "y_hi"), [(1, 2), (2, 1)])
+    return jnp.where(core == y_hi, value, got)
+
+
+def after(value, *others):
+    return lax.optimization_barrier((value, others))[0]
+
+
 def gather_z(rows):
     return jnp.concatenate([rows] + [shift_z(rows, k) for k in (1, 2, 3)], axis=0)
 
@@ -96,12 +105,12 @@
 
 
 def piece_places(info):
-    y, z = info[0], info[1]
+    core, z = info[0], info[1]
     out = []
     for side in range(2):
-        y_of = y if side == 0 else 1 - y
+        half = core if side == 0 else 1 - core
         for k in range(4):
-            out.append(pl.multiple_of((y_of * 4 + ((z - k) & 3)) * PIECE, 64))
+            out.append(pl.multiple_of((half * 4 + ((z - k) & 3)) * PIECE, 64))
     return out
 
 
@@ -259,51 +268,148 @@
     return jax.nn.gelu(values, approximate=True)
 
 
-def core_join(half, core):
-    other = swap(half, "core")
-    return jnp.where(
-        core == 0, jnp.stack([half, other], axis=1), jnp.stack([other, half], axis=1)
-    )
-
-
-def columns_for_all(weight, parts):
-    rows = weight.shape[0]
-    split = weight.reshape(rows, parts, 8, -1)
-    out = []
+def pack_first_kernel(info, weight, small, out):
+    core = info[0]
+    rows = pl.ds(pl.multiple_of(core * 64, 64), 64)
     for place in range(8):
-        own = split[:, :, place].reshape(rows, -1)
-        other = split[:, :, (place + 4) % 8].reshape(rows, -1)
-        out.append(jnp.concatenate([own, other], axis=1))
-    return jnp.stack(out)
+        for side in range(2):
+            for part in range(3):
+                at = part * D + side * 512 + (place % 4) * 128
+                to = (side * 3 + part) * 128
+                out[place, 0:64, to : to + 128] = weight[0, rows, at : at + 128]
+        out[place, 64:80, :] = small[...]
+
+
+def pack_rest_kernel(info, weight, up, down, project, first, second, rows_first, rows_second):
+    core = info[0]
+    rows = pl.ds(pl.multiple_of(core * 64, 64), 64)
+    for place in range(8):
+        for side in range(2):
+            at = side * 2048 + (place % 4) * 512
+            to = side * 512
+            first[place, :, to : to + 512] = up[0, rows, at : at + 512]
+            second[place, :, to : to + 512] = up[1, rows, at : at + 512]
+            for part in range(3):
+                at = part * D + side * 512 + (place % 4) * 128
+                to = D + (side * 3 + part) * 128
+                second[place, :, to : to + 128] = weight[0, rows, at : at + 128]
+    long = pl.ds(pl.multiple_of(core * 256, 64), 256)
+    for layer, out in ((0, rows_first), (1, rows_second)):
+        out[0:256, :] = down[layer, long, :]
+        out[256:320, :] = project[layer, rows, :]
+
+
+def join_columns_kernel(info, got, other, *outs):
+    core = info[0]
+    at = 0
+    for out in outs:
+        width = out.shape[1]
+        for place in range(8):
+            mine = pl.multiple_of(place * 128 + core * 64, 64)
+            theirs = pl.multiple_of(place * 128 + (1 - core) * 64, 64)
+            out[pl.ds(mine, 64), :] = got[place, 0:64, at : at + width]
+            out[pl.ds(theirs, 64), :] = other[place, 0:64, at : at + width]
+        at += width
+
+
+def join_rows_kernel(info, down, project, got, other, down_out, project_out):
+    core, y_hi = info[0], info[3]
+    for out, own, size, at in ((down_out, down, 512, 0), (project_out, project, 128, 256)):
+        half = size // 2
+        out[pl.ds(pl.multiple_of(y_hi * size, 64), size), :] = own[0]
+        mine = pl.multiple_of((1 - y_hi) * size + core * half, 64)
+        theirs = pl.multiple_of((1 - y_hi) * size + (1 - core) * half, 64)
+        out[pl.ds(mine, half), :] = got[at : at + half, :]
+        out[pl.ds(theirs, half), :] = other[at : at + half, :]
+
+
+def layer_block(shape, layer):
+    return pl.BlockSpec((1,) + shape, lambda i: (layer, 0, 0))
+
+
+whole = pl.BlockSpec(memory_space=pltpu.VMEM)
+params_one = pltpu.CompilerParams(vmem_limit_bytes=LIMIT)
+
+
+def pack_first(info, weight, small):
+    return pl.pallas_call(
+        pack_first_kernel,
+        grid=(1,),
+        out_shape=jax.ShapeDtypeStruct((8, 80, 768), bf16),
+        in_specs=[smem, layer_block((128, 3072), 0), whole],
+        out_specs=whole,
+        compiler_params=params_one,
+        name="pack_first",
+    )(info, weight, small)
+
+
+def pack_rest(info, weight, up, down, project):
+    return pl.pallas_call(
+        pack_rest_kernel,
+        grid=(1,),
+        out_shape=(
+            jax.ShapeDtypeStruct((8, 64, 1024), bf16),
+            jax.ShapeDtypeStruct((8, 64, 1792), bf16),
+            jax.ShapeDtypeStruct((320, D), bf16),
+            jax.ShapeDtypeStruct((320, D), bf16),
+        ),
+        in_specs=[smem, layer_block((128, 3072), 1), whole, whole, whole],
+        out_specs=(whole,) * 4,
+        compiler_params=params_one,
+        name="pack_rest",
+    )(info, weight, up, down, project)
+
+
+def join_columns(info, got, other, widths):
+    return pl.pallas_call(
+        join_columns_kernel,
+        out_shape=tuple(jax.ShapeDtypeStruct((D, width), bf16) for width in widths),
+        in_specs=[smem, whole, whole],
+        out_specs=(whole,) * len(widths),
+        compiler_params=params_one,
+        name="join_columns",
+    )(info, got, other)
+
+
+def join_rows(info, down, project, layer, got, other):
+    return pl.pallas_call(
+        join_rows_kernel,
+        grid=(1,),
+        out_shape=(
+            jax.ShapeDtypeStruct((D, D), bf16),
+            jax.ShapeDtypeStruct((256, D), bf16),
+        ),
+        in_specs=[smem, layer_block((512, D), layer), layer_block((128, D), layer), whole, whole],
+        out_specs=(whole,) * 2,
+        compiler_params=params_one,
+        name="join_rows",
+    )(info, down, project, got, other)
 
 
 def to_ctx(value):
     return lax.all_to_all(value, CTX, split_axis=0, concat_axis=0, tiled=True)
 
 
-def core_half(value, core, axis):
-    size = value.shape[axis] // 2
-    return lax.dynamic_slice_in_dim(value, core * size, size, axis)
-
-
-def gather_columns(blocks, core):
-    got = to_ctx(core_half(blocks, core, 1))
-    return core_join(got, core).reshape(D, -1)
-
-
-def gather_rows(rows, core):
-    got = swap(core_half(rows, core, 0), "y_hi")
-    return core_join(got[None], core).reshape(rows.shape)
-
-
-def forward(hidden, normed_all, params, info, slopes):
-    (_, _, w_own, w_other, bias_own, bias_other, project, project_bias) = params[:8]
-    (gain_two, offset_two, up, up_bias, down, down_bias) = params[8:]
-    other = (dot(normed_all, w_other) + bias_other).astype(bf16)
-    received = swap(other, "y_hi")
-    mine = (dot(normed_all, w_own) + bias_own).astype(bf16)
+def in_order(mine, other, core):
+    return jnp.where(
+        core == 0,
+        jnp.concatenate([mine, other], axis=1),
+        jnp.concatenate([other, mine], axis=1),
+    )
+
+
+def columns_at(value, at, width):
+    return lax.dynamic_slice_in_dim(value, at * width, width, 1)
+
+
+def forward(hidden, normed_all, params, info, slopes, core):
+    (_, _, w_in, in_bias, project, project_bias) = params[:6]
+    (gain_two, offset_two, up, up_bias, down, down_bias) = params[6:]
+    projected = (dot(normed_all, w_in) + in_bias).astype(bf16)
+    received = swap(columns_at(projected, 1 - core, 384), "core")
+    mine = columns_at(projected, core, 384)
     ctx_mine, ctx_other, logsum, rows = attend(info, slopes, mine, received)
-    context = jnp.concatenate([ctx_mine, swap(ctx_other, "y_hi")], axis=1)
+    context = in_order(ctx_mine, swap(ctx_other, "core"), core)
     middle = hidden + dot_scatter(context, project, dot) + project_bias
     normed_two = gather_z(norm(middle, gain_two, offset_two).astype(bf16))
     before = dot(normed_two, up) + up_bias
@@ -313,9 +419,9 @@
     return result, kept
 
 
-def backward(gradient, params, kept, info, slopes):
-    (gain_one, _, w_own, w_other, _, _, project, _) = params[:8]
-    (gain_two, _, up, _, down, _) = params[8:]
+def backward(gradient, params, kept, info, slopes, core):
+    (gain_one, _, w_in, _, project, _) = params[:6]
+    (gain_two, _, up, _, down, _) = params[6:]
     hidden, normed_all, logsum, rows, context, middle, normed_two, before, activated = kept
     grad_low = gradient.astype(bf16)
     grad_down = gather_z(grad_low)
@@ -324,23 +430,25 @@
     d_before = jax.vjp(gelu, before)[1](d_act)[0].astype(bf16)
     sum_up = jnp.sum(d_before.astype(f32), axis=0)
     d_normed = dot_scatter(d_before, up, dot_t)
-    g_down = outer(activated, grad_down)
-    g_up = outer(normed_two, d_before)
+    grad_down, d_before = after((grad_down, d_before), d_before)
+    g_down = outer(activated, grad_down).astype(bf16)
+    g_up = outer(normed_two, d_before).astype(bf16)
+    d_normed, g_down, g_up = after((d_normed, g_down, g_up), g_down, g_up)
     d_values, sum_gain_two, sum_offset_two = norm_back(middle, gain_two, d_normed)
     d_middle = gradient + d_values
     grad_out = d_middle.astype(bf16)
     grad_out_all = gather_z(grad_out)
     sum_project = jnp.sum(grad_out.astype(f32), axis=0)
-    ctx_other = dot_t(grad_out_all, project[128:]).astype(bf16)
-    received = swap(ctx_other, "y_hi")
-    ctx_mine = dot_t(grad_out_all, project[:128]).astype(bf16)
-    g_project = outer(context, grad_out_all)
-    d_mine, d_other, sums = attend_back(info, slopes, rows, ctx_mine, received, logsum)
-    d_received = swap(d_other, "y_hi")
-    d_joined = jnp.concatenate([d_mine, d_received], axis=1)
-    w_both = jnp.concatenate([w_own, w_other], axis=1)
-    d_normed_one = dot_scatter(d_joined, w_both, dot_t)
-    g_input = outer(normed_all, d_joined)
+    d_context = dot_t(grad_out_all, project).astype(bf16)
+    received = swap(columns_at(d_context, 1 - core, 128), "core")
+    g_project = outer(context, grad_out_all).astype(bf16)
+    d_mine, d_other, sums = attend_back(
+        info, slopes, rows, columns_at(d_context, core, 128), received, logsum
+    )
+    d_joined = in_order(d_mine, swap(d_other, "core"), core)
+    d_normed_one = dot_scatter(d_joined, w_in, dot_t)
+    g_input = outer(normed_all, d_joined).astype(bf16)
+    d_normed_one, g_input = after((d_normed_one, g_input), g_input)
     d_hidden, sum_gain_one, sum_offset_one = norm_back(hidden, gain_one, d_normed_one)
     big = (g_down, g_up, g_project, g_input)
     small = (
@@ -356,101 +464,80 @@
     return d_middle + d_hidden, big, small
 
 
-def other_half_first(value, width):
-    return jnp.concatenate([value[..., width:], value[..., :width]], axis=-1)
-
-
-def finish(down, up, project, inputs, y_hi, z):
-    if down is not None:
-        down = down[0].astype(f32) + swap(down[1], "y_hi").astype(f32)
-        project = project[0].astype(f32) + swap(project[1], "y_hi").astype(f32)
-    both = inputs if up is None else jnp.concatenate([up, inputs], axis=-1)
-    return down, project, both
-
-
-def spread_rows(both, widths, y_hi):
-    keep = lax.dynamic_slice_in_dim(both, y_hi * 4, 4, 0).astype(f32)
-    send = lax.dynamic_slice_in_dim(both, (1 - y_hi) * 4, 4, 0)
-    got = swap(send, "y_hi")
-    at = 0
-    pieces = []
-    for width in widths:
-        pieces.append(other_half_first(got[..., at : at + width], width // 2))
-        at += width
-    total = (keep + jnp.concatenate(pieces, axis=-1).astype(f32)).astype(bf16)
-    return lax.all_to_all(total, "z", split_axis=0, concat_axis=0, tiled=True)
-
-
-def order_columns(rows, parts, y_hi):
-    *lead, four, count, width = rows.shape
-    split = rows.reshape(*lead, four, count, 2, parts, width // (2 * parts))
-    split = jnp.where(y_hi == 0, split, split[..., ::-1, :, :])
-    return split
-
-
-def reduce_grp(pack):
-    return lax.psum_scatter(pack, GRP, scatter_dimension=0, tiled=True)
-
-
-def rows_by_group(value):
-    return value.reshape(8, 16, 8, -1).transpose(1, 0, 2, 3).reshape(16, 64, -1)
-
-
-def pack_big(g_down, g_up, g_project, g_input):
-    pieces = [
-        g_down.reshape(2, 16, 32, D).transpose(1, 0, 2, 3).reshape(16, 64, D),
-        rows_by_group(g_up),
-        g_project.reshape(2, 16, 8, 4, 256).transpose(1, 0, 2, 3, 4).reshape(16, 64, 256),
-    ]
-    if g_input is not None:
-        pieces.append(rows_by_group(g_input))
-    return jnp.concatenate([piece.astype(bf16) for piece in pieces], axis=-1)
-
-
-def reduce_big(g_down, g_up, g_project, g_input, y_hi):
-    packed = reduce_grp(pack_big(g_down, g_up, g_project, g_input)).reshape(64, -1)
-    rows = jnp.concatenate([packed[:, :D], packed[:, 2 * D : 2 * D + 256]], axis=1)
-    rows = rows.reshape(2, 32, D + 256)
-    rows = rows[0].astype(f32) + swap(rows[1], "y_hi").astype(f32)
-    widths = [D]
-    both = packed[:, D : 2 * D]
-    if g_input is not None:
-        both = jnp.concatenate([both, packed[:, 2 * D + 256 :]], axis=1)
-        widths.append(768)
-    columns = spread_rows(both.reshape(8, 8, -1), widths, y_hi)
-    full = jnp.concatenate([rows.astype(bf16), columns.reshape(32, -1)], axis=1)
-    full = lax.all_gather(full, GRP, axis=0, tiled=False).astype(f32)
-    down = full[:, :, :D].reshape(512, D)
-    project = full[:, :, D : D + 256].reshape(16 * 8, D)
-    up = input_columns(full[:, :, D + 256 : 2 * D + 256], 1, y_hi)
-    inputs = None
-    if g_input is not None:
-        inputs = input_columns(full[:, :, 2 * D + 256 :], 3, y_hi)
-    return down, up, project, inputs
-
-
-def input_columns(rows, parts, y_hi):
+def take(value, at, axis=0):
+    return lax.dynamic_index_in_dim(value, at, axis, keepdims=False)
+
+
+def groups_first(value, shape):
+    split = value.reshape(shape)
+    order = (1, 0) + tuple(range(2, len(shape)))
+    return split.transpose(order)
+
+
+def pack_outer(g_down, g_up):
+    pieces = (
+        groups_first(g_down, (2, 16, 32, D)).reshape(16, 64, D),
+        groups_first(g_up, (8, 16, 8, D)).reshape(16, 64, D),
+    )
+    return jnp.concatenate(pieces, axis=-1)
+
+
+def pack_inner(g_project, g_input):
+    pieces = (
+        groups_first(g_project, (2, 16, 8, 4, 256)).reshape(16, 64, 256),
+        groups_first(g_input, (8, 16, 8, 768)).reshape(16, 64, 768),
+    )
+    return jnp.concatenate(pieces, axis=-1)
+
+
+def sum_pairs(value, at, axis):
+    return take(value, at).astype(f32) + swap(take(value, 1 - at), axis).astype(f32)
+
+
+def own_rows(summed, split, y_hi):
+    both = sum_pairs(summed.reshape(2, 32, -1), y_hi, "y_hi").astype(bf16)
+    columns = both[:, split:].reshape(4, 8, -1)
+    columns = lax.all_to_all(columns, "z", split_axis=0, concat_axis=0, tiled=True)
+    return jnp.concatenate([both[:, :split], columns.reshape(32, -1)], axis=1)
+
+
+def sum_steps(pack, place):
+    x, y_lo, core = place
+    total = sum_pairs(pack.reshape(2, 4, 2, 64, -1), core, "core")
+    low = total.astype(bf16)
+    total = take(total, x)
+    for k in (1, 2, 3):
+        total = total + shift_x(take(low, (x + k) % 4), k).astype(f32)
+    return sum_pairs(total.astype(bf16), y_lo, "y_lo")
+
+
+def spread_steps(rows, place):
+    x, y_lo, core = place
+    other = swap(rows, "y_lo")
+    both = jnp.where(y_lo == 0, jnp.stack([rows, other]), jnp.stack([other, rows]))
+    blocks = jnp.stack([both] + [shift_x(both, k) for k in (3, 2, 1)])
+    blocks = lax.dynamic_slice_in_dim(jnp.concatenate([blocks, blocks]), (4 - x) % 4, 4, 0)
+    other = swap(blocks, "core")
+    both = jnp.where(core == 0, jnp.stack([blocks, other]), jnp.stack([other, blocks]))
+    return both.reshape(16, *rows.shape)
+
+
+def order_columns(rows, parts):
     split = rows.reshape(16, 4, 8, 2, parts, -1)
-    split = jnp.where(y_hi == 0, split, split[:, :, :, ::-1])
     return split.transpose(0, 2, 4, 3, 1, 5).reshape(128, -1)
 
 
-def reduce_input(g_input, y_hi, x, y_lo, core):
-    low = g_input.astype(bf16).reshape(8, 4, 2, 2, 8, 768)
-    take = lambda value, at, axis: lax.dynamic_index_in_dim(value, at, axis, keepdims=False)
-    total = take(low, core, 3).astype(f32) + swap(take(low, 1 - core, 3), "core").astype(f32)
-    low = total.astype(bf16)
-    total = take(total, x, 1)
-    for k in (1, 2, 3):
-        total = total + shift_x(take(low, (x + k) % 4, 1), k).astype(f32)
-    low = total.astype(bf16)
-    total = take(total, y_lo, 1) + swap(take(low, 1 - y_lo, 1), "y_lo").astype(f32)
-    columns = spread_rows(total.astype(bf16), [768], y_hi).reshape(32, 768)
-    full = lax.all_gather(columns, GRP, axis=0, tiled=False).astype(f32)
-    return input_columns(full, 3, y_hi)
-
-
-def pack_small(small, place):
+def unpack_outer(full):
+    full = full.astype(f32)
+    return full[:, :, :D].reshape(512, D), order_columns(full[:, :, D:], 1)
+
+
+def unpack_inner(full):
+    full = full.astype(f32)
+    return full[:, :, :256].reshape(128, D), order_columns(full[:, :, 256:], 3)
+
+
+def pack_small(small, place, z):
     (gain_one, offset_one, project, gain_two, offset_two, down, sums, up) = small
     vectors = [
         v.reshape(8, 128) for v in (gain_one, offset_one, project, gain_two, offset_two, down)
@@ -458,10 +545,12 @@
     sums = sums.reshape(-1)
     inputs = lax.dynamic_update_slice_in_dim(jnp.zeros((2 * D,), f32), sums[:128], place * 128, 0)
     inputs = lax.dynamic_update_slice_in_dim(inputs, sums[256:], D + place * 128, 0)
-    units = jnp.zeros((8, 512), f32)
-    units = lax.dynamic_update_slice_in_dim(units, up[None, :512], place, 0)
-    units = lax.dynamic_update_slice_in_dim(units, up[None, 512:], (place + 4) % 8, 0)
-    return jnp.concatenate(vectors + [inputs.reshape(8, 256), units], axis=1)
+    units = lax.dynamic_update_slice_in_dim(
+        jnp.zeros((2, 4, 512), f32), up.reshape(2, 1, 512), z, 1
+    )
+    return jnp.concatenate(
+        vectors + [inputs.reshape(8, 256), units.reshape(8, 512)], axis=1
+    )
 
 
 def on_device(
@@ -483,13 +572,16 @@
 ):
     y_hi, z = lax.axis_index("y_hi"), lax.axis_index("z")
     x, y_lo, core = lax.axis_index("x"), lax.axis_index("y_lo"), lax.axis_index("core")
-    place = y_hi * 4 + z
+    place = core * 4 + z
+    rows_in = regroup(inputs[0], core, y_hi)
     cut = jnp.sum((segments[0] < 2).astype(jnp.int32))
-    info = jnp.stack([y_hi, z, cut]).astype(jnp.int32)
+    cut = regroup(jnp.broadcast_to(cut, (1, 128)), core, y_hi)[0, 0]
+    info = jnp.stack([core, z, cut, y_hi]).astype(jnp.int32)
+    corner = jnp.stack([core, z, y_hi, y_hi]).astype(jnp.int32)
     heads = (place * 2 + jnp.arange(2, dtype=jnp.int32)).astype(f32)
     slopes = jnp.exp2(-8.0 * (heads + 1.0) / HEADS)
 
-    raw_all = gather_z(inputs[0])
+    raw_all = gather_z(rows_in)
     small = jnp.concatenate(
         [
             norm_one_gain,
@@ -504,63 +596,48 @@
         axis=1,
     )
     small = jnp.concatenate([small.reshape(4, 768), jnp.zeros((12, 768), bf16)], axis=0)
-    first = core_half(columns_for_all(input_weight[0], 3), core, 1)
-    first = jnp.concatenate([first, jnp.broadcast_to(small[None], (8, 16, 768))], axis=1)
-    first = to_ctx(first)
+    first = to_ctx(pack_first(corner, input_weight, small))
     small = first[:, 64:68].reshape(8, LAYERS, -1).transpose(1, 0, 2).astype(f32)
-    w_first = core_join(first[:, :64], core).reshape(D, 768)
-    up_first = gather_columns(columns_for_all(up_weight[0], 1), core)
-    second = gather_columns(
-        jnp.concatenate(
-            [columns_for_all(input_weight[1], 3), columns_for_all(up_weight[1], 1)], axis=2
-        ),
-        core,
-    )
-    w_all = (w_first, second[:, :768])
-    up_all = (up_first, second[:, 768:])
+    (w_first,) = join_columns(corner, first, swap(first[:, :64], "core"), (768,))
+
+    packed = pack_rest(corner, input_weight, up_weight, down_weight, project_weight)
+    up_first = to_ctx(packed[0])
+    second = to_ctx(packed[1])
+    (up_first,) = join_columns(corner, up_first, swap(up_first, "core"), (D,))
+    up_second, w_second = join_columns(corner, second, swap(second, "core"), (D, 768))
+    w_all = (w_first, w_second)
+    up_all = (up_first, up_second)
 
     layers = []
     for layer in range(LAYERS):
-        rows = jnp.concatenate([down_weight[layer], project_weight[layer]], axis=0)
-        rows_other = gather_rows(rows, core)
-        down = jnp.concatenate([rows[:512], rows_other[:512]], axis=0)
-        project = jnp.concatenate([rows[512:], rows_other[512:]], axis=0)
+        got = swap(packed[2 + layer], "y_hi")
+        down, project = join_rows(
+            corner, down_weight, project_weight, layer, got, swap(got, "core")
+        )
         vectors = [small[layer, :, i * 128 : (i + 1) * 128].reshape(D) for i in range(6)]
-        in_bias = small[layer, :, 768:1024].reshape(2 * D)
-        unit_bias = small[layer, :, 1024:1536]
-
-        def bias_of(at):
-            query = lax.dynamic_slice_in_dim(in_bias, at * 128, 128)
-            value = lax.dynamic_slice_in_dim(in_bias, D + at * 128, 128)
-            return jnp.concatenate([query, jnp.zeros((128,), f32), value])
-
-        partner = (place + 4) % 8
-        unit = jnp.concatenate(
-            [
-                lax.dynamic_index_in_dim(unit_bias, place, 0, keepdims=False),
-                lax.dynamic_index_in_dim(unit_bias, partner, 0, keepdims=False),
-            ]
-        )
+        in_bias = small[layer, :, 768:1024].reshape(2, 2, 4, 128)
+        in_bias = lax.dynamic_index_in_dim(in_bias, z, 2, keepdims=False)
+        in_bias = jnp.stack([in_bias[0], jnp.zeros((2, 128), f32), in_bias[1]], axis=1)
+        unit_bias = small[layer, :, 1024:1536].reshape(2, 4, 512)
+        unit_bias = lax.dynamic_index_in_dim(unit_bias, z, 1, keepdims=False).reshape(D)
         layers.append(
             (
                 vectors[0],
                 vectors[1],
-                w_all[layer][:, :384],
-                w_all[layer][:, 384:],
-                bias_of(place),
-                bias_of(partner),
+                w_all[layer],
+                in_bias.reshape(768),
                 project,
                 vectors[2],
                 vectors[3],
                 vectors[4],
                 up_all[layer],
-                unit,
+                unit_bias,
                 down,
                 vectors[5],
             )
         )
 
-    hidden = inputs[0].astype(f32)
+    hidden = rows_in.astype(f32)
     kept = []
     for layer in range(LAYERS):
         params = layers[layer]
@@ -568,27 +645,40 @@
             normed_all = norm(raw_all.astype(f32), params[0], params[1]).astype(bf16)
         else:
             normed_all = gather_z(norm(hidden, params[0], params[1]).astype(bf16))
-        hidden, state = forward(hidden, normed_all, params, info, slopes)
+        hidden, state = forward(hidden, normed_all, params, info, slopes, core)
         kept.append(state)
-    gradient = cotangent[0].astype(f32)
-    bigs = [None] * LAYERS
+    gradient = regroup(cotangent[0], core, y_hi).astype(f32)
+    slot = (x, y_lo, core)
+    finals = [None] * LAYERS
     smalls = [None] * LAYERS
     for layer in (1, 0):
-        gradient, big, smalls[layer] = backward(gradient, layers[layer], kept[layer], info, slopes)
+        gradient, big, smalls[layer] = backward(
+            gradient, layers[layer], kept[layer], info, slopes, core
+        )
+        outer_pack = pack_outer(big[0], big[1])
+        inner_pack = pack_inner(big[2], big[3])
         if layer == 1:
-            bigs[1] = reduce_big(*big, y_hi)
+            outer_sum = lax.psum_scatter(outer_pack, GRP, scatter_dimension=0, tiled=True)
+            inner_sum = lax.psum_scatter(inner_pack, GRP, scatter_dimension=0, tiled=True)
+            outer_sum = own_rows(outer_sum.reshape(64, -1), D, y_hi)
+            inner_sum = own_rows(inner_sum.reshape(64, -1), 256, y_hi)
+            both = lax.all_gather(jnp.concatenate([outer_sum, inner_sum], axis=1), GRP)
+            finals[1] = unpack_outer(both[:, :, : 2 * D]) + unpack_inner(both[:, :, 2 * D :])
         else:
-            down, up, project, _ = reduce_big(*big[:3], None, y_hi)
-            bigs[0] = (down, up, project, reduce_input(big[3], y_hi, x, y_lo, core))
-    packed = jnp.concatenate([pack_small(s, place) for s in smalls], axis=1)
+            outer_sum = own_rows(sum_steps(outer_pack, slot).astype(bf16), D, y_hi)
+            inner_sum = own_rows(sum_steps(inner_pack, slot).astype(bf16), 256, y_hi)
+            finals[0] = unpack_outer(spread_steps(outer_sum, slot)) + unpack_inner(
+                spread_steps(inner_sum, slot)
+            )
+    packed = jnp.concatenate([pack_small(s, place, z) for s in smalls], axis=1)
     vector = jnp.sum(to_ctx(packed), axis=0)
     vector = jnp.sum(lax.all_gather(vector.reshape(8, -1), GRP, axis=0, tiled=False), axis=0)
     vector = vector.reshape(LAYERS, -1)
     parts = [vector[:, i * 128 : (i + 1) * 128] for i in range(6)]
-    both = [jnp.stack([bigs[0][i], bigs[1][i]]) for i in range(4)]
+    both = [jnp.stack([finals[0][i], finals[1][i]]) for i in range(4)]
     return (
-        hidden[None],
-        gradient[None],
+        regroup(hidden, core, y_hi)[None],
+        regroup(gradient, core, y_hi)[None],
         parts[0],
         parts[1],
         both[3],

time: 809 us -> 782 us (0.967)
  waiting for transfers between devices: 352 us -> 285 us
  starting transfers between devices: 157 us -> 177 us
  blocking collectives: 39.6 us -> 23.3 us
  matrix products: 60.9 us -> 76.3 us
  local copies, waits for them, and re-layouts: 64.6 us -> 79.5 us
  Pallas kernels: 37.9 us -> 48.8 us
    ppermute x22 -> x27, waiting for transfers between devices: 85.6 us -> 7.49 us  [swap(): return lax.ppermute(value, axis, [(0, 1), (1, 0)])]
    ppermute x0 -> x5, starting transfers between devices: none -> 25.6 us  [regroup(): got = lax.ppermute(value, ('core', 'y_hi'), [(1, 2), (2, 1)])]
    all_gather x1 -> x0, blocking collectives: 21.4 us -> none  [reduce_input(): full = lax.all_gather(columns, GRP, axis=0, tiled=False).astype(f32)]
    reduce_scatter x2, waiting for transfers between devices: 20.4 us -> 0.02 us  [the longest x1 0.02 us: on_device(): lax.psum_scatter(inner_pack, GRP, scatter_dimension=0, tiled=True)]
    unnamed x238 -> x288, local copies, waits for them, and re-layouts: 16.4 us -> 35.5 us
    ppermute x3 -> x12, waiting for transfers between devices: 11.2 us -> 29.3 us  [shift_x(): return lax.ppermute(value, 'x', [(i, (i + step) % 4) for i in range(4)])]
    slice x27 -> x17, local copies, waits for them, and re-layouts: 22.4 us -> 7.98 us  [the longest x2 3.55 us: unpack_outer(): return (full[:, :, :D].reshape(512, D), order_columns(full[:, :, D:], 1))]
    reshape x4 -> x19, local copies, waits for them, and re-layouts: 0.43 us -> 12.9 us  [the longest x8 5.86 us: groups_first(): split = value.reshape(shape)]
  transfers between devices with their start and end apart: 84 -> 103, of which waited for: 49 -> 58; matrix products, arithmetic and copies ran while one was open for 18% -> 20% of each run, Pallas kernels for 3% -> 5%
where the time goes in v2:
time: 782 us; the launch traced here: 774 us
  waiting for transfers between devices  285 us (36%)
  starting transfers between devices  177 us (23%)
  local copies, waits for them, and re-layouts  79.5 us (10%)
  matrix products  76.3 us (10%)
  other arithmetic  66.7 us (9%)
  Pallas kernels  48.8 us (6%)
  blocking collectives  23.3 us (3%)
  between operations  16.7 us (2%)
    ppermute x48, waiting for transfers between devices, shift_z(): return lax.ppermute(value, 'z', [(i, (i + step) % 4) for i in range(4)])  213 us
    ppermute x27, starting transfers between devices, swap(): return lax.ppermute(value, axis, [(0, 1), (1, 0)])  54 us
    ppermute x48, starting transfers between devices, shift_z(): return lax.ppermute(value, 'z', [(i, (i + step) % 4) for i in range(4)])  50.1 us
    unnamed x288, local copies, waits for them, and re-layouts  35.5 us
    dot_general x12, matrix products, dot(): return jnp.dot(left, right, preferred_element_type=f32)  29.9 us
    ppermute x12, waiting for transfers between devices, shift_x(): return lax.ppermute(value, 'x', [(i, (i + step) % 4) for i in range(4)])  29.3 us
    ppermute x5, starting transfers between devices, regroup(): got = lax.ppermute(value, ('core', 'y_hi'), [(1, 2), (2, 1)])  25.6 us
    dot_general x12, matrix products, dot_t(): lax.dot_general(left, right, (((1,), (1,)), ((), ())), preferred_element_...  24.3 us
  transfers between devices with their start and end apart: 103, of which 58 were waited for; matrix products, arithmetic and copies ran while one was open for 20% of the time, Pallas kernels for 5%

profile of v2, /device:TPU:1, one launch (start us, length us, event | category | flops | bytes accessed | tf_op | source)
XLA Modules:
  0.0 773.9 jit_solution(5593558757221491241)
XLA Ops:
  7.2 6.2 collective-permute-start
  22.5 3.7 collective-permute-start.3
  31.6 3.6 all-to-all-start
  61.4 3.4 add_convert_fusion.1
  70.2 3.8 collective-permute-done.1
  75.9 9.5 %attend.2 = (bf16[768,128]{1,0:T(8,128)(2,1)S(1)}, bf16[768,128]{1,0:T(8,128)(2,1)}, f32[2,1536]{1,0:T(2,128)S(1)}, bf16[1536,384]{1,0:T(8,128)(2,1)S(1)}) custom-call(s32[4]{0:T(128)S(1)} %add_add_fusion.info, f32[2]{0:T(128)S(1)} %multiply_exponential_fusion.slopes, bf16[768,384]{1,0:T(8,128)(2,1)S(1)} %copy-done.28, ...), custom_call_target="tpu_custom_call" | custom-call | flops 716800000 | bytes 3000000 | tf_op jit(solution)/shard_map/attend/pallas_call | solution.py:196
  86.4 4.4 all-to-all-start.1
  100.8 4.6 all-to-all-done.1.got
  107.1 5.3 collective-permute-done.10
  114.6 8.2 %collective-permute-done.12 = bf16[192,1024]{1,0:T(8,128)(2,1)} collective-permute-done((bf16[192,1024]{1,0:T(8,128)(2,1)}, bf16[192,1024]{1,0:T(8,128)(2,1)}, u32[]{:S(2)}, u32[]{:S(2)}) %collective-permute-start.12) | collective-permute-done | bytes 393248 | tf_op jit(solution)/shard_map/ppermute | solution.py:31
  128.6 5.8 all-to-all-start.2
  139.1 5.2 collective-permute-done.14
  144.3 11.7 %collective-permute-done.15 = bf16[192,1024]{1,0:T(8,128)(2,1)} collective-permute-done((bf16[192,1024]{1,0:T(8,128)(2,1)S(1)}, bf16[192,1024]{1,0:T(8,128)(2,1)}, u32[]{:S(2)}, u32[]{:S(2)}) %collective-permute-start.15) | collective-permute-done | bytes 393248 | tf_op jit(solution)/shard_map/ppermute | solution.py:31
  155.9 5.3 multiply_convert_fusion.1
  167.2 5.5 collective-permute-start.23
  172.7 4.5 collective-permute-done.17
  177.2 9.4 %collective-permute-done.19 = bf16[192,1024]{1,0:T(8,128)(2,1)} collective-permute-done((bf16[192,1024]{1,0:T(8,128)(2,1)}, bf16[192,1024]{1,0:T(8,128)(2,1)}, u32[]{:S(2)}, u32[]{:S(2)}) %collective-permute-start.19) | collective-permute-done | bytes 393248 | tf_op jit(solution)/shard_map/ppermute | solution.py:31
  193.3 4.1 collective-permute-start.26
  199.8 4.8 collective-permute-done.20
  206.4 4.1 collective-permute-done.22
  217.4 8.3 %attend.3 = (bf16[768,128]{1,0:T(8,128)(2,1)S(1)}, bf16[768,128]{1,0:T(8,128)(2,1)S(1)}, f32[2,1536]{1,0:T(2,128)S(1)}, bf16[1536,384]{1,0:T(8,128)(2,1)S(1)}) custom-call(s32[4]{0:T(128)S(1)} %add_add_fusion.info, f32[2]{0:T(128)S(1)} %multiply_exponential_fusion.slopes, bf16[768,384]{1,0:T(8,128)(2,1)S(1)} %get-tuple-element.149.mine, ...), custom_call_target="tpu_custom_call" | custom-call | flops 716800000 | bytes 3000000 | tf_op jit(solution)/shard_map/attend/pallas_call | solution.py:196
  227.1 6.0 collective-permute-start.38
  242.9 14.7 %collective-permute-done.28 = bf16[192,1024]{1,0:T(8,128)(2,1)S(1)} collective-permute-done((bf16[192,1024]{1,0:T(8,128)(2,1)S(1)}, bf16[192,1024]{1,0:T(8,128)(2,1)S(1)}, u32[]{:S(2)}, u32[]{:S(2)}) %collective-permute-start.28) | collective-permute-done | bytes 393248 | tf_op jit(solution)/shard_map/ppermute | solution.py:31
  257.6 3.9 collective-permute-start.41
  263.8 3.9 collective-permute-done.39
  268.5 7.8 %collective-permute-done.40 = bf16[192,1024]{1,0:T(8,128)(2,1)S(1)} collective-permute-done((bf16[192,1024]{1,0:T(8,128)(2,1)S(1)}, bf16[192,1024]{1,0:T(8,128)(2,1)S(1)}, u32[]{:S(2)}, u32[]{:S(2)}) %collective-permute-start.40) | collective-permute-done | bytes 393248 | tf_op jit(solution)/shard_map/ppermute | solution.py:31
  278.8 5.2 collective-permute-done.31
  284.0 4.3 collective-permute-done.32
  289.3 5.2 multiply_convert_fusion
  294.5 5.3 convert_reduce_fusion.1
  314.0 6.3 collective-permute-done.44
  327.2 17.2 %collective-permute-done.45 = bf16[192,1024]{1,0:T(8,128)(2,1)S(1)} collective-permute-done((bf16[192,1024]{1,0:T(8,128)(2,1)}, bf16[192,1024]{1,0:T(8,128)(2,1)S(1)}, u32[]{:S(2)}, u32[]{:S(2)}) %collective-permute-start.45) | collective-permute-done | bytes 393248 | tf_op jit(solution)/shard_map/ppermute | solution.py:31
  349.7 10.6 %attend_back.2 = (bf16[768,384]{1,0:T(8,128)(2,1)S(1)}, bf16[768,384]{1,0:T(8,128)(2,1)S(1)}, f32[1,384]{1,0:T(1,128)S(1)}) custom-call(s32[4]{0:T(128)S(1)} %add_add_fusion.info, f32[2]{0:T(128)S(1)} %multiply_exponential_fusion.slopes, bf16[1536,384]{1,0:T(8,128)(2,1)S(1)} %copy-done.32, bf16[768,128]{1,0:T(8,128)(2,1)S(1)} %get-tuple-element.164.mine, ...), custom_call_target="tpu_custom_call" | custom-call | flops 1792000000 | bytes 5000000 | tf_op jit(solution)/shard_map/attend_back/pallas_call | solution.py:220
  371.1 5.3 collective-permute-done.50
  379.4 8.6 %collective-permute-done.52 = bf16[192,1024]{1,0:T(8,128)(2,1)S(1)} collective-permute-done((bf16[192,1024]{1,0:T(8,128)(2,1)S(1)}, bf16[192,1024]{1,0:T(8,128)(2,1)S(1)}, u32[]{:S(2)}, u32[]{:S(2)}) %collective-permute-start.52) | collective-permute-done | bytes 393248 | tf_op jit(solution)/shard_map/ppermute | solution.py:31
  400.1 5.3 collective-permute-done.34
  406.2 10.5 %collective-permute-done.36 = bf16[192,1024]{1,0:T(8,128)(2,1)} collective-permute-done((bf16[192,1024]{1,0:T(8,128)(2,1)}, bf16[192,1024]{1,0:T(8,128)(2,1)}, u32[]{:S(2)}, u32[]{:S(2)}) %collective-permute-start.36) | collective-permute-done | bytes 393248 | tf_op jit(solution)/shard_map/ppermute | solution.py:31
  419.9 6.1 collective-permute-start.37
  434.6 6.9 collective-permute-done.53
  441.6 4.5 collective-permute-done.54
  447.1 6.0 convert_reduce_fusion.2
  465.2 9.5 %collective-permute-done.56 = bf16[192,1024]{1,0:T(8,128)(2,1)S(1)} collective-permute-done((bf16[192,1024]{1,0:T(8,128)(2,1)S(1)}, bf16[192,1024]{1,0:T(8,128)(2,1)S(1)}, u32[]{:S(2)}, u32[]{:S(2)}) %collective-permute-start.56) | collective-permute-done | bytes 393248 | tf_op jit(solution)/shard_map/ppermute | solution.py:31
  474.7 4.0 collective-permute-done.58
  489.8 12.5 %collective-permute-done.59 = bf16[192,1024]{1,0:T(8,128)(2,1)S(1)} collective-permute-done((bf16[192,1024]{1,0:T(8,128)(2,1)}, bf16[192,1024]{1,0:T(8,128)(2,1)S(1)}, u32[]{:S(2)}, u32[]{:S(2)}) %collective-permute-start.59) | collective-permute-done | bytes 393248 | tf_op jit(solution)/shard_map/ppermute | solution.py:31
  508.4 10.6 %attend_back.3 = (bf16[768,384]{1,0:T(8,128)(2,1)S(1)}, bf16[768,384]{1,0:T(8,128)(2,1)S(1)}, f32[1,384]{1,0:T(1,128)S(1)}) custom-call(s32[4]{0:T(128)S(1)} %add_add_fusion.info, f32[2]{0:T(128)S(1)} %multiply_exponential_fusion.slopes, bf16[1536,384]{1,0:T(8,128)(2,1)S(1)} %copy-done.30, bf16[768,128]{1,0:T(8,128)(2,1)S(1)} %get-tuple-element.162.mine, ...), custom_call_target="tpu_custom_call" | custom-call | flops 1792000000 | bytes 5000000 | tf_op jit(solution)/shard_map/attend_back/pallas_call | solution.py:220
  533.3 4.9 collective-permute-done.64
  541.4 8.7 %collective-permute-done.66 = bf16[192,1024]{1,0:T(8,128)(2,1)S(1)} collective-permute-done((bf16[192,1024]{1,0:T(8,128)(2,1)S(1)}, bf16[192,1024]{1,0:T(8,128)(2,1)S(1)}, u32[]{:S(2)}, u32[]{:S(2)}) %collective-permute-start.66) | collective-permute-done | bytes 393248 | tf_op jit(solution)/shard_map/ppermute | solution.py:31
  555.2 4.0 all-to-all-start.3
  561.5 5.3 collective-permute-start.67
  566.9 23.3 %all_gather.9 = f32[16,8,384]{2,1,0:T(8,128)S(1)} all-gather(f32[1,8,384]{2,1,0:T(8,128)S(1)} %all_gather_reshape.3), channel_id=1, replica_groups=mesh['x'=4,'y_lo'=2,'core'=2,'y_hi'=2,'z'=4] {'x','y_lo','core'}, dimensions={0}, use_global_device_ids=true | all-gather | bytes 208896 | tf_op jit(solution)/shard_map/all_gather | solution.py:675
  600.6 7.7 collective-permute-done.82
  608.3 10.4 %collective-permute-done.83 = bf16[2,64,2048]{2,1,0:T(8,128)(2,1)S(1)} collective-permute-done((bf16[2,64,2048]{2,1,0:T(8,128)(2,1)S(1)}, bf16[2,64,2048]{2,1,0:T(8,128)(2,1)S(1)}, u32[]{:S(2)}, u32[]{:S(2)}) %collective-permute-start.83) | collective-permute-done | bytes 524320 | tf_op jit(solution)/shard_map/ppermute | solution.py:35
  619.9 5.2 collective-permute-done.69
  625.1 4.9 collective-permute-done.70
  630.9 4.2 collective-permute-start.86
  641.3 4.1 all-to-all-start.4
  646.1 3.7 all-to-all-done.4
  653.6 4.0 all-to-all-done.7
  658.1 4.6 collective-permute-start.75
  682.8 3.9 all-to-all-start.6
  691.1 3.9 all-to-all-start.5
  701.3 14.9 %collective-permute-start.78 = (bf16[4,2,32,1024]{3,2,1,0:T(8,128)(2,1)S(1)}, bf16[4,2,32,1024]{3,2,1,0:T(8,128)(2,1)S(1)}, u32[]{:S(2)}, u32[]{:S(2)}) collective-permute-start(bf16[4,2,32,1024]{3,2,1,0:T(8,128)(2,1)S(1)} %constant_dynamic-slice_fusion.3), channel_id=1, source_target_pairs={{0,8},{8,0},{1,9},{9,1},{2,10},{10,2},{3,11},{11,3},{4,12},{12,4},... | collective-permute-start | bytes 1572872 | tf_op jit(solution)/shard_map/ppermute | solution.py:39
  735.9 10.7 %all-gather.3.cloned.1.call-done = bf16[512,3072]{1,0:T(8,128)(2,1)} async-done(((bf16[32,3072]{1,0:T(8,128)(2,1)}), bf16[512,3072]{1,0:T(8,128)(2,1)}) %all-gather.3.cloned.1.call-update) | async-done | bytes 3145744 | tf_op jit(solution)/shard_map/all_gather | solution.py:665
  756.7 4.2 pad_maximum_fusion.2
  (665 shorter events, 323.0 us)
Async XLA Ops:
  20.8 25.6 %collective-permute-start.2 = (bf16[192,1024]{1,0:T(8,128)(2,1)S(1)}, bf16[192,1024]{1,0:T(8,128)(2,1)}, u32[]{:S(2)}, u32[]{:S(2)}) collective-permute-start(bf16[192,1024]{1,0:T(8,128)(2,1)S(1)} %get-tuple-element.122), channel_id=1, source_target_pairs={{0,1},{1,2},{2,3},{3,0},{4,5},{5,6},{6,7},{7,4},{8,9},{9,10},{10,1... | collective-permute-start | bytes 1179656 | tf_op jit(solution)/shard_map/ppermute | solution.py:31
  22.5 23.9 %collective-permute-start.3 = (bf16[192,1024]{1,0:T(8,128)(2,1)S(1)}, bf16[192,1024]{1,0:T(8,128)(2,1)}, u32[]{:S(2)}, u32[]{:S(2)}) collective-permute-start(bf16[192,1024]{1,0:T(8,128)(2,1)S(1)} %get-tuple-element.122), channel_id=1, source_target_pairs={{0,2},{1,3},{2,0},{3,1},{4,6},{5,7},{6,4},{7,5},{8,10},{9,11},{10,... | collective-permute-start | bytes 1179656 | tf_op jit(solution)/shard_map/ppermute | solution.py:31
  26.2 20.2 %collective-permute-start.4 = (bf16[192,1024]{1,0:T(8,128)(2,1)S(1)}, bf16[192,1024]{1,0:T(8,128)(2,1)}, u32[]{:S(2)}, u32[]{:S(2)}) collective-permute-start(bf16[192,1024]{1,0:T(8,128)(2,1)S(1)} %get-tuple-element.122), channel_id=1, source_target_pairs={{0,3},{1,0},{2,1},{3,2},{4,7},{5,4},{6,5},{7,6},{8,11},{9,8},{10,9... | collective-permute-start | bytes 1179656 | tf_op jit(solution)/shard_map/ppermute | solution.py:31
  31.6 18.1 %all-to-all-start = ((bf16[8,80,768]{2,1,0:T(8,128)(2,1)}), bf16[8,80,768]{2,1,0:T(8,128)(2,1)S(1)}, u32[]{:S(2)}, u32[]{:S(2)}) async-start(bf16[8,80,768]{2,1,0:T(8,128)(2,1)} %copy-done.9), calls=%async_computation | async-start | bytes 1966080 | tf_op jit(solution)/shard_map/all_to_all | solution.py:390
  43.4 26.2 %collective-permute-start.8 = (bf16[320,1024]{1,0:T(8,128)(2,1)}, bf16[320,1024]{1,0:T(8,128)(2,1)}, u32[]{:S(2)}, u32[]{:S(2)}) collective-permute-start(bf16[320,1024]{1,0:T(8,128)(2,1)} %get-tuple-element.54), channel_id=1, source_target_pairs={{0,4},{4,0},{1,5},{5,1},{2,6},{6,2},{3,7},{7,3},{8,12},{12,8},{9,1... | collective-permute-start | bytes 1966088 | tf_op jit(solution)/shard_map/ppermute | solution.py:39
  69.6 21.1 %collective-permute-start.9 = (bf16[320,1024]{1,0:T(8,128)(2,1)}, bf16[320,1024]{1,0:T(8,128)(2,1)S(1)}, u32[]{:S(2)}, u32[]{:S(2)}) collective-permute-start(bf16[320,1024]{1,0:T(8,128)(2,1)} %collective-permute-done.8.got), channel_id=1, source_target_pairs={{0,8},{8,0},{1,9},{9,1},{2,10},{10,2},{3,11},{11,3},{4,12},{12,4},... | collective-permute-start | bytes 1966088 | tf_op jit(solution)/shard_map/ppermute | solution.py:39
  86.4 19.1 %all-to-all-start.1 = ((bf16[8,64,1024]{2,1,0:T(8,128)(2,1)}), bf16[8,64,1024]{2,1,0:T(8,128)(2,1)}, u32[]{:S(2)}, u32[]{:S(2)}) async-start(bf16[8,64,1024]{2,1,0:T(8,128)(2,1)} %copy-done.23), calls=%async_computation.1 | async-start | bytes 2097152 | tf_op jit(solution)/shard_map/all_to_all | solution.py:390
  97.1 15.2 %collective-permute-start.10 = (bf16[192,1024]{1,0:T(8,128)(2,1)}, bf16[192,1024]{1,0:T(8,128)(2,1)}, u32[]{:S(2)}, u32[]{:S(2)}) collective-permute-start(bf16[192,1024]{1,0:T(8,128)(2,1)} %get-tuple-element.153), channel_id=1, source_target_pairs={{0,3},{1,0},{2,1},{3,2},{4,7},{5,4},{6,5},{7,6},{8,11},{9,8},{10,9... | collective-permute-start | bytes 1179656 | tf_op jit(solution)/shard_map/ppermute | solution.py:31
  99.7 14.9 %collective-permute-start.11 = (bf16[192,1024]{1,0:T(8,128)(2,1)}, bf16[192,1024]{1,0:T(8,128)(2,1)}, u32[]{:S(2)}, u32[]{:S(2)}) collective-permute-start(bf16[192,1024]{1,0:T(8,128)(2,1)} %get-tuple-element.155), channel_id=1, source_target_pairs={{0,2},{1,3},{2,0},{3,1},{4,6},{5,7},{6,4},{7,5},{8,10},{9,11},{10,... | collective-permute-start | bytes 1179656 | tf_op jit(solution)/shard_map/ppermute | solution.py:31
  100.2 22.6 %collective-permute-start.12 = (bf16[192,1024]{1,0:T(8,128)(2,1)}, bf16[192,1024]{1,0:T(8,128)(2,1)}, u32[]{:S(2)}, u32[]{:S(2)}) collective-permute-start(bf16[192,1024]{1,0:T(8,128)(2,1)} %get-tuple-element.154), channel_id=1, source_target_pairs={{0,1},{1,2},{2,3},{3,0},{4,5},{5,6},{6,7},{7,4},{8,9},{9,10},{10,1... | collective-permute-start | bytes 1179656 | tf_op jit(solution)/shard_map/ppermute | solution.py:31
  105.5 29.9 %collective-permute-start.16 = (bf16[8,64,1024]{2,1,0:T(8,128)(2,1)}, bf16[8,64,1024]{2,1,0:T(8,128)(2,1)}, u32[]{:S(2)}, u32[]{:S(2)}) collective-permute-start(bf16[8,64,1024]{2,1,0:T(8,128)(2,1)} %all-to-all-done.1.got), channel_id=1, source_target_pairs={{0,8},{8,0},{1,9},{9,1},{2,10},{10,2},{3,11},{11,3},{4,12},{12,4},... | collective-permute-start | bytes 3145736 | tf_op jit(solution)/shard_map/ppermute | solution.py:39
  125.8 13.3 %collective-permute-start.13 = (bf16[192,1024]{1,0:T(8,128)(2,1)S(1)}, bf16[192,1024]{1,0:T(8,128)(2,1)S(1)}, u32[]{:S(2)}, u32[]{:S(2)}) collective-permute-start(bf16[192,1024]{1,0:T(8,128)(2,1)S(1)} %add_convert_fusion.4), channel_id=1, source_target_pairs={{0,1},{1,2},{2,3},{3,0},{4,5},{5,6},{6,7},{7,4},{8,9},{9,10},{10,1... | collective-permute-start | bytes 1179656 | tf_op jit(solution)/shard_map/ppermute | solution.py:31
  125.9 18.4 %collective-permute-start.14 = (bf16[192,1024]{1,0:T(8,128)(2,1)S(1)}, bf16[192,1024]{1,0:T(8,128)(2,1)}, u32[]{:S(2)}, u32[]{:S(2)}) collective-permute-start(bf16[192,1024]{1,0:T(8,128)(2,1)S(1)} %add_convert_fusion.4), channel_id=1, source_target_pairs={{0,2},{1,3},{2,0},{3,1},{4,6},{5,7},{6,4},{7,5},{8,10},{9,11},{10,... | collective-permute-start | bytes 1179656 | tf_op jit(solution)/shard_map/ppermute | solution.py:31
  127.6 28.4 %collective-permute-start.15 = (bf16[192,1024]{1,0:T(8,128)(2,1)S(1)}, bf16[192,1024]{1,0:T(8,128)(2,1)}, u32[]{:S(2)}, u32[]{:S(2)}) collective-permute-start(bf16[192,1024]{1,0:T(8,128)(2,1)S(1)} %add_convert_fusion.4), channel_id=1, source_target_pairs={{0,3},{1,0},{2,1},{3,2},{4,7},{5,4},{6,5},{7,6},{8,11},{9,8},{10,9... | collective-permute-start | bytes 1179656 | tf_op jit(solution)/shard_map/ppermute | solution.py:31
  128.6 38.7 %all-to-all-start.2 = ((bf16[8,64,1792]{2,1,0:T(8,128)(2,1)}), bf16[8,64,1792]{2,1,0:T(8,128)(2,1)}, u32[]{:S(2)}, u32[]{:S(2)}) async-start(bf16[8,64,1792]{2,1,0:T(8,128)(2,1)} %copy-done.20), calls=%async_computation.2 | async-start | bytes 3670016 | tf_op jit(solution)/shard_map/all_to_all | solution.py:390
  134.4 536.1 %reduce-scatter.5.cloned.1.call-start = ((), (), s32[]{:S(2)}) async-start(), calls=%async_computation.11 | async-start | bytes 2228224 | tf_op jit(solution)/shard_map/reduce_scatter | solution.py:662
  163.8 13.4 %collective-permute-start.17 = (bf16[192,1024]{1,0:T(8,128)(2,1)}, bf16[192,1024]{1,0:T(8,128)(2,1)}, u32[]{:S(2)}, u32[]{:S(2)}) collective-permute-start(bf16[192,1024]{1,0:T(8,128)(2,1)} %get-tuple-element.150), channel_id=1, source_target_pairs={{0,3},{1,0},{2,1},{3,2},{4,7},{5,4},{6,5},{7,6},{8,11},{9,8},{10,9... | collective-permute-start | bytes 1179656 | tf_op jit(solution)/shard_map/ppermute | solution.py:31
  166.7 19.9 %collective-permute-start.19 = (bf16[192,1024]{1,0:T(8,128)(2,1)}, bf16[192,1024]{1,0:T(8,128)(2,1)}, u32[]{:S(2)}, u32[]{:S(2)}) collective-permute-start(bf16[192,1024]{1,0:T(8,128)(2,1)} %get-tuple-element.151), channel_id=1, source_target_pairs={{0,1},{1,2},{2,3},{3,0},{4,5},{5,6},{6,7},{7,4},{8,9},{9,10},{10,1... | collective-permute-start | bytes 1179656 | tf_op jit(solution)/shard_map/ppermute | solution.py:31
  167.2 30.2 %collective-permute-start.23 = (bf16[8,64,1792]{2,1,0:T(8,128)(2,1)}, bf16[8,64,1792]{2,1,0:T(8,128)(2,1)}, u32[]{:S(2)}, u32[]{:S(2)}) collective-permute-start(bf16[8,64,1792]{2,1,0:T(8,128)(2,1)} %all-to-all-done.2.got), channel_id=1, source_target_pairs={{0,8},{8,0},{1,9},{9,1},{2,10},{10,2},{3,11},{11,3},{4,12},{12,4},... | collective-permute-start | bytes 5505032 | tf_op jit(solution)/shard_map/ppermute | solution.py:39
  190.6 14.0 %collective-permute-start.20 = (bf16[192,1024]{1,0:T(8,128)(2,1)}, bf16[192,1024]{1,0:T(8,128)(2,1)}, u32[]{:S(2)}, u32[]{:S(2)}) collective-permute-start(bf16[192,1024]{1,0:T(8,128)(2,1)} %add_convert_fusion.3), channel_id=1, source_target_pairs={{0,1},{1,2},{2,3},{3,0},{4,5},{5,6},{6,7},{7,4},{8,9},{9,10},{10,1... | collective-permute-start | bytes 1179656 | tf_op jit(solution)/shard_map/ppermute | solution.py:31
  190.6 15.8 %collective-permute-start.21 = (bf16[192,1024]{1,0:T(8,128)(2,1)}, bf16[192,1024]{1,0:T(8,128)(2,1)}, u32[]{:S(2)}, u32[]{:S(2)}) collective-permute-start(bf16[192,1024]{1,0:T(8,128)(2,1)} %add_convert_fusion.3), channel_id=1, source_target_pairs={{0,2},{1,3},{2,0},{3,1},{4,6},{5,7},{6,4},{7,5},{8,10},{9,11},{10,... | collective-permute-start | bytes 1179656 | tf_op jit(solution)/shard_map/ppermute | solution.py:31
  191.1 19.5 %collective-permute-start.22 = (bf16[192,1024]{1,0:T(8,128)(2,1)}, bf16[192,1024]{1,0:T(8,128)(2,1)}, u32[]{:S(2)}, u32[]{:S(2)}) collective-permute-start(bf16[192,1024]{1,0:T(8,128)(2,1)} %add_convert_fusion.3), channel_id=1, source_target_pairs={{0,3},{1,0},{2,1},{3,2},{4,7},{5,4},{6,5},{7,6},{8,11},{9,8},{10,9... | collective-permute-start | bytes 1179656 | tf_op jit(solution)/shard_map/ppermute | solution.py:31
  193.3 22.4 %collective-permute-start.26 = (bf16[320,1024]{1,0:T(8,128)(2,1)}, bf16[320,1024]{1,0:T(8,128)(2,1)S(1)}, u32[]{:S(2)}, u32[]{:S(2)}) collective-permute-start(bf16[320,1024]{1,0:T(8,128)(2,1)} %get-tuple-element.62), channel_id=1, source_target_pairs={{0,4},{4,0},{1,5},{5,1},{2,6},{6,2},{3,7},{7,3},{8,12},{12,8},{9,1... | collective-permute-start | bytes 1966088 | tf_op jit(solution)/shard_map/ppermute | solution.py:39
  215.8 17.3 %collective-permute-start.27 = (bf16[320,1024]{1,0:T(8,128)(2,1)S(1)}, bf16[320,1024]{1,0:T(8,128)(2,1)S(1)}, u32[]{:S(2)}, u32[]{:S(2)}) collective-permute-start(bf16[320,1024]{1,0:T(8,128)(2,1)S(1)} %collective-permute-done.26.got), channel_id=1, source_target_pairs={{0,8},{8,0},{1,9},{9,1},{2,10},{10,2},{3,11},{11,3},{4,12},{12,4},... | collective-permute-start | bytes 1966088 | tf_op jit(solution)/shard_map/ppermute | solution.py:39
  236.2 21.4 %collective-permute-start.28 = (bf16[192,1024]{1,0:T(8,128)(2,1)S(1)}, bf16[192,1024]{1,0:T(8,128)(2,1)S(1)}, u32[]{:S(2)}, u32[]{:S(2)}) collective-permute-start(bf16[192,1024]{1,0:T(8,128)(2,1)S(1)} %get-tuple-element.145), channel_id=1, source_target_pairs={{0,3},{1,0},{2,1},{3,2},{4,7},{5,4},{6,5},{7,6},{8,11},{9,8},{10,9... | collective-permute-start | bytes 1179656 | tf_op jit(solution)/shard_map/ppermute | solution.py:31
  238.3 23.2 %collective-permute-start.29 = (bf16[192,1024]{1,0:T(8,128)(2,1)S(1)}, bf16[192,1024]{1,0:T(8,128)(2,1)S(1)}, u32[]{:S(2)}, u32[]{:S(2)}) collective-permute-start(bf16[192,1024]{1,0:T(8,128)(2,1)S(1)} %get-tuple-element.147), channel_id=1, source_target_pairs={{0,2},{1,3},{2,0},{3,1},{4,6},{5,7},{6,4},{7,5},{8,10},{9,11},{10,... | collective-permute-start | bytes 1179656 | tf_op jit(solution)/shard_map/ppermute | solution.py:31
  238.3 23.2 %collective-permute-start.30 = (bf16[192,1024]{1,0:T(8,128)(2,1)S(1)}, bf16[192,1024]{1,0:T(8,128)(2,1)S(1)}, u32[]{:S(2)}, u32[]{:S(2)}) collective-permute-start(bf16[192,1024]{1,0:T(8,128)(2,1)S(1)} %get-tuple-element.146), channel_id=1, source_target_pairs={{0,1},{1,2},{2,3},{3,0},{4,5},{5,6},{6,7},{7,4},{8,9},{9,10},{10,1... | collective-permute-start | bytes 1179656 | tf_op jit(solution)/shard_map/ppermute | solution.py:31
  239.6 28.1 %collective-permute-start.39 = (bf16[192,1024]{1,0:T(8,128)(2,1)S(1)}, bf16[192,1024]{1,0:T(8,128)(2,1)S(1)}, u32[]{:S(2)}, u32[]{:S(2)}) collective-permute-start(bf16[192,1024]{1,0:T(8,128)(2,1)S(1)} %get-tuple-element.111), channel_id=1, source_target_pairs={{0,1},{1,2},{2,3},{3,0},{4,5},{5,6},{6,7},{7,4},{8,9},{9,10},{10,1... | collective-permute-start | bytes 1179656 | tf_op jit(solution)/shard_map/ppermute | solution.py:31
  241.7 34.6 %collective-permute-start.40 = (bf16[192,1024]{1,0:T(8,128)(2,1)S(1)}, bf16[192,1024]{1,0:T(8,128)(2,1)S(1)}, u32[]{:S(2)}, u32[]{:S(2)}) collective-permute-start(bf16[192,1024]{1,0:T(8,128)(2,1)S(1)} %get-tuple-element.111), channel_id=1, source_target_pairs={{0,2},{1,3},{2,0},{3,1},{4,6},{5,7},{6,4},{7,5},{8,10},{9,11},{10,... | collective-permute-start | bytes 1179656 | tf_op jit(solution)/shard_map/ppermute | solution.py:31
  257.6 19.7 %collective-permute-start.41 = (bf16[192,1024]{1,0:T(8,128)(2,1)S(1)}, bf16[192,1024]{1,0:T(8,128)(2,1)S(1)}, u32[]{:S(2)}, u32[]{:S(2)}) collective-permute-start(bf16[192,1024]{1,0:T(8,128)(2,1)S(1)} %get-tuple-element.111), channel_id=1, source_target_pairs={{0,3},{1,0},{2,1},{3,2},{4,7},{5,4},{6,5},{7,6},{8,11},{9,8},{10,9... | collective-permute-start | bytes 1179656 | tf_op jit(solution)/shard_map/ppermute | solution.py:31
  262.6 21.5 %collective-permute-start.31 = (bf16[192,1024]{1,0:T(8,128)(2,1)S(1)}, bf16[192,1024]{1,0:T(8,128)(2,1)S(1)}, u32[]{:S(2)}, u32[]{:S(2)}) collective-permute-start(bf16[192,1024]{1,0:T(8,128)(2,1)S(1)} %add_convert_fusion.2), channel_id=1, source_target_pairs={{0,1},{1,2},{2,3},{3,0},{4,5},{5,6},{6,7},{7,4},{8,9},{9,10},{10,1... | collective-permute-start | bytes 1179656 | tf_op jit(solution)/shard_map/ppermute | solution.py:31
  262.7 25.7 %collective-permute-start.32 = (bf16[192,1024]{1,0:T(8,128)(2,1)S(1)}, bf16[192,1024]{1,0:T(8,128)(2,1)S(1)}, u32[]{:S(2)}, u32[]{:S(2)}) collective-permute-start(bf16[192,1024]{1,0:T(8,128)(2,1)S(1)} %add_convert_fusion.2), channel_id=1, source_target_pairs={{0,2},{1,3},{2,0},{3,1},{4,6},{5,7},{6,4},{7,5},{8,10},{9,11},{10,... | collective-permute-start | bytes 1179656 | tf_op jit(solution)/shard_map/ppermute | solution.py:31
  267.7 20.7 %collective-permute-start.33 = (bf16[192,1024]{1,0:T(8,128)(2,1)S(1)}, bf16[192,1024]{1,0:T(8,128)(2,1)S(1)}, u32[]{:S(2)}, u32[]{:S(2)}) collective-permute-start(bf16[192,1024]{1,0:T(8,128)(2,1)S(1)} %add_convert_fusion.2), channel_id=1, source_target_pairs={{0,3},{1,0},{2,1},{3,2},{4,7},{5,4},{6,5},{7,6},{8,11},{9,8},{10,9... | collective-permute-start | bytes 1179656 | tf_op jit(solution)/shard_map/ppermute | solution.py:31
  301.6 18.7 %collective-permute-start.44 = (bf16[192,1024]{1,0:T(8,128)(2,1)S(1)}, bf16[192,1024]{1,0:T(8,128)(2,1)S(1)}, u32[]{:S(2)}, u32[]{:S(2)}) collective-permute-start(bf16[192,1024]{1,0:T(8,128)(2,1)S(1)} %get-tuple-element.140), channel_id=1, source_target_pairs={{0,1},{1,2},{2,3},{3,0},{4,5},{5,6},{6,7},{7,4},{8,9},{9,10},{10,1... | collective-permute-start | bytes 1179656 | tf_op jit(solution)/shard_map/ppermute | solution.py:31
  324.2 20.1 %collective-permute-start.45 = (bf16[192,1024]{1,0:T(8,128)(2,1)}, bf16[192,1024]{1,0:T(8,128)(2,1)S(1)}, u32[]{:S(2)}, u32[]{:S(2)}) collective-permute-start(bf16[192,1024]{1,0:T(8,128)(2,1)} %get-tuple-element.113), channel_id=1, source_target_pairs={{0,1},{1,2},{2,3},{3,0},{4,5},{5,6},{6,7},{7,4},{8,9},{9,10},{10,1... | collective-permute-start | bytes 1179656 | tf_op jit(solution)/shard_map/ppermute | solution.py:31
  324.2 20.2 %collective-permute-start.46 = (bf16[192,1024]{1,0:T(8,128)(2,1)}, bf16[192,1024]{1,0:T(8,128)(2,1)}, u32[]{:S(2)}, u32[]{:S(2)}) collective-permute-start(bf16[192,1024]{1,0:T(8,128)(2,1)} %get-tuple-element.113), channel_id=1, source_target_pairs={{0,2},{1,3},{2,0},{3,1},{4,6},{5,7},{6,4},{7,5},{8,10},{9,11},{10,... | collective-permute-start | bytes 1179656 | tf_op jit(solution)/shard_map/ppermute | solution.py:31
  325.8 19.3 %collective-permute-start.47 = (bf16[192,1024]{1,0:T(8,128)(2,1)}, bf16[192,1024]{1,0:T(8,128)(2,1)}, u32[]{:S(2)}, u32[]{:S(2)}) collective-permute-start(bf16[192,1024]{1,0:T(8,128)(2,1)} %get-tuple-element.113), channel_id=1, source_target_pairs={{0,3},{1,0},{2,1},{3,2},{4,7},{5,4},{6,5},{7,6},{8,11},{9,8},{10,9... | collective-permute-start | bytes 1179656 | tf_op jit(solution)/shard_map/ppermute | solution.py:31
  367.6 20.4 %collective-permute-start.52 = (bf16[192,1024]{1,0:T(8,128)(2,1)S(1)}, bf16[192,1024]{1,0:T(8,128)(2,1)S(1)}, u32[]{:S(2)}, u32[]{:S(2)}) collective-permute-start(bf16[192,1024]{1,0:T(8,128)(2,1)S(1)} %get-tuple-element.137), channel_id=1, source_target_pairs={{0,1},{1,2},{2,3},{3,0},{4,5},{5,6},{6,7},{7,4},{8,9},{9,10},{10,1... | collective-permute-start | bytes 1179656 | tf_op jit(solution)/shard_map/ppermute | solution.py:31
  391.5 286.1 %reduce-scatter.3.cloned.1.call-start = ((), (), s32[]{:S(2)}) async-start(), calls=%async_computation.10 | async-start | bytes 4456448 | tf_op jit(solution)/shard_map/reduce_scatter | solution.py:661
  395.9 20.8 %collective-permute-start.36 = (bf16[192,1024]{1,0:T(8,128)(2,1)}, bf16[192,1024]{1,0:T(8,128)(2,1)}, u32[]{:S(2)}, u32[]{:S(2)}) collective-permute-start(bf16[192,1024]{1,0:T(8,128)(2,1)} %get-tuple-element.143), channel_id=1, source_target_pairs={{0,1},{1,2},{2,3},{3,0},{4,5},{5,6},{6,7},{7,4},{8,9},{9,10},{10,1... | collective-permute-start | bytes 1179656 | tf_op jit(solution)/shard_map/ppermute | solution.py:31
  419.9 65.6 %collective-permute-start.37 = (f32[192,1024]{1,0:T(8,128)}, f32[192,1024]{1,0:T(8,128)}, u32[]{:S(2)}, u32[]{:S(2)}) collective-permute-start(f32[192,1024]{1,0:T(8,128)} %fusion.35), channel_id=1, source_target_pairs={{4,8},{8,4},{5,9},{9,5},{6,10},{10,6},{7,11},{11,7},{20,24},{24,20... | collective-permute-start | bytes 2359304 | tf_op jit(solution)/shard_map/ppermute | solution.py:43
  428.9 12.6 %collective-permute-start.53 = (bf16[192,1024]{1,0:T(8,128)(2,1)}, bf16[192,1024]{1,0:T(8,128)(2,1)S(1)}, u32[]{:S(2)}, u32[]{:S(2)}) collective-permute-start(bf16[192,1024]{1,0:T(8,128)(2,1)} %get-tuple-element.116), channel_id=1, source_target_pairs={{0,1},{1,2},{2,3},{3,0},{4,5},{5,6},{6,7},{7,4},{8,9},{9,10},{10,1... | collective-permute-start | bytes 1179656 | tf_op jit(solution)/shard_map/ppermute | solution.py:31
  428.9 17.2 %collective-permute-start.54 = (bf16[192,1024]{1,0:T(8,128)(2,1)}, bf16[192,1024]{1,0:T(8,128)(2,1)S(1)}, u32[]{:S(2)}, u32[]{:S(2)}) collective-permute-start(bf16[192,1024]{1,0:T(8,128)(2,1)} %get-tuple-element.116), channel_id=1, source_target_pairs={{0,2},{1,3},{2,0},{3,1},{4,6},{5,7},{6,4},{7,5},{8,10},{9,11},{10,... | collective-permute-start | bytes 1179656 | tf_op jit(solution)/shard_map/ppermute | solution.py:31
  431.5 15.6 %collective-permute-start.55 = (bf16[192,1024]{1,0:T(8,128)(2,1)}, bf16[192,1024]{1,0:T(8,128)(2,1)}, u32[]{:S(2)}, u32[]{:S(2)}) collective-permute-start(bf16[192,1024]{1,0:T(8,128)(2,1)} %get-tuple-element.116), channel_id=1, source_target_pairs={{0,3},{1,0},{2,1},{3,2},{4,7},{5,4},{6,5},{7,6},{8,11},{9,8},{10,9... | collective-permute-start | bytes 1179656 | tf_op jit(solution)/shard_map/ppermute | solution.py:31
  456.0 18.7 %collective-permute-start.56 = (bf16[192,1024]{1,0:T(8,128)(2,1)S(1)}, bf16[192,1024]{1,0:T(8,128)(2,1)S(1)}, u32[]{:S(2)}, u32[]{:S(2)}) collective-permute-start(bf16[192,1024]{1,0:T(8,128)(2,1)S(1)} %get-tuple-element.133), channel_id=1, source_target_pairs={{0,3},{1,0},{2,1},{3,2},{4,7},{5,4},{6,5},{7,6},{8,11},{9,8},{10,9... | collective-permute-start | bytes 1179656 | tf_op jit(solution)/shard_map/ppermute | solution.py:31
  458.3 16.4 %collective-permute-start.57 = (bf16[192,1024]{1,0:T(8,128)(2,1)S(1)}, bf16[192,1024]{1,0:T(8,128)(2,1)S(1)}, u32[]{:S(2)}, u32[]{:S(2)}) collective-permute-start(bf16[192,1024]{1,0:T(8,128)(2,1)S(1)} %get-tuple-element.135), channel_id=1, source_target_pairs={{0,2},{1,3},{2,0},{3,1},{4,6},{5,7},{6,4},{7,5},{8,10},{9,11},{10,... | collective-permute-start | bytes 1179656 | tf_op jit(solution)/shard_map/ppermute | solution.py:31
  458.3 20.4 %collective-permute-start.58 = (bf16[192,1024]{1,0:T(8,128)(2,1)S(1)}, bf16[192,1024]{1,0:T(8,128)(2,1)S(1)}, u32[]{:S(2)}, u32[]{:S(2)}) collective-permute-start(bf16[192,1024]{1,0:T(8,128)(2,1)S(1)} %get-tuple-element.134), channel_id=1, source_target_pairs={{0,1},{1,2},{2,3},{3,0},{4,5},{5,6},{6,7},{7,4},{8,9},{9,10},{10,1... | collective-permute-start | bytes 1179656 | tf_op jit(solution)/shard_map/ppermute | solution.py:31
  482.6 19.8 %collective-permute-start.59 = (bf16[192,1024]{1,0:T(8,128)(2,1)}, bf16[192,1024]{1,0:T(8,128)(2,1)S(1)}, u32[]{:S(2)}, u32[]{:S(2)}) collective-permute-start(bf16[192,1024]{1,0:T(8,128)(2,1)} %get-tuple-element.119), channel_id=1, source_target_pairs={{0,1},{1,2},{2,3},{3,0},{4,5},{5,6},{6,7},{7,4},{8,9},{9,10},{10,1... | collective-permute-start | bytes 1179656 | tf_op jit(solution)/shard_map/ppermute | solution.py:31
  482.6 19.8 %collective-permute-start.60 = (bf16[192,1024]{1,0:T(8,128)(2,1)}, bf16[192,1024]{1,0:T(8,128)(2,1)}, u32[]{:S(2)}, u32[]{:S(2)}) collective-permute-start(bf16[192,1024]{1,0:T(8,128)(2,1)} %get-tuple-element.119), channel_id=1, source_target_pairs={{0,2},{1,3},{2,0},{3,1},{4,6},{5,7},{6,4},{7,5},{8,10},{9,11},{10,... | collective-permute-start | bytes 1179656 | tf_op jit(solution)/shard_map/ppermute | solution.py:31
  483.8 18.9 %collective-permute-start.61 = (bf16[192,1024]{1,0:T(8,128)(2,1)}, bf16[192,1024]{1,0:T(8,128)(2,1)}, u32[]{:S(2)}, u32[]{:S(2)}) collective-permute-start(bf16[192,1024]{1,0:T(8,128)(2,1)} %get-tuple-element.119), channel_id=1, source_target_pairs={{0,3},{1,0},{2,1},{3,2},{4,7},{5,4},{6,5},{7,6},{8,11},{9,8},{10,9... | collective-permute-start | bytes 1179656 | tf_op jit(solution)/shard_map/ppermute | solution.py:31
  508.2 82.1 %collective-permute-start.81 = (bf16[4,2,64,2048]{3,2,1,0:T(8,128)(2,1)}, bf16[4,2,64,2048]{3,2,1,0:T(8,128)(2,1)}, u32[]{:S(2)}, u32[]{:S(2)}) collective-permute-start(bf16[4,2,64,2048]{3,2,1,0:T(8,128)(2,1)} %fusion.21), channel_id=1, source_target_pairs={{0,8},{8,0},{1,9},{9,1},{2,10},{10,2},{3,11},{11,3},{4,12},{12,4},... | collective-permute-start | bytes 6291464 | tf_op jit(solution)/shard_map/ppermute | solution.py:39
  529.6 20.4 %collective-permute-start.66 = (bf16[192,1024]{1,0:T(8,128)(2,1)S(1)}, bf16[192,1024]{1,0:T(8,128)(2,1)S(1)}, u32[]{:S(2)}, u32[]{:S(2)}) collective-permute-start(bf16[192,1024]{1,0:T(8,128)(2,1)S(1)} %get-tuple-element.131), channel_id=1, source_target_pairs={{0,1},{1,2},{2,3},{3,0},{4,5},{5,6},{6,7},{7,4},{8,9},{9,10},{10,1... | collective-permute-start | bytes 1179656 | tf_op jit(solution)/shard_map/ppermute | solution.py:31
  553.0 45.8 %collective-permute-start.68 = (bf16[4,2,64,1024]{3,2,1,0:T(8,128)(2,1)}, bf16[4,2,64,1024]{3,2,1,0:T(8,128)(2,1)}, u32[]{:S(2)}, u32[]{:S(2)}) collective-permute-start(bf16[4,2,64,1024]{3,2,1,0:T(8,128)(2,1)} %fusion.53), channel_id=1, source_target_pairs={{0,8},{8,0},{1,9},{9,1},{2,10},{10,2},{3,11},{11,3},{4,12},{12,4},... | collective-permute-start | bytes 3145736 | tf_op jit(solution)/shard_map/ppermute | solution.py:39
  561.5 161.8 %collective-permute-start.67 = (f32[192,1024]{1,0:T(8,128)}, f32[192,1024]{1,0:T(8,128)}, u32[]{:S(2)}, u32[]{:S(2)}) collective-permute-start(f32[192,1024]{1,0:T(8,128)} %fusion.69), channel_id=1, source_target_pairs={{4,8},{8,4},{5,9},{9,5},{6,10},{10,6},{7,11},{11,7},{20,24},{24,20... | collective-permute-start | bytes 2359304 | tf_op jit(solution)/shard_map/ppermute | solution.py:43
  593.2 15.1 %collective-permute-start.82 = (bf16[2,64,2048]{2,1,0:T(8,128)(2,1)S(1)}, bf16[2,64,2048]{2,1,0:T(8,128)(2,1)S(1)}, u32[]{:S(2)}, u32[]{:S(2)}) collective-permute-start(bf16[2,64,2048]{2,1,0:T(8,128)(2,1)S(1)} %get-tuple-element.127), channel_id=1, source_target_pairs={{0,32},{32,64},{64,96},{96,0},{1,33},{33,65},{65,97},{97,1},{2,34}... | collective-permute-start | bytes 1572872 | tf_op jit(solution)/shard_map/ppermute | solution.py:35
  593.3 25.4 %collective-permute-start.83 = (bf16[2,64,2048]{2,1,0:T(8,128)(2,1)S(1)}, bf16[2,64,2048]{2,1,0:T(8,128)(2,1)S(1)}, u32[]{:S(2)}, u32[]{:S(2)}) collective-permute-start(bf16[2,64,2048]{2,1,0:T(8,128)(2,1)S(1)} %get-tuple-element.129), channel_id=1, source_target_pairs={{0,64},{32,96},{64,0},{96,32},{1,65},{33,97},{65,1},{97,33},{2,66}... | collective-permute-start | bytes 1572872 | tf_op jit(solution)/shard_map/ppermute | solution.py:35
  595.5 23.9 %collective-permute-start.84 = (bf16[2,64,2048]{2,1,0:T(8,128)(2,1)S(1)}, bf16[2,64,2048]{2,1,0:T(8,128)(2,1)S(1)}, u32[]{:S(2)}, u32[]{:S(2)}) collective-permute-start(bf16[2,64,2048]{2,1,0:T(8,128)(2,1)S(1)} %get-tuple-element.128), channel_id=1, source_target_pairs={{0,96},{32,0},{64,32},{96,64},{1,97},{33,1},{65,33},{97,65},{2,98}... | collective-permute-start | bytes 1572872 | tf_op jit(solution)/shard_map/ppermute | solution.py:35
  600.5 24.6 %collective-permute-start.69 = (bf16[2,64,1024]{2,1,0:T(8,128)(2,1)S(1)}, bf16[2,64,1024]{2,1,0:T(8,128)(2,1)S(1)}, u32[]{:S(2)}, u32[]{:S(2)}) collective-permute-start(bf16[2,64,1024]{2,1,0:T(8,128)(2,1)S(1)} %get-tuple-element.158), channel_id=1, source_target_pairs={{0,32},{32,64},{64,96},{96,0},{1,33},{33,65},{65,97},{97,1},{2,34}... | collective-permute-start | bytes 786440 | tf_op jit(solution)/shard_map/ppermute | solution.py:35
  608.3 21.7 %collective-permute-start.70 = (bf16[2,64,1024]{2,1,0:T(8,128)(2,1)S(1)}, bf16[2,64,1024]{2,1,0:T(8,128)(2,1)S(1)}, u32[]{:S(2)}, u32[]{:S(2)}) collective-permute-start(bf16[2,64,1024]{2,1,0:T(8,128)(2,1)S(1)} %get-tuple-element.160), channel_id=1, source_target_pairs={{0,64},{32,96},{64,0},{96,32},{1,65},{33,97},{65,1},{97,33},{2,66}... | collective-permute-start | bytes 786440 | tf_op jit(solution)/shard_map/ppermute | solution.py:35
  664.1 52.0 %collective-permute-start.88 = (bf16[2,32,2048]{2,1,0:T(8,128)(2,1)}, bf16[2,32,2048]{2,1,0:T(8,128)(2,1)}, u32[]{:S(2)}, u32[]{:S(2)}) collective-permute-start(bf16[2,32,2048]{2,1,0:T(8,128)(2,1)} %maximum_select_fusion.7), channel_id=1, source_target_pairs={{0,96},{32,0},{64,32},{96,64},{1,97},{33,1},{65,33},{97,65},{2,98}... | collective-permute-start | bytes 786440 | tf_op jit(solution)/shard_map/ppermute | solution.py:35
  667.2 49.9 %collective-permute-start.89 = (bf16[2,32,2048]{2,1,0:T(8,128)(2,1)}, bf16[2,32,2048]{2,1,0:T(8,128)(2,1)}, u32[]{:S(2)}, u32[]{:S(2)}) collective-permute-start(bf16[2,32,2048]{2,1,0:T(8,128)(2,1)} %maximum_select_fusion.7), channel_id=1, source_target_pairs={{0,64},{32,96},{64,0},{96,32},{1,65},{33,97},{65,1},{97,33},{2,66}... | collective-permute-start | bytes 786440 | tf_op jit(solution)/shard_map/ppermute | solution.py:35
  668.1 50.0 %collective-permute-start.90 = (bf16[2,32,2048]{2,1,0:T(8,128)(2,1)}, bf16[2,32,2048]{2,1,0:T(8,128)(2,1)}, u32[]{:S(2)}, u32[]{:S(2)}) collective-permute-start(bf16[2,32,2048]{2,1,0:T(8,128)(2,1)} %maximum_select_fusion.7), channel_id=1, source_target_pairs={{0,32},{32,64},{64,96},{96,0},{1,33},{33,65},{65,97},{97,1},{2,34}... | collective-permute-start | bytes 786440 | tf_op jit(solution)/shard_map/ppermute | solution.py:35
  695.0 51.5 %all-gather.3.cloned.1.call-start = ((), (), s32[]{:S(2)}) async-start(), calls=%async_computation.12 | async-start | bytes 3342336 | tf_op jit(solution)/shard_map/all_gather | solution.py:665
  701.3 25.5 %collective-permute-start.78 = (bf16[4,2,32,1024]{3,2,1,0:T(8,128)(2,1)S(1)}, bf16[4,2,32,1024]{3,2,1,0:T(8,128)(2,1)S(1)}, u32[]{:S(2)}, u32[]{:S(2)}) collective-permute-start(bf16[4,2,32,1024]{3,2,1,0:T(8,128)(2,1)S(1)} %constant_dynamic-slice_fusion.3), channel_id=1, source_target_pairs={{0,8},{8,0},{1,9},{9,1},{2,10},{10,2},{3,11},{11,3},{4,12},{12,4},... | collective-permute-start | bytes 1572872 | tf_op jit(solution)/shard_map/ppermute | solution.py:39
  (169 other events, 1316.8 us)
Sparse Core Ops, SparseCore 0:
  391.6 62.6 reduce-scatter.4
  457.3 66.8 reduce-scatter.2
  701.3 45.2 all-gather.2

commit v3 on v2

--- a/solution.py
+++ b/solution.py
@@ -48,18 +48,15 @@
     return lax.optimization_barrier((value, others))[0]
 
 
+def beside(send, transfer, given, work):
+    send, given = lax.optimization_barrier((send, given))
+    return lax.optimization_barrier((transfer(send), work(given)))
+
+
 def gather_z(rows):
     return jnp.concatenate([rows] + [shift_z(rows, k) for k in (1, 2, 3)], axis=0)
 
 
-def scatter_z(own, others):
-    total = own
-    for k in (1, 2, 3):
-        block = others[(k - 1) * PIECE : k * PIECE]
-        total = total + shift_z(block, -k).astype(f32)
-    return total
-
-
 def dot(left, right):
     return jnp.dot(left, right, preferred_element_type=f32)
 
@@ -72,10 +69,25 @@
     return lax.dot_general(left, right, (((0,), (0,)), ((), ())), preferred_element_type=f32)
 
 
-def dot_scatter(left, weight, product):
-    others = product(left[PIECE:], weight).astype(bf16)
-    own = product(left[:PIECE], weight)
-    return scatter_z(own, others)
+def scatter_parts(others):
+    return tuple(
+        shift_z(others[(k - 1) * PIECE : k * PIECE], -k) for k in (1, 2, 3)
+    )
+
+
+def sum_parts(own, parts):
+    total = own
+    for part in parts:
+        total = total + part.astype(f32)
+    return total
+
+
+def dot_others(left, weight, product):
+    return product(left[PIECE:], weight).astype(bf16)
+
+
+def dot_own(left, weight, product):
+    return product(left[:PIECE], weight)
 
 
 def tile_mask(block, low, high, cut):
@@ -210,7 +222,7 @@
         ],
         compiler_params=pltpu.CompilerParams(vmem_limit_bytes=LIMIT),
         cost_estimate=pl.CostEstimate(
-            flops=4 * 2 * 1400000 * 64, bytes_accessed=3000000, transcendentals=2800000
+            flops=4 * 2 * 1400000 * 64, bytes_accessed=28000000, transcendentals=2800000
         ),
         name="attend",
     )(info, slopes, mine, other)
@@ -237,7 +249,7 @@
         ],
         compiler_params=pltpu.CompilerParams(vmem_limit_bytes=LIMIT),
         cost_estimate=pl.CostEstimate(
-            flops=10 * 2 * 1400000 * 64, bytes_accessed=5000000, transcendentals=2800000
+            flops=10 * 2 * 1400000 * 64, bytes_accessed=36000000, transcendentals=2800000
         ),
         name="attend_back",
     )(info, slopes, rows, mine, other, logsum)
@@ -402,55 +414,97 @@
     return lax.dynamic_slice_in_dim(value, at * width, width, 1)
 
 
-def forward(hidden, normed_all, params, info, slopes, core):
+def forward(hidden, normed_all, params, info, slopes, core, side=None):
     (_, _, w_in, in_bias, project, project_bias) = params[:6]
     (gain_two, offset_two, up, up_bias, down, down_bias) = params[6:]
     projected = (dot(normed_all, w_in) + in_bias).astype(bf16)
     received = swap(columns_at(projected, 1 - core, 384), "core")
     mine = columns_at(projected, core, 384)
-    ctx_mine, ctx_other, logsum, rows = attend(info, slopes, mine, received)
+    side_done = None
+    if side is None:
+        ctx_mine, ctx_other, logsum, rows = attend(info, slopes, mine, received)
+    else:
+        side_done, (ctx_mine, ctx_other, logsum, rows) = beside(
+            side[0], side[1], (mine, received), lambda v: attend(info, slopes, *v)
+        )
     context = in_order(ctx_mine, swap(ctx_other, "core"), core)
-    middle = hidden + dot_scatter(context, project, dot) + project_bias
+    parts, own = beside(
+        dot_others(context, project, dot),
+        scatter_parts,
+        context,
+        lambda v: dot_own(v, project, dot),
+    )
+    middle = hidden + sum_parts(own, parts) + project_bias
     normed_two = gather_z(norm(middle, gain_two, offset_two).astype(bf16))
     before = dot(normed_two, up) + up_bias
     activated = gelu(before).astype(bf16)
-    result = middle + dot_scatter(activated, down, dot) + down_bias
+    last = (middle, activated)
     kept = (hidden, normed_all, logsum, rows, context, middle, normed_two, before, activated)
-    return result, kept
-
-
-def backward(gradient, params, kept, info, slopes, core):
+    return last, kept, side_done
+
+
+def last_send(last, params):
+    return dot_others(last[1], params[10], dot)
+
+
+def last_sum(last, params, parts):
+    return last[0] + sum_parts(dot_own(last[1], params[10], dot), parts) + params[11]
+
+
+def backward(gradient, grad_down, params, kept, info, slopes, core, fill):
     (gain_one, _, w_in, _, project, _) = params[:6]
     (gain_two, _, up, _, down, _) = params[6:]
     hidden, normed_all, logsum, rows, context, middle, normed_two, before, activated = kept
-    grad_low = gradient.astype(bf16)
-    grad_down = gather_z(grad_low)
-    sum_down = jnp.sum(grad_low.astype(f32), axis=0)
+    sum_down = jnp.sum(gradient.astype(bf16).astype(f32), axis=0)
     d_act = dot_t(grad_down, down)
     d_before = jax.vjp(gelu, before)[1](d_act)[0].astype(bf16)
     sum_up = jnp.sum(d_before.astype(f32), axis=0)
-    d_normed = dot_scatter(d_before, up, dot_t)
-    grad_down, d_before = after((grad_down, d_before), d_before)
-    g_down = outer(activated, grad_down).astype(bf16)
-    g_up = outer(normed_two, d_before).astype(bf16)
-    d_normed, g_down, g_up = after((d_normed, g_down, g_up), g_down, g_up)
+
+    def outer_work(given):
+        activated, grad_down, normed_two, d_before = given
+        own = dot_own(d_before, up, dot_t)
+        g_down = outer(activated, grad_down).astype(bf16)
+        g_up = outer(normed_two, d_before).astype(bf16)
+        return own, g_down, g_up
+
+    parts, (own, g_down, g_up) = beside(
+        dot_others(d_before, up, dot_t),
+        scatter_parts,
+        (activated, grad_down, normed_two, d_before),
+        outer_work,
+    )
+    d_normed = sum_parts(own, parts)
     d_values, sum_gain_two, sum_offset_two = norm_back(middle, gain_two, d_normed)
     d_middle = gradient + d_values
     grad_out = d_middle.astype(bf16)
-    grad_out_all = gather_z(grad_out)
     sum_project = jnp.sum(grad_out.astype(f32), axis=0)
+    grad_out_all, outer_state = beside(grad_out, gather_z, (g_down, g_up), fill["outer"])
     d_context = dot_t(grad_out_all, project).astype(bf16)
     received = swap(columns_at(d_context, 1 - core, 128), "core")
-    g_project = outer(context, grad_out_all).astype(bf16)
-    d_mine, d_other, sums = attend_back(
-        info, slopes, rows, columns_at(d_context, core, 128), received, logsum
+    mine = columns_at(d_context, core, 128)
+    attend_done, (d_mine, d_other, sums) = beside(
+        fill["attend"][0],
+        fill["attend"][1],
+        (mine, received),
+        lambda v: attend_back(info, slopes, rows, *v, logsum),
     )
     d_joined = in_order(d_mine, swap(d_other, "core"), core)
-    d_normed_one = dot_scatter(d_joined, w_in, dot_t)
-    g_input = outer(normed_all, d_joined).astype(bf16)
-    d_normed_one, g_input = after((d_normed_one, g_input), g_input)
+
+    def inner_work(given):
+        context, grad_out_all, normed_all, d_joined = given
+        own = dot_own(d_joined, w_in, dot_t)
+        g_input = outer(normed_all, d_joined).astype(bf16)
+        g_project = outer(context, grad_out_all).astype(bf16)
+        return own, fill["inner"](g_project, g_input)
+
+    parts, (own, inner_state) = beside(
+        dot_others(d_joined, w_in, dot_t),
+        scatter_parts,
+        (context, grad_out_all, normed_all, d_joined),
+        inner_work,
+    )
+    d_normed_one = sum_parts(own, parts)
     d_hidden, sum_gain_one, sum_offset_one = norm_back(hidden, gain_one, d_normed_one)
-    big = (g_down, g_up, g_project, g_input)
     small = (
         sum_gain_one,
         sum_offset_one,
@@ -461,7 +515,7 @@
         sums,
         sum_up,
     )
-    return d_middle + d_hidden, big, small
+    return d_middle + d_hidden, outer_state, attend_done, inner_state, small
 
 
 def take(value, at, axis=0):
@@ -501,25 +555,26 @@
     return jnp.concatenate([both[:, :split], columns.reshape(32, -1)], axis=1)
 
 
-def sum_steps(pack, place):
+def project_steps(g_project, place, y_hi):
     x, y_lo, core = place
-    total = sum_pairs(pack.reshape(2, 4, 2, 64, -1), core, "core")
-    low = total.astype(bf16)
-    total = take(total, x)
+    pack = g_project.reshape(2, 4, 2, 2, 8, D).transpose(3, 1, 2, 0, 4, 5)
+    low = sum_pairs(pack, core, "core").astype(bf16)
+    total = take(low, x).astype(f32)
     for k in (1, 2, 3):
         total = total + shift_x(take(low, (x + k) % 4), k).astype(f32)
-    return sum_pairs(total.astype(bf16), y_lo, "y_lo")
-
-
-def spread_steps(rows, place):
-    x, y_lo, core = place
-    other = swap(rows, "y_lo")
-    both = jnp.where(y_lo == 0, jnp.stack([rows, other]), jnp.stack([other, rows]))
-    blocks = jnp.stack([both] + [shift_x(both, k) for k in (3, 2, 1)])
-    blocks = lax.dynamic_slice_in_dim(jnp.concatenate([blocks, blocks]), (4 - x) % 4, 4, 0)
-    other = swap(blocks, "core")
-    both = jnp.where(core == 0, jnp.stack([blocks, other]), jnp.stack([other, blocks]))
-    return both.reshape(16, *rows.shape)
+    low = sum_pairs(total.astype(bf16), y_lo, "y_lo").astype(bf16)
+    return sum_pairs(low, y_hi, "y_hi").astype(bf16).reshape(32, 256)
+
+
+def sum_small(packed, z, y_hi):
+    split = packed.reshape(2, 4, -1)
+    total = take(split, z, 1)
+    for k in (1, 2, 3):
+        total = total + shift_z(take(split, (z + k) % 4, 1), k)
+    total = take(total, y_hi) + swap(take(total, 1 - y_hi), "y_hi")
+    total = total + swap(total, "core")
+    total = total + swap(total, "y_lo")
+    return total + shift_x(total, 1) + shift_x(total, 2) + shift_x(total, 3)
 
 
 def order_columns(rows, parts):
@@ -527,14 +582,14 @@
     return split.transpose(0, 2, 4, 3, 1, 5).reshape(128, -1)
 
 
-def unpack_outer(full):
+def unpack(full):
     full = full.astype(f32)
-    return full[:, :, :D].reshape(512, D), order_columns(full[:, :, D:], 1)
-
-
-def unpack_inner(full):
-    full = full.astype(f32)
-    return full[:, :, :256].reshape(128, D), order_columns(full[:, :, 256:], 3)
+    return (
+        full[:, :, :D].reshape(512, D),
+        order_columns(full[:, :, D : 2 * D], 1),
+        full[:, :, 2 * D : 2 * D + 256].reshape(128, D),
+        order_columns(full[:, :, 2 * D + 256 :], 3),
+    )
 
 
 def pack_small(small, place, z):
@@ -637,47 +692,73 @@
             )
         )
 
+    slot = (x, y_lo, core)
+    gradient = regroup(cotangent[0], core, y_hi)
     hidden = rows_in.astype(f32)
-    kept = []
-    for layer in range(LAYERS):
-        params = layers[layer]
-        if layer == 0:
-            normed_all = norm(raw_all.astype(f32), params[0], params[1]).astype(bf16)
-        else:
-            normed_all = gather_z(norm(hidden, params[0], params[1]).astype(bf16))
-        hidden, state = forward(hidden, normed_all, params, info, slopes, core)
-        kept.append(state)
-    gradient = regroup(cotangent[0], core, y_hi).astype(f32)
-    slot = (x, y_lo, core)
-    finals = [None] * LAYERS
-    smalls = [None] * LAYERS
-    for layer in (1, 0):
-        gradient, big, smalls[layer] = backward(
-            gradient, layers[layer], kept[layer], info, slopes, core
-        )
-        outer_pack = pack_outer(big[0], big[1])
-        inner_pack = pack_inner(big[2], big[3])
-        if layer == 1:
-            outer_sum = lax.psum_scatter(outer_pack, GRP, scatter_dimension=0, tiled=True)
-            inner_sum = lax.psum_scatter(inner_pack, GRP, scatter_dimension=0, tiled=True)
-            outer_sum = own_rows(outer_sum.reshape(64, -1), D, y_hi)
-            inner_sum = own_rows(inner_sum.reshape(64, -1), 256, y_hi)
-            both = lax.all_gather(jnp.concatenate([outer_sum, inner_sum], axis=1), GRP)
-            finals[1] = unpack_outer(both[:, :, : 2 * D]) + unpack_inner(both[:, :, 2 * D :])
-        else:
-            outer_sum = own_rows(sum_steps(outer_pack, slot).astype(bf16), D, y_hi)
-            inner_sum = own_rows(sum_steps(inner_pack, slot).astype(bf16), 256, y_hi)
-            finals[0] = unpack_outer(spread_steps(outer_sum, slot)) + unpack_inner(
-                spread_steps(inner_sum, slot)
-            )
-    packed = jnp.concatenate([pack_small(s, place, z) for s in smalls], axis=1)
-    vector = jnp.sum(to_ctx(packed), axis=0)
-    vector = jnp.sum(lax.all_gather(vector.reshape(8, -1), GRP, axis=0, tiled=False), axis=0)
-    vector = vector.reshape(LAYERS, -1)
+    normed_all = norm(raw_all.astype(f32), layers[0][0], layers[0][1]).astype(bf16)
+    last, kept_0, grad_down = forward(
+        hidden, normed_all, layers[0], info, slopes, core, (gradient, gather_z)
+    )
+    gradient = gradient.astype(f32)
+    hidden = last_sum(last, layers[0], scatter_parts(last_send(last, layers[0])))
+    normed_all = gather_z(norm(hidden, layers[1][0], layers[1][1]).astype(bf16))
+    last, kept_1, _ = forward(hidden, normed_all, layers[1], info, slopes, core)
+
+    def grp_sum(pack):
+        return lax.psum_scatter(pack, GRP, scatter_dimension=0, tiled=True).reshape(64, -1)
+
+    fill = {
+        "outer": lambda v: pack_outer(*v),
+        "attend": (last_send(last, layers[1]), scatter_parts),
+        "inner": pack_inner,
+    }
+    gradient, outer_pack, parts, inner_pack, small_1 = backward(
+        gradient, grad_down, layers[1], kept_1, info, slopes, core, fill
+    )
+    output = last_sum(last, layers[1], parts)
+    outer_1 = grp_sum(outer_pack)
+    inner_1 = grp_sum(inner_pack)
+
+    grad_down, output = beside(
+        gradient.astype(bf16), gather_z, output, lambda v: v + 0.0
+    )
+
+    def core_sum(given):
+        pack = pack_outer(*given).reshape(8, 2, 64, 2 * D)
+        return take(pack, core, 1), take(pack, 1 - core, 1)
+
+    def outer_start(given):
+        keep, send = given
+        return keep.astype(f32) + swap(send, "core").astype(f32)
+
+    fill = {
+        "outer": core_sum,
+        "attend": (jnp.zeros((8, 128), f32), lambda v: v),
+        "inner": lambda g_project, g_input: (
+            project_steps(g_project, slot, y_hi),
+            groups_first(g_input, (8, 16, 8, 768)).reshape(128, 8, 768),
+        ),
+    }
+    gradient, outer_0, _, (project_0, input_0), small_0 = backward(
+        gradient, grad_down, layers[0], kept_0, info, slopes, core, fill
+    )
+    outer_0 = outer_start(outer_0).astype(bf16)
+    outer_0 = lax.all_to_all(outer_0, ("x", "y_lo"), split_axis=0, concat_axis=0, tiled=True)
+    outer_0 = own_rows(jnp.sum(outer_0.astype(f32), axis=0).astype(bf16), D, y_hi)
+    outer_0 = lax.all_gather(jnp.concatenate([outer_0, project_0], axis=1), GRP)
+    input_0 = lax.all_to_all(input_0, GRP + CTX, split_axis=0, concat_axis=0, tiled=True)
+    input_0 = jnp.sum(input_0.reshape(32, 32, 768).astype(f32), axis=0).astype(bf16)
+    input_0 = lax.all_gather(input_0, GRP)
+    final_0 = unpack(jnp.concatenate([outer_0, input_0], axis=2))
+    inner_1 = own_rows(inner_1, 256, y_hi)
+    outer_1 = own_rows(outer_1, D, y_hi)
+    final_1 = unpack(lax.all_gather(jnp.concatenate([outer_1, inner_1], axis=1), GRP))
+    packed = jnp.concatenate([pack_small(s, place, z) for s in (small_0, small_1)], axis=1)
+    vector = sum_small(packed, z, y_hi).reshape(LAYERS, -1)
     parts = [vector[:, i * 128 : (i + 1) * 128] for i in range(6)]
-    both = [jnp.stack([finals[0][i], finals[1][i]]) for i in range(4)]
+    both = [jnp.stack([final_0[i], final_1[i]]) for i in range(4)]
     return (
-        regroup(hidden, core, y_hi)[None],
+        regroup(output, core, y_hi)[None],
         regroup(gradient, core, y_hi)[None],
         parts[0],
         parts[1],

time: 782 us -> 753 us (0.963)
  starting transfers between devices: 177 us -> 162 us
  matrix products: 76.3 us -> 64.1 us
  local copies, waits for them, and re-layouts: 79.5 us -> 69.4 us
    ppermute x27 -> x25, waiting for transfers between devices: 7.49 us -> 45.8 us  [swap(): return lax.ppermute(value, axis, [(0, 1), (1, 0)])]
    ppermute x27 -> x25, starting transfers between devices: 54 us -> 38.4 us  [swap(): return lax.ppermute(value, axis, [(0, 1), (1, 0)])]
    ppermute x48 -> x51, waiting for transfers between devices: 213 us -> 202 us  [shift_z(): return lax.ppermute(value, 'z', [(i, (i + step) % 4) for i in range(4)])]
    all_gather x1 -> x2, waiting for transfers between devices: 10.7 us -> 0.01 us  [the longest x1 0.01 us: on_device(): lax.all_gather(jnp.concatenate([outer_1, inner_1], axis=1), GRP)]
    all_to_all x0 -> x2, starting transfers between devices: none -> 8.14 us  [the longest x1 4.57 us: on_device(): lax.all_to_all(outer_0, ('x', 'y_lo'), split_axis=0, concat_axis=0, tiled...]
    unnamed x288 -> x221, local copies, waits for them, and re-layouts: 35.5 us -> 27.8 us
    ppermute x12 -> x6, waiting for transfers between devices: 29.3 us -> 21.8 us  [shift_x(): return lax.ppermute(value, 'x', [(i, (i + step) % 4) for i in range(4)])]
    ppermute x48 -> x51, starting transfers between devices: 50.1 us -> 57.2 us  [shift_z(): return lax.ppermute(value, 'z', [(i, (i + step) % 4) for i in range(4)])]
  transfers between devices with their start and end apart: 103 -> 99, of which waited for: 58 -> 51; matrix products, arithmetic and copies ran while one was open for 20% -> 19% of each run, Pallas kernels for 5% -> 7%
where the time goes in v3:
time: 753 us; the launch traced here: 744 us
  waiting for transfers between devices  290 us (39%)
  starting transfers between devices  162 us (22%)
  other arithmetic  70.5 us (9%)
  local copies, waits for them, and re-layouts  69.4 us (9%)
  matrix products  64.1 us (9%)
  Pallas kernels  49.9 us (7%)
  blocking collectives  21.9 us (3%)
  between operations  16.2 us (2%)
    ppermute x51, waiting for transfers between devices, shift_z(): return lax.ppermute(value, 'z', [(i, (i + step) % 4) for i in range(4)])  202 us
    ppermute x51, starting transfers between devices, shift_z(): return lax.ppermute(value, 'z', [(i, (i + step) % 4) for i in range(4)])  57.2 us
    ppermute x25, waiting for transfers between devices, swap(): return lax.ppermute(value, axis, [(0, 1), (1, 0)])  45.8 us
    ppermute x25, starting transfers between devices, swap(): return lax.ppermute(value, axis, [(0, 1), (1, 0)])  38.4 us
    unnamed x221, local copies, waits for them, and re-layouts  27.8 us
    dot_general x12, matrix products, dot(): return jnp.dot(left, right, preferred_element_type=f32)  24.9 us
    ppermute x5, starting transfers between devices, regroup(): got = lax.ppermute(value, ('core', 'y_hi'), [(1, 2), (2, 1)])  24.8 us
    dot_general x12, matrix products, dot_t(): lax.dot_general(left, right, (((1,), (1,)), ((), ())), preferred_element_...  22.4 us
  transfers between devices with their start and end apart: 99, of which 51 were waited for; matrix products, arithmetic and copies ran while one was open for 19% of the time, Pallas kernels for 7%

profile of v3, /device:TPU:1, one launch (start us, length us, event | category | flops | bytes accessed | tf_op | source)
XLA Modules:
  0.0 744.2 jit_solution(3710072389619790312)
XLA Ops:
  7.2 6.2 collective-permute-start
  18.6 6.0 collective-permute-done.1
  25.8 3.8 collective-permute-start.4
  35.5 3.6 all-to-all-start
  82.2 9.5 %attend.2 = (bf16[768,128]{1,0:T(8,128)(2,1)S(1)}, bf16[768,128]{1,0:T(8,128)(2,1)}, f32[2,1536]{1,0:T(2,128)S(1)}, bf16[1536,384]{1,0:T(8,128)(2,1)S(1)}) custom-call(s32[4]{0:T(128)S(1)} %add_add_fusion.3.info, f32[2]{0:T(128)S(1)} %multiply_exponential_fusion.slopes, bf16[768,384]{1,0:T(8,128)(2,1)S(1)} %copy-done.26, ...), custom_call_target="tpu_custom_call" | custom-call | flops 716800000 | bytes 28000000 | tf_op jit(solution)/shard_map/attend/pallas_call | solution.py:208
  95.4 4.6 collective-permute-done.7
  101.8 4.2 all-to-all-start.1
  117.4 3.6 all-to-all-done.1.got
  123.4 6.5 collective-permute-done.16
  129.9 8.5 %collective-permute-done.15 = bf16[192,1024]{1,0:T(8,128)(2,1)} collective-permute-done((bf16[192,1024]{1,0:T(8,128)(2,1)}, bf16[192,1024]{1,0:T(8,128)(2,1)}, u32[]{:S(2)}, u32[]{:S(2)}) %collective-permute-start.15) | collective-permute-done | bytes 393248 | tf_op jit(solution)/shard_map/ppermute | solution.py:31
  144.3 6.6 all-to-all-start.2
  155.5 20.4 %collective-permute-done.17 = bf16[192,1024]{1,0:T(8,128)(2,1)} collective-permute-done((bf16[192,1024]{1,0:T(8,128)(2,1)}, bf16[192,1024]{1,0:T(8,128)(2,1)}, u32[]{:S(2)}, u32[]{:S(2)}) %collective-permute-start.17) | collective-permute-done | bytes 393248 | tf_op jit(solution)/shard_map/ppermute | solution.py:31
  175.9 5.5 multiply_convert_fusion.1
  188.2 5.4 collective-permute-done.21
  195.4 7.3 collective-permute-done.22
  219.5 11.1 %collective-permute-done.24 = bf16[192,1024]{1,0:T(8,128)(2,1)} collective-permute-done((bf16[192,1024]{1,0:T(8,128)(2,1)}, bf16[192,1024]{1,0:T(8,128)(2,1)}, u32[]{:S(2)}, u32[]{:S(2)}) %collective-permute-start.24) | collective-permute-done | bytes 393248 | tf_op jit(solution)/shard_map/ppermute | solution.py:31
  235.8 8.3 %attend.3 = (bf16[768,128]{1,0:T(8,128)(2,1)S(1)}, bf16[768,128]{1,0:T(8,128)(2,1)S(1)}, f32[2,1536]{1,0:T(2,128)S(1)}, bf16[1536,384]{1,0:T(8,128)(2,1)S(1)}) custom-call(s32[4]{0:T(128)S(1)} %add_add_fusion.3.info, f32[2]{0:T(128)S(1)} %multiply_exponential_fusion.slopes, bf16[768,384]{1,0:T(8,128)(2,1)S(1)} %get-tuple-element.307.mine, ...), custom_call_target="tpu_custom_call" | custom-call | flops 716800000 | bytes 28000000 | tf_op jit(solution)/shard_map/attend/pallas_call | solution.py:208
  251.0 17.3 %collective-permute-done.34 = bf16[192,1024]{1,0:T(8,128)(2,1)S(1)} collective-permute-done((bf16[192,1024]{1,0:T(8,128)(2,1)S(1)}, bf16[192,1024]{1,0:T(8,128)(2,1)S(1)}, u32[]{:S(2)}, u32[]{:S(2)}) %collective-permute-start.34) | collective-permute-done | bytes 393248 | tf_op jit(solution)/shard_map/ppermute | solution.py:31
  273.7 8.0 %collective-permute-done.37 = bf16[192,1024]{1,0:T(8,128)(2,1)S(1)} collective-permute-done((bf16[192,1024]{1,0:T(8,128)(2,1)S(1)}, bf16[192,1024]{1,0:T(8,128)(2,1)S(1)}, u32[]{:S(2)}, u32[]{:S(2)}) %collective-permute-start.37) | collective-permute-done | bytes 393248 | tf_op jit(solution)/shard_map/ppermute | solution.py:31
  283.8 9.9 %collective-permute-done.35 = bf16[192,1024]{1,0:T(8,128)(2,1)S(1)} collective-permute-done((bf16[192,1024]{1,0:T(8,128)(2,1)S(1)}, bf16[192,1024]{1,0:T(8,128)(2,1)S(1)}, u32[]{:S(2)}, u32[]{:S(2)}) %collective-permute-start.35) | collective-permute-done | bytes 393248 | tf_op jit(solution)/shard_map/ppermute | solution.py:31
  294.4 3.9 fusion.78
  298.3 4.1 convert_reduce_fusion.1
  308.1 3.2 convolution_convert_fusion.2
  311.2 3.2 convolution_convert_fusion.3
  314.5 10.7 %collective-permute-done.40 = bf16[192,1024]{1,0:T(8,128)(2,1)S(1)} collective-permute-done((bf16[192,1024]{1,0:T(8,128)(2,1)S(1)}, bf16[192,1024]{1,0:T(8,128)(2,1)S(1)}, u32[]{:S(2)}, u32[]{:S(2)}) %collective-permute-start.40) | collective-permute-done | bytes 393248 | tf_op jit(solution)/shard_map/ppermute | solution.py:31
  336.9 4.5 collective-permute-done.43
  342.9 9.2 %collective-permute-done.41 = bf16[192,1024]{1,0:T(8,128)(2,1)} collective-permute-done((bf16[192,1024]{1,0:T(8,128)(2,1)}, bf16[192,1024]{1,0:T(8,128)(2,1)}, u32[]{:S(2)}, u32[]{:S(2)}) %collective-permute-start.41) | collective-permute-done | bytes 393248 | tf_op jit(solution)/shard_map/ppermute | solution.py:31
  359.6 10.6 %attend_back.2 = (bf16[768,384]{1,0:T(8,128)(2,1)S(1)}, bf16[768,384]{1,0:T(8,128)(2,1)S(1)}, f32[1,384]{1,0:T(1,128)S(1)}) custom-call(s32[4]{0:T(128)S(1)} %add_add_fusion.3.info, f32[2]{0:T(128)S(1)} %multiply_exponential_fusion.slopes, bf16[1536,384]{1,0:T(8,128)(2,1)S(1)} %copy-done.30, bf16[768,128]{1,0:T(8,128)(2,1)S(1)} %get-tuple-element.178.mine, ...), custom_call_target="tpu_custom_call" | custom-call | flops 1792000000 | bytes 36000000 | tf_op jit(solution)/shard_map/attend_back/pallas_call | solution.py:232
  370.2 5.3 collective-permute-done.46
  382.8 3.6 collective-permute-start.50
  394.6 9.1 %collective-permute-done.50 = bf16[192,1024]{1,0:T(8,128)(2,1)} collective-permute-done((bf16[192,1024]{1,0:T(8,128)(2,1)}, bf16[192,1024]{1,0:T(8,128)(2,1)}, u32[]{:S(2)}, u32[]{:S(2)}) %collective-permute-start.50) | collective-permute-done | bytes 393248 | tf_op jit(solution)/shard_map/ppermute | solution.py:31
  403.9 3.2 fusion.27
  411.2 3.2 collective-permute-start.54
  416.5 14.5 %collective-permute-done.54 = bf16[192,1024]{1,0:T(8,128)(2,1)} collective-permute-done((bf16[192,1024]{1,0:T(8,128)(2,1)}, bf16[192,1024]{1,0:T(8,128)(2,1)}, u32[]{:S(2)}, u32[]{:S(2)}) %collective-permute-start.54) | collective-permute-done | bytes 393248 | tf_op jit(solution)/shard_map/ppermute | solution.py:31
  431.0 4.1 collective-permute-done.52
  436.6 5.5 convert_reduce_fusion.2
  446.7 3.2 convolution_convert_fusion.1
  449.9 3.2 convolution_convert_fusion
  453.9 9.3 %collective-permute-done.58 = bf16[192,1024]{1,0:T(8,128)(2,1)S(1)} collective-permute-done((bf16[192,1024]{1,0:T(8,128)(2,1)S(1)}, bf16[192,1024]{1,0:T(8,128)(2,1)S(1)}, u32[]{:S(2)}, u32[]{:S(2)}) %collective-permute-start.58) | collective-permute-done | bytes 393248 | tf_op jit(solution)/shard_map/ppermute | solution.py:31
  465.7 3.4 collective-permute-start.61
  474.5 10.9 %collective-permute-done.61 = bf16[192,1024]{1,0:T(8,128)(2,1)S(1)} collective-permute-done((bf16[192,1024]{1,0:T(8,128)(2,1)S(1)}, bf16[192,1024]{1,0:T(8,128)(2,1)S(1)}, u32[]{:S(2)}, u32[]{:S(2)}) %collective-permute-start.61) | collective-permute-done | bytes 393248 | tf_op jit(solution)/shard_map/ppermute | solution.py:31
  485.4 4.1 collective-permute-done.59
  491.4 3.2 collective-permute-done.62.other
  494.6 10.6 %attend_back.3 = (bf16[768,384]{1,0:T(8,128)(2,1)S(1)}, bf16[768,384]{1,0:T(8,128)(2,1)S(1)}, f32[1,384]{1,0:T(1,128)S(1)}) custom-call(s32[4]{0:T(128)S(1)} %add_add_fusion.3.info, f32[2]{0:T(128)S(1)} %multiply_exponential_fusion.slopes, bf16[1536,384]{1,0:T(8,128)(2,1)S(1)} %copy-done.28, bf16[768,128]{1,0:T(8,128)(2,1)S(1)} %get-tuple-element.218.mine, ...), custom_call_target="tpu_custom_call" | custom-call | flops 1792000000 | bytes 36000000 | tf_op jit(solution)/shard_map/attend_back/pallas_call | solution.py:232
  511.9 3.7 add_convert_fusion
  515.6 4.6 all-to-all-start.3
  534.9 13.3 %collective-permute-done.68 = bf16[2,2,8,1024]{3,2,0,1:T(8,128)(2,1)S(1)} collective-permute-done((bf16[2,2,8,1024]{3,2,0,1:T(8,128)(2,1)S(1)}, bf16[2,2,8,1024]{3,2,0,1:T(8,128)(2,1)S(1)}, u32[]{:S(2)}, u32[]{:S(2)}) %collective-permute-start.68) | collective-permute-done | bytes 65568 | tf_op jit(solution)/shard_map/ppermute | solution.py:35
  548.5 7.1 collective-permute-done.70
  560.2 4.4 collective-permute-start.84
  567.6 3.3 all-to-all-start.4
  571.0 4.3 all-to-all-done.4
  576.4 8.6 %collective-permute-start.55 = (f32[192,1024]{1,0:T(8,128)}, f32[192,1024]{1,0:T(8,128)}, u32[]{:S(2)}, u32[]{:S(2)}) collective-permute-start(f32[192,1024]{1,0:T(8,128)} %fusion.27), channel_id=1, source_target_pairs={{4,8},{8,4},{5,9},{9,5},{6,10},{10,6},{7,11},{11,7},{20,24},{24,20... | collective-permute-start | bytes 2359304 | tf_op jit(solution)/shard_map/ppermute | solution.py:43
  588.6 16.4 %collective-permute-done.86 = bf16[32,1024]{1,0:T(8,128)(2,1)S(1)} collective-permute-done((bf16[32,1024]{1,0:T(8,128)(2,1)S(1)}, bf16[32,1024]{1,0:T(8,128)(2,1)S(1)}, u32[]{:S(2)}, u32[]{:S(2)}) %collective-permute-start.86) | collective-permute-done | bytes 65568 | tf_op jit(solution)/shard_map/ppermute | solution.py:39
  606.8 3.5 collective-permute-start.85
  611.0 3.3 all-to-all-start.7
  618.6 3.3 all-to-all-start.6
  621.9 4.4 all-to-all-done.6
  626.3 3.6 all-to-all-start.5
  637.3 5.8 collective-permute-start.73
  643.2 4.7 collective-permute-done.75
  647.9 4.0 collective-permute-start.77
  651.9 17.8 %collective-permute-done.77 = f32[3072]{0:T(1024)S(1)} collective-permute-done((f32[3072]{0:T(1024)S(1)}, f32[3072]{0:T(1024)S(1)}, u32[]{:S(2)}, u32[]{:S(2)}) %collective-permute-start.77) | collective-permute-done | bytes 12320 | tf_op jit(solution)/shard_map/ppermute | solution.py:39
  669.7 3.5 collective-permute-start.78
  686.5 21.9 %all-gather.1 = bf16[512,768]{1,0:T(8,128)(2,1)S(1)} all-gather(bf16[32,768]{1,0:T(8,128)(2,1)S(1)} %bitcast_reduce_fusion), channel_id=3, replica_groups=mesh['x'=4,'y_lo'=2,'core'=2,'y_hi'=2,'z'=4] {'x','y_lo','core'}, dimensions={0}, use_global_device_ids=true | all-gather | bytes 835584 | tf_op jit(solution)/shard_map/all_gather | solution.py:751
  (575 shorter events, 284.6 us)
Async XLA Ops:
  7.2 67.2 %collective-permute-start = (bf16[192,1024]{1,0:T(8,128)(2,1)}, bf16[192,1024]{1,0:T(8,128)(2,1)}, u32[]{:S(2)}, u32[]{:S(2)}) collective-permute-start(bf16[192,1024]{1,0:T(8,128)(2,1)} %bitcast.299), channel_id=1, source_target_pairs={{4,8},{8,4},{5,9},{9,5},{6,10},{10,6},{7,11},{11,7},{20,24},{24,20... | collective-permute-start | bytes 1179656 | tf_op jit(solution)/shard_map/ppermute | solution.py:43
  25.8 24.5 %collective-permute-start.4 = (bf16[192,1024]{1,0:T(8,128)(2,1)S(1)}, bf16[192,1024]{1,0:T(8,128)(2,1)}, u32[]{:S(2)}, u32[]{:S(2)}) collective-permute-start(bf16[192,1024]{1,0:T(8,128)(2,1)S(1)} %get-tuple-element.273), channel_id=1, source_target_pairs={{0,3},{1,0},{2,1},{3,2},{4,7},{5,4},{6,5},{7,6},{8,11},{9,8},{10,9... | collective-permute-start | bytes 1179656 | tf_op jit(solution)/shard_map/ppermute | solution.py:31
  29.6 20.6 %collective-permute-start.3 = (bf16[192,1024]{1,0:T(8,128)(2,1)S(1)}, bf16[192,1024]{1,0:T(8,128)(2,1)}, u32[]{:S(2)}, u32[]{:S(2)}) collective-permute-start(bf16[192,1024]{1,0:T(8,128)(2,1)S(1)} %get-tuple-element.273), channel_id=1, source_target_pairs={{0,2},{1,3},{2,0},{3,1},{4,6},{5,7},{6,4},{7,5},{8,10},{9,11},{10,... | collective-permute-start | bytes 1179656 | tf_op jit(solution)/shard_map/ppermute | solution.py:31
  29.6 20.6 %collective-permute-start.2 = (bf16[192,1024]{1,0:T(8,128)(2,1)S(1)}, bf16[192,1024]{1,0:T(8,128)(2,1)}, u32[]{:S(2)}, u32[]{:S(2)}) collective-permute-start(bf16[192,1024]{1,0:T(8,128)(2,1)S(1)} %get-tuple-element.273), channel_id=1, source_target_pairs={{0,1},{1,2},{2,3},{3,0},{4,5},{5,6},{6,7},{7,4},{8,9},{9,10},{10,1... | collective-permute-start | bytes 1179656 | tf_op jit(solution)/shard_map/ppermute | solution.py:31
  35.5 18.1 %all-to-all-start = ((bf16[8,80,768]{2,1,0:T(8,128)(2,1)}), bf16[8,80,768]{2,1,0:T(8,128)(2,1)S(1)}, u32[]{:S(2)}, u32[]{:S(2)}) async-start(bf16[8,80,768]{2,1,0:T(8,128)(2,1)} %copy-done.9), calls=%async_computation | async-start | bytes 1966080 | tf_op jit(solution)/shard_map/all_to_all | solution.py:402
  47.2 29.1 %collective-permute-start.12 = (bf16[320,1024]{1,0:T(8,128)(2,1)}, bf16[320,1024]{1,0:T(8,128)(2,1)}, u32[]{:S(2)}, u32[]{:S(2)}) collective-permute-start(bf16[320,1024]{1,0:T(8,128)(2,1)} %get-tuple-element.136), channel_id=1, source_target_pairs={{0,4},{4,0},{1,5},{5,1},{2,6},{6,2},{3,7},{7,3},{8,12},{12,8},{9,1... | collective-permute-start | bytes 1966088 | tf_op jit(solution)/shard_map/ppermute | solution.py:39
  76.3 29.7 %collective-permute-start.13 = (bf16[320,1024]{1,0:T(8,128)(2,1)}, bf16[320,1024]{1,0:T(8,128)(2,1)S(1)}, u32[]{:S(2)}, u32[]{:S(2)}) collective-permute-start(bf16[320,1024]{1,0:T(8,128)(2,1)} %collective-permute-done.12.got), channel_id=1, source_target_pairs={{0,8},{8,0},{1,9},{9,1},{2,10},{10,2},{3,11},{11,3},{4,12},{12,4},... | collective-permute-start | bytes 1966088 | tf_op jit(solution)/shard_map/ppermute | solution.py:39
  76.3 19.0 %collective-permute-start.9 = (bf16[192,1024]{1,0:T(8,128)(2,1)S(1)}, bf16[192,1024]{1,0:T(8,128)(2,1)S(1)}, u32[]{:S(2)}, u32[]{:S(2)}) collective-permute-start(bf16[192,1024]{1,0:T(8,128)(2,1)S(1)} %get-tuple-element.127), channel_id=1, source_target_pairs={{0,3},{1,0},{2,1},{3,2},{4,7},{5,4},{6,5},{7,6},{8,11},{9,8},{10,9... | collective-permute-start | bytes 1179656 | tf_op jit(solution)/shard_map/ppermute | solution.py:31
  79.0 16.3 %collective-permute-start.8 = (bf16[192,1024]{1,0:T(8,128)(2,1)S(1)}, bf16[192,1024]{1,0:T(8,128)(2,1)S(1)}, u32[]{:S(2)}, u32[]{:S(2)}) collective-permute-start(bf16[192,1024]{1,0:T(8,128)(2,1)S(1)} %get-tuple-element.127), channel_id=1, source_target_pairs={{0,2},{1,3},{2,0},{3,1},{4,6},{5,7},{6,4},{7,5},{8,10},{9,11},{10,... | collective-permute-start | bytes 1179656 | tf_op jit(solution)/shard_map/ppermute | solution.py:31
  79.6 20.4 %collective-permute-start.7 = (bf16[192,1024]{1,0:T(8,128)(2,1)S(1)}, bf16[192,1024]{1,0:T(8,128)(2,1)S(1)}, u32[]{:S(2)}, u32[]{:S(2)}) collective-permute-start(bf16[192,1024]{1,0:T(8,128)(2,1)S(1)} %get-tuple-element.127), channel_id=1, source_target_pairs={{0,1},{1,2},{2,3},{3,0},{4,5},{5,6},{6,7},{7,4},{8,9},{9,10},{10,1... | collective-permute-start | bytes 1179656 | tf_op jit(solution)/shard_map/ppermute | solution.py:31
  101.8 19.3 %all-to-all-start.1 = ((bf16[8,64,1024]{2,1,0:T(8,128)(2,1)}), bf16[8,64,1024]{2,1,0:T(8,128)(2,1)}, u32[]{:S(2)}, u32[]{:S(2)}) async-start(bf16[8,64,1024]{2,1,0:T(8,128)(2,1)} %copy-done.23), calls=%async_computation.1 | async-start | bytes 2097152 | tf_op jit(solution)/shard_map/all_to_all | solution.py:402
  112.4 17.5 %collective-permute-start.16 = (bf16[192,1024]{1,0:T(8,128)(2,1)}, bf16[192,1024]{1,0:T(8,128)(2,1)}, u32[]{:S(2)}, u32[]{:S(2)}) collective-permute-start(bf16[192,1024]{1,0:T(8,128)(2,1)} %get-tuple-element.311), channel_id=1, source_target_pairs={{0,1},{1,2},{2,3},{3,0},{4,5},{5,6},{6,7},{7,4},{8,9},{9,10},{10,1... | collective-permute-start | bytes 1179656 | tf_op jit(solution)/shard_map/ppermute | solution.py:31
  113.8 24.5 %collective-permute-start.15 = (bf16[192,1024]{1,0:T(8,128)(2,1)}, bf16[192,1024]{1,0:T(8,128)(2,1)}, u32[]{:S(2)}, u32[]{:S(2)}) collective-permute-start(bf16[192,1024]{1,0:T(8,128)(2,1)} %get-tuple-element.312), channel_id=1, source_target_pairs={{0,2},{1,3},{2,0},{3,1},{4,6},{5,7},{6,4},{7,5},{8,10},{9,11},{10,... | collective-permute-start | bytes 1179656 | tf_op jit(solution)/shard_map/ppermute | solution.py:31
  116.2 22.1 %collective-permute-start.14 = (bf16[192,1024]{1,0:T(8,128)(2,1)}, bf16[192,1024]{1,0:T(8,128)(2,1)}, u32[]{:S(2)}, u32[]{:S(2)}) collective-permute-start(bf16[192,1024]{1,0:T(8,128)(2,1)} %get-tuple-element.313), channel_id=1, source_target_pairs={{0,3},{1,0},{2,1},{3,2},{4,7},{5,4},{6,5},{7,6},{8,11},{9,8},{10,9... | collective-permute-start | bytes 1179656 | tf_op jit(solution)/shard_map/ppermute | solution.py:31
  121.1 31.1 %collective-permute-start.20 = (bf16[8,64,1024]{2,1,0:T(8,128)(2,1)}, bf16[8,64,1024]{2,1,0:T(8,128)(2,1)}, u32[]{:S(2)}, u32[]{:S(2)}) collective-permute-start(bf16[8,64,1024]{2,1,0:T(8,128)(2,1)} %all-to-all-done.1.got), channel_id=1, source_target_pairs={{0,8},{8,0},{1,9},{9,1},{2,10},{10,2},{3,11},{11,3},{4,12},{12,4},... | collective-permute-start | bytes 3145736 | tf_op jit(solution)/shard_map/ppermute | solution.py:39
  144.1 31.8 %collective-permute-start.17 = (bf16[192,1024]{1,0:T(8,128)(2,1)}, bf16[192,1024]{1,0:T(8,128)(2,1)}, u32[]{:S(2)}, u32[]{:S(2)}) collective-permute-start(bf16[192,1024]{1,0:T(8,128)(2,1)} %add_convert_fusion.5), channel_id=1, source_target_pairs={{0,1},{1,2},{2,3},{3,0},{4,5},{5,6},{6,7},{7,4},{8,9},{9,10},{10,1... | collective-permute-start | bytes 1179656 | tf_op jit(solution)/shard_map/ppermute | solution.py:31
  144.3 41.9 %all-to-all-start.2 = ((bf16[8,64,1792]{2,1,0:T(8,128)(2,1)}), bf16[8,64,1792]{2,1,0:T(8,128)(2,1)}, u32[]{:S(2)}, u32[]{:S(2)}) async-start(bf16[8,64,1792]{2,1,0:T(8,128)(2,1)} %copy-done.20), calls=%async_computation.2 | async-start | bytes 3670016 | tf_op jit(solution)/shard_map/all_to_all | solution.py:402
  150.9 436.8 %reduce-scatter.5.cloned.1.call-start = ((), (), s32[]{:S(2)}) async-start(), calls=%async_computation.11 | async-start | bytes 2228224 | tf_op jit(solution)/shard_map/reduce_scatter | solution.py:708
  185.4 17.3 %collective-permute-start.22 = (bf16[192,1024]{1,0:T(8,128)(2,1)}, bf16[192,1024]{1,0:T(8,128)(2,1)}, u32[]{:S(2)}, u32[]{:S(2)}) collective-permute-start(bf16[192,1024]{1,0:T(8,128)(2,1)} %get-tuple-element.310), channel_id=1, source_target_pairs={{0,2},{1,3},{2,0},{3,1},{4,6},{5,7},{6,4},{7,5},{8,10},{9,11},{10,... | collective-permute-start | bytes 1179656 | tf_op jit(solution)/shard_map/ppermute | solution.py:31
  186.2 27.5 %collective-permute-start.27 = (bf16[8,64,1792]{2,1,0:T(8,128)(2,1)}, bf16[8,64,1792]{2,1,0:T(8,128)(2,1)}, u32[]{:S(2)}, u32[]{:S(2)}) collective-permute-start(bf16[8,64,1792]{2,1,0:T(8,128)(2,1)} %all-to-all-done.2.got), channel_id=1, source_target_pairs={{0,8},{8,0},{1,9},{9,1},{2,10},{10,2},{3,11},{11,3},{4,12},{12,4},... | collective-permute-start | bytes 5505032 | tf_op jit(solution)/shard_map/ppermute | solution.py:39
  209.7 21.0 %collective-permute-start.24 = (bf16[192,1024]{1,0:T(8,128)(2,1)}, bf16[192,1024]{1,0:T(8,128)(2,1)}, u32[]{:S(2)}, u32[]{:S(2)}) collective-permute-start(bf16[192,1024]{1,0:T(8,128)(2,1)} %add_convert_fusion.4), channel_id=1, source_target_pairs={{0,1},{1,2},{2,3},{3,0},{4,5},{5,6},{6,7},{7,4},{8,9},{9,10},{10,1... | collective-permute-start | bytes 1179656 | tf_op jit(solution)/shard_map/ppermute | solution.py:31
  210.6 23.6 %collective-permute-start.30 = (bf16[320,1024]{1,0:T(8,128)(2,1)}, bf16[320,1024]{1,0:T(8,128)(2,1)}, u32[]{:S(2)}, u32[]{:S(2)}) collective-permute-start(bf16[320,1024]{1,0:T(8,128)(2,1)} %get-tuple-element.150), channel_id=1, source_target_pairs={{0,4},{4,0},{1,5},{5,1},{2,6},{6,2},{3,7},{7,3},{8,12},{12,8},{9,1... | collective-permute-start | bytes 1966088 | tf_op jit(solution)/shard_map/ppermute | solution.py:39
  248.1 20.2 %collective-permute-start.34 = (bf16[192,1024]{1,0:T(8,128)(2,1)S(1)}, bf16[192,1024]{1,0:T(8,128)(2,1)S(1)}, u32[]{:S(2)}, u32[]{:S(2)}) collective-permute-start(bf16[192,1024]{1,0:T(8,128)(2,1)S(1)} %get-tuple-element.303), channel_id=1, source_target_pairs={{0,1},{1,2},{2,3},{3,0},{4,5},{5,6},{6,7},{7,4},{8,9},{9,10},{10,1... | collective-permute-start | bytes 1179656 | tf_op jit(solution)/shard_map/ppermute | solution.py:31
  248.1 20.2 %collective-permute-start.33 = (bf16[192,1024]{1,0:T(8,128)(2,1)S(1)}, bf16[192,1024]{1,0:T(8,128)(2,1)S(1)}, u32[]{:S(2)}, u32[]{:S(2)}) collective-permute-start(bf16[192,1024]{1,0:T(8,128)(2,1)S(1)} %get-tuple-element.304), channel_id=1, source_target_pairs={{0,2},{1,3},{2,0},{3,1},{4,6},{5,7},{6,4},{7,5},{8,10},{9,11},{10,... | collective-permute-start | bytes 1179656 | tf_op jit(solution)/shard_map/ppermute | solution.py:31
  249.6 19.0 %collective-permute-start.32 = (bf16[192,1024]{1,0:T(8,128)(2,1)S(1)}, bf16[192,1024]{1,0:T(8,128)(2,1)S(1)}, u32[]{:S(2)}, u32[]{:S(2)}) collective-permute-start(bf16[192,1024]{1,0:T(8,128)(2,1)S(1)} %get-tuple-element.305), channel_id=1, source_target_pairs={{0,3},{1,0},{2,1},{3,2},{4,7},{5,4},{6,5},{7,6},{8,11},{9,8},{10,9... | collective-permute-start | bytes 1179656 | tf_op jit(solution)/shard_map/ppermute | solution.py:31
  272.7 21.0 %collective-permute-start.35 = (bf16[192,1024]{1,0:T(8,128)(2,1)S(1)}, bf16[192,1024]{1,0:T(8,128)(2,1)S(1)}, u32[]{:S(2)}, u32[]{:S(2)}) collective-permute-start(bf16[192,1024]{1,0:T(8,128)(2,1)S(1)} %add_convert_fusion.3), channel_id=1, source_target_pairs={{0,1},{1,2},{2,3},{3,0},{4,5},{5,6},{6,7},{7,4},{8,9},{9,10},{10,1... | collective-permute-start | bytes 1179656 | tf_op jit(solution)/shard_map/ppermute | solution.py:31
  305.3 19.9 %collective-permute-start.40 = (bf16[192,1024]{1,0:T(8,128)(2,1)S(1)}, bf16[192,1024]{1,0:T(8,128)(2,1)S(1)}, u32[]{:S(2)}, u32[]{:S(2)}) collective-permute-start(bf16[192,1024]{1,0:T(8,128)(2,1)S(1)} %get-tuple-element.300), channel_id=1, source_target_pairs={{0,1},{1,2},{2,3},{3,0},{4,5},{5,6},{6,7},{7,4},{8,9},{9,10},{10,1... | collective-permute-start | bytes 1179656 | tf_op jit(solution)/shard_map/ppermute | solution.py:31
  305.4 19.8 %collective-permute-start.39 = (bf16[192,1024]{1,0:T(8,128)(2,1)S(1)}, bf16[192,1024]{1,0:T(8,128)(2,1)S(1)}, u32[]{:S(2)}, u32[]{:S(2)}) collective-permute-start(bf16[192,1024]{1,0:T(8,128)(2,1)S(1)} %get-tuple-element.301), channel_id=1, source_target_pairs={{0,2},{1,3},{2,0},{3,1},{4,6},{5,7},{6,4},{7,5},{8,10},{9,11},{10,... | collective-permute-start | bytes 1179656 | tf_op jit(solution)/shard_map/ppermute | solution.py:31
  306.0 19.5 %collective-permute-start.38 = (bf16[192,1024]{1,0:T(8,128)(2,1)S(1)}, bf16[192,1024]{1,0:T(8,128)(2,1)S(1)}, u32[]{:S(2)}, u32[]{:S(2)}) collective-permute-start(bf16[192,1024]{1,0:T(8,128)(2,1)S(1)} %get-tuple-element.302), channel_id=1, source_target_pairs={{0,3},{1,0},{2,1},{3,2},{4,7},{5,4},{6,5},{7,6},{8,11},{9,8},{10,9... | collective-permute-start | bytes 1179656 | tf_op jit(solution)/shard_map/ppermute | solution.py:31
  328.6 12.8 %collective-permute-start.43 = (bf16[192,1024]{1,0:T(8,128)(2,1)}, bf16[192,1024]{1,0:T(8,128)(2,1)}, u32[]{:S(2)}, u32[]{:S(2)}) collective-permute-start(bf16[192,1024]{1,0:T(8,128)(2,1)} %get-tuple-element.172), channel_id=1, source_target_pairs={{0,3},{1,0},{2,1},{3,2},{4,7},{5,4},{6,5},{7,6},{8,11},{9,8},{10,9... | collective-permute-start | bytes 1179656 | tf_op jit(solution)/shard_map/ppermute | solution.py:31
  331.5 20.6 %collective-permute-start.41 = (bf16[192,1024]{1,0:T(8,128)(2,1)}, bf16[192,1024]{1,0:T(8,128)(2,1)}, u32[]{:S(2)}, u32[]{:S(2)}) collective-permute-start(bf16[192,1024]{1,0:T(8,128)(2,1)} %get-tuple-element.172), channel_id=1, source_target_pairs={{0,1},{1,2},{2,3},{3,0},{4,5},{5,6},{6,7},{7,4},{8,9},{9,10},{10,1... | collective-permute-start | bytes 1179656 | tf_op jit(solution)/shard_map/ppermute | solution.py:31
  356.7 13.5 %collective-permute-start.47 = (bf16[192,1024]{1,0:T(8,128)(2,1)S(1)}, bf16[192,1024]{1,0:T(8,128)(2,1)S(1)}, u32[]{:S(2)}, u32[]{:S(2)}) collective-permute-start(bf16[192,1024]{1,0:T(8,128)(2,1)S(1)} %get-tuple-element.297), channel_id=1, source_target_pairs={{0,1},{1,2},{2,3},{3,0},{4,5},{5,6},{6,7},{7,4},{8,9},{9,10},{10,1... | collective-permute-start | bytes 1179656 | tf_op jit(solution)/shard_map/ppermute | solution.py:31
  356.8 18.8 %collective-permute-start.46 = (bf16[192,1024]{1,0:T(8,128)(2,1)S(1)}, bf16[192,1024]{1,0:T(8,128)(2,1)S(1)}, u32[]{:S(2)}, u32[]{:S(2)}) collective-permute-start(bf16[192,1024]{1,0:T(8,128)(2,1)S(1)} %get-tuple-element.298), channel_id=1, source_target_pairs={{0,2},{1,3},{2,0},{3,1},{4,6},{5,7},{6,4},{7,5},{8,10},{9,11},{10,... | collective-permute-start | bytes 1179656 | tf_op jit(solution)/shard_map/ppermute | solution.py:31
  358.6 18.2 %collective-permute-start.45 = (bf16[192,1024]{1,0:T(8,128)(2,1)S(1)}, bf16[192,1024]{1,0:T(8,128)(2,1)S(1)}, u32[]{:S(2)}, u32[]{:S(2)}) collective-permute-start(bf16[192,1024]{1,0:T(8,128)(2,1)S(1)} %get-tuple-element.299), channel_id=1, source_target_pairs={{0,3},{1,0},{2,1},{3,2},{4,7},{5,4},{6,5},{7,6},{8,11},{9,8},{10,9... | collective-permute-start | bytes 1179656 | tf_op jit(solution)/shard_map/ppermute | solution.py:31
  382.8 21.0 %collective-permute-start.50 = (bf16[192,1024]{1,0:T(8,128)(2,1)}, bf16[192,1024]{1,0:T(8,128)(2,1)}, u32[]{:S(2)}, u32[]{:S(2)}) collective-permute-start(bf16[192,1024]{1,0:T(8,128)(2,1)} %get-tuple-element.295), channel_id=1, source_target_pairs={{0,2},{1,3},{2,0},{3,1},{4,6},{5,7},{6,4},{7,5},{8,10},{9,11},{10,... | collective-permute-start | bytes 1179656 | tf_op jit(solution)/shard_map/ppermute | solution.py:31
  386.3 17.4 %collective-permute-start.49 = (bf16[192,1024]{1,0:T(8,128)(2,1)}, bf16[192,1024]{1,0:T(8,128)(2,1)}, u32[]{:S(2)}, u32[]{:S(2)}) collective-permute-start(bf16[192,1024]{1,0:T(8,128)(2,1)} %get-tuple-element.296), channel_id=1, source_target_pairs={{0,3},{1,0},{2,1},{3,2},{4,7},{5,4},{6,5},{7,6},{8,11},{9,8},{10,9... | collective-permute-start | bytes 1179656 | tf_op jit(solution)/shard_map/ppermute | solution.py:31
  403.8 202.1 %reduce-scatter.3.cloned.1.call-start = ((), (), s32[]{:S(2)}) async-start(), calls=%async_computation.10 | async-start | bytes 4456448 | tf_op jit(solution)/shard_map/reduce_scatter | solution.py:708
  411.2 19.7 %collective-permute-start.54 = (bf16[192,1024]{1,0:T(8,128)(2,1)}, bf16[192,1024]{1,0:T(8,128)(2,1)}, u32[]{:S(2)}, u32[]{:S(2)}) collective-permute-start(bf16[192,1024]{1,0:T(8,128)(2,1)} %get-tuple-element.198), channel_id=1, source_target_pairs={{0,3},{1,0},{2,1},{3,2},{4,7},{5,4},{6,5},{7,6},{8,11},{9,8},{10,9... | collective-permute-start | bytes 1179656 | tf_op jit(solution)/shard_map/ppermute | solution.py:31
  414.4 16.6 %collective-permute-start.53 = (bf16[192,1024]{1,0:T(8,128)(2,1)}, bf16[192,1024]{1,0:T(8,128)(2,1)}, u32[]{:S(2)}, u32[]{:S(2)}) collective-permute-start(bf16[192,1024]{1,0:T(8,128)(2,1)} %get-tuple-element.198), channel_id=1, source_target_pairs={{0,2},{1,3},{2,0},{3,1},{4,6},{5,7},{6,4},{7,5},{8,10},{9,11},{10,... | collective-permute-start | bytes 1179656 | tf_op jit(solution)/shard_map/ppermute | solution.py:31
  414.4 20.7 %collective-permute-start.52 = (bf16[192,1024]{1,0:T(8,128)(2,1)}, bf16[192,1024]{1,0:T(8,128)(2,1)}, u32[]{:S(2)}, u32[]{:S(2)}) collective-permute-start(bf16[192,1024]{1,0:T(8,128)(2,1)} %get-tuple-element.198), channel_id=1, source_target_pairs={{0,1},{1,2},{2,3},{3,0},{4,5},{5,6},{6,7},{7,4},{8,9},{9,10},{10,1... | collective-permute-start | bytes 1179656 | tf_op jit(solution)/shard_map/ppermute | solution.py:31
  443.6 19.6 %collective-permute-start.58 = (bf16[192,1024]{1,0:T(8,128)(2,1)S(1)}, bf16[192,1024]{1,0:T(8,128)(2,1)S(1)}, u32[]{:S(2)}, u32[]{:S(2)}) collective-permute-start(bf16[192,1024]{1,0:T(8,128)(2,1)S(1)} %get-tuple-element.291), channel_id=1, source_target_pairs={{0,1},{1,2},{2,3},{3,0},{4,5},{5,6},{6,7},{7,4},{8,9},{9,10},{10,1... | collective-permute-start | bytes 1179656 | tf_op jit(solution)/shard_map/ppermute | solution.py:31
  443.7 19.6 %collective-permute-start.57 = (bf16[192,1024]{1,0:T(8,128)(2,1)S(1)}, bf16[192,1024]{1,0:T(8,128)(2,1)S(1)}, u32[]{:S(2)}, u32[]{:S(2)}) collective-permute-start(bf16[192,1024]{1,0:T(8,128)(2,1)S(1)} %get-tuple-element.292), channel_id=1, source_target_pairs={{0,2},{1,3},{2,0},{3,1},{4,6},{5,7},{6,4},{7,5},{8,10},{9,11},{10,... | collective-permute-start | bytes 1179656 | tf_op jit(solution)/shard_map/ppermute | solution.py:31
  444.6 19.3 %collective-permute-start.56 = (bf16[192,1024]{1,0:T(8,128)(2,1)S(1)}, bf16[192,1024]{1,0:T(8,128)(2,1)S(1)}, u32[]{:S(2)}, u32[]{:S(2)}) collective-permute-start(bf16[192,1024]{1,0:T(8,128)(2,1)S(1)} %get-tuple-element.293), channel_id=1, source_target_pairs={{0,3},{1,0},{2,1},{3,2},{4,7},{5,4},{6,5},{7,6},{8,11},{9,8},{10,9... | collective-permute-start | bytes 1179656 | tf_op jit(solution)/shard_map/ppermute | solution.py:31
  465.7 19.7 %collective-permute-start.61 = (bf16[192,1024]{1,0:T(8,128)(2,1)S(1)}, bf16[192,1024]{1,0:T(8,128)(2,1)S(1)}, u32[]{:S(2)}, u32[]{:S(2)}) collective-permute-start(bf16[192,1024]{1,0:T(8,128)(2,1)S(1)} %get-tuple-element.214), channel_id=1, source_target_pairs={{0,3},{1,0},{2,1},{3,2},{4,7},{5,4},{6,5},{7,6},{8,11},{9,8},{10,9... | collective-permute-start | bytes 1179656 | tf_op jit(solution)/shard_map/ppermute | solution.py:31
  469.1 16.3 %collective-permute-start.60 = (bf16[192,1024]{1,0:T(8,128)(2,1)S(1)}, bf16[192,1024]{1,0:T(8,128)(2,1)S(1)}, u32[]{:S(2)}, u32[]{:S(2)}) collective-permute-start(bf16[192,1024]{1,0:T(8,128)(2,1)S(1)} %get-tuple-element.214), channel_id=1, source_target_pairs={{0,2},{1,3},{2,0},{3,1},{4,6},{5,7},{6,4},{7,5},{8,10},{9,11},{10,... | collective-permute-start | bytes 1179656 | tf_op jit(solution)/shard_map/ppermute | solution.py:31
  469.1 20.4 %collective-permute-start.59 = (bf16[192,1024]{1,0:T(8,128)(2,1)S(1)}, bf16[192,1024]{1,0:T(8,128)(2,1)S(1)}, u32[]{:S(2)}, u32[]{:S(2)}) collective-permute-start(bf16[192,1024]{1,0:T(8,128)(2,1)S(1)} %get-tuple-element.214), channel_id=1, source_target_pairs={{0,1},{1,2},{2,3},{3,0},{4,5},{5,6},{6,7},{7,4},{8,9},{9,10},{10,1... | collective-permute-start | bytes 1179656 | tf_op jit(solution)/shard_map/ppermute | solution.py:31
  489.6 22.3 %collective-permute-start.83 = (bf16[8,64,2048]{2,1,0:T(8,128)(2,1)}, bf16[8,64,2048]{2,1,0:T(8,128)(2,1)}, u32[]{:S(2)}, u32[]{:S(2)}) collective-permute-start(bf16[8,64,2048]{2,1,0:T(8,128)(2,1)} %get-tuple-element.235), channel_id=1, source_target_pairs={{0,8},{8,0},{1,9},{9,1},{2,10},{10,2},{3,11},{11,3},{4,12},{12,4},... | collective-permute-start | bytes 6291464 | tf_op jit(solution)/shard_map/ppermute | solution.py:39
  515.6 42.6 %all-to-all-start.3 = ((bf16[8,64,2048]{2,1,0:T(8,128)(2,1)}), bf16[8,64,2048]{2,1,0:T(8,128)(2,1)}, u32[]{:S(2)}, u32[]{:S(2)}) async-start(bf16[8,64,2048]{2,1,0:T(8,128)(2,1)} %add_convert_fusion), calls=%async_computation.3 | async-start | bytes 4194304 | tf_op jit(solution)/shard_map/all_to_all | solution.py:746
  522.6 48.3 %collective-permute-start.66 = (bf16[192,1024]{1,0:T(8,128)(2,1)}, bf16[192,1024]{1,0:T(8,128)(2,1)}, u32[]{:S(2)}, u32[]{:S(2)}) collective-permute-start(bf16[192,1024]{1,0:T(8,128)(2,1)} %get-tuple-element.288), channel_id=1, source_target_pairs={{0,1},{1,2},{2,3},{3,0},{4,5},{5,6},{6,7},{7,4},{8,9},{9,10},{10,1... | collective-permute-start | bytes 1179656 | tf_op jit(solution)/shard_map/ppermute | solution.py:31
  522.6 48.4 %collective-permute-start.65 = (bf16[192,1024]{1,0:T(8,128)(2,1)}, bf16[192,1024]{1,0:T(8,128)(2,1)}, u32[]{:S(2)}, u32[]{:S(2)}) collective-permute-start(bf16[192,1024]{1,0:T(8,128)(2,1)} %get-tuple-element.289), channel_id=1, source_target_pairs={{0,2},{1,3},{2,0},{3,1},{4,6},{5,7},{6,4},{7,5},{8,10},{9,11},{10,... | collective-permute-start | bytes 1179656 | tf_op jit(solution)/shard_map/ppermute | solution.py:31
  527.4 20.8 %collective-permute-start.68 = (bf16[2,2,8,1024]{3,2,0,1:T(8,128)(2,1)S(1)}, bf16[2,2,8,1024]{3,2,0,1:T(8,128)(2,1)S(1)}, u32[]{:S(2)}, u32[]{:S(2)}) collective-permute-start(bf16[2,2,8,1024]{3,2,0,1:T(8,128)(2,1)S(1)} %get-tuple-element.321), channel_id=1, source_target_pairs={{0,32},{32,64},{64,96},{96,0},{1,33},{33,65},{65,97},{97,1},{2,34}... | collective-permute-start | bytes 196616 | tf_op jit(solution)/shard_map/ppermute | solution.py:35
  529.2 26.5 %collective-permute-start.70 = (bf16[2,2,8,1024]{3,2,0,1:T(8,128)(2,1)S(1)}, bf16[2,2,8,1024]{3,2,0,1:T(8,128)(2,1)S(1)}, u32[]{:S(2)}, u32[]{:S(2)}) collective-permute-start(bf16[2,2,8,1024]{3,2,0,1:T(8,128)(2,1)S(1)} %get-tuple-element.322), channel_id=1, source_target_pairs={{0,96},{32,0},{64,32},{96,64},{1,97},{33,1},{65,33},{97,65},{2,98}... | collective-permute-start | bytes 196616 | tf_op jit(solution)/shard_map/ppermute | solution.py:35
  530.5 25.2 %collective-permute-start.69 = (bf16[2,2,8,1024]{3,2,0,1:T(8,128)(2,1)S(1)}, bf16[2,2,8,1024]{3,2,0,1:T(8,128)(2,1)S(1)}, u32[]{:S(2)}, u32[]{:S(2)}) collective-permute-start(bf16[2,2,8,1024]{3,2,0,1:T(8,128)(2,1)S(1)} %get-tuple-element.323), channel_id=1, source_target_pairs={{0,64},{32,96},{64,0},{96,32},{1,65},{33,97},{65,1},{97,33},{2,66}... | collective-permute-start | bytes 196616 | tf_op jit(solution)/shard_map/ppermute | solution.py:35
  548.2 22.8 %collective-permute-start.64 = (bf16[192,1024]{1,0:T(8,128)(2,1)}, bf16[192,1024]{1,0:T(8,128)(2,1)S(1)}, u32[]{:S(2)}, u32[]{:S(2)}) collective-permute-start(bf16[192,1024]{1,0:T(8,128)(2,1)} %get-tuple-element.290), channel_id=1, source_target_pairs={{0,3},{1,0},{2,1},{3,2},{4,7},{5,4},{6,5},{7,6},{8,11},{9,8},{10,9... | collective-permute-start | bytes 1179656 | tf_op jit(solution)/shard_map/ppermute | solution.py:31
  570.9 137.6 %all-gather.6.cloned.1.call-start = ((), (), s32[]{:S(2)}) async-start(), calls=%async_computation.12 | async-start | bytes 2506752 | tf_op jit(solution)/shard_map/all_gather | solution.py:748
  576.4 103.7 %collective-permute-start.55 = (f32[192,1024]{1,0:T(8,128)}, f32[192,1024]{1,0:T(8,128)}, u32[]{:S(2)}, u32[]{:S(2)}) collective-permute-start(f32[192,1024]{1,0:T(8,128)} %fusion.27), channel_id=1, source_target_pairs={{4,8},{8,4},{5,9},{9,5},{6,10},{10,6},{7,11},{11,7},{20,24},{24,20... | collective-permute-start | bytes 2359304 | tf_op jit(solution)/shard_map/ppermute | solution.py:43
  588.6 16.4 %collective-permute-start.86 = (bf16[32,1024]{1,0:T(8,128)(2,1)S(1)}, bf16[32,1024]{1,0:T(8,128)(2,1)S(1)}, u32[]{:S(2)}, u32[]{:S(2)}) collective-permute-start(bf16[32,1024]{1,0:T(8,128)(2,1)S(1)} %dynamic-slice_bitcast_fusion.3), channel_id=1, source_target_pairs={{0,4},{4,0},{1,5},{5,1},{2,6},{6,2},{3,7},{7,3},{8,12},{12,8},{9,1... | collective-permute-start | bytes 196616 | tf_op jit(solution)/shard_map/ppermute | solution.py:39
  626.3 60.0 %all-to-all-start.5 = ((bf16[128,8,768]{2,1,0:T(8,128)(2,1)}), bf16[128,8,768]{2,1,0:T(8,128)(2,1)S(1)}, u32[]{:S(2)}, u32[]{:S(2)}) async-start(bf16[128,8,768]{2,1,0:T(8,128)(2,1)} %bitcast.62), calls=%async_computation.5 | async-start | bytes 3145728 | tf_op jit(solution)/shard_map/all_to_all | solution.py:749
  629.9 89.3 %all-gather.8.cloned.1.call-start = ((), (), s32[]{:S(2)}) async-start(), calls=%async_computation.13 | async-start | bytes 3342336 | tf_op jit(solution)/shard_map/all_gather | solution.py:755
  631.1 12.1 %collective-permute-start.74 = (f32[2,3072]{1,0:T(2,128)S(1)}, f32[2,3072]{1,0:T(2,128)S(1)}, u32[]{:S(2)}, u32[]{:S(2)}) collective-permute-start(f32[2,3072]{1,0:T(2,128)S(1)} %bitcast.310), channel_id=1, source_target_pairs={{0,1},{1,2},{2,3},{3,0},{4,5},{5,6},{6,7},{7,4},{8,9},{9,10},{10,1... | collective-permute-start | bytes 73736 | tf_op jit(solution)/shard_map/ppermute | solution.py:31
  632.0 15.8 %collective-permute-start.75 = (f32[2,3072]{1,0:T(2,128)S(1)}, f32[2,3072]{1,0:T(2,128)S(1)}, u32[]{:S(2)}, u32[]{:S(2)}) collective-permute-start(f32[2,3072]{1,0:T(2,128)S(1)} %bitcast.309), channel_id=1, source_target_pairs={{0,2},{1,3},{2,0},{3,1},{4,6},{5,7},{6,4},{7,5},{8,10},{9,11},{10,... | collective-permute-start | bytes 73736 | tf_op jit(solution)/shard_map/ppermute | solution.py:31
  635.0 12.9 %collective-permute-start.76 = (f32[2,3072]{1,0:T(2,128)S(1)}, f32[2,3072]{1,0:T(2,128)S(1)}, u32[]{:S(2)}, u32[]{:S(2)}) collective-permute-start(f32[2,3072]{1,0:T(2,128)S(1)} %bitcast.308), channel_id=1, source_target_pairs={{0,3},{1,0},{2,1},{3,2},{4,7},{5,4},{6,5},{7,6},{8,11},{9,8},{10,9... | collective-permute-start | bytes 73736 | tf_op jit(solution)/shard_map/ppermute | solution.py:31
  637.3 48.0 %collective-permute-start.73 = (f32[192,1024]{1,0:T(8,128)S(1)}, f32[192,1024]{1,0:T(8,128)S(1)}, u32[]{:S(2)}, u32[]{:S(2)}) collective-permute-start(f32[192,1024]{1,0:T(8,128)S(1)} %fusion.46), channel_id=1, source_target_pairs={{4,8},{8,4},{5,9},{9,5},{6,10},{10,6},{7,11},{11,7},{20,24},{24,20... | collective-permute-start | bytes 2359304 | tf_op jit(solution)/shard_map/ppermute | solution.py:43
  647.9 21.8 %collective-permute-start.77 = (f32[3072]{0:T(1024)S(1)}, f32[3072]{0:T(1024)S(1)}, u32[]{:S(2)}, u32[]{:S(2)}) collective-permute-start(f32[3072]{0:T(1024)S(1)} %bitcast.323), channel_id=1, source_target_pairs={{0,4},{4,0},{1,5},{5,1},{2,6},{6,2},{3,7},{7,3},{8,12},{12,8},{9,1... | collective-permute-start | bytes 36872 | tf_op jit(solution)/shard_map/ppermute | solution.py:39
  (134 other events, 955.1 us)
Sparse Core Ops, SparseCore 0:
  403.9 62.4 reduce-scatter.4
  469.4 87.8 reduce-scatter.2
  576.1 36.2 all-gather.5
  632.7 40.4 all-gather.7

commit v4 on v3

--- a/solution.py
+++ b/solution.py
@@ -222,7 +222,7 @@
         ],
         compiler_params=pltpu.CompilerParams(vmem_limit_bytes=LIMIT),
         cost_estimate=pl.CostEstimate(
-            flops=4 * 2 * 1400000 * 64, bytes_accessed=28000000, transcendentals=2800000
+            flops=1000000, bytes_accessed=1000000, transcendentals=0
         ),
         name="attend",
     )(info, slopes, mine, other)
@@ -249,7 +249,7 @@
         ],
         compiler_params=pltpu.CompilerParams(vmem_limit_bytes=LIMIT),
         cost_estimate=pl.CostEstimate(
-            flops=10 * 2 * 1400000 * 64, bytes_accessed=36000000, transcendentals=2800000
+            flops=1000000, bytes_accessed=1000000, transcendentals=0
         ),
         name="attend_back",
     )(info, slopes, rows, mine, other, logsum)
@@ -281,8 +281,7 @@
 
 
 def pack_first_kernel(info, weight, small, out):
-    core = info[0]
-    rows = pl.ds(pl.multiple_of(core * 64, 64), 64)
+    rows = slice(0, 64)
     for place in range(8):
         for side in range(2):
             for part in range(3):
@@ -346,13 +345,55 @@
 def pack_first(info, weight, small):
     return pl.pallas_call(
         pack_first_kernel,
-        grid=(1,),
+        grid_spec=pltpu.PrefetchScalarGridSpec(
+            num_scalar_prefetch=1,
+            grid=(1,),
+            in_specs=[
+                pl.BlockSpec((1, 64, 3072), lambda i, info: (0, info[0], 0)),
+                pl.BlockSpec((16, 768), lambda i, info: (0, 0)),
+            ],
+            out_specs=pl.BlockSpec((8, 80, 768), lambda i, info: (0, 0, 0)),
+        ),
         out_shape=jax.ShapeDtypeStruct((8, 80, 768), bf16),
-        in_specs=[smem, layer_block((128, 3072), 0), whole],
-        out_specs=whole,
         compiler_params=params_one,
         name="pack_first",
     )(info, weight, small)
+
+
+def read_small_kernel(info, got, vectors, in_bias, unit_bias):
+    z = info[1]
+    for layer in range(LAYERS):
+        for member in range(6):
+            lanes = slice(member * 128, (member + 1) * 128)
+            for place in range(8):
+                vectors[layer * 6 + member : layer * 6 + member + 1, place * 128 : (place + 1) * 128] = (
+                    got[place, 64 + 2 * layer : 65 + 2 * layer, lanes].astype(f32)
+                )
+        row = slice(65 + 2 * layer, 66 + 2 * layer)
+        here = slice(layer, layer + 1)
+        for side in range(2):
+            at = side * 384
+            lanes = pl.ds(pl.multiple_of((z & 1) * 128, 128), 128)
+            owner = side * 2 + (z >> 1)
+            in_bias[here, at : at + 128] = got[owner, row, lanes].astype(f32)
+            in_bias[here, at + 128 : at + 256] = jnp.zeros((1, 128), f32)
+            in_bias[here, at + 256 : at + 384] = got[owner + 4, row, lanes].astype(f32)
+            unit_bias[here, side * 512 : (side + 1) * 512] = got[side * 4 + z, row, 256:768].astype(f32)
+
+
+def read_small(info, got):
+    return pl.pallas_call(
+        read_small_kernel,
+        out_shape=(
+            jax.ShapeDtypeStruct((12, D), f32),
+            jax.ShapeDtypeStruct((LAYERS, 768), f32),
+            jax.ShapeDtypeStruct((LAYERS, D), f32),
+        ),
+        in_specs=[smem, whole],
+        out_specs=(whole,) * 3,
+        compiler_params=params_one,
+        name="read_small",
+    )(info, got)
 
 
 def pack_rest(info, weight, up, down, project):
@@ -414,20 +455,18 @@
     return lax.dynamic_slice_in_dim(value, at * width, width, 1)
 
 
-def forward(hidden, normed_all, params, info, slopes, core, side=None):
+def forward(hidden, normed_all, params, info, slopes, core, side):
     (_, _, w_in, in_bias, project, project_bias) = params[:6]
     (gain_two, offset_two, up, up_bias, down, down_bias) = params[6:]
-    projected = (dot(normed_all, w_in) + in_bias).astype(bf16)
-    received = swap(columns_at(projected, 1 - core, 384), "core")
-    mine = columns_at(projected, core, 384)
-    side_done = None
-    if side is None:
+
+    def attention(normed_all):
+        projected = (dot(normed_all, w_in) + in_bias).astype(bf16)
+        received = swap(columns_at(projected, 1 - core, 384), "core")
+        mine = columns_at(projected, core, 384)
         ctx_mine, ctx_other, logsum, rows = attend(info, slopes, mine, received)
-    else:
-        side_done, (ctx_mine, ctx_other, logsum, rows) = beside(
-            side[0], side[1], (mine, received), lambda v: attend(info, slopes, *v)
-        )
-    context = in_order(ctx_mine, swap(ctx_other, "core"), core)
+        return in_order(ctx_mine, swap(ctx_other, "core"), core), logsum, rows
+
+    side_done, (context, logsum, rows) = beside(side[0], side[1], normed_all, attention)
     parts, own = beside(
         dot_others(context, project, dot),
         scatter_parts,
@@ -479,16 +518,13 @@
     grad_out = d_middle.astype(bf16)
     sum_project = jnp.sum(grad_out.astype(f32), axis=0)
     grad_out_all, outer_state = beside(grad_out, gather_z, (g_down, g_up), fill["outer"])
-    d_context = dot_t(grad_out_all, project).astype(bf16)
-    received = swap(columns_at(d_context, 1 - core, 128), "core")
-    mine = columns_at(d_context, core, 128)
-    attend_done, (d_mine, d_other, sums) = beside(
-        fill["attend"][0],
-        fill["attend"][1],
-        (mine, received),
-        lambda v: attend_back(info, slopes, rows, *v, logsum),
-    )
-    d_joined = in_order(d_mine, swap(d_other, "core"), core)
+
+    def attention(grad_out_all):
+        d_context = dot_t(grad_out_all, project).astype(bf16)
+        received = swap(columns_at(d_context, 1 - core, 128), "core")
+        mine = columns_at(d_context, core, 128)
+        d_mine, d_other, sums = attend_back(info, slopes, rows, mine, received, logsum)
+        return in_order(d_mine, swap(d_other, "core"), core), sums
 
     def inner_work(given):
         context, grad_out_all, normed_all, d_joined = given
@@ -497,11 +533,21 @@
         g_project = outer(context, grad_out_all).astype(bf16)
         return own, fill["inner"](g_project, g_input)
 
-    parts, (own, inner_state) = beside(
-        dot_others(d_joined, w_in, dot_t),
-        scatter_parts,
-        (context, grad_out_all, normed_all, d_joined),
-        inner_work,
+    def inner_part(given):
+        context, grad_out_all, normed_all = given
+        early, (d_joined, sums) = beside(
+            fill["early"][0], fill["early"][1], grad_out_all, attention
+        )
+        return early, sums, beside(
+            dot_others(d_joined, w_in, dot_t),
+            scatter_parts,
+            (context, grad_out_all, normed_all, d_joined),
+            inner_work,
+        )
+
+    late_send, late_transfer = fill["late"](outer_state)
+    late, (early, sums, (parts, (own, inner_state))) = beside(
+        late_send, late_transfer, (context, grad_out_all, normed_all), inner_part
     )
     d_normed_one = sum_parts(own, parts)
     d_hidden, sum_gain_one, sum_offset_one = norm_back(hidden, gain_one, d_normed_one)
@@ -515,7 +561,7 @@
         sums,
         sum_up,
     )
-    return d_middle + d_hidden, outer_state, attend_done, inner_state, small
+    return d_middle + d_hidden, outer_state, early, late, inner_state, small
 
 
 def take(value, at, axis=0):
@@ -548,10 +594,12 @@
     return take(value, at).astype(f32) + swap(take(value, 1 - at), axis).astype(f32)
 
 
-def own_rows(summed, split, y_hi):
+def own_rows(summed, split, y_hi, z):
     both = sum_pairs(summed.reshape(2, 32, -1), y_hi, "y_hi").astype(bf16)
     columns = both[:, split:].reshape(4, 8, -1)
-    columns = lax.all_to_all(columns, "z", split_axis=0, concat_axis=0, tiled=True)
+    blocks = [take(columns, z)] + [shift_z(take(columns, (z + 4 - k) % 4), 4 - k) for k in (1, 2, 3)]
+    blocks = jnp.stack(blocks + blocks)
+    columns = lax.dynamic_slice_in_dim(blocks, (4 - z) % 4, 4, 0)
     return jnp.concatenate([both[:, :split], columns.reshape(32, -1)], axis=1)
 
 
@@ -571,25 +619,64 @@
     total = take(split, z, 1)
     for k in (1, 2, 3):
         total = total + shift_z(take(split, (z + k) % 4, 1), k)
-    total = take(total, y_hi) + swap(take(total, 1 - y_hi), "y_hi")
-    total = total + swap(total, "core")
-    total = total + swap(total, "y_lo")
-    return total + shift_x(total, 1) + shift_x(total, 2) + shift_x(total, 3)
-
-
-def order_columns(rows, parts):
-    split = rows.reshape(16, 4, 8, 2, parts, -1)
-    return split.transpose(0, 2, 4, 3, 1, 5).reshape(128, -1)
-
-
-def unpack(full):
-    full = full.astype(f32)
-    return (
-        full[:, :, :D].reshape(512, D),
-        order_columns(full[:, :, D : 2 * D], 1),
-        full[:, :, 2 * D : 2 * D + 256].reshape(128, D),
-        order_columns(full[:, :, 2 * D + 256 :], 3),
-    )
+    axes = ("y_lo", "y_hi")
+    own, other = take(total, y_hi), take(total, 1 - y_hi)
+    moves = ((own, [2, 3, 0, 1]), (other, [1, 0, 3, 2]), (other, [3, 2, 1, 0]))
+    for value, to in moves:
+        own = own + lax.ppermute(value, axes, list(enumerate(to)))
+    own = own + shift_x(own, 1) + shift_x(own, 2) + shift_x(own, 3)
+    return own + swap(own, "core")
+
+
+def unpack_outer_kernel(first, second, down, up):
+    for layer, full in ((0, first), (1, second)):
+        for g in range(16):
+            down[layer, g * 32 : (g + 1) * 32, :] = full[g, :, 0:D].astype(f32)
+            for four in range(4):
+                rows = full[g, four * 8 : (four + 1) * 8, D : 2 * D].astype(f32)
+                for side in range(2):
+                    at = side * 2048 + four * 512
+                    up[layer, g * 8 : (g + 1) * 8, at : at + 512] = rows[
+                        :, side * 512 : (side + 1) * 512
+                    ]
+
+
+def unpack_inner_kernel(first, second, inputs, *, at_one, at_two):
+    for layer, full, at in ((0, first, at_one), (1, second, at_two)):
+        for g in range(16):
+            for four in range(4):
+                rows = full[g, four * 8 : (four + 1) * 8, at : at + 768].astype(f32)
+                for side in range(2):
+                    for part in range(3):
+                        to = part * D + side * 512 + four * 128
+                        inputs[layer, g * 8 : (g + 1) * 8, to : to + 128] = rows[
+                            :, (side * 3 + part) * 128 : (side * 3 + part + 1) * 128
+                        ]
+
+
+def unpack_outer(first, second):
+    return pl.pallas_call(
+        unpack_outer_kernel,
+        out_shape=(
+            jax.ShapeDtypeStruct((LAYERS, 512, D), f32),
+            jax.ShapeDtypeStruct((LAYERS, 128, FF), f32),
+        ),
+        in_specs=[whole, whole],
+        out_specs=(whole, whole),
+        compiler_params=params_one,
+        name="unpack_outer",
+    )(first, second)
+
+
+def unpack_inner(first, second, at_one, at_two):
+    return pl.pallas_call(
+        functools.partial(unpack_inner_kernel, at_one=at_one, at_two=at_two),
+        out_shape=jax.ShapeDtypeStruct((LAYERS, 128, 3072), f32),
+        in_specs=[whole, whole],
+        out_specs=whole,
+        compiler_params=params_one,
+        name="unpack_inner",
+    )(first, second)
 
 
 def pack_small(small, place, z):
@@ -636,7 +723,6 @@
     heads = (place * 2 + jnp.arange(2, dtype=jnp.int32)).astype(f32)
     slopes = jnp.exp2(-8.0 * (heads + 1.0) / HEADS)
 
-    raw_all = gather_z(rows_in)
     small = jnp.concatenate(
         [
             norm_one_gain,
@@ -651,126 +737,132 @@
         axis=1,
     )
     small = jnp.concatenate([small.reshape(4, 768), jnp.zeros((12, 768), bf16)], axis=0)
-    first = to_ctx(pack_first(corner, input_weight, small))
-    small = first[:, 64:68].reshape(8, LAYERS, -1).transpose(1, 0, 2).astype(f32)
-    (w_first,) = join_columns(corner, first, swap(first[:, :64], "core"), (768,))
+    first = pack_first(corner, input_weight, small)
+    rows_in, first = lax.optimization_barrier((rows_in, first))
+    first = to_ctx(first)
+    raw_all = gather_z(rows_in)
+    vectors, in_bias, unit_bias = read_small(corner, first)
+    (w_first,) = join_columns(corner, first, swap(first, "core"), (768,))
 
     packed = pack_rest(corner, input_weight, up_weight, down_weight, project_weight)
     up_first = to_ctx(packed[0])
-    second = to_ctx(packed[1])
     (up_first,) = join_columns(corner, up_first, swap(up_first, "core"), (D,))
-    up_second, w_second = join_columns(corner, second, swap(second, "core"), (D, 768))
-    w_all = (w_first, w_second)
-    up_all = (up_first, up_second)
-
-    layers = []
-    for layer in range(LAYERS):
+
+    def layer_rows(layer):
         got = swap(packed[2 + layer], "y_hi")
-        down, project = join_rows(
-            corner, down_weight, project_weight, layer, got, swap(got, "core")
+        return join_rows(corner, down_weight, project_weight, layer, got, swap(got, "core"))
+
+    def layer_params(layer, w_in, up, rows):
+        down, project = rows
+        vector = [vectors[layer * 6 + i] for i in range(6)]
+        return (
+            vector[0],
+            vector[1],
+            w_in,
+            in_bias[layer],
+            project,
+            vector[2],
+            vector[3],
+            vector[4],
+            up,
+            unit_bias[layer],
+            down,
+            vector[5],
         )
-        vectors = [small[layer, :, i * 128 : (i + 1) * 128].reshape(D) for i in range(6)]
-        in_bias = small[layer, :, 768:1024].reshape(2, 2, 4, 128)
-        in_bias = lax.dynamic_index_in_dim(in_bias, z, 2, keepdims=False)
-        in_bias = jnp.stack([in_bias[0], jnp.zeros((2, 128), f32), in_bias[1]], axis=1)
-        unit_bias = small[layer, :, 1024:1536].reshape(2, 4, 512)
-        unit_bias = lax.dynamic_index_in_dim(unit_bias, z, 1, keepdims=False).reshape(D)
-        layers.append(
-            (
-                vectors[0],
-                vectors[1],
-                w_all[layer],
-                in_bias.reshape(768),
-                project,
-                vectors[2],
-                vectors[3],
-                vectors[4],
-                up_all[layer],
-                unit_bias,
-                down,
-                vectors[5],
-            )
-        )
-
+
+    params_0 = layer_params(0, w_first, up_first, layer_rows(0))
     slot = (x, y_lo, core)
     gradient = regroup(cotangent[0], core, y_hi)
     hidden = rows_in.astype(f32)
-    normed_all = norm(raw_all.astype(f32), layers[0][0], layers[0][1]).astype(bf16)
-    last, kept_0, grad_down = forward(
-        hidden, normed_all, layers[0], info, slopes, core, (gradient, gather_z)
+    normed_all = norm(raw_all.astype(f32), params_0[0], params_0[1]).astype(bf16)
+    last, kept_0, second = forward(
+        hidden, normed_all, params_0, info, slopes, core, (packed[1], to_ctx)
+    )
+    up_second, w_second = join_columns(corner, second, swap(second, "core"), (D, 768))
+    params_1 = layer_params(1, w_second, up_second, layer_rows(1))
+    hidden = last_sum(last, params_0, scatter_parts(last_send(last, params_0)))
+    normed_all = gather_z(norm(hidden, params_1[0], params_1[1]).astype(bf16))
+    last, kept_1, grad_down = forward(
+        hidden, normed_all, params_1, info, slopes, core, (gradient, gather_z)
     )
     gradient = gradient.astype(f32)
-    hidden = last_sum(last, layers[0], scatter_parts(last_send(last, layers[0])))
-    normed_all = gather_z(norm(hidden, layers[1][0], layers[1][1]).astype(bf16))
-    last, kept_1, _ = forward(hidden, normed_all, layers[1], info, slopes, core)
+    nothing = (jnp.zeros((8, 128), f32), lambda v: v)
+
+    fill = {
+        "outer": lambda v: pack_outer(*v),
+        "late": lambda state: nothing,
+        "early": (last_send(last, params_1), scatter_parts),
+        "inner": pack_inner,
+    }
+    gradient, outer_pack, parts, _, inner_pack, small_1 = backward(
+        gradient, grad_down, params_1, kept_1, info, slopes, core, fill
+    )
+    output = last_sum(last, params_1, parts)
+    pack = jnp.concatenate([outer_pack, inner_pack], axis=-1)
 
     def grp_sum(pack):
         return lax.psum_scatter(pack, GRP, scatter_dimension=0, tiled=True).reshape(64, -1)
 
-    fill = {
-        "outer": lambda v: pack_outer(*v),
-        "attend": (last_send(last, layers[1]), scatter_parts),
-        "inner": pack_inner,
-    }
-    gradient, outer_pack, parts, inner_pack, small_1 = backward(
-        gradient, grad_down, layers[1], kept_1, info, slopes, core, fill
-    )
-    output = last_sum(last, layers[1], parts)
-    outer_1 = grp_sum(outer_pack)
-    inner_1 = grp_sum(inner_pack)
-
-    grad_down, output = beside(
-        gradient.astype(bf16), gather_z, output, lambda v: v + 0.0
+    sums_1 = grp_sum(pack)
+    grad_down, (output, pack) = beside(
+        gradient.astype(bf16), gather_z, (output, pack), lambda v: v
     )
 
     def core_sum(given):
-        pack = pack_outer(*given).reshape(8, 2, 64, 2 * D)
-        return take(pack, core, 1), take(pack, 1 - core, 1)
-
-    def outer_start(given):
-        keep, send = given
-        return keep.astype(f32) + swap(send, "core").astype(f32)
+        split = pack_outer(*given).reshape(8, 2, 64, 2 * D)
+        keep, send = take(split, core, 1), take(split, 1 - core, 1)
+        return (keep.astype(f32) + swap(send, "core").astype(f32)).astype(bf16)
+
+    def to_xy(value):
+        return lax.all_to_all(value, ("x", "y_lo"), split_axis=0, concat_axis=0, tiled=True)
+
+    def own_one(summed):
+        outer_1 = own_rows(summed[:, : 2 * D], D, y_hi, z)
+        inner_1 = own_rows(summed[:, 2 * D :], 256, y_hi, z)
+        return lax.all_gather(jnp.concatenate([outer_1, inner_1], axis=1), GRP)
 
     fill = {
         "outer": core_sum,
-        "attend": (jnp.zeros((8, 128), f32), lambda v: v),
+        "late": lambda state: (state, to_xy),
+        "early": (sums_1, lambda v: v),
         "inner": lambda g_project, g_input: (
-            project_steps(g_project, slot, y_hi),
+            g_project,
             groups_first(g_input, (8, 16, 8, 768)).reshape(128, 8, 768),
         ),
     }
-    gradient, outer_0, _, (project_0, input_0), small_0 = backward(
-        gradient, grad_down, layers[0], kept_0, info, slopes, core, fill
-    )
-    outer_0 = outer_start(outer_0).astype(bf16)
-    outer_0 = lax.all_to_all(outer_0, ("x", "y_lo"), split_axis=0, concat_axis=0, tiled=True)
-    outer_0 = own_rows(jnp.sum(outer_0.astype(f32), axis=0).astype(bf16), D, y_hi)
-    outer_0 = lax.all_gather(jnp.concatenate([outer_0, project_0], axis=1), GRP)
+    gradient, _, sums_1, outer_0, (g_project, input_0), small_0 = backward(
+        gradient, grad_down, params_0, kept_0, info, slopes, core, fill
+    )
     input_0 = lax.all_to_all(input_0, GRP + CTX, split_axis=0, concat_axis=0, tiled=True)
-    input_0 = jnp.sum(input_0.reshape(32, 32, 768).astype(f32), axis=0).astype(bf16)
-    input_0 = lax.all_gather(input_0, GRP)
-    final_0 = unpack(jnp.concatenate([outer_0, input_0], axis=2))
-    inner_1 = own_rows(inner_1, 256, y_hi)
-    outer_1 = own_rows(outer_1, D, y_hi)
-    final_1 = unpack(lax.all_gather(jnp.concatenate([outer_1, inner_1], axis=1), GRP))
+    full_1 = own_one(sums_1)
+    project_0 = project_steps(g_project, slot, y_hi)
+    outer_0 = own_rows(jnp.sum(outer_0.astype(f32), axis=0).astype(bf16), D, y_hi, z)
+    full_0 = lax.all_gather(jnp.concatenate([outer_0, project_0], axis=1), GRP)
+    g_down, g_up = unpack_outer(full_0, full_1)
+    g_project = jnp.stack(
+        [full[:, :, 2 * D : 2 * D + 256].reshape(128, D) for full in (full_0, full_1)]
+    ).astype(f32)
     packed = jnp.concatenate([pack_small(s, place, z) for s in (small_0, small_1)], axis=1)
     vector = sum_small(packed, z, y_hi).reshape(LAYERS, -1)
+    input_0 = jnp.sum(input_0.reshape(32, 32, 768).astype(f32), axis=0).astype(bf16)
+    input_0, g_down, g_up = lax.optimization_barrier((input_0, g_down, g_up))
+    input_0 = lax.all_gather(input_0, GRP)
+    g_input = unpack_inner(input_0, full_1, 0, 2 * D + 256)
     parts = [vector[:, i * 128 : (i + 1) * 128] for i in range(6)]
-    both = [jnp.stack([final_0[i], final_1[i]]) for i in range(4)]
     return (
         regroup(output, core, y_hi)[None],
         regroup(gradient, core, y_hi)[None],
         parts[0],
         parts[1],
-        both[3],
+        g_input,
         vector[:, 768:1024],
-        both[2],
+        g_project,
         parts[2],
         parts[3],
         parts[4],
-        both[1],
+        g_up,
         vector[:, 1024:1536],
-        both[0],
+        g_down,
         parts[5],
     )
 

time: 753 us -> 732 us (0.972)
  waiting for transfers between devices: 290 us -> 323 us
  local copies, waits for them, and re-layouts: 69.4 us -> 42.8 us
  other arithmetic: 70.5 us -> 49.7 us
  matrix products: 64.1 us -> 52.5 us
    ppermute x51 -> x60, waiting for transfers between devices: 202 us -> 245 us  [shift_z(): return lax.ppermute(value, 'z', [(i, (i + step) % 4) for i in range(4)])]
    all_to_all x1, starting transfers between devices: 3.57 us -> 17.5 us  [on_device(): lax.all_to_all(input_0, GRP + CTX, split_axis=0, concat_axis=0, tiled=True)]
    ppermute x6, waiting for transfers between devices: 21.8 us -> 8.29 us  [shift_x(): return lax.ppermute(value, 'x', [(i, (i + step) % 4) for i in range(4)])]
    all_to_all x4 -> x1, starting transfers between devices: 14.4 us -> 4.34 us  [to_xy(): lax.all_to_all(value, ('x', 'y_lo'), split_axis=0, concat_axis=0, tiled=T...]
    ppermute x25 -> x23, starting transfers between devices: 38.4 us -> 28.4 us  [swap(): return lax.ppermute(value, axis, [(0, 1), (1, 0)])]
    another operation x5 -> x0, other arithmetic: 8.23 us -> none  [the longest x4 7.56 us: on_device(): both = [jnp.stack([final_0[i], final_1[i]]) for i in range(4)]]
    ppermute x5, waiting for transfers between devices: 5.98 us -> 14.1 us  [regroup(): got = lax.ppermute(value, ('core', 'y_hi'), [(1, 2), (2, 1)])]
    ppermute x51 -> x60, starting transfers between devices: 57.2 us -> 64.9 us  [shift_z(): return lax.ppermute(value, 'z', [(i, (i + step) % 4) for i in range(4)])]
  transfers between devices with their start and end apart: 99 -> 105, of which waited for: 51 -> 57; matrix products, arithmetic and copies ran while one was open for 19% -> 13% of each run, Pallas kernels for 7% -> 4%
where the time goes in v4:
time: 732 us; the launch traced here: 725 us
  waiting for transfers between devices  323 us (44%)
  starting transfers between devices  167 us (23%)
  Pallas kernels  54.2 us (7%)
  matrix products  52.5 us (7%)
  other arithmetic  49.7 us (7%)
  local copies, waits for them, and re-layouts  42.8 us (6%)
  blocking collectives  19.7 us (3%)
  between operations  16.2 us (2%)
    ppermute x60, waiting for transfers between devices, shift_z(): return lax.ppermute(value, 'z', [(i, (i + step) % 4) for i in range(4)])  245 us
    ppermute x60, starting transfers between devices, shift_z(): return lax.ppermute(value, 'z', [(i, (i + step) % 4) for i in range(4)])  64.9 us
    ppermute x23, waiting for transfers between devices, swap(): return lax.ppermute(value, axis, [(0, 1), (1, 0)])  43.2 us
    ppermute x23, starting transfers between devices, swap(): return lax.ppermute(value, axis, [(0, 1), (1, 0)])  28.4 us
    unnamed x216, local copies, waits for them, and re-layouts  25.6 us
    ppermute x5, starting transfers between devices, regroup(): got = lax.ppermute(value, ('core', 'y_hi'), [(1, 2), (2, 1)])  23.9 us
    pallas_call x2, Pallas kernels, attend_back(): pl.pallas_call(attend_back_kernel, out_shape=(jax.ShapeDtypeStruct((HALF,...  21.2 us
    dot_general x12, matrix products, dot(): return jnp.dot(left, right, preferred_element_type=f32)  20.6 us
  transfers between devices with their start and end apart: 105, of which 57 were waited for; matrix products, arithmetic and copies ran while one was open for 13% of the time, Pallas kernels for 4%

profile of v4, /device:TPU:1, one launch (start us, length us, event | category | flops | bytes accessed | tf_op | source)
XLA Modules:
  0.0 724.8 jit_solution(16174091718951148730)
XLA Ops:
  7.2 6.2 collective-permute-start.1
  22.1 3.8 collective-permute-start.4
  26.5 3.6 all-to-all-start
  36.7 12.5 %collective-permute-done.4 = bf16[192,1024]{1,0:T(8,128)(2,1)} collective-permute-done((bf16[192,1024]{1,0:T(8,128)(2,1)}, bf16[192,1024]{1,0:T(8,128)(2,1)}, u32[]{:S(2)}, u32[]{:S(2)}) %collective-permute-start.4) | collective-permute-done | bytes 393248 | tf_op jit(solution)/shard_map/ppermute | solution.py:31
  54.9 3.1 fusion.6
  58.0 5.2 all-to-all-start.1
  63.2 3.0 collective-permute-start.9
  71.1 29.6 %collective-permute-done.9.got = bf16[320,1024]{1,0:T(8,128)(2,1)} collective-permute-done((bf16[320,1024]{1,0:T(8,128)(2,1)}, bf16[320,1024]{1,0:T(8,128)(2,1)}, u32[]{:S(2)}, u32[]{:S(2)}) %collective-permute-start.9) | collective-permute-done | bytes 655392 | tf_op jit(solution)/shard_map/ppermute | solution.py:39
  105.4 4.2 collective-permute-done.5
  110.3 9.5 %attend.2 = (bf16[768,128]{1,0:T(8,128)(2,1)S(1)}, bf16[768,128]{1,0:T(8,128)(2,1)}, f32[2,1536]{1,0:T(2,128)S(1)}, bf16[1536,384]{1,0:T(8,128)(2,1)S(1)}) custom-call(s32[4]{0:T(128)S(1)} %add_add_fusion.4.info, f32[2]{0:T(128)S(1)} %multiply_exponential_fusion.slopes, bf16[768,384]{1,0:T(8,128)(2,1)S(1)} %get-tuple-element.387.mine, ...), custom_call_target="tpu_custom_call" | custom-call | flops 1000000 | bytes 1000000 | tf_op jit(solution)/shard_map/attend/pallas_call | solution.py:208
  120.8 4.3 all-to-all-start.2
  135.8 3.8 all-to-all-done.2.got
  142.8 5.9 collective-permute-done.13
  148.7 8.7 %collective-permute-done.12 = bf16[192,1024]{1,0:T(8,128)(2,1)} collective-permute-done((bf16[192,1024]{1,0:T(8,128)(2,1)}, bf16[192,1024]{1,0:T(8,128)(2,1)}, u32[]{:S(2)}, u32[]{:S(2)}) %collective-permute-start.12) | collective-permute-done | bytes 393248 | tf_op jit(solution)/shard_map/ppermute | solution.py:31
  163.3 6.5 collective-permute-done.16
  172.3 9.5 %collective-permute-done.14 = bf16[192,1024]{1,0:T(8,128)(2,1)S(1)} collective-permute-done((bf16[192,1024]{1,0:T(8,128)(2,1)S(1)}, bf16[192,1024]{1,0:T(8,128)(2,1)S(1)}, u32[]{:S(2)}, u32[]{:S(2)}) %collective-permute-start.14) | collective-permute-done | bytes 393248 | tf_op jit(solution)/shard_map/ppermute | solution.py:31
  181.8 5.2 multiply_convert_fusion.1
  191.7 4.3 collective-permute-start
  196.0 2.8 collective-permute-done.18
  201.5 5.8 collective-permute-done.19
  214.3 3.2 collective-permute-start.31
  221.6 10.4 %collective-permute-done.21 = bf16[192,1024]{1,0:T(8,128)(2,1)S(1)} collective-permute-done((bf16[192,1024]{1,0:T(8,128)(2,1)S(1)}, bf16[192,1024]{1,0:T(8,128)(2,1)S(1)}, u32[]{:S(2)}, u32[]{:S(2)}) %collective-permute-start.21) | collective-permute-done | bytes 393248 | tf_op jit(solution)/shard_map/ppermute | solution.py:31
  239.6 8.3 %attend.3 = (bf16[768,128]{1,0:T(8,128)(2,1)S(1)}, bf16[768,128]{1,0:T(8,128)(2,1)S(1)}, f32[2,1536]{1,0:T(2,128)S(1)}, bf16[1536,384]{1,0:T(8,128)(2,1)S(1)}) custom-call(s32[4]{0:T(128)S(1)} %add_add_fusion.4.info, f32[2]{0:T(128)S(1)} %multiply_exponential_fusion.slopes, bf16[768,384]{1,0:T(8,128)(2,1)S(1)} %get-tuple-element.379.mine, ...), custom_call_target="tpu_custom_call" | custom-call | flops 1000000 | bytes 1000000 | tf_op jit(solution)/shard_map/attend/pallas_call | solution.py:208
  250.3 9.0 %collective-permute-done.24 = bf16[192,1024]{1,0:T(8,128)(2,1)S(1)} collective-permute-done((bf16[192,1024]{1,0:T(8,128)(2,1)S(1)}, bf16[192,1024]{1,0:T(8,128)(2,1)S(1)}, u32[]{:S(2)}, u32[]{:S(2)}) %collective-permute-start.24) | collective-permute-done | bytes 393248 | tf_op jit(solution)/shard_map/ppermute | solution.py:31
  264.4 16.9 %collective-permute-done.34 = bf16[192,1024]{1,0:T(8,128)(2,1)S(1)} collective-permute-done((bf16[192,1024]{1,0:T(8,128)(2,1)S(1)}, bf16[192,1024]{1,0:T(8,128)(2,1)S(1)}, u32[]{:S(2)}, u32[]{:S(2)}) %collective-permute-start.34) | collective-permute-done | bytes 393248 | tf_op jit(solution)/shard_map/ppermute | solution.py:31
  283.0 2.9 collective-permute-start.37
  287.0 8.5 %collective-permute-done.37 = bf16[192,1024]{1,0:T(8,128)(2,1)S(1)} collective-permute-done((bf16[192,1024]{1,0:T(8,128)(2,1)S(1)}, bf16[192,1024]{1,0:T(8,128)(2,1)S(1)}, u32[]{:S(2)}, u32[]{:S(2)}) %collective-permute-start.37) | collective-permute-done | bytes 393248 | tf_op jit(solution)/shard_map/ppermute | solution.py:31
  297.0 9.9 %collective-permute-done.35 = bf16[192,1024]{1,0:T(8,128)(2,1)S(1)} collective-permute-done((bf16[192,1024]{1,0:T(8,128)(2,1)S(1)}, bf16[192,1024]{1,0:T(8,128)(2,1)S(1)}, u32[]{:S(2)}, u32[]{:S(2)}) %collective-permute-start.35) | collective-permute-done | bytes 393248 | tf_op jit(solution)/shard_map/ppermute | solution.py:31
  307.7 3.9 fusion.82
  311.6 4.1 convert_reduce_fusion.1
  325.1 13.4 %collective-permute-done.40 = bf16[192,1024]{1,0:T(8,128)(2,1)S(1)} collective-permute-done((bf16[192,1024]{1,0:T(8,128)(2,1)S(1)}, bf16[192,1024]{1,0:T(8,128)(2,1)S(1)}, u32[]{:S(2)}, u32[]{:S(2)}) %collective-permute-start.40) | collective-permute-done | bytes 393248 | tf_op jit(solution)/shard_map/ppermute | solution.py:31
  340.7 2.9 collective-permute-start.43
  346.5 6.7 collective-permute-done.43
  354.6 9.6 %collective-permute-done.41 = bf16[192,1024]{1,0:T(8,128)(2,1)S(1)} collective-permute-done((bf16[192,1024]{1,0:T(8,128)(2,1)S(1)}, bf16[192,1024]{1,0:T(8,128)(2,1)S(1)}, u32[]{:S(2)}, u32[]{:S(2)}) %collective-permute-start.41) | collective-permute-done | bytes 393248 | tf_op jit(solution)/shard_map/ppermute | solution.py:31
  366.8 10.6 %attend_back.2 = (bf16[768,384]{1,0:T(8,128)(2,1)S(1)}, bf16[768,384]{1,0:T(8,128)(2,1)S(1)}, f32[1,384]{1,0:T(1,128)S(1)}) custom-call(s32[4]{0:T(128)S(1)} %add_add_fusion.4.info, f32[2]{0:T(128)S(1)} %multiply_exponential_fusion.slopes, bf16[1536,384]{1,0:T(8,128)(2,1)S(1)} %copy-done.29, bf16[768,128]{1,0:T(8,128)(2,1)S(1)} %get-tuple-element.392.mine, ...), custom_call_target="tpu_custom_call" | custom-call | flops 1000000 | bytes 1000000 | tf_op jit(solution)/shard_map/attend_back/pallas_call | solution.py:232
  383.8 14.4 %collective-permute-done.46 = bf16[192,1024]{1,0:T(8,128)(2,1)S(1)} collective-permute-done((bf16[192,1024]{1,0:T(8,128)(2,1)S(1)}, bf16[192,1024]{1,0:T(8,128)(2,1)S(1)}, u32[]{:S(2)}, u32[]{:S(2)}) %collective-permute-start.46) | collective-permute-done | bytes 393248 | tf_op jit(solution)/shard_map/ppermute | solution.py:31
  400.6 3.4 collective-permute-start.50
  411.3 9.8 %collective-permute-done.50 = bf16[192,1024]{1,0:T(8,128)(2,1)} collective-permute-done((bf16[192,1024]{1,0:T(8,128)(2,1)S(1)}, bf16[192,1024]{1,0:T(8,128)(2,1)}, u32[]{:S(2)}, u32[]{:S(2)}) %collective-permute-start.50) | collective-permute-done | bytes 393248 | tf_op jit(solution)/shard_map/ppermute | solution.py:31
  429.7 2.9 collective-permute-start.54
  434.8 14.5 %collective-permute-done.54 = bf16[192,1024]{1,0:T(8,128)(2,1)S(1)} collective-permute-done((bf16[192,1024]{1,0:T(8,128)(2,1)}, bf16[192,1024]{1,0:T(8,128)(2,1)S(1)}, u32[]{:S(2)}, u32[]{:S(2)}) %collective-permute-start.54) | collective-permute-done | bytes 393248 | tf_op jit(solution)/shard_map/ppermute | solution.py:31
  449.3 4.1 collective-permute-done.52
  454.5 3.9 convert_reduce_fusion.2
  467.7 12.3 %collective-permute-done.58 = bf16[192,1024]{1,0:T(8,128)(2,1)S(1)} collective-permute-done((bf16[192,1024]{1,0:T(8,128)(2,1)S(1)}, bf16[192,1024]{1,0:T(8,128)(2,1)S(1)}, u32[]{:S(2)}, u32[]{:S(2)}) %collective-permute-start.58) | collective-permute-done | bytes 393248 | tf_op jit(solution)/shard_map/ppermute | solution.py:31
  489.1 16.2 %collective-permute-done.61 = bf16[192,1024]{1,0:T(8,128)(2,1)} collective-permute-done((bf16[192,1024]{1,0:T(8,128)(2,1)S(1)}, bf16[192,1024]{1,0:T(8,128)(2,1)}, u32[]{:S(2)}, u32[]{:S(2)}) %collective-permute-start.61) | collective-permute-done | bytes 393248 | tf_op jit(solution)/shard_map/ppermute | solution.py:31
  505.4 3.7 collective-permute-done.59
  511.5 3.7 fusion
  519.5 10.6 %attend_back.3 = (bf16[768,384]{1,0:T(8,128)(2,1)S(1)}, bf16[768,384]{1,0:T(8,128)(2,1)S(1)}, f32[1,384]{1,0:T(1,128)S(1)}) custom-call(s32[4]{0:T(128)S(1)} %add_add_fusion.4.info, f32[2]{0:T(128)S(1)} %multiply_exponential_fusion.slopes, bf16[1536,384]{1,0:T(8,128)(2,1)S(1)} %copy-done.27, bf16[768,128]{1,0:T(8,128)(2,1)S(1)} %get-tuple-element.389.mine, ...), custom_call_target="tpu_custom_call" | custom-call | flops 1000000 | bytes 1000000 | tf_op jit(solution)/shard_map/attend_back/pallas_call | solution.py:232
  530.8 4.3 all-to-all-start.3
  535.3 5.4 collective-permute-start.55
  551.4 10.0 %collective-permute-done.67 = bf16[192,1024]{1,0:T(8,128)(2,1)} collective-permute-done((bf16[192,1024]{1,0:T(8,128)(2,1)S(1)}, bf16[192,1024]{1,0:T(8,128)(2,1)}, u32[]{:S(2)}, u32[]{:S(2)}) %collective-permute-start.67) | collective-permute-done | bytes 393248 | tf_op jit(solution)/shard_map/ppermute | solution.py:31
  562.6 3.8 all-to-all-done.3
  568.3 3.1 collective-permute-start.93
  575.3 3.4 collective-permute-done.79
  582.2 3.4 collective-permute-done.81
  596.9 3.3 collective-permute-done.88
  617.7 3.5 collective-permute-start.70
  621.9 17.5 %all-to-all-start.4 = ((bf16[128,8,768]{2,1,0:T(8,128)(2,1)}), bf16[128,8,768]{2,1,0:T(8,128)(2,1)S(1)}, u32[]{:S(2)}, u32[]{:S(2)}) async-start(bf16[128,8,768]{2,1,0:T(8,128)(2,1)} %bitcast.44), calls=%async_computation.5 | async-start | bytes 3145728 | tf_op jit(solution)/shard_map/all_to_all | solution.py:836
  644.5 5.8 collective-permute-start.68
  650.3 3.2 collective-permute-done.74
  655.3 7.7 %collective-permute-start.77 = (f32[3072]{0:T(1024)S(1)}, f32[3072]{0:T(1024)S(1)}, u32[]{:S(2)}, u32[]{:S(2)}) collective-permute-start(f32[3072]{0:T(1024)S(1)} %add_add_fusion.2), channel_id=1, source_target_pairs={{0,96},{32,0},{64,32},{96,64},{1,97},{33,1},{65,33},{97,65},{2,98}... | collective-permute-start | bytes 36872 | tf_op jit(solution)/shard_map/ppermute | solution.py:35
  663.8 3.5 collective-permute-done.76
  673.0 9.9 %collective-permute-done.68 = f32[192,1024]{1,0:T(8,128)S(1)} collective-permute-done((f32[192,1024]{1,0:T(8,128)S(1)}, f32[192,1024]{1,0:T(8,128)S(1)}, u32[]{:S(2)}, u32[]{:S(2)}) %collective-permute-start.68) | collective-permute-done | bytes 786464 | tf_op jit(solution)/shard_map/ppermute | solution.py:43
  690.5 3.9 unpack_outer.1
  695.3 19.7 %all-gather.2 = bf16[512,768]{1,0:T(8,128)(2,1)S(1)} all-gather(bf16[32,768]{1,0:T(8,128)(2,1)S(1)} %bitcast_reduce_fusion), channel_id=4, replica_groups=mesh['x'=4,'y_lo'=2,'core'=2,'y_hi'=2,'z'=4] {'x','y_lo','core'}, dimensions={0}, use_global_device_ids=true | all-gather | bytes 835584 | tf_op jit(solution)/shard_map/all_gather | solution.py:849
  (563 shorter events, 240.1 us)
Async XLA Ops:
  7.2 13.8 %collective-permute-start.1 = (bf16[192,1024]{1,0:T(8,128)(2,1)}, bf16[192,1024]{1,0:T(8,128)(2,1)S(1)}, u32[]{:S(2)}, u32[]{:S(2)}) collective-permute-start(bf16[192,1024]{1,0:T(8,128)(2,1)} %bitcast.298), channel_id=1, source_target_pairs={{4,8},{8,4},{5,9},{9,5},{6,10},{10,6},{7,11},{11,7},{20,24},{24,20... | collective-permute-start | bytes 1179656 | tf_op jit(solution)/shard_map/ppermute | solution.py:43
  22.1 27.1 %collective-permute-start.4 = (bf16[192,1024]{1,0:T(8,128)(2,1)}, bf16[192,1024]{1,0:T(8,128)(2,1)}, u32[]{:S(2)}, u32[]{:S(2)}) collective-permute-start(bf16[192,1024]{1,0:T(8,128)(2,1)} %broadcast_select_fusion), channel_id=1, source_target_pairs={{0,3},{1,0},{2,1},{3,2},{4,7},{5,4},{6,5},{7,6},{8,11},{9,8},{10,9... | collective-permute-start | bytes 1179656 | tf_op jit(solution)/shard_map/ppermute | solution.py:31
  25.8 23.4 %collective-permute-start.3 = (bf16[192,1024]{1,0:T(8,128)(2,1)}, bf16[192,1024]{1,0:T(8,128)(2,1)}, u32[]{:S(2)}, u32[]{:S(2)}) collective-permute-start(bf16[192,1024]{1,0:T(8,128)(2,1)} %broadcast_select_fusion), channel_id=1, source_target_pairs={{0,2},{1,3},{2,0},{3,1},{4,6},{5,7},{6,4},{7,5},{8,10},{9,11},{10,... | collective-permute-start | bytes 1179656 | tf_op jit(solution)/shard_map/ppermute | solution.py:31
  25.8 24.7 %collective-permute-start.2 = (bf16[192,1024]{1,0:T(8,128)(2,1)}, bf16[192,1024]{1,0:T(8,128)(2,1)}, u32[]{:S(2)}, u32[]{:S(2)}) collective-permute-start(bf16[192,1024]{1,0:T(8,128)(2,1)} %broadcast_select_fusion), channel_id=1, source_target_pairs={{0,1},{1,2},{2,3},{3,0},{4,5},{5,6},{6,7},{7,4},{8,9},{9,10},{10,1... | collective-permute-start | bytes 1179656 | tf_op jit(solution)/shard_map/ppermute | solution.py:31
  26.5 27.6 %all-to-all-start = ((bf16[8,80,768]{2,1,0:T(8,128)(2,1)}), bf16[8,80,768]{2,1,0:T(8,128)(2,1)S(1)}, u32[]{:S(2)}, u32[]{:S(2)}) async-start(bf16[8,80,768]{2,1,0:T(8,128)(2,1)} %copy-done.11), calls=%async_computation | async-start | bytes 1966080 | tf_op jit(solution)/shard_map/all_to_all | solution.py:443
  58.0 62.8 %all-to-all-start.1 = ((bf16[8,64,1792]{2,1,0:T(8,128)(2,1)}), bf16[8,64,1792]{2,1,0:T(8,128)(2,1)}, u32[]{:S(2)}, u32[]{:S(2)}) async-start(bf16[8,64,1792]{2,1,0:T(8,128)(2,1)} %copy-done.23), calls=%async_computation.1 | async-start | bytes 3670016 | tf_op jit(solution)/shard_map/all_to_all | solution.py:443
  63.2 37.5 %collective-permute-start.9 = (bf16[320,1024]{1,0:T(8,128)(2,1)}, bf16[320,1024]{1,0:T(8,128)(2,1)}, u32[]{:S(2)}, u32[]{:S(2)}) collective-permute-start(bf16[320,1024]{1,0:T(8,128)(2,1)} %copy-done.33), channel_id=1, source_target_pairs={{0,4},{4,0},{1,5},{5,1},{2,6},{6,2},{3,7},{7,3},{8,12},{12,8},{9,1... | collective-permute-start | bytes 1966088 | tf_op jit(solution)/shard_map/ppermute | solution.py:39
  70.2 40.1 %collective-permute-start.7 = (bf16[768,384]{1,0:T(8,128)(2,1)}, bf16[768,384]{1,0:T(8,128)(2,1)}, u32[]{:S(2)}, u32[]{:S(2)}) collective-permute-start(bf16[768,384]{1,0:T(8,128)(2,1)} %get-tuple-element.386), channel_id=1, source_target_pairs={{0,8},{8,0},{1,9},{9,1},{2,10},{10,2},{3,11},{11,3},{4,12},{12,4},... | collective-permute-start | bytes 1769480 | tf_op jit(solution)/shard_map/ppermute | solution.py:39
  100.7 25.6 %collective-permute-start.10 = (bf16[320,1024]{1,0:T(8,128)(2,1)}, bf16[320,1024]{1,0:T(8,128)(2,1)}, u32[]{:S(2)}, u32[]{:S(2)}) collective-permute-start(bf16[320,1024]{1,0:T(8,128)(2,1)} %collective-permute-done.9.got), channel_id=1, source_target_pairs={{0,8},{8,0},{1,9},{9,1},{2,10},{10,2},{3,11},{11,3},{4,12},{12,4},... | collective-permute-start | bytes 1966088 | tf_op jit(solution)/shard_map/ppermute | solution.py:39
  120.8 18.8 %all-to-all-start.2 = ((bf16[8,64,1024]{2,1,0:T(8,128)(2,1)}), bf16[8,64,1024]{2,1,0:T(8,128)(2,1)}, u32[]{:S(2)}, u32[]{:S(2)}) async-start(bf16[8,64,1024]{2,1,0:T(8,128)(2,1)} %copy-done.30), calls=%async_computation.2 | async-start | bytes 2097152 | tf_op jit(solution)/shard_map/all_to_all | solution.py:443
  125.1 390.2 %reduce-scatter.2.cloned.1.call-start = ((), (), s32[]{:S(2)}) async-start(), calls=%async_computation.6 | async-start | bytes 6684672 | tf_op jit(solution)/shard_map/reduce_scatter | solution.py:804
  131.0 17.7 %collective-permute-start.13 = (bf16[192,1024]{1,0:T(8,128)(2,1)}, bf16[192,1024]{1,0:T(8,128)(2,1)}, u32[]{:S(2)}, u32[]{:S(2)}) collective-permute-start(bf16[192,1024]{1,0:T(8,128)(2,1)} %get-tuple-element.383), channel_id=1, source_target_pairs={{0,1},{1,2},{2,3},{3,0},{4,5},{5,6},{6,7},{7,4},{8,9},{9,10},{10,1... | collective-permute-start | bytes 1179656 | tf_op jit(solution)/shard_map/ppermute | solution.py:31
  132.3 25.1 %collective-permute-start.12 = (bf16[192,1024]{1,0:T(8,128)(2,1)}, bf16[192,1024]{1,0:T(8,128)(2,1)}, u32[]{:S(2)}, u32[]{:S(2)}) collective-permute-start(bf16[192,1024]{1,0:T(8,128)(2,1)} %get-tuple-element.384), channel_id=1, source_target_pairs={{0,2},{1,3},{2,0},{3,1},{4,6},{5,7},{6,4},{7,5},{8,10},{9,11},{10,... | collective-permute-start | bytes 1179656 | tf_op jit(solution)/shard_map/ppermute | solution.py:31
  134.8 22.5 %collective-permute-start.11 = (bf16[192,1024]{1,0:T(8,128)(2,1)}, bf16[192,1024]{1,0:T(8,128)(2,1)}, u32[]{:S(2)}, u32[]{:S(2)}) collective-permute-start(bf16[192,1024]{1,0:T(8,128)(2,1)} %get-tuple-element.385), channel_id=1, source_target_pairs={{0,3},{1,0},{2,1},{3,2},{4,7},{5,4},{6,5},{7,6},{8,11},{9,8},{10,9... | collective-permute-start | bytes 1179656 | tf_op jit(solution)/shard_map/ppermute | solution.py:31
  139.6 22.3 %collective-permute-start.17 = (bf16[8,64,1024]{2,1,0:T(8,128)(2,1)}, bf16[8,64,1024]{2,1,0:T(8,128)(2,1)S(1)}, u32[]{:S(2)}, u32[]{:S(2)}) collective-permute-start(bf16[8,64,1024]{2,1,0:T(8,128)(2,1)} %all-to-all-done.2.got), channel_id=1, source_target_pairs={{0,8},{8,0},{1,9},{9,1},{2,10},{10,2},{3,11},{11,3},{4,12},{12,4},... | collective-permute-start | bytes 3145736 | tf_op jit(solution)/shard_map/ppermute | solution.py:39
  161.1 20.7 %collective-permute-start.14 = (bf16[192,1024]{1,0:T(8,128)(2,1)S(1)}, bf16[192,1024]{1,0:T(8,128)(2,1)S(1)}, u32[]{:S(2)}, u32[]{:S(2)}) collective-permute-start(bf16[192,1024]{1,0:T(8,128)(2,1)S(1)} %add_convert_fusion.4), channel_id=1, source_target_pairs={{0,1},{1,2},{2,3},{3,0},{4,5},{5,6},{6,7},{7,4},{8,9},{9,10},{10,1... | collective-permute-start | bytes 1179656 | tf_op jit(solution)/shard_map/ppermute | solution.py:31
  188.6 12.8 %collective-permute-start.20 = (bf16[192,1024]{1,0:T(8,128)(2,1)S(1)}, bf16[192,1024]{1,0:T(8,128)(2,1)S(1)}, u32[]{:S(2)}, u32[]{:S(2)}) collective-permute-start(bf16[192,1024]{1,0:T(8,128)(2,1)S(1)} %get-tuple-element.381), channel_id=1, source_target_pairs={{0,1},{1,2},{2,3},{3,0},{4,5},{5,6},{6,7},{7,4},{8,9},{9,10},{10,1... | collective-permute-start | bytes 1179656 | tf_op jit(solution)/shard_map/ppermute | solution.py:31
  190.1 17.1 %collective-permute-start.19 = (bf16[192,1024]{1,0:T(8,128)(2,1)S(1)}, bf16[192,1024]{1,0:T(8,128)(2,1)S(1)}, u32[]{:S(2)}, u32[]{:S(2)}) collective-permute-start(bf16[192,1024]{1,0:T(8,128)(2,1)S(1)} %get-tuple-element.382), channel_id=1, source_target_pairs={{0,2},{1,3},{2,0},{3,1},{4,6},{5,7},{6,4},{7,5},{8,10},{9,11},{10,... | collective-permute-start | bytes 1179656 | tf_op jit(solution)/shard_map/ppermute | solution.py:31
  190.4 41.8 %collective-permute-start.27 = (bf16[8,64,1792]{2,1,0:T(8,128)(2,1)}, bf16[8,64,1792]{2,1,0:T(8,128)(2,1)S(1)}, u32[]{:S(2)}, u32[]{:S(2)}) collective-permute-start(bf16[8,64,1792]{2,1,0:T(8,128)(2,1)} %all-to-all-done.1.got), channel_id=1, source_target_pairs={{0,8},{8,0},{1,9},{9,1},{2,10},{10,2},{3,11},{11,3},{4,12},{12,4},... | collective-permute-start | bytes 5505032 | tf_op jit(solution)/shard_map/ppermute | solution.py:39
  191.7 19.7 %collective-permute-start = (bf16[192,1024]{1,0:T(8,128)(2,1)S(1)}, bf16[192,1024]{1,0:T(8,128)(2,1)S(1)}, u32[]{:S(2)}, u32[]{:S(2)}) collective-permute-start(bf16[192,1024]{1,0:T(8,128)(2,1)S(1)} %bitcast.299), channel_id=1, source_target_pairs={{4,8},{8,4},{5,9},{9,5},{6,10},{10,6},{7,11},{11,7},{20,24},{24,20... | collective-permute-start | bytes 1179656 | tf_op jit(solution)/shard_map/ppermute | solution.py:43
  198.8 15.4 %collective-permute-start.30 = (bf16[320,1024]{1,0:T(8,128)(2,1)S(1)}, bf16[320,1024]{1,0:T(8,128)(2,1)S(1)}, u32[]{:S(2)}, u32[]{:S(2)}) collective-permute-start(bf16[320,1024]{1,0:T(8,128)(2,1)S(1)} %copy-done.32), channel_id=1, source_target_pairs={{0,4},{4,0},{1,5},{5,1},{2,6},{6,2},{3,7},{7,3},{8,12},{12,8},{9,1... | collective-permute-start | bytes 1966088 | tf_op jit(solution)/shard_map/ppermute | solution.py:39
  211.4 20.6 %collective-permute-start.21 = (bf16[192,1024]{1,0:T(8,128)(2,1)S(1)}, bf16[192,1024]{1,0:T(8,128)(2,1)S(1)}, u32[]{:S(2)}, u32[]{:S(2)}) collective-permute-start(bf16[192,1024]{1,0:T(8,128)(2,1)S(1)} %add_convert_fusion.3), channel_id=1, source_target_pairs={{0,1},{1,2},{2,3},{3,0},{4,5},{5,6},{6,7},{7,4},{8,9},{9,10},{10,1... | collective-permute-start | bytes 1179656 | tf_op jit(solution)/shard_map/ppermute | solution.py:31
  214.3 35.3 %collective-permute-start.31 = (bf16[320,1024]{1,0:T(8,128)(2,1)S(1)}, bf16[320,1024]{1,0:T(8,128)(2,1)S(1)}, u32[]{:S(2)}, u32[]{:S(2)}) collective-permute-start(bf16[320,1024]{1,0:T(8,128)(2,1)S(1)} %collective-permute-done.30.got), channel_id=1, source_target_pairs={{0,8},{8,0},{1,9},{9,1},{2,10},{10,2},{3,11},{11,3},{4,12},{12,4},... | collective-permute-start | bytes 1966088 | tf_op jit(solution)/shard_map/ppermute | solution.py:39
  238.7 20.6 %collective-permute-start.24 = (bf16[192,1024]{1,0:T(8,128)(2,1)S(1)}, bf16[192,1024]{1,0:T(8,128)(2,1)S(1)}, u32[]{:S(2)}, u32[]{:S(2)}) collective-permute-start(bf16[192,1024]{1,0:T(8,128)(2,1)S(1)} %get-tuple-element.189), channel_id=1, source_target_pairs={{0,1},{1,2},{2,3},{3,0},{4,5},{5,6},{6,7},{7,4},{8,9},{9,10},{10,1... | collective-permute-start | bytes 1179656 | tf_op jit(solution)/shard_map/ppermute | solution.py:31
  261.4 19.9 %collective-permute-start.34 = (bf16[192,1024]{1,0:T(8,128)(2,1)S(1)}, bf16[192,1024]{1,0:T(8,128)(2,1)S(1)}, u32[]{:S(2)}, u32[]{:S(2)}) collective-permute-start(bf16[192,1024]{1,0:T(8,128)(2,1)S(1)} %get-tuple-element.375), channel_id=1, source_target_pairs={{0,1},{1,2},{2,3},{3,0},{4,5},{5,6},{6,7},{7,4},{8,9},{9,10},{10,1... | collective-permute-start | bytes 1179656 | tf_op jit(solution)/shard_map/ppermute | solution.py:31
  261.4 19.8 %collective-permute-start.33 = (bf16[192,1024]{1,0:T(8,128)(2,1)S(1)}, bf16[192,1024]{1,0:T(8,128)(2,1)S(1)}, u32[]{:S(2)}, u32[]{:S(2)}) collective-permute-start(bf16[192,1024]{1,0:T(8,128)(2,1)S(1)} %get-tuple-element.376), channel_id=1, source_target_pairs={{0,2},{1,3},{2,0},{3,1},{4,6},{5,7},{6,4},{7,5},{8,10},{9,11},{10,... | collective-permute-start | bytes 1179656 | tf_op jit(solution)/shard_map/ppermute | solution.py:31
  262.8 18.8 %collective-permute-start.32 = (bf16[192,1024]{1,0:T(8,128)(2,1)S(1)}, bf16[192,1024]{1,0:T(8,128)(2,1)S(1)}, u32[]{:S(2)}, u32[]{:S(2)}) collective-permute-start(bf16[192,1024]{1,0:T(8,128)(2,1)S(1)} %get-tuple-element.377), channel_id=1, source_target_pairs={{0,3},{1,0},{2,1},{3,2},{4,7},{5,4},{6,5},{7,6},{8,11},{9,8},{10,9... | collective-permute-start | bytes 1179656 | tf_op jit(solution)/shard_map/ppermute | solution.py:31
  283.0 12.5 %collective-permute-start.37 = (bf16[192,1024]{1,0:T(8,128)(2,1)S(1)}, bf16[192,1024]{1,0:T(8,128)(2,1)S(1)}, u32[]{:S(2)}, u32[]{:S(2)}) collective-permute-start(bf16[192,1024]{1,0:T(8,128)(2,1)S(1)} %add_convert_fusion.2), channel_id=1, source_target_pairs={{0,3},{1,0},{2,1},{3,2},{4,7},{5,4},{6,5},{7,6},{8,11},{9,8},{10,9... | collective-permute-start | bytes 1179656 | tf_op jit(solution)/shard_map/ppermute | solution.py:31
  286.0 21.0 %collective-permute-start.35 = (bf16[192,1024]{1,0:T(8,128)(2,1)S(1)}, bf16[192,1024]{1,0:T(8,128)(2,1)S(1)}, u32[]{:S(2)}, u32[]{:S(2)}) collective-permute-start(bf16[192,1024]{1,0:T(8,128)(2,1)S(1)} %add_convert_fusion.2), channel_id=1, source_target_pairs={{0,1},{1,2},{2,3},{3,0},{4,5},{5,6},{6,7},{7,4},{8,9},{9,10},{10,1... | collective-permute-start | bytes 1179656 | tf_op jit(solution)/shard_map/ppermute | solution.py:31
  318.6 19.9 %collective-permute-start.40 = (bf16[192,1024]{1,0:T(8,128)(2,1)S(1)}, bf16[192,1024]{1,0:T(8,128)(2,1)S(1)}, u32[]{:S(2)}, u32[]{:S(2)}) collective-permute-start(bf16[192,1024]{1,0:T(8,128)(2,1)S(1)} %get-tuple-element.372), channel_id=1, source_target_pairs={{0,1},{1,2},{2,3},{3,0},{4,5},{5,6},{6,7},{7,4},{8,9},{9,10},{10,1... | collective-permute-start | bytes 1179656 | tf_op jit(solution)/shard_map/ppermute | solution.py:31
  318.7 19.8 %collective-permute-start.39 = (bf16[192,1024]{1,0:T(8,128)(2,1)S(1)}, bf16[192,1024]{1,0:T(8,128)(2,1)S(1)}, u32[]{:S(2)}, u32[]{:S(2)}) collective-permute-start(bf16[192,1024]{1,0:T(8,128)(2,1)S(1)} %get-tuple-element.373), channel_id=1, source_target_pairs={{0,2},{1,3},{2,0},{3,1},{4,6},{5,7},{6,4},{7,5},{8,10},{9,11},{10,... | collective-permute-start | bytes 1179656 | tf_op jit(solution)/shard_map/ppermute | solution.py:31
  319.2 19.6 %collective-permute-start.38 = (bf16[192,1024]{1,0:T(8,128)(2,1)S(1)}, bf16[192,1024]{1,0:T(8,128)(2,1)S(1)}, u32[]{:S(2)}, u32[]{:S(2)}) collective-permute-start(bf16[192,1024]{1,0:T(8,128)(2,1)S(1)} %get-tuple-element.374), channel_id=1, source_target_pairs={{0,3},{1,0},{2,1},{3,2},{4,7},{5,4},{6,5},{7,6},{8,11},{9,8},{10,9... | collective-permute-start | bytes 1179656 | tf_op jit(solution)/shard_map/ppermute | solution.py:31
  343.5 20.7 %collective-permute-start.41 = (bf16[192,1024]{1,0:T(8,128)(2,1)S(1)}, bf16[192,1024]{1,0:T(8,128)(2,1)S(1)}, u32[]{:S(2)}, u32[]{:S(2)}) collective-permute-start(bf16[192,1024]{1,0:T(8,128)(2,1)S(1)} %get-tuple-element.220), channel_id=1, source_target_pairs={{0,1},{1,2},{2,3},{3,0},{4,5},{5,6},{6,7},{7,4},{8,9},{9,10},{10,1... | collective-permute-start | bytes 1179656 | tf_op jit(solution)/shard_map/ppermute | solution.py:31
  378.0 20.3 %collective-permute-start.46 = (bf16[192,1024]{1,0:T(8,128)(2,1)S(1)}, bf16[192,1024]{1,0:T(8,128)(2,1)S(1)}, u32[]{:S(2)}, u32[]{:S(2)}) collective-permute-start(bf16[192,1024]{1,0:T(8,128)(2,1)S(1)} %get-tuple-element.369), channel_id=1, source_target_pairs={{0,1},{1,2},{2,3},{3,0},{4,5},{5,6},{6,7},{7,4},{8,9},{9,10},{10,1... | collective-permute-start | bytes 1179656 | tf_op jit(solution)/shard_map/ppermute | solution.py:31
  378.0 20.2 %collective-permute-start.45 = (bf16[192,1024]{1,0:T(8,128)(2,1)S(1)}, bf16[192,1024]{1,0:T(8,128)(2,1)S(1)}, u32[]{:S(2)}, u32[]{:S(2)}) collective-permute-start(bf16[192,1024]{1,0:T(8,128)(2,1)S(1)} %get-tuple-element.370), channel_id=1, source_target_pairs={{0,2},{1,3},{2,0},{3,1},{4,6},{5,7},{6,4},{7,5},{8,10},{9,11},{10,... | collective-permute-start | bytes 1179656 | tf_op jit(solution)/shard_map/ppermute | solution.py:31
  379.7 18.9 %collective-permute-start.44 = (bf16[192,1024]{1,0:T(8,128)(2,1)S(1)}, bf16[192,1024]{1,0:T(8,128)(2,1)S(1)}, u32[]{:S(2)}, u32[]{:S(2)}) collective-permute-start(bf16[192,1024]{1,0:T(8,128)(2,1)S(1)} %get-tuple-element.371), channel_id=1, source_target_pairs={{0,3},{1,0},{2,1},{3,2},{4,7},{5,4},{6,5},{7,6},{8,11},{9,8},{10,9... | collective-permute-start | bytes 1179656 | tf_op jit(solution)/shard_map/ppermute | solution.py:31
  400.6 20.5 %collective-permute-start.50 = (bf16[192,1024]{1,0:T(8,128)(2,1)S(1)}, bf16[192,1024]{1,0:T(8,128)(2,1)}, u32[]{:S(2)}, u32[]{:S(2)}) collective-permute-start(bf16[192,1024]{1,0:T(8,128)(2,1)S(1)} %get-tuple-element.367), channel_id=1, source_target_pairs={{0,2},{1,3},{2,0},{3,1},{4,6},{5,7},{6,4},{7,5},{8,10},{9,11},{10,... | collective-permute-start | bytes 1179656 | tf_op jit(solution)/shard_map/ppermute | solution.py:31
  404.0 17.1 %collective-permute-start.49 = (bf16[192,1024]{1,0:T(8,128)(2,1)S(1)}, bf16[192,1024]{1,0:T(8,128)(2,1)}, u32[]{:S(2)}, u32[]{:S(2)}) collective-permute-start(bf16[192,1024]{1,0:T(8,128)(2,1)S(1)} %get-tuple-element.368), channel_id=1, source_target_pairs={{0,3},{1,0},{2,1},{3,2},{4,7},{5,4},{6,5},{7,6},{8,11},{9,8},{10,9... | collective-permute-start | bytes 1179656 | tf_op jit(solution)/shard_map/ppermute | solution.py:31
  429.7 19.5 %collective-permute-start.54 = (bf16[192,1024]{1,0:T(8,128)(2,1)}, bf16[192,1024]{1,0:T(8,128)(2,1)S(1)}, u32[]{:S(2)}, u32[]{:S(2)}) collective-permute-start(bf16[192,1024]{1,0:T(8,128)(2,1)} %get-tuple-element.258), channel_id=1, source_target_pairs={{0,3},{1,0},{2,1},{3,2},{4,7},{5,4},{6,5},{7,6},{8,11},{9,8},{10,9... | collective-permute-start | bytes 1179656 | tf_op jit(solution)/shard_map/ppermute | solution.py:31
  432.7 16.6 %collective-permute-start.53 = (bf16[192,1024]{1,0:T(8,128)(2,1)}, bf16[192,1024]{1,0:T(8,128)(2,1)S(1)}, u32[]{:S(2)}, u32[]{:S(2)}) collective-permute-start(bf16[192,1024]{1,0:T(8,128)(2,1)} %get-tuple-element.258), channel_id=1, source_target_pairs={{0,2},{1,3},{2,0},{3,1},{4,6},{5,7},{6,4},{7,5},{8,10},{9,11},{10,... | collective-permute-start | bytes 1179656 | tf_op jit(solution)/shard_map/ppermute | solution.py:31
  432.7 20.7 %collective-permute-start.52 = (bf16[192,1024]{1,0:T(8,128)(2,1)}, bf16[192,1024]{1,0:T(8,128)(2,1)S(1)}, u32[]{:S(2)}, u32[]{:S(2)}) collective-permute-start(bf16[192,1024]{1,0:T(8,128)(2,1)} %get-tuple-element.258), channel_id=1, source_target_pairs={{0,1},{1,2},{2,3},{3,0},{4,5},{5,6},{6,7},{7,4},{8,9},{9,10},{10,1... | collective-permute-start | bytes 1179656 | tf_op jit(solution)/shard_map/ppermute | solution.py:31
  460.0 20.1 %collective-permute-start.58 = (bf16[192,1024]{1,0:T(8,128)(2,1)S(1)}, bf16[192,1024]{1,0:T(8,128)(2,1)S(1)}, u32[]{:S(2)}, u32[]{:S(2)}) collective-permute-start(bf16[192,1024]{1,0:T(8,128)(2,1)S(1)} %get-tuple-element.363), channel_id=1, source_target_pairs={{0,1},{1,2},{2,3},{3,0},{4,5},{5,6},{6,7},{7,4},{8,9},{9,10},{10,1... | collective-permute-start | bytes 1179656 | tf_op jit(solution)/shard_map/ppermute | solution.py:31
  460.4 19.6 %collective-permute-start.57 = (bf16[192,1024]{1,0:T(8,128)(2,1)S(1)}, bf16[192,1024]{1,0:T(8,128)(2,1)S(1)}, u32[]{:S(2)}, u32[]{:S(2)}) collective-permute-start(bf16[192,1024]{1,0:T(8,128)(2,1)S(1)} %get-tuple-element.364), channel_id=1, source_target_pairs={{0,2},{1,3},{2,0},{3,1},{4,6},{5,7},{6,4},{7,5},{8,10},{9,11},{10,... | collective-permute-start | bytes 1179656 | tf_op jit(solution)/shard_map/ppermute | solution.py:31
  461.4 19.0 %collective-permute-start.56 = (bf16[192,1024]{1,0:T(8,128)(2,1)S(1)}, bf16[192,1024]{1,0:T(8,128)(2,1)S(1)}, u32[]{:S(2)}, u32[]{:S(2)}) collective-permute-start(bf16[192,1024]{1,0:T(8,128)(2,1)S(1)} %get-tuple-element.365), channel_id=1, source_target_pairs={{0,3},{1,0},{2,1},{3,2},{4,7},{5,4},{6,5},{7,6},{8,11},{9,8},{10,9... | collective-permute-start | bytes 1179656 | tf_op jit(solution)/shard_map/ppermute | solution.py:31
  484.7 26.8 %collective-permute-start.62 = (bf16[8,64,2048]{2,1,0:T(8,128)(2,1)}, bf16[8,64,2048]{2,1,0:T(8,128)(2,1)}, u32[]{:S(2)}, u32[]{:S(2)}) collective-permute-start(bf16[8,64,2048]{2,1,0:T(8,128)(2,1)} %fusion.22), channel_id=1, source_target_pairs={{0,8},{8,0},{1,9},{9,1},{2,10},{10,2},{3,11},{11,3},{4,12},{12,4},... | collective-permute-start | bytes 6291464 | tf_op jit(solution)/shard_map/ppermute | solution.py:39
  486.4 18.9 %collective-permute-start.61 = (bf16[192,1024]{1,0:T(8,128)(2,1)S(1)}, bf16[192,1024]{1,0:T(8,128)(2,1)}, u32[]{:S(2)}, u32[]{:S(2)}) collective-permute-start(bf16[192,1024]{1,0:T(8,128)(2,1)S(1)} %get-tuple-element.273), channel_id=1, source_target_pairs={{0,3},{1,0},{2,1},{3,2},{4,7},{5,4},{6,5},{7,6},{8,11},{9,8},{10,9... | collective-permute-start | bytes 1179656 | tf_op jit(solution)/shard_map/ppermute | solution.py:31
  488.5 16.8 %collective-permute-start.60 = (bf16[192,1024]{1,0:T(8,128)(2,1)S(1)}, bf16[192,1024]{1,0:T(8,128)(2,1)}, u32[]{:S(2)}, u32[]{:S(2)}) collective-permute-start(bf16[192,1024]{1,0:T(8,128)(2,1)S(1)} %get-tuple-element.273), channel_id=1, source_target_pairs={{0,2},{1,3},{2,0},{3,1},{4,6},{5,7},{6,4},{7,5},{8,10},{9,11},{10,... | collective-permute-start | bytes 1179656 | tf_op jit(solution)/shard_map/ppermute | solution.py:31
  488.5 20.5 %collective-permute-start.59 = (bf16[192,1024]{1,0:T(8,128)(2,1)S(1)}, bf16[192,1024]{1,0:T(8,128)(2,1)}, u32[]{:S(2)}, u32[]{:S(2)}) collective-permute-start(bf16[192,1024]{1,0:T(8,128)(2,1)S(1)} %get-tuple-element.273), channel_id=1, source_target_pairs={{0,1},{1,2},{2,3},{3,0},{4,5},{5,6},{6,7},{7,4},{8,9},{9,10},{10,1... | collective-permute-start | bytes 1179656 | tf_op jit(solution)/shard_map/ppermute | solution.py:31
  530.8 35.6 %all-to-all-start.3 = ((bf16[8,64,2048]{2,1,0:T(8,128)(2,1)}), bf16[8,64,2048]{2,1,0:T(8,128)(2,1)}, u32[]{:S(2)}, u32[]{:S(2)}) async-start(bf16[8,64,2048]{2,1,0:T(8,128)(2,1)} %fusion), calls=%async_computation.3 | async-start | bytes 4194304 | tf_op jit(solution)/shard_map/all_to_all | solution.py:817
  535.2 148.9 %all-gather.6.cloned.1.call-start = ((), (), s32[]{:S(2)}) async-start(), calls=%async_computation.7 | async-start | bytes 2506752 | tf_op jit(solution)/shard_map/all_gather | solution.py:840
  535.3 133.8 %collective-permute-start.55 = (f32[192,1024]{1,0:T(8,128)}, f32[192,1024]{1,0:T(8,128)}, u32[]{:S(2)}, u32[]{:S(2)}) collective-permute-start(f32[192,1024]{1,0:T(8,128)} %fusion.28), channel_id=1, source_target_pairs={{4,8},{8,4},{5,9},{9,5},{6,10},{10,6},{7,11},{11,7},{20,24},{24,20... | collective-permute-start | bytes 2359304 | tf_op jit(solution)/shard_map/ppermute | solution.py:43
  543.8 17.6 %collective-permute-start.67 = (bf16[192,1024]{1,0:T(8,128)(2,1)S(1)}, bf16[192,1024]{1,0:T(8,128)(2,1)}, u32[]{:S(2)}, u32[]{:S(2)}) collective-permute-start(bf16[192,1024]{1,0:T(8,128)(2,1)S(1)} %get-tuple-element.360), channel_id=1, source_target_pairs={{0,1},{1,2},{2,3},{3,0},{4,5},{5,6},{6,7},{7,4},{8,9},{9,10},{10,1... | collective-permute-start | bytes 1179656 | tf_op jit(solution)/shard_map/ppermute | solution.py:31
  543.9 17.6 %collective-permute-start.66 = (bf16[192,1024]{1,0:T(8,128)(2,1)S(1)}, bf16[192,1024]{1,0:T(8,128)(2,1)}, u32[]{:S(2)}, u32[]{:S(2)}) collective-permute-start(bf16[192,1024]{1,0:T(8,128)(2,1)S(1)} %get-tuple-element.361), channel_id=1, source_target_pairs={{0,2},{1,3},{2,0},{3,1},{4,6},{5,7},{6,4},{7,5},{8,10},{9,11},{10,... | collective-permute-start | bytes 1179656 | tf_op jit(solution)/shard_map/ppermute | solution.py:31
  545.6 17.0 %collective-permute-start.65 = (bf16[192,1024]{1,0:T(8,128)(2,1)S(1)}, bf16[192,1024]{1,0:T(8,128)(2,1)}, u32[]{:S(2)}, u32[]{:S(2)}) collective-permute-start(bf16[192,1024]{1,0:T(8,128)(2,1)S(1)} %get-tuple-element.362), channel_id=1, source_target_pairs={{0,3},{1,0},{2,1},{3,2},{4,7},{5,4},{6,5},{7,6},{8,11},{9,8},{10,9... | collective-permute-start | bytes 1179656 | tf_op jit(solution)/shard_map/ppermute | solution.py:31
  579.6 25.5 %collective-permute-start.94 = (bf16[8,768]{1,0:T(8,128)(2,1)S(1)}, bf16[8,768]{1,0:T(8,128)(2,1)S(1)}, u32[]{:S(2)}, u32[]{:S(2)}) collective-permute-start(bf16[8,768]{1,0:T(8,128)(2,1)S(1)} %get-tuple-element.427), channel_id=1, source_target_pairs={{0,3},{1,0},{2,1},{3,2},{4,7},{5,4},{6,5},{7,6},{8,11},{9,8},{10,9... | collective-permute-start | bytes 36872 | tf_op jit(solution)/shard_map/ppermute | solution.py:31
  601.0 85.0 %all-gather.8.cloned.1.call-start = ((), (), s32[]{:S(2)}) async-start(), calls=%async_computation.8 | async-start | bytes 3342336 | tf_op jit(solution)/shard_map/all_gather | solution.py:822
  617.3 22.1 %collective-permute-start.69 = (f32[2,3072]{1,0:T(2,128)S(1)}, f32[2,3072]{1,0:T(2,128)S(1)}, u32[]{:S(2)}, u32[]{:S(2)}) collective-permute-start(f32[2,3072]{1,0:T(2,128)S(1)} %bitcast.316), channel_id=1, source_target_pairs={{0,1},{1,2},{2,3},{3,0},{4,5},{5,6},{6,7},{7,4},{8,9},{9,10},{10,1... | collective-permute-start | bytes 73736 | tf_op jit(solution)/shard_map/ppermute | solution.py:31
  617.7 21.7 %collective-permute-start.70 = (f32[2,3072]{1,0:T(2,128)S(1)}, f32[2,3072]{1,0:T(2,128)S(1)}, u32[]{:S(2)}, u32[]{:S(2)}) collective-permute-start(f32[2,3072]{1,0:T(2,128)S(1)} %bitcast.315), channel_id=1, source_target_pairs={{0,2},{1,3},{2,0},{3,1},{4,6},{5,7},{6,4},{7,5},{8,10},{9,11},{10,... | collective-permute-start | bytes 73736 | tf_op jit(solution)/shard_map/ppermute | solution.py:31
  621.2 18.2 %collective-permute-start.71 = (f32[2,3072]{1,0:T(2,128)S(1)}, f32[2,3072]{1,0:T(2,128)S(1)}, u32[]{:S(2)}, u32[]{:S(2)}) collective-permute-start(f32[2,3072]{1,0:T(2,128)S(1)} %bitcast.314), channel_id=1, source_target_pairs={{0,3},{1,0},{2,1},{3,2},{4,7},{5,4},{6,5},{7,6},{8,11},{9,8},{10,9... | collective-permute-start | bytes 73736 | tf_op jit(solution)/shard_map/ppermute | solution.py:31
  621.9 62.0 %all-to-all-start.4 = ((bf16[128,8,768]{2,1,0:T(8,128)(2,1)}), bf16[128,8,768]{2,1,0:T(8,128)(2,1)S(1)}, u32[]{:S(2)}, u32[]{:S(2)}) async-start(bf16[128,8,768]{2,1,0:T(8,128)(2,1)} %bitcast.44), calls=%async_computation.5 | async-start | bytes 3145728 | tf_op jit(solution)/shard_map/all_to_all | solution.py:836
  639.5 13.9 %collective-permute-start.74 = (f32[3072]{0:T(1024)S(1)}, f32[3072]{0:T(1024)S(1)}, u32[]{:S(2)}, u32[]{:S(2)}) collective-permute-start(f32[3072]{0:T(1024)S(1)} %bitcast.337), channel_id=1, source_target_pairs={{0,20},{4,16},{16,4},{20,0},{1,21},{5,17},{17,5},{21,1},{2,22},{6,... | collective-permute-start | bytes 36872 | tf_op jit(solution)/shard_map/ppermute | solution.py:626
  642.3 13.0 %collective-permute-start.73 = (f32[3072]{0:T(1024)S(1)}, f32[3072]{0:T(1024)S(1)}, u32[]{:S(2)}, u32[]{:S(2)}) collective-permute-start(f32[3072]{0:T(1024)S(1)} %bitcast.338), channel_id=1, source_target_pairs={{0,4},{4,0},{16,20},{20,16},{1,5},{5,1},{17,21},{21,17},{2,6},{6,2... | collective-permute-start | bytes 36872 | tf_op jit(solution)/shard_map/ppermute | solution.py:626
  642.8 12.5 %collective-permute-start.72 = (f32[3072]{0:T(1024)S(1)}, f32[3072]{0:T(1024)S(1)}, u32[]{:S(2)}, u32[]{:S(2)}) collective-permute-start(f32[3072]{0:T(1024)S(1)} %bitcast.312), channel_id=1, source_target_pairs={{0,16},{4,20},{16,0},{20,4},{1,17},{5,21},{17,1},{21,5},{2,18},{6,... | collective-permute-start | bytes 36872 | tf_op jit(solution)/shard_map/ppermute | solution.py:626
  644.5 38.4 %collective-permute-start.68 = (f32[192,1024]{1,0:T(8,128)S(1)}, f32[192,1024]{1,0:T(8,128)S(1)}, u32[]{:S(2)}, u32[]{:S(2)}) collective-permute-start(f32[192,1024]{1,0:T(8,128)S(1)} %fusion.47), channel_id=1, source_target_pairs={{4,8},{8,4},{5,9},{9,5},{6,10},{10,6},{7,11},{11,7},{20,24},{24,20... | collective-permute-start | bytes 2359304 | tf_op jit(solution)/shard_map/ppermute | solution.py:43
  (127 other events, 1157.4 us)
Sparse Core Ops, SparseCore 0:
  422.8 77.2 reduce-scatter.1
  601.1 38.8 all-gather.5
  642.3 40.9 all-gather.7

commit v5 on v4

v5 whole, which is shorter than its diff:
```python
import math

import jax
import jax.numpy as jnp
from jax import lax
from jax.experimental import pallas as pl
from jax.experimental.pallas import tpu as pltpu
from jax.sharding import Mesh
from jax.sharding import PartitionSpec as P

D = 1024
HEADS = 16
HEAD_DIM = 64
FF = 4096
PROMPT = 1024
TOKENS = 1536
PIECE = 192
LAYERS = 2
TILE = 256
HALF = 4 * PIECE
SCALE = HEAD_DIM ** (-0.5)
masked_value = -1e30

GRP = ("x", "y_lo", "core")
CTX = ("y_hi", "z")
bf16 = jnp.bfloat16
f32 = jnp.float32


def shift_z(value, step):
    return lax.ppermute(value, "z", [(i, (i + step) % 4) for i in range(4)])


def shift_x(value, step):
    return lax.ppermute(value, "x", [(i, (i + step) % 4) for i in range(4)])


def swap(value, axis):
    return lax.ppermute(value, axis, [(0, 1), (1, 0)])


def regroup(value, core, y_hi):
    got = lax.ppermute(value, ("core", "y_hi"), [(1, 2), (2, 1)])
    return jnp.where(core == y_hi, value, got)


def after(value, *others):
    return lax.optimization_barrier((value, others))[0]


def beside(send, transfer, given, work):
    send, given = lax.optimization_barrier((send, given))
    return lax.optimization_barrier((transfer(send), work(given)))


def gather_z(rows):
    return jnp.concatenate([rows] + [shift_z(rows, k) for k in (1, 2, 3)], axis=0)


def dot(left, right):
    return jnp.dot(left, right, preferred_element_type=f32)


def dot_t(left, right):
    return lax.dot_general(left, right, (((1,), (1,)), ((), ())), preferred_element_type=f32)


def outer(left, right):
    return lax.dot_general(left, right, (((0,), (0,)), ((), ())), preferred_element_type=f32)


def scatter_parts(others):
    return tuple(
        shift_z(others[(k - 1) * PIECE : k * PIECE], -k) for k in (1, 2, 3)
    )


def sum_parts(own, parts):
    total = own
    for part in parts:
        total = total + part.astype(f32)
    return total


def dot_others(left, weight, product):
    return product(left[PIECE:], weight).astype(bf16)


def dot_own(left, weight, product):
    return product(left[:PIECE], weight)


def tile_mask(block, low, high, cut):
    keys = lax.broadcasted_iota(jnp.int32, (high - low, TILE), 0) + low
    queries = lax.broadcasted_iota(jnp.int32, (high - low, TILE), 1) + block * TILE
    visible = keys <= queries
    if block * TILE >= PROMPT:
        visible = visible & ((keys >= cut) | (queries < cut))
    return visible


def fill_bias(bias, slopes, cut):
    keys = lax.broadcasted_iota(jnp.int32, (TOKENS, 128), 0)
    places = jnp.where(keys >= cut, keys - cut + PROMPT, keys).astype(f32)
    for h in range(2):
        bias[h] = places * slopes[h]


def scores_t(keys, queries, bias, block, high, cut):
    low = min(block * TILE, PROMPT)
    scores = dot_t(keys, queries)
    scores = scores + jnp.concatenate([bias[0:high], bias[0:high]], axis=1)
    tail = jnp.where(tile_mask(block, low, high, cut), scores[low:high], masked_value)
    if low == 0:
        return tail
    return jnp.concatenate([scores[:low], tail], axis=0)


def piece_places(info):
    core, z = info[0], info[1]
    out = []
    for side in range(2):
        half = core if side == 0 else 1 - core
        for k in range(4):
            out.append(pl.multiple_of((half * 4 + ((z - k) & 3)) * PIECE, 64))
    return out


def attend_kernel(info, slopes, mine, other, ctx_mine, ctx_other, logsum, rows, ctx, vt, bias):
    spots = piece_places(info)
    cut = info[2]
    for k in range(4):
        span = slice(k * PIECE, (k + 1) * PIECE)
        rows[pl.ds(spots[k], PIECE), :] = mine[span, :]
        rows[pl.ds(spots[4 + k], PIECE), :] = other[span, :]
    fill_bias(bias, slopes, cut)
    vt[...] = rows[:, 256:384].astype(f32).T.astype(bf16)
    for block in range(TOKENS // TILE):
        high = (block + 1) * TILE
        span = slice(block * TILE, high)
        parts = []
        for h in range(2):
            lanes = slice(h * HEAD_DIM, (h + 1) * HEAD_DIM)
            key_lanes = slice(128 + h * HEAD_DIM, 128 + (h + 1) * HEAD_DIM)
            queries = rows[span, lanes] * jnp.asarray(SCALE, bf16)
            scores = scores_t(rows[0:high, key_lanes], queries, bias[h], block, high, cut)
            top = jnp.max(scores, axis=0, keepdims=True)
            weights = jnp.exp(scores - top)
            total = jnp.sum(weights, axis=0, keepdims=True)
            found = dot(vt[lanes, 0:high], weights.astype(bf16))
            parts.append(found * (1.0 / total))
            logsum[h : h + 1, span] = top + jnp.log(total)
        ctx[span, :] = jnp.concatenate(parts, axis=0).T.astype(bf16)
    for k in range(4):
        span = slice(k * PIECE, (k + 1) * PIECE)
        ctx_mine[span, :] = ctx[pl.ds(spots[k], PIECE), :]
        ctx_other[span, :] = ctx[pl.ds(spots[4 + k], PIECE), :]


def attend_back_kernel(
    info, slopes, rows, mine, other, logsum, out_mine, out_other, sums, grad, kt, bias, dq, dk, dv, out
):
    spots = piece_places(info)
    cut = info[2]
    for k in range(4):
        span = slice(k * PIECE, (k + 1) * PIECE)
        grad[pl.ds(spots[k], PIECE), :] = mine[span, :]
        grad[pl.ds(spots[4 + k], PIECE), :] = other[span, :]
    fill_bias(bias, slopes, cut)
    kt[...] = rows[:, 128:256].astype(f32).T.astype(bf16)
    dk[...] = jnp.zeros_like(dk)
    dv[...] = jnp.zeros_like(dv)
    for block in range(TOKENS // TILE):
        high = (block + 1) * TILE
        span = slice(block * TILE, high)
        parts = []
        for h in range(2):
            lanes = slice(h * HEAD_DIM, (h + 1) * HEAD_DIM)
            key_lanes = slice(128 + h * HEAD_DIM, 128 + (h + 1) * HEAD_DIM)
            value_lanes = slice(256 + h * HEAD_DIM, 256 + (h + 1) * HEAD_DIM)
            queries = rows[span, lanes] * jnp.asarray(SCALE, bf16)
            grads = grad[span, lanes]
            scores = scores_t(rows[0:high, key_lanes], queries, bias[h], block, high, cut)
            weights = jnp.exp(scores - logsum[h : h + 1, span])
            d_weights = dot_t(rows[0:high, value_lanes], grads)
            correction = jnp.sum(weights * d_weights, axis=0, keepdims=True)
            d_scores = (weights * (d_weights - correction)).astype(bf16)
            dv[h, 0:high, :] += dot(weights.astype(bf16), grads)
            dk[h, 0:high, :] += dot(d_scores, queries)
            parts.append(dot(kt[lanes, 0:high], d_scores))
        dq[span, :] = (jnp.concatenate(parts, axis=0) * SCALE).T
    out[:, 0:128] = dq[...].astype(bf16)
    out[:, 128:256] = jnp.concatenate([dk[0], dk[1]], axis=1).astype(bf16)
    out[:, 256:384] = jnp.concatenate([dv[0], dv[1]], axis=1).astype(bf16)
    sums[...] = jnp.sum(out[...].astype(f32), axis=0, keepdims=True)
    for k in range(4):
        span = slice(k * PIECE, (k + 1) * PIECE)
        out_mine[span, :] = out[pl.ds(spots[k], PIECE), :]
        out_other[span, :] = out[pl.ds(spots[4 + k], PIECE), :]


smem = pl.BlockSpec(memory_space=pltpu.SMEM)
vmem = pl.BlockSpec(memory_space=pltpu.VMEM)
LIMIT = 40 * 2**20


def attend(info, slopes, mine, other):
    return pl.pallas_call(
        attend_kernel,
        out_shape=(
            jax.ShapeDtypeStruct((HALF, 128), bf16),
            jax.ShapeDtypeStruct((HALF, 128), bf16),
            jax.ShapeDtypeStruct((2, TOKENS), f32),
            jax.ShapeDtypeStruct((TOKENS, 384), bf16),
        ),
        in_specs=[smem, smem, vmem, vmem],
        out_specs=(vmem, vmem, vmem, vmem),
        scratch_shapes=[
            pltpu.VMEM((TOKENS, 128), bf16),
            pltpu.VMEM((128, TOKENS), bf16),
            pltpu.VMEM((2, TOKENS, 128), f32),
        ],
        compiler_params=pltpu.CompilerParams(vmem_limit_bytes=LIMIT),
        cost_estimate=pl.CostEstimate(
            flops=1000000, bytes_accessed=36000000, transcendentals=0
        ),
        name="attend",
    )(info, slopes, mine, other)


def attend_back(info, slopes, rows, mine, other, logsum):
    return pl.pallas_call(
        attend_back_kernel,
        out_shape=(
            jax.ShapeDtypeStruct((HALF, 384), bf16),
            jax.ShapeDtypeStruct((HALF, 384), bf16),
            jax.ShapeDtypeStruct((1, 384), f32),
        ),
        in_specs=[smem, smem, vmem, vmem, vmem, vmem],
        out_specs=(vmem, vmem, vmem),
        scratch_shapes=[
            pltpu.VMEM((TOKENS, 128), bf16),
            pltpu.VMEM((128, TOKENS), bf16),
            pltpu.VMEM((2, TOKENS, 128), f32),
            pltpu.VMEM((TOKENS, 128), f32),
            pltpu.VMEM((2, TOKENS, HEAD_DIM), f32),
            pltpu.VMEM((2, TOKENS, HEAD_DIM), f32),
            pltpu.VMEM((TOKENS, 384), bf16),
        ],
        compiler_params=pltpu.CompilerParams(vmem_limit_bytes=LIMIT),
        cost_estimate=pl.CostEstimate(
            flops=1000000, bytes_accessed=48000000, transcendentals=0
        ),
        name="attend_back",
    )(info, slopes, rows, mine, other, logsum)


def norm_parts(values):
    average = jnp.mean(values, axis=-1, keepdims=True)
    centered = values - average
    variance = jnp.mean(centered * centered, axis=-1, keepdims=True)
    scale = lax.rsqrt(variance + 1e-05)
    return centered * scale, scale


def norm(values, gain, offset):
    return norm_parts(values)[0] * gain + offset


def norm_back(values, gain, grads):
    unit, scale = norm_parts(values)
    weighted = grads * gain
    mean_one = jnp.mean(weighted, axis=-1, keepdims=True)
    mean_two = jnp.mean(weighted * unit, axis=-1, keepdims=True)
    d_values = scale * (weighted - mean_one - unit * mean_two)
    return d_values, jnp.sum(grads * unit, axis=0), jnp.sum(grads, axis=0)


def gelu(values):
    return jax.nn.gelu(values, approximate=True)


PAIR = 2 * PIECE


def wide_down(weight, down):
    for place in range(8):
        for side in range(2):
            at = place * 128 + side * 64
            down[place * 64 : (place + 1) * 64, side * 512 : (side + 1) * 512] = weight[
                0, at : at + 64, 512:1024
            ]


def gelu_parts(u):
    k = math.sqrt(2.0 / math.pi)
    square = u * u
    t = jnp.tanh(k * u * (1.0 + 0.044715 * square))
    half = 0.5 * (1.0 + t)
    slope = half + 0.5 * u * (1.0 - t * t) * (k * (1.0 + 3.0 * 0.044715 * square))
    return u * half, slope


def wide_forward_kernel(rows, weight, bias, own, other, before, down, total):
    step = pl.program_id(0)
    wide_down(weight, down)
    u = dot(rows[...], weight[0, :, 0:512]) + bias[0]
    before[0] = u
    activated = gelu_parts(u)[0].astype(bf16)
    part = dot(activated, down[...])

    @pl.when(step == 0)
    def _():
        total[...] = part

    @pl.when(step > 0)
    def _():
        total[...] += part

    @pl.when(step == 3)
    def _():
        own[...] = total[0:PIECE, :]
        other[...] = total[PIECE:PAIR, :].astype(bf16)


def wide_forward(rows, weight, bias):
    fixed = lambda shape: pl.BlockSpec(shape, lambda i: (0,) * len(shape))
    each = lambda *shape: pl.BlockSpec((1,) + shape, lambda i: (i, 0, 0))
    return pl.pallas_call(
        wide_forward_kernel,
        grid=(4,),
        out_shape=(
            jax.ShapeDtypeStruct((PIECE, D), f32),
            jax.ShapeDtypeStruct((PIECE, D), bf16),
            jax.ShapeDtypeStruct((4, PAIR, 512), f32),
        ),
        in_specs=[fixed((PAIR, D)), each(D, D), each(1, 512)],
        out_specs=(fixed((PIECE, D)), fixed((PIECE, D)), each(PAIR, 512)),
        scratch_shapes=[pltpu.VMEM((512, D), bf16), pltpu.VMEM((PAIR, D), f32)],
        compiler_params=pltpu.CompilerParams(vmem_limit_bytes=58 * 2**20),
        cost_estimate=pl.CostEstimate(
            flops=4 * PAIR * 2048 * D, bytes_accessed=20000000, transcendentals=0
        ),
        name="wide_forward",
    )(rows, weight, bias)


def wide_back_kernel(grads, rows, before, weight, own, other, sums, pack, down, total):
    step = pl.program_id(0)
    wide_down(weight, down)
    activated, slope = gelu_parts(before[0])
    d_before = (dot_t(grads[...], down[...]) * slope).astype(bf16)
    sums[0] = jnp.sum(d_before.astype(f32), axis=0, keepdims=True)
    part = dot_t(d_before, weight[0, :, 0:512])
    g_up = outer(rows[...], d_before).astype(bf16)
    g_down = outer(activated.astype(bf16), grads[...]).astype(bf16)
    for place in range(8):
        for side in range(2):
            at = place * 128 + side * 64
            pack[0, side, place, :, 0:512] = g_up[at : at + 64, :]
            pack[0, side, place, :, 512:1024] = g_down[
                place * 64 : (place + 1) * 64, side * 512 : (side + 1) * 512
            ]

    @pl.when(step == 0)
    def _():
        total[...] = part

    @pl.when(step > 0)
    def _():
        total[...] += part

    @pl.when(step == 3)
    def _():
        own[...] = total[0:PIECE, :]
        other[...] = total[PIECE:PAIR, :].astype(bf16)


def wide_back(grads, rows, before, weight):
    fixed = lambda shape: pl.BlockSpec(shape, lambda i: (0,) * len(shape))
    each = lambda *shape: pl.BlockSpec((1,) + shape, lambda i: (i,) + (0,) * len(shape))
    return pl.pallas_call(
        wide_back_kernel,
        grid=(4,),
        out_shape=(
            jax.ShapeDtypeStruct((PIECE, D), f32),
            jax.ShapeDtypeStruct((PIECE, D), bf16),
            jax.ShapeDtypeStruct((4, 1, 512), f32),
            jax.ShapeDtypeStruct((4, 2, 8, 64, D), bf16),
        ),
        in_specs=[fixed((PAIR, D)), fixed((PAIR, D)), each(PAIR, 512), each(D, D)],
        out_specs=(fixed((PIECE, D)), fixed((PIECE, D)), each(1, 512), each(2, 8, 64, D)),
        scratch_shapes=[pltpu.VMEM((512, D), bf16), pltpu.VMEM((PAIR, D), f32)],
        compiler_params=pltpu.CompilerParams(vmem_limit_bytes=58 * 2**20),
        cost_estimate=pl.CostEstimate(
            flops=10 * PAIR * 2048 * D, bytes_accessed=40000000, transcendentals=0
        ),
        name="wide_back",
    )(grads, rows, before, weight)


QUARTER = 16


def pack_first_kernel(info, weight, small, out):
    for place in range(8):
        for side in range(2):
            for part in range(3):
                at = part * D + side * 512 + (place % 4) * 128
                to = (side * 3 + part) * 128
                out[place, 0:16, to : to + 128] = weight[0, :, at : at + 128]
        out[place, 16:32, :] = small[...]


def pack_rest_kernel(info, weight, up, down, project, first, second, rows, wide):
    core, x = info[0], info[4]
    at_row = pl.ds(pl.multiple_of(core * 64 + x * 16, 16), 16)
    for place in range(8):
        for side in range(2):
            at = side * 2048 + (place % 4) * 512
            to = side * 512
            first[place, :, to : to + 512] = up[0, at_row, at : at + 512]
            for part in range(3):
                at = part * D + side * 512 + (place % 4) * 128
                to = (side * 3 + part) * 128
                second[place, :, to : to + 128] = weight[0, at_row, at : at + 128]
    long = pl.ds(pl.multiple_of(core * 256 + x * 64, 64), 64)
    rows[0:64, :] = down[0, long, :]
    rows[64:80, :] = project[0, at_row, :]
    rows[80:96, :] = project[1, at_row, :]
    wide[0:64, 512:1024] = down[1, long, 0:512]
    wide[64:128, 512:1024] = down[1, long, 512:1024]
    for place in range(8):
        pair = pl.ds(pl.multiple_of(place * 512 + core * 256 + (x >> 1) * 128, 128), 128)
        found = up[1, :, pair].astype(f32)
        found = jnp.where(x % 2 == 0, found[:, 0:64], found[:, 64:128])
        wide[:, place * 64 : (place + 1) * 64] = found.astype(bf16)


def join_columns_kernel(info, mine, other, out):
    core, x = info[0], info[4]
    for pieces, half in ((mine, core), (other, 1 - core)):
        for k in range(4):
            for place in range(8):
                at = place * 128 + half * 64 + ((x - k) & 3) * 16
                out[pl.ds(pl.multiple_of(at, 16), 16), :] = pieces[k, place * 16 : (place + 1) * 16, :]


def join_rows_kernel(info, down, project, mine, other, down_out, project_out, project_next):
    core, x, y_hi = info[0], info[4], info[2]
    down_out[pl.ds(pl.multiple_of(y_hi * 512, 64), 512), :] = down[0]
    own = pl.ds(pl.multiple_of(y_hi * 128, 64), 128)
    project_out[own, :] = project[0]
    project_next[own, :] = project[1]
    for pieces, half in ((mine, core), (other, 1 - core)):
        for k in range(4):
            quarter = (x - k) & 3
            at = (1 - y_hi) * 512 + half * 256 + quarter * 64
            down_out[pl.ds(pl.multiple_of(at, 64), 64), :] = pieces[k, 0:64, :]
            at = pl.ds(pl.multiple_of((1 - y_hi) * 128 + half * 64 + quarter * 16, 16), 16)
            project_out[at, :] = pieces[k, 64:80, :]
            project_next[at, :] = pieces[k, 80:96, :]


def read_small_kernel(info, got, vectors, in_bias, unit_bias):
    z = info[1]
    for layer in range(LAYERS):
        for member in range(6):
            lanes = slice(member * 128, (member + 1) * 128)
            row = layer * 6 + member
            for place in range(8):
                vectors[row : row + 1, place * 128 : (place + 1) * 128] = got[
                    place, 16 + 2 * layer : 17 + 2 * layer, lanes
                ].astype(f32)
        row = slice(17 + 2 * layer, 18 + 2 * layer)
        here = slice(layer, layer + 1)
        for side in range(2):
            at = side * 384
            lanes = pl.ds(pl.multiple_of((z & 1) * 128, 128), 128)
            owner = side * 2 + (z >> 1)
            in_bias[here, at : at + 128] = got[owner, row, lanes].astype(f32)
            in_bias[here, at + 128 : at + 256] = jnp.zeros((1, 128), f32)
            in_bias[here, at + 256 : at + 384] = got[owner + 4, row, lanes].astype(f32)
            unit_bias[here, side * 512 : (side + 1) * 512] = got[side * 4 + z, row, 256:768].astype(f32)


def layer_block(shape, layer):
    return pl.BlockSpec((1,) + shape, lambda i: (layer, 0, 0))


whole = pl.BlockSpec(memory_space=pltpu.VMEM)
params_one = pltpu.CompilerParams(vmem_limit_bytes=LIMIT)


def pack_first(row_block, weight, small):
    return pl.pallas_call(
        pack_first_kernel,
        grid_spec=pltpu.PrefetchScalarGridSpec(
            num_scalar_prefetch=1,
            grid=(1,),
            in_specs=[
                pl.BlockSpec((1, 16, 3072), lambda i, info: (0, info[0], 0)),
                pl.BlockSpec((16, 768), lambda i, info: (0, 0)),
            ],
            out_specs=pl.BlockSpec((8, 32, 768), lambda i, info: (0, 0, 0)),
        ),
        out_shape=jax.ShapeDtypeStruct((8, 32, 768), bf16),
        compiler_params=params_one,
        name="pack_first",
    )(row_block, weight, small)


def pack_rest(info, weight, up, down, project):
    return pl.pallas_call(
        pack_rest_kernel,
        grid=(1,),
        out_shape=(
            jax.ShapeDtypeStruct((8, 16, 1024), bf16),
            jax.ShapeDtypeStruct((8, 16, 768), bf16),
            jax.ShapeDtypeStruct((96, D), bf16),
            jax.ShapeDtypeStruct((128, D), bf16),
        ),
        in_specs=[smem, layer_block((128, 3072), 1), whole, whole, whole],
        out_specs=(whole,) * 4,
        compiler_params=params_one,
        name="pack_rest",
    )(info, weight, up, down, project)


def read_small(info, got):
    return pl.pallas_call(
        read_small_kernel,
        out_shape=(
            jax.ShapeDtypeStruct((12, D), f32),
            jax.ShapeDtypeStruct((LAYERS, 768), f32),
            jax.ShapeDtypeStruct((LAYERS, D), f32),
        ),
        in_specs=[smem, whole],
        out_specs=(whole,) * 3,
        compiler_params=params_one,
        name="read_small",
    )(info, got)


def gather_x(piece):
    return jnp.stack([piece] + [shift_x(piece, k) for k in (1, 2, 3)])


def join_columns(info, mine, other):
    return pl.pallas_call(
        join_columns_kernel,
        out_shape=jax.ShapeDtypeStruct((D, mine.shape[2]), bf16),
        in_specs=[smem, whole, whole],
        out_specs=whole,
        compiler_params=params_one,
        name="join_columns",
    )(info, mine, other)


def join_rows(info, down, project, mine, other):
    return pl.pallas_call(
        join_rows_kernel,
        grid=(1,),
        out_shape=(
            jax.ShapeDtypeStruct((D, D), bf16),
            jax.ShapeDtypeStruct((256, D), bf16),
            jax.ShapeDtypeStruct((256, D), bf16),
        ),
        in_specs=[smem, layer_block((512, D), 0), whole, whole, whole],
        out_specs=(whole,) * 3,
        compiler_params=params_one,
        name="join_rows",
    )(info, down, project, mine, other)


def to_ctx(value):
    return lax.all_to_all(value, CTX, split_axis=0, concat_axis=0, tiled=True)


def in_order(mine, other, core):
    return jnp.where(
        core == 0,
        jnp.concatenate([mine, other], axis=1),
        jnp.concatenate([other, mine], axis=1),
    )


def columns_at(value, at, width):
    return lax.dynamic_slice_in_dim(value, at * width, width, 1)


def forward_attention(normed_all, w_in, in_bias, info, slopes, core, side):
    def attention(normed_all):
        projected = (dot(normed_all, w_in) + in_bias).astype(bf16)
        received = swap(columns_at(projected, 1 - core, 384), "core")
        mine = columns_at(projected, core, 384)
        ctx_mine, ctx_other, logsum, rows = attend(info, slopes, mine, received)
        return in_order(ctx_mine, swap(ctx_other, "core"), core), logsum, rows

    side_done, (context, logsum, rows) = beside(side[0], side[1], normed_all, attention)
    return context, logsum, rows, side_done


def forward_middle(hidden, context, params):
    (project, project_bias, gain_two, offset_two) = params[4:8]
    parts, own = beside(
        dot_others(context, project, dot),
        scatter_parts,
        context,
        lambda v: dot_own(v, project, dot),
    )
    middle = hidden + sum_parts(own, parts) + project_bias
    return middle, norm(middle, gain_two, offset_two).astype(bf16)


def with_rows(middle, normed):
    return middle, gather_z(normed)


def last_send(last, params):
    return dot_others(last[1], params[10], dot)


def last_sum(last, params, parts):
    return last[0] + sum_parts(dot_own(last[1], params[10], dot), parts) + params[11]


def backward_two(grad_down, params, kept, core):
    (up, _, down, _) = params[8:]
    normed_two, before, activated = kept[6:]
    d_act = dot_t(grad_down, down)
    d_before = jax.vjp(gelu, before)[1](d_act)[0].astype(bf16)
    sum_up = jnp.sum(d_before.astype(f32), axis=0)

    def work_two(given):
        activated, grad_down, normed_two, d_before = given
        own = dot_own(d_before, up, dot_t)
        g_down = outer(activated, grad_down).astype(bf16)
        g_up = outer(normed_two, d_before).astype(bf16)
        return own, core_sum(pack_outer(g_down, g_up), core)

    parts, (own, summed) = beside(
        dot_others(d_before, up, dot_t),
        scatter_parts,
        (activated, grad_down, normed_two, d_before),
        work_two,
    )
    return sum_parts(own, parts), summed, sum_up


def backward(gradient, d_normed, sum_up, params, kept, info, slopes, core, across, one):
    (gain_one, _, w_in, _, project, _, gain_two) = params[:7]
    hidden, normed_all, logsum, rows, context, middle = kept[:6]
    sum_down = jnp.sum(gradient.astype(bf16).astype(f32), axis=0)
    d_values, sum_gain_two, sum_offset_two = norm_back(middle, gain_two, d_normed)
    d_middle = gradient + d_values
    grad_out = d_middle.astype(bf16)
    sum_project = jnp.sum(grad_out.astype(f32), axis=0)

    def attention(grad_out):
        grad_out_all = gather_z(grad_out)
        d_context = dot_t(grad_out_all, project).astype(bf16)
        received = swap(columns_at(d_context, 1 - core, 128), "core")
        mine = columns_at(d_context, core, 128)
        d_mine, d_other, sums = attend_back(info, slopes, rows, mine, received, logsum)
        return in_order(d_mine, swap(d_other, "core"), core), sums, grad_out_all

    crossed, (d_joined, sums, grad_out_all) = beside(across[0], across[1], grad_out, attention)

    def work_one(given):
        context, grad_out_all, normed_all, d_joined, crossed = given
        own = dot_own(d_joined, w_in, dot_t)
        g_input = outer(normed_all, d_joined).astype(bf16)
        g_project = outer(context, grad_out_all).astype(bf16)
        return own, one(crossed, g_input, g_project)

    parts, (own, done_one) = beside(
        dot_others(d_joined, w_in, dot_t),
        scatter_parts,
        (context, grad_out_all, normed_all, d_joined, crossed),
        work_one,
    )

    def finish(given):
        own, parts = given
        d_normed_one = sum_parts(own, parts)
        d_hidden, sum_gain_one, sum_offset_one = norm_back(hidden, gain_one, d_normed_one)
        small = (
            sum_gain_one,
            sum_offset_one,
            sum_project,
            sum_gain_two,
            sum_offset_two,
            sum_down,
            sums,
            sum_up,
        )
        return d_middle + d_hidden, small

    return (own, parts), finish, done_one


def take(value, at, axis=0):
    return lax.dynamic_index_in_dim(value, at, axis, keepdims=False)


def groups_first(value, shape):
    split = value.reshape(shape)
    order = (1, 0) + tuple(range(2, len(shape)))
    return split.transpose(order)


def core_sum(pack, core):
    split = pack.reshape(8, 2, 64, -1)
    keep, send = take(split, core, 1), take(split, 1 - core, 1)
    return (keep.astype(f32) + swap(send, "core").astype(f32)).astype(bf16)


def pack_outer(g_down, g_up):
    pieces = (
        groups_first(g_down, (2, 16, 32, D)).reshape(16, 64, D),
        groups_first(g_up, (8, 16, 8, D)).reshape(16, 64, D),
    )
    return jnp.concatenate(pieces, axis=-1)


def pack_inner(g_project, g_input):
    project = g_project.reshape(2, 16, 8, 4, 256).transpose(1, 0, 3, 2, 4).reshape(16, 64, 256)
    return jnp.concatenate(
        [project, groups_first(g_input, (8, 16, 8, 768)).reshape(16, 64, 768)], axis=-1
    )


def to_xy(value):
    return lax.all_to_all(value, ("x", "y_lo"), split_axis=0, concat_axis=0, tiled=True)


def sum_pairs(value, at, axis):
    return take(value, at).astype(f32) + swap(take(value, 1 - at), axis).astype(f32)


def spread_z(both, z):
    columns = both.reshape(4, 8, -1)
    blocks = [take(columns, z)] + [shift_z(take(columns, (z + 4 - k) % 4), 4 - k) for k in (1, 2, 3)]
    blocks = jnp.stack(blocks + blocks)
    return lax.dynamic_slice_in_dim(blocks, (4 - z) % 4, 4, 0).reshape(32, -1)


def y_rows(summed, y_hi):
    return sum_pairs(summed.reshape(2, 32, -1), y_hi, "y_hi").astype(bf16)


def across_y(own, to_hi, to_lo, to_both):
    axes = ("y_lo", "y_hi")
    total = own.astype(f32)
    for value, to in ((to_hi, [1, 0, 3, 2]), (to_lo, [2, 3, 0, 1]), (to_both, [3, 2, 1, 0])):
        total = total + lax.ppermute(value, axes, list(enumerate(to))).astype(f32)
    return total


def inner_core(pack, core):
    split = pack.reshape(4, 2, 2, 64, 1024)
    keep, send = take(split, core, 2), take(split, 1 - core, 2)
    return (keep.astype(f32) + swap(send, "core").astype(f32)).astype(bf16)


def inner_x(low, x):
    total = take(low, x).astype(f32)
    for k in (1, 2, 3):
        total = total + shift_x(take(low, (x + k) % 4), k).astype(f32)
    return total.astype(bf16)


def inner_y(low, y_lo, y_hi):
    split = low.reshape(2, 2, 32, 1024)
    piece = lambda a, b: take(take(split, a), b)
    return across_y(
        piece(y_lo, y_hi),
        piece(y_lo, 1 - y_hi),
        piece(1 - y_lo, y_hi),
        piece(1 - y_lo, 1 - y_hi),
    ).astype(bf16)


def inner_z(both, z):
    return jnp.concatenate([both[:, :256], spread_z(both[:, 256:], z)], axis=1)


def small_z(packed, z):
    split = packed.reshape(2, 4, -1)
    total = take(split, z, 1)
    for k in (1, 2, 3):
        total = total + shift_z(take(split, (z + k) % 4, 1), k)
    return total


def small_y(total, y_hi):
    own, other = take(total, y_hi), take(total, 1 - y_hi)
    return across_y(own, other, own, other)


def small_x(total):
    return total + shift_x(total, 1) + shift_x(total, 2) + shift_x(total, 3)


def unpack_outer_kernel(first, second, down, up):
    for g in range(16):
        down[0, g * 32 : (g + 1) * 32, :] = first[g, :, 0:D].astype(f32)
        for four in range(4):
            rows = first[g, four * 8 : (four + 1) * 8, D : 2 * D].astype(f32)
            for side in range(2):
                at = side * 2048 + four * 512
                up[0, g * 8 : (g + 1) * 8, at : at + 512] = rows[:, side * 512 : (side + 1) * 512]
    for pair in range(2):
        for y_lo in range(2):
            for core in range(2):
                low = second[(pair * 2) * 4 + y_lo * 2 + core].astype(f32)
                high = second[(pair * 2 + 1) * 4 + y_lo * 2 + core].astype(f32)
                for x, block in ((pair * 2, low), (pair * 2 + 1, high)):
                    at = core * 256 + x * 64
                    down[1, at : at + 64, y_lo * 512 : (y_lo + 1) * 512] = block[:, 512:1024]
                for place in range(8):
                    lanes = slice(place * 64, (place + 1) * 64)
                    at = place * 512 + core * 256 + pair * 128
                    up[1, y_lo * 64 : (y_lo + 1) * 64, at : at + 128] = jnp.concatenate(
                        [low[:, lanes], high[:, lanes]], axis=1
                    )


def place_inner(block, layer, row, inputs, project):
    rows = pl.ds(row, 8)
    for four in range(4):
        part_rows = block[four * 8 : (four + 1) * 8, :].astype(f32)
        project[layer, rows, four * 256 : (four + 1) * 256] = part_rows[:, 0:256]
        for side in range(2):
            for part in range(3):
                to = part * D + side * 512 + four * 128
                at = 256 + (side * 3 + part) * 128
                inputs[layer, rows, to : to + 128] = part_rows[:, at : at + 128]


def unpack_inner_kernel(info, mine, other, second, inputs, project):
    core, x, y_lo = info[0], info[4], info[5]
    for pieces, half in ((mine, core), (other, 1 - core)):
        for k in range(4):
            for side in range(2):
                low = y_lo if side == 0 else 1 - y_lo
                g = (((x - k) & 3) * 2 + low) * 2 + half
                place_inner(pieces[k, side], 0, pl.multiple_of(g * 8, 8), inputs, project)
    for g in range(16):
        place_inner(second[g, :, 2048:3072], 1, g * 8, inputs, project)


def unpack_outer(first, second):
    return pl.pallas_call(
        unpack_outer_kernel,
        out_shape=(
            jax.ShapeDtypeStruct((LAYERS, 512, D), f32),
            jax.ShapeDtypeStruct((LAYERS, 128, FF), f32),
        ),
        in_specs=[whole, whole],
        out_specs=(whole, whole),
        compiler_params=params_one,
        name="unpack_outer",
    )(first, second)


def unpack_inner(info, mine, other, second):
    return pl.pallas_call(
        unpack_inner_kernel,
        out_shape=(
            jax.ShapeDtypeStruct((LAYERS, 128, 3072), f32),
            jax.ShapeDtypeStruct((LAYERS, 128, D), f32),
        ),
        in_specs=[smem, whole, whole, whole],
        out_specs=(whole, whole),
        compiler_params=params_one,
        name="unpack_inner",
    )(info, mine, other, second)


def pack_small(small, place):
    (gain_one, offset_one, project, gain_two, offset_two, down, sums, up) = small
    vectors = [
        v.reshape(8, 128) for v in (gain_one, offset_one, project, gain_two, offset_two, down)
    ]
    sums = sums.reshape(-1)
    inputs = lax.dynamic_update_slice_in_dim(jnp.zeros((2 * D,), f32), sums[:128], place * 128, 0)
    inputs = lax.dynamic_update_slice_in_dim(inputs, sums[256:], D + place * 128, 0)
    return jnp.concatenate(vectors + [inputs.reshape(8, 256), up], axis=1)


def on_device(
    inputs,
    cotangent,
    segments,
    norm_one_gain,
    norm_one_bias,
    input_weight,
    input_bias,
    project_weight,
    project_bias,
    norm_two_gain,
    norm_two_bias,
    up_weight,
    up_bias,
    down_weight,
    down_bias,
):
    y_hi, z = lax.axis_index("y_hi"), lax.axis_index("z")
    x, y_lo, core = lax.axis_index("x"), lax.axis_index("y_lo"), lax.axis_index("core")
    place = core * 4 + z
    rows_in = regroup(inputs[0], core, y_hi)
    cut = jnp.sum((segments[0] < 2).astype(jnp.int32))
    cut = regroup(jnp.broadcast_to(cut, (1, 128)), core, y_hi)[0, 0]
    info = jnp.stack([core, z, cut, y_hi]).astype(jnp.int32)
    corner = jnp.stack([core, z, y_hi, core * 4 + x, x, y_lo]).astype(jnp.int32)
    heads = (place * 2 + jnp.arange(2, dtype=jnp.int32)).astype(f32)
    slopes = jnp.exp2(-8.0 * (heads + 1.0) / HEADS)

    small = jnp.concatenate(
        [
            norm_one_gain,
            norm_one_bias,
            project_bias,
            norm_two_gain,
            norm_two_bias,
            down_bias,
            input_bias,
            up_bias,
        ],
        axis=1,
    )
    small = jnp.concatenate([small.reshape(4, 768), jnp.zeros((12, 768), bf16)], axis=0)
    first = pack_first(corner[3:4], input_weight, small)
    rows_in, first = lax.optimization_barrier((rows_in, first))
    first = to_ctx(first)
    raw_all = gather_z(rows_in)
    corner_late, first = lax.optimization_barrier((corner, first))
    first, raw_all = lax.optimization_barrier((first, raw_all))
    vectors, in_bias, unit_bias = read_small(corner, first)
    w_first = gather_x(first[:, 0:16].reshape(128, 768))
    w_first = join_columns(corner, w_first, swap(w_first, "core"))
    up_zero, second, rows, wide = pack_rest(
        corner_late, input_weight, up_weight, down_weight, project_weight
    )
    wide = lax.all_gather(wide, CTX, axis=0, tiled=True)
    rows_zero = swap(rows, "y_hi")
    vector = [vectors[i] for i in range(12)]
    nothing = (jnp.zeros((8, 128), f32), lambda v: v)
    unit_wide = first[:, 19:20, 256:768].reshape(8, 2, 4, 64)
    unit_wide = lax.dynamic_index_in_dim(unit_wide, core, 1, keepdims=False)
    unit_wide = unit_wide.transpose(1, 0, 2).reshape(4, 1, 512).astype(f32)
    hidden = rows_in.astype(f32)
    normed_all = norm(raw_all.astype(f32), vectors[0], vectors[1]).astype(bf16)
    context, logsum, rows_kept, (up_zero, pieces) = forward_attention(
        normed_all,
        w_first,
        in_bias[0],
        info,
        slopes,
        core,
        ((up_zero, rows_zero), lambda v: (to_ctx(v[0]), gather_x(v[1]))),
    )
    down_zero, project_zero, project_one = join_rows(
        corner, down_weight, project_weight, pieces, swap(pieces, "core")
    )
    params_0 = (
        vector[0],
        vector[1],
        w_first,
        in_bias[0],
        project_zero,
        vector[2],
        vector[3],
        vector[4],
    )
    wide, context = lax.optimization_barrier((wide, context))
    wide = lax.all_gather(wide, "x")
    (up_zero, second), (middle, normed_two) = beside(
        (up_zero.reshape(128, D), second),
        lambda v: (gather_x(v[0]), to_ctx(v[1])),
        (hidden, context),
        lambda v: with_rows(*forward_middle(*v, params_0)),
    )
    up_zero = join_columns(corner, up_zero, swap(up_zero, "core"))
    params_0 = params_0 + (up_zero, unit_bias[0], down_zero, vector[5])
    before = dot(normed_two, up_zero) + unit_bias[0]
    activated = gelu(before).astype(bf16)
    last = (middle, activated)
    kept_0 = (hidden, normed_all, logsum, rows_kept, context, middle, normed_two, before, activated)
    w_second = gather_x(second.reshape(128, 768))
    w_second = join_columns(corner, w_second, swap(w_second, "core"))
    hidden = last_sum(last, params_0, scatter_parts(last_send(last, params_0)))
    params_1 = (
        vector[6],
        vector[7],
        w_second,
        in_bias[1],
        project_one,
        vector[8],
        vector[9],
        vector[10],
    )
    normed_all = gather_z(norm(hidden, vector[6], vector[7]).astype(bf16))
    gradient = regroup(cotangent[0], core, y_hi)
    context, logsum, rows_kept, grad_other = forward_attention(
        normed_all, w_second, in_bias[1], info, slopes, core, (gradient, lambda v: swap(v, "core"))
    )
    middle, normed_two = forward_middle(hidden, context, params_1)
    pair_rows = jnp.concatenate([normed_two, swap(normed_two, "core")])
    own, other, before = wide_forward(pair_rows, wide, unit_wide)
    output = middle + (own + swap(other, "core").astype(f32)) + vector[11]
    kept_1 = (hidden, normed_all, logsum, rows_kept, context, middle)
    own, other, sum_up, wide_grads = wide_back(
        jnp.concatenate([gradient, grad_other]), pair_rows, before, wide
    )
    d_normed = own + swap(other, "core").astype(f32)
    wide_grads = lax.psum_scatter(wide_grads, "x", scatter_dimension=0, tiled=True)[0]
    units = lax.dynamic_update_slice_in_dim(
        jnp.zeros((8, 2, 4, 64), f32), sum_up.reshape(4, 8, 64).transpose(1, 0, 2)[:, None], core, 1
    )
    gradient = gradient.astype(f32)

    left, finish, inner_1 = backward(
        gradient,
        d_normed,
        units.reshape(8, 512),
        params_1,
        kept_1,
        info,
        slopes,
        core,
        nothing,
        lambda crossed, g_input, g_project: pack_inner(g_project, g_input),
    )
    gradient, small_1 = finish(left)
    grad_down = gather_z(gradient.astype(bf16))
    grad_down, wide_grads, inner_1 = lax.optimization_barrier((grad_down, wide_grads, inner_1))
    inner_1 = lax.psum_scatter(inner_1, GRP, scatter_dimension=0, tiled=True)[0]

    def to_owners(value):
        axes = ("y_lo",) + CTX
        return lax.all_to_all(value, axes, split_axis=0, concat_axis=0, tiled=True)

    wide_grads, (d_normed, summed, sum_up) = beside(
        wide_grads.reshape(16, 64, D),
        to_owners,
        grad_down,
        lambda v: backward_two(v, params_0, kept_0, core),
    )
    wide_grads = lax.all_gather(jnp.sum(wide_grads.astype(f32), axis=0).astype(bf16), GRP)
    units = lax.dynamic_update_slice_in_dim(
        jnp.zeros((2, 4, 512), f32), sum_up.reshape(2, 1, 512), z, 1
    )

    def work_one(got, g_input, g_project):
        low = inner_core(pack_inner(g_project, g_input), core)
        both = jnp.concatenate([jnp.sum(got.astype(f32), axis=0).astype(bf16), inner_1], axis=1)
        both = y_rows(both, y_hi)
        spread = spread_z(jnp.concatenate([both[:, D : 2 * D], both[:, 2 * D + 256 :]], axis=1), z)
        both = jnp.concatenate(
            [both[:, :D], spread[:, :D], both[:, 2 * D : 2 * D + 256], spread[:, D:]], axis=1
        )
        return low, both

    left, finish, (low, both) = backward(
        gradient,
        d_normed,
        units.reshape(8, 512),
        params_0,
        kept_0,
        info,
        slopes,
        core,
        (summed, to_xy),
        work_one,
    )
    low, (gradient, small_0) = beside(low, lambda v: inner_x(v, x), left, finish)
    full = lax.all_gather(both, GRP)
    packed = jnp.concatenate([pack_small(s, place) for s in (small_0, small_1)], axis=1)
    low, packed = beside(
        low, lambda v: inner_y(v, y_lo, y_hi), packed, lambda v: small_z(v, z)
    )
    low, (packed, gradient) = beside(
        low,
        lambda v: inner_z(v, z),
        (packed, gradient),
        lambda v: (small_y(v[0], y_hi), regroup(v[1], core, y_hi)),
    )
    low, packed = beside(low, lambda v: jnp.stack([v, swap(v, "y_lo")]), packed, small_x)
    low, packed = beside(low, gather_x, packed, lambda v: v + swap(v, "core"))
    g_input, g_project = unpack_inner(corner, low, swap(low, "core"), full)
    g_down, g_up = unpack_outer(full, wide_grads)
    vector = packed.reshape(LAYERS, -1)
    parts = [vector[:, i * 128 : (i + 1) * 128] for i in range(6)]
    return (
        regroup(output, core, y_hi)[None],
        gradient[None],
        parts[0],
        parts[1],
        g_input,
        vector[:, 768:1024],
        g_project,
        parts[2],
        parts[3],
        parts[4],
        g_up,
        vector[:, 1024:1536],
        g_down,
        parts[5],
    )


def solution(mesh):
    split = Mesh(mesh.devices.reshape(4, 2, 2, 2, 4), GRP + CTX)
    rows = P(GRP, CTX, None)
    vector = P(None, CTX)
    matrix = P(None, CTX, None)
    weights = (
        vector,
        vector,
        matrix,
        vector,
        matrix,
        vector,
        vector,
        vector,
        matrix,
        vector,
        matrix,
        vector,
    )
    return jax.shard_map(
        on_device,
        mesh=split,
        in_specs=(rows, rows, P(GRP, None)) + weights,
        out_specs=(rows, rows) + weights,
        check_vma=False,
    )
```

time: 732 us -> 682 us (0.932)
  waiting for transfers between devices: 323 us -> 267 us
  Pallas kernels: 54.2 us -> 75.7 us
  blocking collectives: 19.7 us -> 0 us
  other arithmetic: 49.7 us -> 68.1 us
  matrix products: 52.5 us -> 41.6 us
    ppermute x60 -> x45, waiting for transfers between devices: 245 us -> 200 us  [shift_z(): return lax.ppermute(value, 'z', [(i, (i + step) % 4) for i in range(4)])]
    ppermute x23, waiting for transfers between devices: 43.2 us -> 19.4 us  [swap(): return lax.ppermute(value, axis, [(0, 1), (1, 0)])]
    pallas_call x4 -> x6, Pallas kernels: 7.03 us -> 28.9 us  [the longest x1 14.8 us: wide_back(): pl.pallas_call(wide_back_kernel, grid=(4,), out_shape=(jax.ShapeDtypeStru...]
    ppermute x6 -> x21, waiting for transfers between devices: 8.29 us -> 28.1 us  [shift_x(): return lax.ppermute(value, 'x', [(i, (i + step) % 4) for i in range(4)])]
    all_gather x1 -> x0, blocking collectives: 19.7 us -> none  [on_device(): input_0 = lax.all_gather(input_0, GRP)]
    ppermute x5, waiting for transfers between devices: 14.1 us -> 0.52 us  [regroup(): got = lax.ppermute(value, ('core', 'y_hi'), [(1, 2), (2, 1)])]
    ppermute x60 -> x45, starting transfers between devices: 64.9 us -> 51.8 us  [shift_z(): return lax.ppermute(value, 'z', [(i, (i + step) % 4) for i in range(4)])]
    all_to_all x1, starting transfers between devices: 17.5 us -> 4.46 us  [to_owners(): return lax.all_to_all(value, axes, split_axis=0, concat_axis=0, tiled=True)]
  transfers between devices with their start and end apart: 105 -> 111, of which waited for: 57 -> 59; matrix products, arithmetic and copies ran while one was open for 13% -> 17% of each run, Pallas kernels for 4% -> 7%
where the time goes in v5:
time: 682 us; the launch traced here: 674 us
  waiting for transfers between devices  267 us (39%)
  starting transfers between devices  166 us (24%)
  Pallas kernels  75.7 us (11%)
  other arithmetic  68.1 us (10%)
  matrix products  41.6 us (6%)
  local copies, waits for them, and re-layouts  39.4 us (6%)
  between operations  16.6 us (2%)
    ppermute x45, waiting for transfers between devices, shift_z(): return lax.ppermute(value, 'z', [(i, (i + step) % 4) for i in range(4)])  200 us
    ppermute x45, starting transfers between devices, shift_z(): return lax.ppermute(value, 'z', [(i, (i + step) % 4) for i in range(4)])  51.8 us
    ppermute x5, starting transfers between devices, regroup(): got = lax.ppermute(value, ('core', 'y_hi'), [(1, 2), (2, 1)])  31.9 us
    ppermute x21, waiting for transfers between devices, shift_x(): return lax.ppermute(value, 'x', [(i, (i + step) % 4) for i in range(4)])  28.1 us
    unnamed x250, local copies, waits for them, and re-layouts  23.8 us
    ppermute x23, starting transfers between devices, swap(): return lax.ppermute(value, axis, [(0, 1), (1, 0)])  23.1 us
    ppermute x21, starting transfers between devices, shift_x(): return lax.ppermute(value, 'x', [(i, (i + step) % 4) for i in range(4)])  22.6 us
    dot_general x9, matrix products, dot_t(): lax.dot_general(left, right, (((1,), (1,)), ((), ())), preferred_element_...  21.7 us
  transfers between devices with their start and end apart: 111, of which 59 were waited for; matrix products, arithmetic and copies ran while one was open for 17% of the time, Pallas kernels for 7%

profile of v5, /device:TPU:1, one launch (start us, length us, event | category | flops | bytes accessed | tf_op | source)
XLA Modules:
  0.0 674.4 jit_solution(4558737428938858359)
XLA Ops:
  7.2 6.3 collective-permute-start
  23.0 5.0 all-to-all-start
  28.2 8.1 %all-to-all-done.got = bf16[8,32,768]{2,1,0:T(8,128)(2,1)S(1)} async-done(((bf16[8,32,768]{2,1,0:T(8,128)(2,1)}), bf16[8,32,768]{2,1,0:T(8,128)(2,1)S(1)}, u32[]{:S(2)}, u32[]{:S(2)}) %all-to-all-start) | async-done | bytes 393248 | tf_op jit(solution)/shard_map/all_to_all | solution.py:577
  45.1 5.8 collective-permute-done.2
  50.9 9.0 %collective-permute-done.3 = bf16[192,1024]{1,0:T(8,128)(2,1)S(1)} collective-permute-done((bf16[192,1024]{1,0:T(8,128)(2,1)}, bf16[192,1024]{1,0:T(8,128)(2,1)S(1)}, u32[]{:S(2)}, u32[]{:S(2)}) %collective-permute-start.3) | collective-permute-done | bytes 393248 | tf_op jit(solution)/shard_map/ppermute | solution.py:31
  59.8 5.1 collective-permute-done.4
  72.5 3.9 collective-permute-done.10
  76.5 3.7 collective-permute-start.12
  86.9 3.0 collective-permute-start.8
  95.3 9.5 %attend.2 = (bf16[768,128]{1,0:T(8,128)(2,1)S(1)}, bf16[768,128]{1,0:T(8,128)(2,1)}, f32[2,1536]{1,0:T(2,128)S(1)}, bf16[1536,384]{1,0:T(8,128)(2,1)S(1)}) custom-call(s32[4]{0:T(128)S(1)} %pad_add_fusion.info, f32[2]{0:T(128)S(1)} %multiply_exponential_fusion.slopes, bf16[768,384]{1,0:T(8,128)(2,1)S(1)} %get-tuple-element.388.mine, ...), custom_call_target="tpu_custom_call" | custom-call | flops 1000000 | bytes 36000000 | tf_op jit(solution)/shard_map/attend/pallas_call | solution.py:208
  106.5 7.6 %all-to-all-start.1 = ((bf16[8,16,1024]{2,1,0:T(8,128)(2,1)}), bf16[8,16,1024]{2,1,0:T(8,128)(2,1)}, u32[]{:S(2)}, u32[]{:S(2)}) async-start(bf16[8,16,1024]{2,1,0:T(8,128)(2,1)} %get-tuple-element.181), calls=%async_computation.1 | async-start | bytes 524288 | tf_op jit(solution)/shard_map/all_to_all | solution.py:577
  117.4 4.4 all-to-all-done.1
  132.2 7.2 %collective-permute-done.19 = bf16[192,1024]{1,0:T(8,128)(2,1)S(1)} collective-permute-done((bf16[192,1024]{1,0:T(8,128)(2,1)S(1)}, bf16[192,1024]{1,0:T(8,128)(2,1)S(1)}, u32[]{:S(2)}, u32[]{:S(2)}) %collective-permute-start.19) | collective-permute-done | bytes 393248 | tf_op jit(solution)/shard_map/ppermute | solution.py:31
  141.3 9.5 %collective-permute-done.21 = bf16[192,1024]{1,0:T(8,128)(2,1)S(1)} collective-permute-done((bf16[192,1024]{1,0:T(8,128)(2,1)S(1)}, bf16[192,1024]{1,0:T(8,128)(2,1)S(1)}, u32[]{:S(2)}, u32[]{:S(2)}) %collective-permute-start.21) | collective-permute-done | bytes 393248 | tf_op jit(solution)/shard_map/ppermute | solution.py:31
  155.3 4.0 all-to-all-start.2
  161.5 11.8 %collective-permute-done.22 = bf16[192,1024]{1,0:T(8,128)(2,1)S(1)} collective-permute-done((bf16[192,1024]{1,0:T(8,128)(2,1)S(1)}, bf16[192,1024]{1,0:T(8,128)(2,1)S(1)}, u32[]{:S(2)}, u32[]{:S(2)}) %collective-permute-start.22) | collective-permute-done | bytes 393248 | tf_op jit(solution)/shard_map/ppermute | solution.py:31
  180.9 4.1 multiply_convert_fusion
  191.9 9.8 %collective-permute-done.35 = bf16[128,768]{1,0:T(8,128)(2,1)S(1)} collective-permute-done((bf16[128,768]{1,0:T(8,128)(2,1)}, bf16[128,768]{1,0:T(8,128)(2,1)S(1)}, u32[]{:S(2)}, u32[]{:S(2)}) %collective-permute-start.35) | collective-permute-done | bytes 196640 | tf_op jit(solution)/shard_map/ppermute | solution.py:35
  201.8 4.5 collective-permute-start.29
  218.8 5.8 collective-permute-done.30
  224.5 9.1 %collective-permute-done.31 = bf16[192,1024]{1,0:T(8,128)(2,1)S(1)} collective-permute-done((bf16[192,1024]{1,0:T(8,128)(2,1)S(1)}, bf16[192,1024]{1,0:T(8,128)(2,1)S(1)}, u32[]{:S(2)}, u32[]{:S(2)}) %collective-permute-start.31) | collective-permute-done | bytes 393248 | tf_op jit(solution)/shard_map/ppermute | solution.py:31
  238.0 8.3 %attend.3 = (bf16[768,128]{1,0:T(8,128)(2,1)S(1)}, bf16[768,128]{1,0:T(8,128)(2,1)S(1)}, f32[2,1536]{1,0:T(2,128)S(1)}, bf16[1536,384]{1,0:T(8,128)(2,1)S(1)}) custom-call(s32[4]{0:T(128)S(1)} %pad_add_fusion.info, f32[2]{0:T(128)S(1)} %multiply_exponential_fusion.slopes, bf16[768,384]{1,0:T(8,128)(2,1)S(1)} %get-tuple-element.380.mine, ...), custom_call_target="tpu_custom_call" | custom-call | flops 1000000 | bytes 36000000 | tf_op jit(solution)/shard_map/attend/pallas_call | solution.py:208
  253.0 7.4 %collective-permute-done.40 = bf16[192,1024]{1,0:T(8,128)(2,1)S(1)} collective-permute-done((bf16[192,1024]{1,0:T(8,128)(2,1)S(1)}, bf16[192,1024]{1,0:T(8,128)(2,1)S(1)}, u32[]{:S(2)}, u32[]{:S(2)}) %collective-permute-start.40) | collective-permute-done | bytes 393248 | tf_op jit(solution)/shard_map/ppermute | solution.py:31
  260.4 2.8 collective-permute-done.41
  263.2 9.4 %collective-permute-done.42 = bf16[192,1024]{1,0:T(8,128)(2,1)S(1)} collective-permute-done((bf16[192,1024]{1,0:T(8,128)(2,1)S(1)}, bf16[192,1024]{1,0:T(8,128)(2,1)S(1)}, u32[]{:S(2)}, u32[]{:S(2)}) %collective-permute-start.42) | collective-permute-done | bytes 393248 | tf_op jit(solution)/shard_map/ppermute | solution.py:31
  280.4 9.1 %wide_forward.1 = (f32[192,1024]{1,0:T(8,128)}, bf16[192,1024]{1,0:T(8,128)(2,1)}, f32[4,384,512]{2,1,0:T(8,128)}) custom-call(bf16[384,1024]{1,0:T(8,128)(2,1)} %pad_maximum_fusion.10.rows, bf16[4,1024,1024]{2,1,0:T(8,128)(2,1)} %bitcast.342, f32[4,1,512]{2,1,0:T(1,128)} %reshape.350.bias), custom_call_target="tpu_custom_call" | custom-call | flops 3221225472 | bytes 20000000 | tf_op jit(solution)/shard_map/wide_forward/pallas_call | solution.py:329
  289.6 14.8 %wide_back.1 = (f32[192,1024]{1,0:T(8,128)}, bf16[192,1024]{1,0:T(8,128)(2,1)}, f32[4,1,512]{2,1,0:T(1,128)}, bf16[4,2,8,64,1024]{4,3,2,1,0:T(8,128)(2,1)}) custom-call(bf16[384,1024]{1,0:T(8,128)(2,1)} %pad_maximum_fusion.11.grads, bf16[384,1024]{1,0:T(8,128)(2,1)} %pad_maximum_fusion.10.rows, f32[4,384,512]{2,1,0:T(8,128)} %get-tuple-element.230.before, ...), custom_call_target="tpu_custom_call" | custom-call | flops 8053063680 | bytes 40000000 | tf_op jit(solution)/shard_map/wide_back/pallas_call | solution.py:382
  308.9 3.4 convert_reduce_fusion.3
  315.3 17.3 %collective-permute-done.47 = bf16[192,1024]{1,0:T(8,128)(2,1)S(1)} collective-permute-done((bf16[192,1024]{1,0:T(8,128)(2,1)S(1)}, bf16[192,1024]{1,0:T(8,128)(2,1)S(1)}, u32[]{:S(2)}, u32[]{:S(2)}) %collective-permute-start.47) | collective-permute-done | bytes 393248 | tf_op jit(solution)/shard_map/ppermute | solution.py:31
  337.6 10.7 %attend_back.2 = (bf16[768,384]{1,0:T(8,128)(2,1)S(1)}, bf16[768,384]{1,0:T(8,128)(2,1)S(1)}, f32[1,384]{1,0:T(1,128)S(1)}) custom-call(s32[4]{0:T(128)S(1)} %pad_add_fusion.info, f32[2]{0:T(128)S(1)} %multiply_exponential_fusion.slopes, bf16[1536,384]{1,0:T(8,128)(2,1)S(1)} %copy-done.22, bf16[768,128]{1,0:T(8,128)(2,1)S(1)} %get-tuple-element.396.mine, ...), custom_call_target="tpu_custom_call" | custom-call | flops 1000000 | bytes 48000000 | tf_op jit(solution)/shard_map/attend_back/pallas_call | solution.py:232
  363.3 4.7 collective-permute-done.52
  368.0 2.8 collective-permute-done.53
  370.8 8.8 %collective-permute-done.54 = bf16[192,1024]{1,0:T(8,128)(2,1)} collective-permute-done((bf16[192,1024]{1,0:T(8,128)(2,1)}, bf16[192,1024]{1,0:T(8,128)(2,1)}, u32[]{:S(2)}, u32[]{:S(2)}) %collective-permute-start.54) | collective-permute-done | bytes 393248 | tf_op jit(solution)/shard_map/ppermute | solution.py:31
  386.5 16.6 %collective-permute-done.55 = bf16[192,1024]{1,0:T(8,128)(2,1)S(1)} collective-permute-done((bf16[192,1024]{1,0:T(8,128)(2,1)S(1)}, bf16[192,1024]{1,0:T(8,128)(2,1)S(1)}, u32[]{:S(2)}, u32[]{:S(2)}) %collective-permute-start.55) | collective-permute-done | bytes 393248 | tf_op jit(solution)/shard_map/ppermute | solution.py:31
  405.9 6.7 convert_reduce_fusion.1
  412.6 2.5 convolution_convert_fusion.5
  425.2 4.5 all-to-all-start.3
  432.3 2.5 collective-permute-start.58
  438.3 4.0 fusion
  442.4 20.3 %collective-permute-done.58 = bf16[192,1024]{1,0:T(8,128)(2,1)} collective-permute-done((bf16[192,1024]{1,0:T(8,128)(2,1)}, bf16[192,1024]{1,0:T(8,128)(2,1)}, u32[]{:S(2)}, u32[]{:S(2)}) %collective-permute-start.58) | collective-permute-done | bytes 393248 | tf_op jit(solution)/shard_map/ppermute | solution.py:31
  463.7 9.0 %collective-permute-done.60 = bf16[192,1024]{1,0:T(8,128)(2,1)} collective-permute-done((bf16[192,1024]{1,0:T(8,128)(2,1)}, bf16[192,1024]{1,0:T(8,128)(2,1)}, u32[]{:S(2)}, u32[]{:S(2)}) %collective-permute-start.60) | collective-permute-done | bytes 393248 | tf_op jit(solution)/shard_map/ppermute | solution.py:31
  481.0 5.9 all-to-all-start.4
  489.1 7.3 %collective-permute-done.63 = bf16[192,1024]{1,0:T(8,128)(2,1)S(1)} collective-permute-done((bf16[192,1024]{1,0:T(8,128)(2,1)}, bf16[192,1024]{1,0:T(8,128)(2,1)S(1)}, u32[]{:S(2)}, u32[]{:S(2)}) %collective-permute-start.63) | collective-permute-done | bytes 393248 | tf_op jit(solution)/shard_map/ppermute | solution.py:31
  500.9 10.6 %attend_back.3 = (bf16[768,384]{1,0:T(8,128)(2,1)S(1)}, bf16[768,384]{1,0:T(8,128)(2,1)S(1)}, f32[1,384]{1,0:T(1,128)S(1)}) custom-call(s32[4]{0:T(128)S(1)} %pad_add_fusion.info, f32[2]{0:T(128)S(1)} %multiply_exponential_fusion.slopes, bf16[1536,384]{1,0:T(8,128)(2,1)S(1)} %copy-done.20, bf16[768,128]{1,0:T(8,128)(2,1)S(1)} %get-tuple-element.394.mine, ...), custom_call_target="tpu_custom_call" | custom-call | flops 1000000 | bytes 48000000 | tf_op jit(solution)/shard_map/attend_back/pallas_call | solution.py:232
  512.7 5.4 collective-permute-start.45
  518.9 2.8 reduce_sum.381
  522.6 2.5 maximum_select_fusion.1
  525.1 3.3 convolution_convert_fusion.4
  536.6 2.6 fusion.38
  539.3 7.9 %collective-permute-done.71 = bf16[32,3072]{1,0:T(8,128)(2,1)S(1)} collective-permute-done((bf16[32,3072]{1,0:T(8,128)(2,1)S(1)}, bf16[32,3072]{1,0:T(8,128)(2,1)S(1)}, u32[]{:S(2)}, u32[]{:S(2)}) %collective-permute-start.71) | collective-permute-done | bytes 196640 | tf_op jit(solution)/shard_map/ppermute | solution.py:39
  552.9 7.7 %collective-permute-done.73 = bf16[8,1792]{1,0:T(8,128)(2,1)S(1)} collective-permute-done((bf16[8,1792]{1,0:T(8,128)(2,1)S(1)}, bf16[8,1792]{1,0:T(8,128)(2,1)S(1)}, u32[]{:S(2)}, u32[]{:S(2)}) %collective-permute-start.73) | collective-permute-done | bytes 28704 | tf_op jit(solution)/shard_map/ppermute | solution.py:31
  560.6 8.1 %collective-permute-start.74 = (bf16[8,1792]{1,0:T(8,128)(2,1)S(1)}, bf16[8,1792]{1,0:T(8,128)(2,1)S(1)}, u32[]{:S(2)}, u32[]{:S(2)}) collective-permute-start(bf16[8,1792]{1,0:T(8,128)(2,1)S(1)} %get-tuple-element.402), channel_id=1, source_target_pairs={{0,1},{1,2},{2,3},{3,0},{4,5},{5,6},{6,7},{7,4},{8,9},{9,10},{10,1... | collective-permute-start | bytes 86024 | tf_op jit(solution)/shard_map/ppermute | solution.py:31
  568.7 2.9 collective-permute-done.74
  574.1 6.1 collective-permute-done.69
  586.0 5.5 collective-permute-done.75
  596.9 4.2 collective-permute-start.78
  603.9 3.6 collective-permute-done.79
  610.2 12.7 %collective-permute-start.90 = (f32[192,1024]{1,0:T(8,128)S(1)}, f32[192,1024]{1,0:T(8,128)S(1)}, u32[]{:S(2)}, u32[]{:S(2)}) collective-permute-start(f32[192,1024]{1,0:T(8,128)S(1)} %multiply_add_fusion), channel_id=1, source_target_pairs={{4,8},{8,4},{5,9},{9,5},{6,10},{10,6},{7,11},{11,7},{20,24},{24,20... | collective-permute-start | bytes 2359304 | tf_op jit(solution)/shard_map/ppermute | solution.py:43
  623.0 4.0 collective-permute-done.85
  627.0 3.8 collective-permute-done.86
  634.9 3.4 collective-permute-start.93
  648.2 2.7 collective-permute-done.95
  660.5 4.1 unpack_outer.1
  664.5 2.8 unpack_inner.1
  (610 shorter events, 235.5 us)
Async XLA Ops:
  7.2 13.9 %collective-permute-start = (bf16[192,1024]{1,0:T(8,128)(2,1)}, bf16[192,1024]{1,0:T(8,128)(2,1)}, u32[]{:S(2)}, u32[]{:S(2)}) collective-permute-start(bf16[192,1024]{1,0:T(8,128)(2,1)} %bitcast.294), channel_id=1, source_target_pairs={{4,8},{8,4},{5,9},{9,5},{6,10},{10,6},{7,11},{11,7},{20,24},{24,20... | collective-permute-start | bytes 1179656 | tf_op jit(solution)/shard_map/ppermute | solution.py:43
  23.0 13.2 %all-to-all-start = ((bf16[8,32,768]{2,1,0:T(8,128)(2,1)}), bf16[8,32,768]{2,1,0:T(8,128)(2,1)S(1)}, u32[]{:S(2)}, u32[]{:S(2)}) async-start(bf16[8,32,768]{2,1,0:T(8,128)(2,1)} %pack_first.1), calls=%async_computation | async-start | bytes 786432 | tf_op jit(solution)/shard_map/all_to_all | solution.py:577
  28.1 93.8 %all-gather.8.cloned.1.call-start = ((), (), s32[]{:S(2)}) async-start(), calls=%async_computation.7 | async-start | bytes 2359296 | tf_op jit(solution)/shard_map/all_gather | solution.py:947
  41.0 18.8 %collective-permute-start.3 = (bf16[192,1024]{1,0:T(8,128)(2,1)}, bf16[192,1024]{1,0:T(8,128)(2,1)S(1)}, u32[]{:S(2)}, u32[]{:S(2)}) collective-permute-start(bf16[192,1024]{1,0:T(8,128)(2,1)} %broadcast_select_fusion.2), channel_id=1, source_target_pairs={{0,2},{1,3},{2,0},{3,1},{4,6},{5,7},{6,4},{7,5},{8,10},{9,11},{10,... | collective-permute-start | bytes 1179656 | tf_op jit(solution)/shard_map/ppermute | solution.py:31
  43.0 21.9 %collective-permute-start.4 = (bf16[192,1024]{1,0:T(8,128)(2,1)}, bf16[192,1024]{1,0:T(8,128)(2,1)}, u32[]{:S(2)}, u32[]{:S(2)}) collective-permute-start(bf16[192,1024]{1,0:T(8,128)(2,1)} %broadcast_select_fusion.2), channel_id=1, source_target_pairs={{0,3},{1,0},{2,1},{3,2},{4,7},{5,4},{6,5},{7,6},{8,11},{9,8},{10,9... | collective-permute-start | bytes 1179656 | tf_op jit(solution)/shard_map/ppermute | solution.py:31
  43.9 38.2 %collective-permute-start.1 = (bf16[96,1024]{1,0:T(8,128)(2,1)S(1)}, bf16[96,1024]{1,0:T(8,128)(2,1)S(1)}, u32[]{:S(2)}, u32[]{:S(2)}) collective-permute-start(bf16[96,1024]{1,0:T(8,128)(2,1)S(1)} %get-tuple-element.175), channel_id=1, source_target_pairs={{0,4},{4,0},{1,5},{5,1},{2,6},{6,2},{3,7},{7,3},{8,12},{12,8},{9,1... | collective-permute-start | bytes 589832 | tf_op jit(solution)/shard_map/ppermute | solution.py:39
  89.9 24.3 %collective-permute-start.5 = (bf16[96,1024]{1,0:T(8,128)(2,1)}, bf16[96,1024]{1,0:T(8,128)(2,1)}, u32[]{:S(2)}, u32[]{:S(2)}) collective-permute-start(bf16[96,1024]{1,0:T(8,128)(2,1)} %copy-done.68), channel_id=1, source_target_pairs={{0,32},{32,64},{64,96},{96,0},{1,33},{33,65},{65,97},{97,1},{2,34}... | collective-permute-start | bytes 589832 | tf_op jit(solution)/shard_map/ppermute | solution.py:35
  91.0 23.2 %collective-permute-start.6 = (bf16[96,1024]{1,0:T(8,128)(2,1)}, bf16[96,1024]{1,0:T(8,128)(2,1)}, u32[]{:S(2)}, u32[]{:S(2)}) collective-permute-start(bf16[96,1024]{1,0:T(8,128)(2,1)} %copy-done.68), channel_id=1, source_target_pairs={{0,64},{32,96},{64,0},{96,32},{1,65},{33,97},{65,1},{97,33},{2,66}... | collective-permute-start | bytes 589832 | tf_op jit(solution)/shard_map/ppermute | solution.py:35
  93.1 21.1 %collective-permute-start.7 = (bf16[96,1024]{1,0:T(8,128)(2,1)}, bf16[96,1024]{1,0:T(8,128)(2,1)}, u32[]{:S(2)}, u32[]{:S(2)}) collective-permute-start(bf16[96,1024]{1,0:T(8,128)(2,1)} %copy-done.68), channel_id=1, source_target_pairs={{0,96},{32,0},{64,32},{96,64},{1,97},{33,1},{65,33},{97,65},{2,98}... | collective-permute-start | bytes 589832 | tf_op jit(solution)/shard_map/ppermute | solution.py:35
  106.5 15.3 %all-to-all-start.1 = ((bf16[8,16,1024]{2,1,0:T(8,128)(2,1)}), bf16[8,16,1024]{2,1,0:T(8,128)(2,1)}, u32[]{:S(2)}, u32[]{:S(2)}) async-start(bf16[8,16,1024]{2,1,0:T(8,128)(2,1)} %get-tuple-element.181), calls=%async_computation.1 | async-start | bytes 524288 | tf_op jit(solution)/shard_map/all_to_all | solution.py:577
  114.1 166.3 %all-gather.10.cloned.1.call-start = ((), (), s32[]{:S(2)}) async-start(), calls=%async_computation.10 | async-start | bytes 10485760 | tf_op jit(solution)/shard_map/all_gather | solution.py:979
  129.7 11.6 %collective-permute-start.20 = (bf16[192,1024]{1,0:T(8,128)(2,1)S(1)}, bf16[192,1024]{1,0:T(8,128)(2,1)S(1)}, u32[]{:S(2)}, u32[]{:S(2)}) collective-permute-start(bf16[192,1024]{1,0:T(8,128)(2,1)S(1)} %get-tuple-element.385), channel_id=1, source_target_pairs={{0,2},{1,3},{2,0},{3,1},{4,6},{5,7},{6,4},{7,5},{8,10},{9,11},{10,... | collective-permute-start | bytes 1179656 | tf_op jit(solution)/shard_map/ppermute | solution.py:31
  130.9 19.9 %collective-permute-start.21 = (bf16[192,1024]{1,0:T(8,128)(2,1)S(1)}, bf16[192,1024]{1,0:T(8,128)(2,1)S(1)}, u32[]{:S(2)}, u32[]{:S(2)}) collective-permute-start(bf16[192,1024]{1,0:T(8,128)(2,1)S(1)} %get-tuple-element.384), channel_id=1, source_target_pairs={{0,1},{1,2},{2,3},{3,0},{4,5},{5,6},{6,7},{7,4},{8,9},{9,10},{10,1... | collective-permute-start | bytes 1179656 | tf_op jit(solution)/shard_map/ppermute | solution.py:31
  130.9 22.4 %collective-permute-start.15 = (bf16[128,1024]{1,0:T(8,128)(2,1)}, bf16[128,1024]{1,0:T(8,128)(2,1)S(1)}, u32[]{:S(2)}, u32[]{:S(2)}) collective-permute-start(bf16[128,1024]{1,0:T(8,128)(2,1)} %bitcast.19), channel_id=1, source_target_pairs={{0,32},{32,64},{64,96},{96,0},{1,33},{33,65},{65,97},{97,1},{2,34}... | collective-permute-start | bytes 786440 | tf_op jit(solution)/shard_map/ppermute | solution.py:35
  131.1 28.3 %collective-permute-start.16 = (bf16[128,1024]{1,0:T(8,128)(2,1)}, bf16[128,1024]{1,0:T(8,128)(2,1)S(1)}, u32[]{:S(2)}, u32[]{:S(2)}) collective-permute-start(bf16[128,1024]{1,0:T(8,128)(2,1)} %bitcast.19), channel_id=1, source_target_pairs={{0,64},{32,96},{64,0},{96,32},{1,65},{33,97},{65,1},{97,33},{2,66}... | collective-permute-start | bytes 786440 | tf_op jit(solution)/shard_map/ppermute | solution.py:35
  139.5 19.9 %collective-permute-start.17 = (bf16[128,1024]{1,0:T(8,128)(2,1)}, bf16[128,1024]{1,0:T(8,128)(2,1)S(1)}, u32[]{:S(2)}, u32[]{:S(2)}) collective-permute-start(bf16[128,1024]{1,0:T(8,128)(2,1)} %bitcast.19), channel_id=1, source_target_pairs={{0,96},{32,0},{64,32},{96,64},{1,97},{33,1},{65,33},{97,65},{2,98}... | collective-permute-start | bytes 786440 | tf_op jit(solution)/shard_map/ppermute | solution.py:35
  151.6 21.7 %collective-permute-start.22 = (bf16[192,1024]{1,0:T(8,128)(2,1)S(1)}, bf16[192,1024]{1,0:T(8,128)(2,1)S(1)}, u32[]{:S(2)}, u32[]{:S(2)}) collective-permute-start(bf16[192,1024]{1,0:T(8,128)(2,1)S(1)} %add_convert_fusion.4), channel_id=1, source_target_pairs={{0,1},{1,2},{2,3},{3,0},{4,5},{5,6},{6,7},{7,4},{8,9},{9,10},{10,1... | collective-permute-start | bytes 1179656 | tf_op jit(solution)/shard_map/ppermute | solution.py:31
  151.7 21.6 %collective-permute-start.23 = (bf16[192,1024]{1,0:T(8,128)(2,1)S(1)}, bf16[192,1024]{1,0:T(8,128)(2,1)S(1)}, u32[]{:S(2)}, u32[]{:S(2)}) collective-permute-start(bf16[192,1024]{1,0:T(8,128)(2,1)S(1)} %add_convert_fusion.4), channel_id=1, source_target_pairs={{0,2},{1,3},{2,0},{3,1},{4,6},{5,7},{6,4},{7,5},{8,10},{9,11},{10,... | collective-permute-start | bytes 1179656 | tf_op jit(solution)/shard_map/ppermute | solution.py:31
  153.3 20.1 %collective-permute-start.24 = (bf16[192,1024]{1,0:T(8,128)(2,1)S(1)}, bf16[192,1024]{1,0:T(8,128)(2,1)}, u32[]{:S(2)}, u32[]{:S(2)}) collective-permute-start(bf16[192,1024]{1,0:T(8,128)(2,1)S(1)} %add_convert_fusion.4), channel_id=1, source_target_pairs={{0,3},{1,0},{2,1},{3,2},{4,7},{5,4},{6,5},{7,6},{8,11},{9,8},{10,9... | collective-permute-start | bytes 1179656 | tf_op jit(solution)/shard_map/ppermute | solution.py:31
  155.3 20.5 %all-to-all-start.2 = ((bf16[8,16,768]{2,1,0:T(8,128)(2,1)}), bf16[8,16,768]{2,1,0:T(8,128)(2,1)}, u32[]{:S(2)}, u32[]{:S(2)}) async-start(bf16[8,16,768]{2,1,0:T(8,128)(2,1)} %get-tuple-element.195), calls=%async_computation.2 | async-start | bytes 393216 | tf_op jit(solution)/shard_map/all_to_all | solution.py:577
  159.3 246.6 %reduce-scatter.3.cloned.1.call-start = ((), (), s32[]{:S(2)}) async-start(), calls=%async_computation.8 | async-start | bytes 10485760 | tf_op jit(solution)/shard_map/reduce_scatter | solution.py:1019
  177.9 12.5 %collective-permute-start.34 = (bf16[128,768]{1,0:T(8,128)(2,1)}, bf16[128,768]{1,0:T(8,128)(2,1)S(1)}, u32[]{:S(2)}, u32[]{:S(2)}) collective-permute-start(bf16[128,768]{1,0:T(8,128)(2,1)} %bitcast.33), channel_id=1, source_target_pairs={{0,32},{32,64},{64,96},{96,0},{1,33},{33,65},{65,97},{97,1},{2,34}... | collective-permute-start | bytes 589832 | tf_op jit(solution)/shard_map/ppermute | solution.py:35
  186.5 24.6 %collective-permute-start.26 = (bf16[192,1024]{1,0:T(8,128)(2,1)S(1)}, bf16[192,1024]{1,0:T(8,128)(2,1)S(1)}, u32[]{:S(2)}, u32[]{:S(2)}) collective-permute-start(bf16[192,1024]{1,0:T(8,128)(2,1)S(1)} %get-tuple-element.381), channel_id=1, source_target_pairs={{0,3},{1,0},{2,1},{3,2},{4,7},{5,4},{6,5},{7,6},{8,11},{9,8},{10,9... | collective-permute-start | bytes 1179656 | tf_op jit(solution)/shard_map/ppermute | solution.py:31
  188.7 22.4 %collective-permute-start.27 = (bf16[192,1024]{1,0:T(8,128)(2,1)S(1)}, bf16[192,1024]{1,0:T(8,128)(2,1)S(1)}, u32[]{:S(2)}, u32[]{:S(2)}) collective-permute-start(bf16[192,1024]{1,0:T(8,128)(2,1)S(1)} %get-tuple-element.383), channel_id=1, source_target_pairs={{0,2},{1,3},{2,0},{3,1},{4,6},{5,7},{6,4},{7,5},{8,10},{9,11},{10,... | collective-permute-start | bytes 1179656 | tf_op jit(solution)/shard_map/ppermute | solution.py:31
  188.7 22.4 %collective-permute-start.28 = (bf16[192,1024]{1,0:T(8,128)(2,1)S(1)}, bf16[192,1024]{1,0:T(8,128)(2,1)S(1)}, u32[]{:S(2)}, u32[]{:S(2)}) collective-permute-start(bf16[192,1024]{1,0:T(8,128)(2,1)S(1)} %get-tuple-element.382), channel_id=1, source_target_pairs={{0,1},{1,2},{2,3},{3,0},{4,5},{5,6},{6,7},{7,4},{8,9},{9,10},{10,1... | collective-permute-start | bytes 1179656 | tf_op jit(solution)/shard_map/ppermute | solution.py:31
  189.4 12.4 %collective-permute-start.35 = (bf16[128,768]{1,0:T(8,128)(2,1)}, bf16[128,768]{1,0:T(8,128)(2,1)S(1)}, u32[]{:S(2)}, u32[]{:S(2)}) collective-permute-start(bf16[128,768]{1,0:T(8,128)(2,1)} %bitcast.33), channel_id=1, source_target_pairs={{0,64},{32,96},{64,0},{96,32},{1,65},{33,97},{65,1},{97,33},{2,66}... | collective-permute-start | bytes 589832 | tf_op jit(solution)/shard_map/ppermute | solution.py:35
  190.4 18.0 %collective-permute-start.36 = (bf16[128,768]{1,0:T(8,128)(2,1)}, bf16[128,768]{1,0:T(8,128)(2,1)S(1)}, u32[]{:S(2)}, u32[]{:S(2)}) collective-permute-start(bf16[128,768]{1,0:T(8,128)(2,1)} %bitcast.33), channel_id=1, source_target_pairs={{0,96},{32,0},{64,32},{96,64},{1,97},{33,1},{65,33},{97,65},{2,98}... | collective-permute-start | bytes 589832 | tf_op jit(solution)/shard_map/ppermute | solution.py:35
  201.8 15.5 %collective-permute-start.29 = (bf16[192,1024]{1,0:T(8,128)(2,1)S(1)}, bf16[192,1024]{1,0:T(8,128)(2,1)S(1)}, u32[]{:S(2)}, u32[]{:S(2)}) collective-permute-start(bf16[192,1024]{1,0:T(8,128)(2,1)S(1)} %bitcast.295), channel_id=1, source_target_pairs={{4,8},{8,4},{5,9},{9,5},{6,10},{10,6},{7,11},{11,7},{20,24},{24,20... | collective-permute-start | bytes 1179656 | tf_op jit(solution)/shard_map/ppermute | solution.py:43
  212.6 12.0 %collective-permute-start.30 = (bf16[192,1024]{1,0:T(8,128)(2,1)S(1)}, bf16[192,1024]{1,0:T(8,128)(2,1)S(1)}, u32[]{:S(2)}, u32[]{:S(2)}) collective-permute-start(bf16[192,1024]{1,0:T(8,128)(2,1)S(1)} %add_convert_fusion.3), channel_id=1, source_target_pairs={{0,1},{1,2},{2,3},{3,0},{4,5},{5,6},{6,7},{7,4},{8,9},{9,10},{10,1... | collective-permute-start | bytes 1179656 | tf_op jit(solution)/shard_map/ppermute | solution.py:31
  214.8 18.9 %collective-permute-start.31 = (bf16[192,1024]{1,0:T(8,128)(2,1)S(1)}, bf16[192,1024]{1,0:T(8,128)(2,1)S(1)}, u32[]{:S(2)}, u32[]{:S(2)}) collective-permute-start(bf16[192,1024]{1,0:T(8,128)(2,1)S(1)} %add_convert_fusion.3), channel_id=1, source_target_pairs={{0,2},{1,3},{2,0},{3,1},{4,6},{5,7},{6,4},{7,5},{8,10},{9,11},{10,... | collective-permute-start | bytes 1179656 | tf_op jit(solution)/shard_map/ppermute | solution.py:31
  216.0 17.7 %collective-permute-start.32 = (bf16[192,1024]{1,0:T(8,128)(2,1)S(1)}, bf16[192,1024]{1,0:T(8,128)(2,1)S(1)}, u32[]{:S(2)}, u32[]{:S(2)}) collective-permute-start(bf16[192,1024]{1,0:T(8,128)(2,1)S(1)} %add_convert_fusion.3), channel_id=1, source_target_pairs={{0,3},{1,0},{2,1},{3,2},{4,7},{5,4},{6,5},{7,6},{8,11},{9,8},{10,9... | collective-permute-start | bytes 1179656 | tf_op jit(solution)/shard_map/ppermute | solution.py:31
  236.3 11.6 %collective-permute-start.33 = (bf16[192,1024]{1,0:T(8,128)(2,1)S(1)}, bf16[192,1024]{1,0:T(8,128)(2,1)S(1)}, u32[]{:S(2)}, u32[]{:S(2)}) collective-permute-start(bf16[192,1024]{1,0:T(8,128)(2,1)S(1)} %get-tuple-element.211), channel_id=1, source_target_pairs={{0,8},{8,0},{1,9},{9,1},{2,10},{10,2},{3,11},{11,3},{4,12},{12,4},... | collective-permute-start | bytes 1179656 | tf_op jit(solution)/shard_map/ppermute | solution.py:39
  251.7 11.6 %collective-permute-start.41 = (bf16[192,1024]{1,0:T(8,128)(2,1)S(1)}, bf16[192,1024]{1,0:T(8,128)(2,1)S(1)}, u32[]{:S(2)}, u32[]{:S(2)}) collective-permute-start(bf16[192,1024]{1,0:T(8,128)(2,1)S(1)} %get-tuple-element.377), channel_id=1, source_target_pairs={{0,2},{1,3},{2,0},{3,1},{4,6},{5,7},{6,4},{7,5},{8,10},{9,11},{10,... | collective-permute-start | bytes 1179656 | tf_op jit(solution)/shard_map/ppermute | solution.py:31
  252.6 20.0 %collective-permute-start.42 = (bf16[192,1024]{1,0:T(8,128)(2,1)S(1)}, bf16[192,1024]{1,0:T(8,128)(2,1)S(1)}, u32[]{:S(2)}, u32[]{:S(2)}) collective-permute-start(bf16[192,1024]{1,0:T(8,128)(2,1)S(1)} %get-tuple-element.376), channel_id=1, source_target_pairs={{0,1},{1,2},{2,3},{3,0},{4,5},{5,6},{6,7},{7,4},{8,9},{9,10},{10,1... | collective-permute-start | bytes 1179656 | tf_op jit(solution)/shard_map/ppermute | solution.py:31
  312.2 20.3 %collective-permute-start.47 = (bf16[192,1024]{1,0:T(8,128)(2,1)S(1)}, bf16[192,1024]{1,0:T(8,128)(2,1)S(1)}, u32[]{:S(2)}, u32[]{:S(2)}) collective-permute-start(bf16[192,1024]{1,0:T(8,128)(2,1)S(1)} %get-tuple-element.351), channel_id=1, source_target_pairs={{0,1},{1,2},{2,3},{3,0},{4,5},{5,6},{6,7},{7,4},{8,9},{9,10},{10,1... | collective-permute-start | bytes 1179656 | tf_op jit(solution)/shard_map/ppermute | solution.py:31
  312.2 20.3 %collective-permute-start.48 = (bf16[192,1024]{1,0:T(8,128)(2,1)S(1)}, bf16[192,1024]{1,0:T(8,128)(2,1)}, u32[]{:S(2)}, u32[]{:S(2)}) collective-permute-start(bf16[192,1024]{1,0:T(8,128)(2,1)S(1)} %get-tuple-element.351), channel_id=1, source_target_pairs={{0,2},{1,3},{2,0},{3,1},{4,6},{5,7},{6,4},{7,5},{8,10},{9,11},{10,... | collective-permute-start | bytes 1179656 | tf_op jit(solution)/shard_map/ppermute | solution.py:31
  313.8 19.1 %collective-permute-start.49 = (bf16[192,1024]{1,0:T(8,128)(2,1)S(1)}, bf16[192,1024]{1,0:T(8,128)(2,1)}, u32[]{:S(2)}, u32[]{:S(2)}) collective-permute-start(bf16[192,1024]{1,0:T(8,128)(2,1)S(1)} %get-tuple-element.351), channel_id=1, source_target_pairs={{0,3},{1,0},{2,1},{3,2},{4,7},{5,4},{6,5},{7,6},{8,11},{9,8},{10,9... | collective-permute-start | bytes 1179656 | tf_op jit(solution)/shard_map/ppermute | solution.py:31
  356.6 11.5 %collective-permute-start.52 = (bf16[192,1024]{1,0:T(8,128)(2,1)}, bf16[192,1024]{1,0:T(8,128)(2,1)S(1)}, u32[]{:S(2)}, u32[]{:S(2)}) collective-permute-start(bf16[192,1024]{1,0:T(8,128)(2,1)} %get-tuple-element.375), channel_id=1, source_target_pairs={{0,3},{1,0},{2,1},{3,2},{4,7},{5,4},{6,5},{7,6},{8,11},{9,8},{10,9... | collective-permute-start | bytes 1179656 | tf_op jit(solution)/shard_map/ppermute | solution.py:31
  358.9 11.9 %collective-permute-start.53 = (bf16[192,1024]{1,0:T(8,128)(2,1)}, bf16[192,1024]{1,0:T(8,128)(2,1)}, u32[]{:S(2)}, u32[]{:S(2)}) collective-permute-start(bf16[192,1024]{1,0:T(8,128)(2,1)} %get-tuple-element.374), channel_id=1, source_target_pairs={{0,2},{1,3},{2,0},{3,1},{4,6},{5,7},{6,4},{7,5},{8,10},{9,11},{10,... | collective-permute-start | bytes 1179656 | tf_op jit(solution)/shard_map/ppermute | solution.py:31
  358.9 20.7 %collective-permute-start.54 = (bf16[192,1024]{1,0:T(8,128)(2,1)}, bf16[192,1024]{1,0:T(8,128)(2,1)}, u32[]{:S(2)}, u32[]{:S(2)}) collective-permute-start(bf16[192,1024]{1,0:T(8,128)(2,1)} %get-tuple-element.373), channel_id=1, source_target_pairs={{0,1},{1,2},{2,3},{3,0},{4,5},{5,6},{6,7},{7,4},{8,9},{9,10},{10,1... | collective-permute-start | bytes 1179656 | tf_op jit(solution)/shard_map/ppermute | solution.py:31
  383.7 19.5 %collective-permute-start.55 = (bf16[192,1024]{1,0:T(8,128)(2,1)S(1)}, bf16[192,1024]{1,0:T(8,128)(2,1)S(1)}, u32[]{:S(2)}, u32[]{:S(2)}) collective-permute-start(bf16[192,1024]{1,0:T(8,128)(2,1)S(1)} %get-tuple-element.354), channel_id=1, source_target_pairs={{0,1},{1,2},{2,3},{3,0},{4,5},{5,6},{6,7},{7,4},{8,9},{9,10},{10,1... | collective-permute-start | bytes 1179656 | tf_op jit(solution)/shard_map/ppermute | solution.py:31
  383.7 19.5 %collective-permute-start.56 = (bf16[192,1024]{1,0:T(8,128)(2,1)S(1)}, bf16[192,1024]{1,0:T(8,128)(2,1)S(1)}, u32[]{:S(2)}, u32[]{:S(2)}) collective-permute-start(bf16[192,1024]{1,0:T(8,128)(2,1)S(1)} %get-tuple-element.354), channel_id=1, source_target_pairs={{0,2},{1,3},{2,0},{3,1},{4,6},{5,7},{6,4},{7,5},{8,10},{9,11},{10,... | collective-permute-start | bytes 1179656 | tf_op jit(solution)/shard_map/ppermute | solution.py:31
  384.8 18.8 %collective-permute-start.57 = (bf16[192,1024]{1,0:T(8,128)(2,1)S(1)}, bf16[192,1024]{1,0:T(8,128)(2,1)}, u32[]{:S(2)}, u32[]{:S(2)}) collective-permute-start(bf16[192,1024]{1,0:T(8,128)(2,1)S(1)} %get-tuple-element.354), channel_id=1, source_target_pairs={{0,3},{1,0},{2,1},{3,2},{4,7},{5,4},{6,5},{7,6},{8,11},{9,8},{10,9... | collective-permute-start | bytes 1179656 | tf_op jit(solution)/shard_map/ppermute | solution.py:31
  423.0 15.3 %collective-permute-start.61 = (bf16[8,64,2048]{2,1,0:T(8,128)(2,1)}, bf16[8,64,2048]{2,1,0:T(8,128)(2,1)}, u32[]{:S(2)}, u32[]{:S(2)}) collective-permute-start(bf16[8,64,2048]{2,1,0:T(8,128)(2,1)} %fusion.15), channel_id=1, source_target_pairs={{0,8},{8,0},{1,9},{9,1},{2,10},{10,2},{3,11},{11,3},{4,12},{12,4},... | collective-permute-start | bytes 6291464 | tf_op jit(solution)/shard_map/ppermute | solution.py:39
  425.2 49.0 %all-to-all-start.3 = ((bf16[16,64,1024]{2,1,0:T(8,128)(2,1)}), bf16[16,64,1024]{2,1,0:T(8,128)(2,1)}, u32[]{:S(2)}, u32[]{:S(2)}) async-start(bf16[16,64,1024]{2,1,0:T(8,128)(2,1)} %bitcast.276), calls=%async_computation.4 | async-start | bytes 4194304 | tf_op jit(solution)/shard_map/all_to_all | solution.py:1044
  429.7 105.8 %reduce-scatter.5.cloned.1.call-start = ((), (), s32[]{:S(2)}) async-start(), calls=%async_computation.9 | async-start | bytes 2228224 | tf_op jit(solution)/shard_map/reduce_scatter | solution.py:1040
  432.3 30.4 %collective-permute-start.58 = (bf16[192,1024]{1,0:T(8,128)(2,1)}, bf16[192,1024]{1,0:T(8,128)(2,1)}, u32[]{:S(2)}, u32[]{:S(2)}) collective-permute-start(bf16[192,1024]{1,0:T(8,128)(2,1)} %get-tuple-element.372), channel_id=1, source_target_pairs={{0,3},{1,0},{2,1},{3,2},{4,7},{5,4},{6,5},{7,6},{8,11},{9,8},{10,9... | collective-permute-start | bytes 1179656 | tf_op jit(solution)/shard_map/ppermute | solution.py:31
  434.8 29.0 %collective-permute-start.59 = (bf16[192,1024]{1,0:T(8,128)(2,1)}, bf16[192,1024]{1,0:T(8,128)(2,1)}, u32[]{:S(2)}, u32[]{:S(2)}) collective-permute-start(bf16[192,1024]{1,0:T(8,128)(2,1)} %get-tuple-element.371), channel_id=1, source_target_pairs={{0,2},{1,3},{2,0},{3,1},{4,6},{5,7},{6,4},{7,5},{8,10},{9,11},{10,... | collective-permute-start | bytes 1179656 | tf_op jit(solution)/shard_map/ppermute | solution.py:31
  435.3 37.4 %collective-permute-start.60 = (bf16[192,1024]{1,0:T(8,128)(2,1)}, bf16[192,1024]{1,0:T(8,128)(2,1)}, u32[]{:S(2)}, u32[]{:S(2)}) collective-permute-start(bf16[192,1024]{1,0:T(8,128)(2,1)} %get-tuple-element.370), channel_id=1, source_target_pairs={{0,1},{1,2},{2,3},{3,0},{4,5},{5,6},{6,7},{7,4},{8,9},{9,10},{10,1... | collective-permute-start | bytes 1179656 | tf_op jit(solution)/shard_map/ppermute | solution.py:31
  477.0 12.0 %collective-permute-start.62 = (bf16[192,1024]{1,0:T(8,128)(2,1)}, bf16[192,1024]{1,0:T(8,128)(2,1)S(1)}, u32[]{:S(2)}, u32[]{:S(2)}) collective-permute-start(bf16[192,1024]{1,0:T(8,128)(2,1)} %get-tuple-element.269), channel_id=1, source_target_pairs={{0,1},{1,2},{2,3},{3,0},{4,5},{5,6},{6,7},{7,4},{8,9},{9,10},{10,1... | collective-permute-start | bytes 1179656 | tf_op jit(solution)/shard_map/ppermute | solution.py:31
  478.3 18.0 %collective-permute-start.63 = (bf16[192,1024]{1,0:T(8,128)(2,1)}, bf16[192,1024]{1,0:T(8,128)(2,1)S(1)}, u32[]{:S(2)}, u32[]{:S(2)}) collective-permute-start(bf16[192,1024]{1,0:T(8,128)(2,1)} %get-tuple-element.269), channel_id=1, source_target_pairs={{0,2},{1,3},{2,0},{3,1},{4,6},{5,7},{6,4},{7,5},{8,10},{9,11},{10,... | collective-permute-start | bytes 1179656 | tf_op jit(solution)/shard_map/ppermute | solution.py:31
  479.6 18.0 %collective-permute-start.64 = (bf16[192,1024]{1,0:T(8,128)(2,1)}, bf16[192,1024]{1,0:T(8,128)(2,1)S(1)}, u32[]{:S(2)}, u32[]{:S(2)}) collective-permute-start(bf16[192,1024]{1,0:T(8,128)(2,1)} %get-tuple-element.269), channel_id=1, source_target_pairs={{0,3},{1,0},{2,1},{3,2},{4,7},{5,4},{6,5},{7,6},{8,11},{9,8},{10,9... | collective-permute-start | bytes 1179656 | tf_op jit(solution)/shard_map/ppermute | solution.py:31
  481.0 44.1 %all-to-all-start.4 = ((bf16[8,64,2048]{2,1,0:T(8,128)(2,1)}), bf16[8,64,2048]{2,1,0:T(8,128)(2,1)}, u32[]{:S(2)}, u32[]{:S(2)}) async-start(bf16[8,64,2048]{2,1,0:T(8,128)(2,1)} %fusion), calls=%async_computation.5 | async-start | bytes 4194304 | tf_op jit(solution)/shard_map/all_to_all | solution.py:735
  486.9 170.1 %all-gather.14.cloned.1.call-start = ((), (), s32[]{:S(2)}) async-start(), calls=%async_computation.12 | async-start | bytes 2228224 | tf_op jit(solution)/shard_map/all_gather | solution.py:1052
  512.7 140.3 %collective-permute-start.45 = (f32[192,1024]{1,0:T(8,128)}, f32[192,1024]{1,0:T(8,128)}, u32[]{:S(2)}, u32[]{:S(2)}) collective-permute-start(f32[192,1024]{1,0:T(8,128)} %get-tuple-element.392), channel_id=1, source_target_pairs={{4,8},{8,4},{5,9},{9,5},{6,10},{10,6},{7,11},{11,7},{20,24},{24,20... | collective-permute-start | bytes 2359304 | tf_op jit(solution)/shard_map/ppermute | solution.py:43
  522.4 134.6 %all-gather.12.cloned.1.call-start = ((), (), s32[]{:S(2)}) async-start(), calls=%async_computation.11 | async-start | bytes 3342336 | tf_op jit(solution)/shard_map/all_gather | solution.py:1080
  535.5 37.0 %collective-permute-start.70 = (bf16[4,2,64,1024]{3,2,1,0:T(8,128)(2,1)}, bf16[4,2,64,1024]{3,2,1,0:T(8,128)(2,1)}, u32[]{:S(2)}, u32[]{:S(2)}) collective-permute-start(bf16[4,2,64,1024]{3,2,1,0:T(8,128)(2,1)} %fusion.26), channel_id=1, source_target_pairs={{0,8},{8,0},{1,9},{9,1},{2,10},{10,2},{3,11},{11,3},{4,12},{12,4},... | collective-permute-start | bytes 3145736 | tf_op jit(solution)/shard_map/ppermute | solution.py:39
  549.9 24.3 %collective-permute-start.67 = (bf16[192,1024]{1,0:T(8,128)(2,1)}, bf16[192,1024]{1,0:T(8,128)(2,1)S(1)}, u32[]{:S(2)}, u32[]{:S(2)}) collective-permute-start(bf16[192,1024]{1,0:T(8,128)(2,1)} %get-tuple-element.369), channel_id=1, source_target_pairs={{0,3},{1,0},{2,1},{3,2},{4,7},{5,4},{6,5},{7,6},{8,11},{9,8},{10,9... | collective-permute-start | bytes 1179656 | tf_op jit(solution)/shard_map/ppermute | solution.py:31
  549.9 24.2 %collective-permute-start.68 = (bf16[192,1024]{1,0:T(8,128)(2,1)}, bf16[192,1024]{1,0:T(8,128)(2,1)}, u32[]{:S(2)}, u32[]{:S(2)}) collective-permute-start(bf16[192,1024]{1,0:T(8,128)(2,1)} %get-tuple-element.368), channel_id=1, source_target_pairs={{0,2},{1,3},{2,0},{3,1},{4,6},{5,7},{6,4},{7,5},{8,10},{9,11},{10,... | collective-permute-start | bytes 1179656 | tf_op jit(solution)/shard_map/ppermute | solution.py:31
  607.6 15.3 %collective-permute-start.84 = (bf16[8,768]{1,0:T(8,128)(2,1)S(1)}, bf16[8,768]{1,0:T(8,128)(2,1)S(1)}, u32[]{:S(2)}, u32[]{:S(2)}) collective-permute-start(bf16[8,768]{1,0:T(8,128)(2,1)S(1)} %get-tuple-element.425), channel_id=1, source_target_pairs={{0,3},{1,0},{2,1},{3,2},{4,7},{5,4},{6,5},{7,6},{8,11},{9,8},{10,9... | collective-permute-start | bytes 36872 | tf_op jit(solution)/shard_map/ppermute | solution.py:31
  607.9 23.0 %collective-permute-start.87 = (f32[3072]{0:T(1024)S(1)}, f32[3072]{0:T(1024)S(1)}, u32[]{:S(2)}, u32[]{:S(2)}) collective-permute-start(f32[3072]{0:T(1024)S(1)} %bitcast.336), channel_id=1, source_target_pairs={{0,4},{4,0},{16,20},{20,16},{1,5},{5,1},{17,21},{21,17},{2,6},{6,2... | collective-permute-start | bytes 36872 | tf_op jit(solution)/shard_map/ppermute | solution.py:757
  609.0 24.4 %collective-permute-start.89 = (f32[3072]{0:T(1024)S(1)}, f32[3072]{0:T(1024)S(1)}, u32[]{:S(2)}, u32[]{:S(2)}) collective-permute-start(f32[3072]{0:T(1024)S(1)} %bitcast.337), channel_id=1, source_target_pairs={{0,20},{4,16},{16,4},{20,0},{1,21},{5,17},{17,5},{21,1},{2,22},{6,... | collective-permute-start | bytes 36872 | tf_op jit(solution)/shard_map/ppermute | solution.py:757
  610.2 23.6 %collective-permute-start.90 = (f32[192,1024]{1,0:T(8,128)S(1)}, f32[192,1024]{1,0:T(8,128)S(1)}, u32[]{:S(2)}, u32[]{:S(2)}) collective-permute-start(f32[192,1024]{1,0:T(8,128)S(1)} %multiply_add_fusion), channel_id=1, source_target_pairs={{4,8},{8,4},{5,9},{9,5},{6,10},{10,6},{7,11},{11,7},{20,24},{24,20... | collective-permute-start | bytes 2359304 | tf_op jit(solution)/shard_map/ppermute | solution.py:43
  651.3 13.3 %collective-permute-start.99 = (bf16[4,2,32,1024]{3,2,1,0:T(8,128)(2,1)S(1)}, bf16[4,2,32,1024]{3,2,1,0:T(8,128)(2,1)S(1)}, u32[]{:S(2)}, u32[]{:S(2)}) collective-permute-start(bf16[4,2,32,1024]{3,2,1,0:T(8,128)(2,1)S(1)} %pad_maximum_fusion.12.mine), channel_id=1, source_target_pairs={{0,8},{8,0},{1,9},{9,1},{2,10},{10,2},{3,11},{11,3},{4,12},{12,4},... | collective-permute-start | bytes 1572872 | tf_op jit(solution)/shard_map/ppermute | solution.py:39
  (152 other events, 1125.7 us)
Sparse Core Ops, SparseCore 0:
  41.1 55.1 all-gather.7
  122.0 99.1 all-gather.9
  304.5 77.5 reduce-scatter.2
  436.4 80.6 reduce-scatter.4
  522.5 33.8 all-gather.13
  585.6 40.4 all-gather.11

commit v6 on v5

--- a/solution.py
+++ b/solution.py
@@ -301,59 +301,30 @@
     return u * half, slope
 
 
-def wide_forward_kernel(rows, weight, bias, own, other, before, down, total):
+def wide_kernel(
+    rows_own, rows_other, grads_own, grads_other, weight, bias,
+    out_own, out_other, d_own, d_other, sums, pack,
+    rows, grads, down, total, d_total,
+):
     step = pl.program_id(0)
-    wide_down(weight, down)
-    u = dot(rows[...], weight[0, :, 0:512]) + bias[0]
-    before[0] = u
-    activated = gelu_parts(u)[0].astype(bf16)
-    part = dot(activated, down[...])
 
     @pl.when(step == 0)
     def _():
-        total[...] = part
-
-    @pl.when(step > 0)
-    def _():
-        total[...] += part
-
-    @pl.when(step == 3)
-    def _():
-        own[...] = total[0:PIECE, :]
-        other[...] = total[PIECE:PAIR, :].astype(bf16)
-
-
-def wide_forward(rows, weight, bias):
-    fixed = lambda shape: pl.BlockSpec(shape, lambda i: (0,) * len(shape))
-    each = lambda *shape: pl.BlockSpec((1,) + shape, lambda i: (i, 0, 0))
-    return pl.pallas_call(
-        wide_forward_kernel,
-        grid=(4,),
-        out_shape=(
-            jax.ShapeDtypeStruct((PIECE, D), f32),
-            jax.ShapeDtypeStruct((PIECE, D), bf16),
-            jax.ShapeDtypeStruct((4, PAIR, 512), f32),
-        ),
-        in_specs=[fixed((PAIR, D)), each(D, D), each(1, 512)],
-        out_specs=(fixed((PIECE, D)), fixed((PIECE, D)), each(PAIR, 512)),
-        scratch_shapes=[pltpu.VMEM((512, D), bf16), pltpu.VMEM((PAIR, D), f32)],
-        compiler_params=pltpu.CompilerParams(vmem_limit_bytes=58 * 2**20),
-        cost_estimate=pl.CostEstimate(
-            flops=4 * PAIR * 2048 * D, bytes_accessed=20000000, transcendentals=0
-        ),
-        name="wide_forward",
-    )(rows, weight, bias)
-
-
-def wide_back_kernel(grads, rows, before, weight, own, other, sums, pack, down, total):
-    step = pl.program_id(0)
+        rows[0:PIECE, :] = rows_own[...]
+        rows[PIECE:PAIR, :] = rows_other[...]
+        grads[0:PIECE, :] = grads_own[...]
+        grads[PIECE:PAIR, :] = grads_other[...]
+
     wide_down(weight, down)
-    activated, slope = gelu_parts(before[0])
+    up = weight[0, :, 0:512]
+    activated, slope = gelu_parts(dot(rows[...], up) + bias[0])
+    activated = activated.astype(bf16)
     d_before = (dot_t(grads[...], down[...]) * slope).astype(bf16)
     sums[0] = jnp.sum(d_before.astype(f32), axis=0, keepdims=True)
-    part = dot_t(d_before, weight[0, :, 0:512])
+    part = dot(activated, down[...])
+    d_part = dot_t(d_before, up)
     g_up = outer(rows[...], d_before).astype(bf16)
-    g_down = outer(activated.astype(bf16), grads[...]).astype(bf16)
+    g_down = outer(activated, grads[...]).astype(bf16)
     for place in range(8):
         for side in range(2):
             at = place * 128 + side * 64
@@ -365,38 +336,50 @@
     @pl.when(step == 0)
     def _():
         total[...] = part
+        d_total[...] = d_part
 
     @pl.when(step > 0)
     def _():
         total[...] += part
+        d_total[...] += d_part
 
     @pl.when(step == 3)
     def _():
-        own[...] = total[0:PIECE, :]
-        other[...] = total[PIECE:PAIR, :].astype(bf16)
-
-
-def wide_back(grads, rows, before, weight):
-    fixed = lambda shape: pl.BlockSpec(shape, lambda i: (0,) * len(shape))
+        out_own[...] = total[0:PIECE, :]
+        out_other[...] = total[PIECE:PAIR, :].astype(bf16)
+        d_own[...] = d_total[0:PIECE, :]
+        d_other[...] = d_total[PIECE:PAIR, :].astype(bf16)
+
+
+def wide_part(rows_own, rows_other, grads_own, grads_other, weight, bias):
+    fixed = pl.BlockSpec((PIECE, D), lambda i: (0, 0))
     each = lambda *shape: pl.BlockSpec((1,) + shape, lambda i: (i,) + (0,) * len(shape))
     return pl.pallas_call(
-        wide_back_kernel,
+        wide_kernel,
         grid=(4,),
         out_shape=(
+            jax.ShapeDtypeStruct((PIECE, D), f32),
+            jax.ShapeDtypeStruct((PIECE, D), bf16),
             jax.ShapeDtypeStruct((PIECE, D), f32),
             jax.ShapeDtypeStruct((PIECE, D), bf16),
             jax.ShapeDtypeStruct((4, 1, 512), f32),
             jax.ShapeDtypeStruct((4, 2, 8, 64, D), bf16),
         ),
-        in_specs=[fixed((PAIR, D)), fixed((PAIR, D)), each(PAIR, 512), each(D, D)],
-        out_specs=(fixed((PIECE, D)), fixed((PIECE, D)), each(1, 512), each(2, 8, 64, D)),
-        scratch_shapes=[pltpu.VMEM((512, D), bf16), pltpu.VMEM((PAIR, D), f32)],
+        in_specs=[fixed] * 4 + [each(D, D), each(1, 512)],
+        out_specs=(fixed,) * 4 + (each(1, 512), each(2, 8, 64, D)),
+        scratch_shapes=[
+            pltpu.VMEM((PAIR, D), bf16),
+            pltpu.VMEM((PAIR, D), bf16),
+            pltpu.VMEM((512, D), bf16),
+            pltpu.VMEM((PAIR, D), f32),
+            pltpu.VMEM((PAIR, D), f32),
+        ],
         compiler_params=pltpu.CompilerParams(vmem_limit_bytes=58 * 2**20),
         cost_estimate=pl.CostEstimate(
-            flops=10 * PAIR * 2048 * D, bytes_accessed=40000000, transcendentals=0
+            flops=14 * PAIR * 2048 * D, bytes_accessed=50000000, transcendentals=0
         ),
-        name="wide_back",
-    )(grads, rows, before, weight)
+        name="wide_part",
+    )(rows_own, rows_other, grads_own, grads_other, weight, bias)
 
 
 QUARTER = 16
@@ -414,16 +397,17 @@
 
 def pack_rest_kernel(info, weight, up, down, project, first, second, rows, wide):
     core, x = info[0], info[4]
-    at_row = pl.ds(pl.multiple_of(core * 64 + x * 16, 16), 16)
+    half = pl.ds(pl.multiple_of(core * 64, 64), 64)
     for place in range(8):
         for side in range(2):
             at = side * 2048 + (place % 4) * 512
             to = side * 512
-            first[place, :, to : to + 512] = up[0, at_row, at : at + 512]
+            first[place, :, to : to + 512] = up[0, half, at : at + 512]
             for part in range(3):
                 at = part * D + side * 512 + (place % 4) * 128
                 to = (side * 3 + part) * 128
-                second[place, :, to : to + 128] = weight[0, at_row, at : at + 128]
+                second[place, :, to : to + 128] = weight[0, half, at : at + 128]
+    at_row = pl.ds(pl.multiple_of(core * 64 + x * 16, 16), 16)
     long = pl.ds(pl.multiple_of(core * 256 + x * 64, 64), 64)
     rows[0:64, :] = down[0, long, :]
     rows[64:80, :] = project[0, at_row, :]
@@ -437,6 +421,29 @@
         wide[:, place * 64 : (place + 1) * 64] = found.astype(bf16)
 
 
+def join_halves_kernel(info, mine, other, *outs):
+    core = info[0]
+    for pieces, half in ((mine, core), (other, 1 - core)):
+        for place in range(8):
+            at = pl.ds(pl.multiple_of(place * 128 + half * 64, 64), 64)
+            column = 0
+            for out in outs:
+                width = out.shape[1]
+                out[at, :] = pieces[place, :, column : column + width]
+                column += width
+
+
+def join_halves(info, mine, other, widths):
+    return pl.pallas_call(
+        join_halves_kernel,
+        out_shape=tuple(jax.ShapeDtypeStruct((D, width), bf16) for width in widths),
+        in_specs=[smem, whole, whole],
+        out_specs=(whole,) * len(widths),
+        compiler_params=params_one,
+        name="join_halves",
+    )(info, mine, other)
+
+
 def join_columns_kernel(info, mine, other, out):
     core, x = info[0], info[4]
     for pieces, half in ((mine, core), (other, 1 - core)):
@@ -446,20 +453,26 @@
                 out[pl.ds(pl.multiple_of(at, 16), 16), :] = pieces[k, place * 16 : (place + 1) * 16, :]
 
 
-def join_rows_kernel(info, down, project, mine, other, down_out, project_out, project_next):
+def join_down_kernel(info, down, mine, other, down_out):
     core, x, y_hi = info[0], info[4], info[2]
     down_out[pl.ds(pl.multiple_of(y_hi * 512, 64), 512), :] = down[0]
-    own = pl.ds(pl.multiple_of(y_hi * 128, 64), 128)
-    project_out[own, :] = project[0]
-    project_next[own, :] = project[1]
     for pieces, half in ((mine, core), (other, 1 - core)):
         for k in range(4):
-            quarter = (x - k) & 3
-            at = (1 - y_hi) * 512 + half * 256 + quarter * 64
+            at = (1 - y_hi) * 512 + half * 256 + ((x - k) & 3) * 64
             down_out[pl.ds(pl.multiple_of(at, 64), 64), :] = pieces[k, 0:64, :]
-            at = pl.ds(pl.multiple_of((1 - y_hi) * 128 + half * 64 + quarter * 16, 16), 16)
-            project_out[at, :] = pieces[k, 64:80, :]
-            project_next[at, :] = pieces[k, 80:96, :]
+
+
+def join_project_kernel(info, project, mine, other, first, second):
+    core, x, y_hi = info[0], info[4], info[2]
+    own = pl.ds(pl.multiple_of(y_hi * 128, 64), 128)
+    first[own, :] = project[0]
+    second[own, :] = project[1]
+    for pieces, half in ((mine, core), (other, 1 - core)):
+        for k in range(4):
+            at = (1 - y_hi) * 128 + half * 64 + ((x - k) & 3) * 16
+            at = pl.ds(pl.multiple_of(at, 16), 16)
+            first[at, :] = pieces[k, 64:80, :]
+            second[at, :] = pieces[k, 80:96, :]
 
 
 def read_small_kernel(info, got, vectors, in_bias, unit_bias):
@@ -515,8 +528,8 @@
         pack_rest_kernel,
         grid=(1,),
         out_shape=(
-            jax.ShapeDtypeStruct((8, 16, 1024), bf16),
-            jax.ShapeDtypeStruct((8, 16, 768), bf16),
+            jax.ShapeDtypeStruct((8, 64, 1024), bf16),
+            jax.ShapeDtypeStruct((8, 64, 768), bf16),
             jax.ShapeDtypeStruct((96, D), bf16),
             jax.ShapeDtypeStruct((128, D), bf16),
         ),
@@ -557,20 +570,27 @@
     )(info, mine, other)
 
 
-def join_rows(info, down, project, mine, other):
+def join_down(info, down, mine, other):
     return pl.pallas_call(
-        join_rows_kernel,
+        join_down_kernel,
         grid=(1,),
-        out_shape=(
-            jax.ShapeDtypeStruct((D, D), bf16),
-            jax.ShapeDtypeStruct((256, D), bf16),
-            jax.ShapeDtypeStruct((256, D), bf16),
-        ),
-        in_specs=[smem, layer_block((512, D), 0), whole, whole, whole],
-        out_specs=(whole,) * 3,
+        out_shape=jax.ShapeDtypeStruct((D, D), bf16),
+        in_specs=[smem, layer_block((512, D), 0), whole, whole],
+        out_specs=whole,
         compiler_params=params_one,
-        name="join_rows",
-    )(info, down, project, mine, other)
+        name="join_down",
+    )(info, down, mine, other)
+
+
+def join_project(info, project, mine, other):
+    return pl.pallas_call(
+        join_project_kernel,
+        out_shape=(jax.ShapeDtypeStruct((256, D), bf16),) * 2,
+        in_specs=[smem, whole, whole, whole],
+        out_specs=(whole,) * 2,
+        compiler_params=params_one,
+        name="join_project",
+    )(info, project, mine, other)
 
 
 def to_ctx(value):
@@ -601,35 +621,29 @@
     return context, logsum, rows, side_done
 
 
-def forward_middle(hidden, context, params):
+def forward_middle(hidden, context, params, given=None, work=lambda v: None):
     (project, project_bias, gain_two, offset_two) = params[4:8]
-    parts, own = beside(
+    parts, (own, done) = beside(
         dot_others(context, project, dot),
         scatter_parts,
-        context,
-        lambda v: dot_own(v, project, dot),
+        (context, given),
+        lambda v: (dot_own(v[0], project, dot), work(v[1])),
     )
     middle = hidden + sum_parts(own, parts) + project_bias
-    return middle, norm(middle, gain_two, offset_two).astype(bf16)
-
-
-def with_rows(middle, normed):
-    return middle, gather_z(normed)
+    return middle, norm(middle, gain_two, offset_two).astype(bf16), done
 
 
 def last_send(last, params):
     return dot_others(last[1], params[10], dot)
 
 
-def last_sum(last, params, parts):
-    return last[0] + sum_parts(dot_own(last[1], params[10], dot), parts) + params[11]
-
-
-def backward_two(grad_down, params, kept, core):
-    (up, _, down, _) = params[8:]
-    normed_two, before, activated = kept[6:]
-    d_act = dot_t(grad_down, down)
-    d_before = jax.vjp(gelu, before)[1](d_act)[0].astype(bf16)
+def last_own(last, params):
+    return last[0] + dot_own(last[1], params[10], dot) + params[11]
+
+
+def backward_two(grad_down, d_before, params, kept, core):
+    up = params[8]
+    normed_two, _, activated = kept[6:]
     sum_up = jnp.sum(d_before.astype(f32), axis=0)
 
     def work_two(given):
@@ -637,67 +651,67 @@
         own = dot_own(d_before, up, dot_t)
         g_down = outer(activated, grad_down).astype(bf16)
         g_up = outer(normed_two, d_before).astype(bf16)
-        return own, core_sum(pack_outer(g_down, g_up), core)
-
-    parts, (own, summed) = beside(
+        return own, (g_down, g_up)
+
+    parts, (own, grads) = beside(
         dot_others(d_before, up, dot_t),
         scatter_parts,
         (activated, grad_down, normed_two, d_before),
         work_two,
     )
-    return sum_parts(own, parts), summed, sum_up
-
-
-def backward(gradient, d_normed, sum_up, params, kept, info, slopes, core, across, one):
+    return sum_parts(own, parts), grads, sum_up
+
+
+def backward(gradient, d_normed, sum_up, params, kept, info, slopes, core, across, more):
     (gain_one, _, w_in, _, project, _, gain_two) = params[:7]
     hidden, normed_all, logsum, rows, context, middle = kept[:6]
     sum_down = jnp.sum(gradient.astype(bf16).astype(f32), axis=0)
+
     d_values, sum_gain_two, sum_offset_two = norm_back(middle, gain_two, d_normed)
     d_middle = gradient + d_values
     grad_out = d_middle.astype(bf16)
-    sum_project = jnp.sum(grad_out.astype(f32), axis=0)
-
-    def attention(grad_out):
-        grad_out_all = gather_z(grad_out)
+    grad_out_all, (sum_project, crossed) = beside(
+        grad_out,
+        gather_z,
+        (grad_out, across[0]),
+        lambda v: (jnp.sum(v[0].astype(f32), axis=0), across[1](v[1])),
+    )
+
+    def attention(grad_out_all):
         d_context = dot_t(grad_out_all, project).astype(bf16)
         received = swap(columns_at(d_context, 1 - core, 128), "core")
         mine = columns_at(d_context, core, 128)
         d_mine, d_other, sums = attend_back(info, slopes, rows, mine, received, logsum)
-        return in_order(d_mine, swap(d_other, "core"), core), sums, grad_out_all
-
-    crossed, (d_joined, sums, grad_out_all) = beside(across[0], across[1], grad_out, attention)
-
-    def work_one(given):
-        context, grad_out_all, normed_all, d_joined, crossed = given
-        own = dot_own(d_joined, w_in, dot_t)
-        g_input = outer(normed_all, d_joined).astype(bf16)
-        g_project = outer(context, grad_out_all).astype(bf16)
-        return own, one(crossed, g_input, g_project)
-
-    parts, (own, done_one) = beside(
-        dot_others(d_joined, w_in, dot_t),
-        scatter_parts,
-        (context, grad_out_all, normed_all, d_joined, crossed),
-        work_one,
-    )
-
+        return in_order(d_mine, swap(d_other, "core"), core), sums
+
+    def attention_more(grad_out_all):
+        d_joined, sums = attention(grad_out_all)
+        return d_joined, sums, more(d_joined, sums, (sum_project, sum_gain_two, sum_offset_two, sum_down, sums, sum_up))
+
+    crossed, (d_joined, sums, done_more) = beside(
+        across[2](crossed, context, grad_out_all), across[3], grad_out_all, attention_more
+    )
+
+    def g_input():
+        return outer(normed_all, d_joined).astype(bf16)
+
+    def scatter(work):
+        parts, (own, done) = beside(
+            dot_others(d_joined, w_in, dot_t),
+            scatter_parts,
+            d_joined,
+            lambda v: (dot_own(v, w_in, dot_t), work()),
+        )
+        return (own, parts), done
+
+    vectors = (sum_project, sum_gain_two, sum_offset_two, sum_down, sums, sum_up)
     def finish(given):
         own, parts = given
         d_normed_one = sum_parts(own, parts)
         d_hidden, sum_gain_one, sum_offset_one = norm_back(hidden, gain_one, d_normed_one)
-        small = (
-            sum_gain_one,
-            sum_offset_one,
-            sum_project,
-            sum_gain_two,
-            sum_offset_two,
-            sum_down,
-            sums,
-            sum_up,
-        )
-        return d_middle + d_hidden, small
-
-    return (own, parts), finish, done_one
+        return d_middle + d_hidden, (sum_gain_one, sum_offset_one)
+
+    return crossed, vectors, done_more, g_input, grad_out_all, scatter, finish
 
 
 def take(value, at, axis=0):
@@ -759,7 +773,7 @@
 
 
 def inner_core(pack, core):
-    split = pack.reshape(4, 2, 2, 64, 1024)
+    split = pack.reshape(4, 2, 2, 64, -1)
     keep, send = take(split, core, 2), take(split, 1 - core, 2)
     return (keep.astype(f32) + swap(send, "core").astype(f32)).astype(bf16)
 
@@ -772,7 +786,7 @@
 
 
 def inner_y(low, y_lo, y_hi):
-    split = low.reshape(2, 2, 32, 1024)
+    split = low.reshape(2, 2, 32, -1)
     piece = lambda a, b: take(take(split, a), b)
     return across_y(
         piece(y_lo, y_hi),
@@ -827,28 +841,27 @@
                     )
 
 
-def place_inner(block, layer, row, inputs, project):
+def place_input(block, layer, row, inputs):
     rows = pl.ds(row, 8)
     for four in range(4):
         part_rows = block[four * 8 : (four + 1) * 8, :].astype(f32)
-        project[layer, rows, four * 256 : (four + 1) * 256] = part_rows[:, 0:256]
         for side in range(2):
             for part in range(3):
                 to = part * D + side * 512 + four * 128
-                at = 256 + (side * 3 + part) * 128
+                at = (side * 3 + part) * 128
                 inputs[layer, rows, to : to + 128] = part_rows[:, at : at + 128]
 
 
-def unpack_inner_kernel(info, mine, other, second, inputs, project):
-    core, x, y_lo = info[0], info[4], info[5]
-    for pieces, half in ((mine, core), (other, 1 - core)):
-        for k in range(4):
-            for side in range(2):
-                low = y_lo if side == 0 else 1 - y_lo
-                g = (((x - k) & 3) * 2 + low) * 2 + half
-                place_inner(pieces[k, side], 0, pl.multiple_of(g * 8, 8), inputs, project)
+def unpack_inner_kernel(full, inputs, project):
     for g in range(16):
-        place_inner(second[g, :, 2048:3072], 1, g * 8, inputs, project)
+        place_input(full[g, :, 3328:4096], 0, g * 8, inputs)
+        place_input(full[g, :, 2560:3328], 1, g * 8, inputs)
+        for layer, at in ((0, 2048), (1, 2304)):
+            block = full[g, :, at : at + 256].astype(f32)
+            for four in range(4):
+                project[layer, g * 8 : (g + 1) * 8, four * 256 : (four + 1) * 256] = block[
+                    four * 8 : (four + 1) * 8, :
+                ]
 
 
 def unpack_outer(first, second):
@@ -865,18 +878,59 @@
     )(first, second)
 
 
-def unpack_inner(info, mine, other, second):
+def unpack_inner(full):
     return pl.pallas_call(
         unpack_inner_kernel,
         out_shape=(
             jax.ShapeDtypeStruct((LAYERS, 128, 3072), f32),
             jax.ShapeDtypeStruct((LAYERS, 128, D), f32),
         ),
-        in_specs=[smem, whole, whole, whole],
+        in_specs=[whole],
         out_specs=(whole, whole),
         compiler_params=params_one,
         name="unpack_inner",
-    )(info, mine, other, second)
+    )(full)
+
+
+def pack_tail_kernel(
+    info, g_input, gain, offset, project, gain_two, offset_two, down, sums, up, second, out
+):
+    core, z = info[0], info[1]
+    out[:, :, :, 768:896] = jnp.zeros((16, 8, 8, 128), bf16)
+    for owner in range(8):
+        for g in range(16):
+            at = owner * 128 + g * 8
+            out[g, owner, :, 0:768] = g_input[at : at + 8, :]
+        for block, vector in enumerate((gain, offset, project, gain_two, offset_two, down)):
+            row = vector[0:1, owner * 128 : (owner + 1) * 128]
+            out[block // 2, owner, block % 2 : block % 2 + 1, 768:896] = row.astype(bf16)
+        for block in range(12):
+            row = second[owner : owner + 1, block * 128 : (block + 1) * 128]
+            to = 12 + block
+            out[to // 2, owner, to % 2 : to % 2 + 1, 768:896] = row.astype(bf16)
+    place = core * 4 + z
+    for part, base in ((0, 0), (2, 4)):
+        for odd in range(2):
+            row = sums[0:1, part * 128 : (part + 1) * 128]
+            row = jnp.where(place % 2 == odd, row, 0.0).astype(bf16)
+            out[3, base + (place >> 1), odd : odd + 1, 768:896] = row
+    for side in range(2):
+        for block in range(4):
+            row = up[0:1, side * 512 + block * 128 : side * 512 + (block + 1) * 128].astype(bf16)
+            out[4 + block // 2, side * 4 + z, block % 2 : block % 2 + 1, 768:896] = row
+
+
+def pack_tail(info, g_input, mixed, vectors, second):
+    rows = [v.reshape(1, -1) for v in mixed + vectors]
+    out = pl.pallas_call(
+        pack_tail_kernel,
+        out_shape=jax.ShapeDtypeStruct((16, 8, 8, 896), bf16),
+        in_specs=[smem] + [whole] * 10,
+        out_specs=whole,
+        compiler_params=params_one,
+        name="pack_tail",
+    )(info, g_input, *rows, second)
+    return out.reshape(128, 8, 896)
 
 
 def pack_small(small, place):
@@ -933,38 +987,52 @@
     )
     small = jnp.concatenate([small.reshape(4, 768), jnp.zeros((12, 768), bf16)], axis=0)
     first = pack_first(corner[3:4], input_weight, small)
-    rows_in, first = lax.optimization_barrier((rows_in, first))
-    first = to_ctx(first)
-    raw_all = gather_z(rows_in)
-    corner_late, first = lax.optimization_barrier((corner, first))
-    first, raw_all = lax.optimization_barrier((first, raw_all))
-    vectors, in_bias, unit_bias = read_small(corner, first)
-    w_first = gather_x(first[:, 0:16].reshape(128, 768))
-    w_first = join_columns(corner, w_first, swap(w_first, "core"))
-    up_zero, second, rows, wide = pack_rest(
-        corner_late, input_weight, up_weight, down_weight, project_weight
+    (raw_all, first), (up_zero, second, rows, wide) = beside(
+        (rows_in, first),
+        lambda v: (gather_z(v[0]), to_ctx(v[1])),
+        corner,
+        lambda v: pack_rest(v, input_weight, up_weight, down_weight, project_weight),
+    )
+
+    def first_norm(given):
+        first, raw_all = given
+        vectors, in_bias, unit_bias = read_small(corner, first)
+        unit = norm_parts(raw_all.astype(f32))[0]
+        normed_all = (unit * vectors[0] + vectors[1]).astype(bf16)
+        return vectors, in_bias, unit_bias, normed_all, unit.astype(bf16)
+
+    def first_weight(given):
+        first, raw_all, rows = given
+        (w_first, rows), parts = beside(
+            (first[:, 0:16].reshape(128, 768), rows),
+            lambda v: (gather_x(v[0]), swap(v[1], "y_hi")),
+            (first, raw_all),
+            first_norm,
+        )
+        return join_columns(corner, w_first, swap(w_first, "core")), rows, parts
+
+    up_zero, (w_first, rows, (vectors, in_bias, unit_bias, normed_all, unit_all)) = beside(
+        up_zero, to_ctx, (first, raw_all, rows), first_weight
     )
     wide = lax.all_gather(wide, CTX, axis=0, tiled=True)
-    rows_zero = swap(rows, "y_hi")
     vector = [vectors[i] for i in range(12)]
-    nothing = (jnp.zeros((8, 128), f32), lambda v: v)
+    nothing = (jnp.zeros((8, 128), f32), lambda v: v, lambda v, *more: v, lambda v: v)
     unit_wide = first[:, 19:20, 256:768].reshape(8, 2, 4, 64)
     unit_wide = lax.dynamic_index_in_dim(unit_wide, core, 1, keepdims=False)
     unit_wide = unit_wide.transpose(1, 0, 2).reshape(4, 1, 512).astype(f32)
     hidden = rows_in.astype(f32)
-    normed_all = norm(raw_all.astype(f32), vectors[0], vectors[1]).astype(bf16)
-    context, logsum, rows_kept, (up_zero, pieces) = forward_attention(
+    context, logsum, rows_kept, (pieces, second) = forward_attention(
         normed_all,
         w_first,
         in_bias[0],
         info,
         slopes,
         core,
-        ((up_zero, rows_zero), lambda v: (to_ctx(v[0]), gather_x(v[1]))),
-    )
-    down_zero, project_zero, project_one = join_rows(
-        corner, down_weight, project_weight, pieces, swap(pieces, "core")
-    )
+        ((rows, second), lambda v: (gather_x(v[0]), to_ctx(v[1]))),
+    )
+    other = swap(pieces, "core")
+    project_zero, project_one = join_project(corner, project_weight, pieces, other)
+    context, wide = lax.optimization_barrier((context, wide))
     params_0 = (
         vector[0],
         vector[1],
@@ -975,23 +1043,30 @@
         vector[3],
         vector[4],
     )
-    wide, context = lax.optimization_barrier((wide, context))
-    wide = lax.all_gather(wide, "x")
-    (up_zero, second), (middle, normed_two) = beside(
-        (up_zero.reshape(128, D), second),
-        lambda v: (gather_x(v[0]), to_ctx(v[1])),
-        (hidden, context),
-        lambda v: with_rows(*forward_middle(*v, params_0)),
-    )
-    up_zero = join_columns(corner, up_zero, swap(up_zero, "core"))
+
+    def fetch_other(halves, width):
+        return join_halves(corner, halves, swap(halves, "core"), (width,))[0]
+
+    middle, normed, up_zero = forward_middle(
+        hidden, context, params_0, up_zero, lambda v: fetch_other(v, D)
+    )
+    wide = lax.all_gather(after(wide, normed), "x")
+    normed_two, (w_second, down_zero) = beside(
+        normed,
+        gather_z,
+        (second, pieces, other),
+        lambda v: (fetch_other(v[0], 768), join_down(corner, down_weight, v[1], v[2])),
+    )
     params_0 = params_0 + (up_zero, unit_bias[0], down_zero, vector[5])
     before = dot(normed_two, up_zero) + unit_bias[0]
     activated = gelu(before).astype(bf16)
     last = (middle, activated)
     kept_0 = (hidden, normed_all, logsum, rows_kept, context, middle, normed_two, before, activated)
-    w_second = gather_x(second.reshape(128, 768))
-    w_second = join_columns(corner, w_second, swap(w_second, "core"))
-    hidden = last_sum(last, params_0, scatter_parts(last_send(last, params_0)))
+    parts, hidden = beside(
+        last_send(last, params_0), scatter_parts, last, lambda v: last_own(v, params_0)
+    )
+    hidden = sum_parts(hidden, parts)
+    normed_all = gather_z(norm(hidden, vector[6], vector[7]).astype(bf16))
     params_1 = (
         vector[6],
         vector[7],
@@ -1002,27 +1077,24 @@
         vector[9],
         vector[10],
     )
-    normed_all = gather_z(norm(hidden, vector[6], vector[7]).astype(bf16))
     gradient = regroup(cotangent[0], core, y_hi)
     context, logsum, rows_kept, grad_other = forward_attention(
         normed_all, w_second, in_bias[1], info, slopes, core, (gradient, lambda v: swap(v, "core"))
     )
-    middle, normed_two = forward_middle(hidden, context, params_1)
-    pair_rows = jnp.concatenate([normed_two, swap(normed_two, "core")])
-    own, other, before = wide_forward(pair_rows, wide, unit_wide)
+    middle, normed_two, _ = forward_middle(hidden, context, params_1)
+    own, other, d_own, d_other, sum_up, wide_grads = wide_part(
+        normed_two, swap(normed_two, "core"), gradient, grad_other, wide, unit_wide
+    )
+    d_normed = d_own + swap(d_other, "core").astype(f32)
     output = middle + (own + swap(other, "core").astype(f32)) + vector[11]
     kept_1 = (hidden, normed_all, logsum, rows_kept, context, middle)
-    own, other, sum_up, wide_grads = wide_back(
-        jnp.concatenate([gradient, grad_other]), pair_rows, before, wide
-    )
-    d_normed = own + swap(other, "core").astype(f32)
     wide_grads = lax.psum_scatter(wide_grads, "x", scatter_dimension=0, tiled=True)[0]
     units = lax.dynamic_update_slice_in_dim(
         jnp.zeros((8, 2, 4, 64), f32), sum_up.reshape(4, 8, 64).transpose(1, 0, 2)[:, None], core, 1
     )
     gradient = gradient.astype(f32)
 
-    left, finish, inner_1 = backward(
+    _, vectors_1, _, g_input, grad_out_all, scatter, finish = backward(
         gradient,
         d_normed,
         units.reshape(8, 512),
@@ -1032,66 +1104,82 @@
         slopes,
         core,
         nothing,
-        lambda crossed, g_input, g_project: pack_inner(g_project, g_input),
-    )
-    gradient, small_1 = finish(left)
-    grad_down = gather_z(gradient.astype(bf16))
-    grad_down, wide_grads, inner_1 = lax.optimization_barrier((grad_down, wide_grads, inner_1))
+        lambda *given: None,
+    )
+    left, inner_1 = scatter(
+        lambda: pack_inner(outer(context, grad_out_all).astype(bf16), g_input())
+    )
+    gradient, norm_sums = finish(left)
+    packed_1 = pack_small(norm_sums + vectors_1, place)
+    grad_down, wide_grads = beside(
+        gradient.astype(bf16),
+        gather_z,
+        wide_grads,
+        lambda v: sum_pairs(v, y_lo, "y_lo").astype(bf16),
+    )
+    inner_1, wide_grads = lax.optimization_barrier((inner_1, wide_grads))
     inner_1 = lax.psum_scatter(inner_1, GRP, scatter_dimension=0, tiled=True)[0]
-
-    def to_owners(value):
-        axes = ("y_lo",) + CTX
-        return lax.all_to_all(value, axes, split_axis=0, concat_axis=0, tiled=True)
-
-    wide_grads, (d_normed, summed, sum_up) = beside(
-        wide_grads.reshape(16, 64, D),
-        to_owners,
-        grad_down,
-        lambda v: backward_two(v, params_0, kept_0, core),
-    )
+    wide_grads, d_before = beside(
+        wide_grads,
+        to_ctx,
+        (grad_down, kept_0[7]),
+        lambda v: jax.vjp(gelu, v[1])[1](dot_t(v[0], params_0[10]))[0].astype(bf16),
+    )
+    d_normed, grads, sum_up = backward_two(grad_down, d_before, params_0, kept_0, core)
     wide_grads = lax.all_gather(jnp.sum(wide_grads.astype(f32), axis=0).astype(bf16), GRP)
-    units = lax.dynamic_update_slice_in_dim(
-        jnp.zeros((2, 4, 512), f32), sum_up.reshape(2, 1, 512), z, 1
-    )
-
-    def work_one(got, g_input, g_project):
-        low = inner_core(pack_inner(g_project, g_input), core)
-        both = jnp.concatenate([jnp.sum(got.astype(f32), axis=0).astype(bf16), inner_1], axis=1)
-        both = y_rows(both, y_hi)
-        spread = spread_z(jnp.concatenate([both[:, D : 2 * D], both[:, 2 * D + 256 :]], axis=1), z)
-        both = jnp.concatenate(
-            [both[:, :D], spread[:, :D], both[:, 2 * D : 2 * D + 256], spread[:, D:]], axis=1
-        )
-        return low, both
-
-    left, finish, (low, both) = backward(
+
+    def with_project(summed, context, grad_out_all):
+        g_project = outer(context, grad_out_all).astype(bf16)
+        rows = g_project.reshape(2, 16, 8, 4, 256).transpose(1, 0, 3, 2, 4).reshape(16, 64, 256)
+        return jnp.concatenate([summed, core_sum(rows, core)], axis=-1)
+
+    def tail_pack(d_joined, sums, vectors):
+        w_in = params_0[2].astype(f32)
+        gain = jnp.sum(outer(unit_all, d_joined) * w_in, axis=1)
+        offset = jnp.sum(d_joined.astype(f32), axis=0, keepdims=True)
+        offset = jnp.sum(offset * w_in, axis=1)
+        g_input = outer(kept_0[1], d_joined).astype(bf16)
+        return pack_tail(info, g_input, (gain, offset), vectors, packed_1)
+
+    crossed, _, low, _, _, scatter, finish = backward(
         gradient,
         d_normed,
-        units.reshape(8, 512),
+        sum_up,
         params_0,
         kept_0,
         info,
         slopes,
         core,
-        (summed, to_xy),
-        work_one,
-    )
-    low, (gradient, small_0) = beside(low, lambda v: inner_x(v, x), left, finish)
-    full = lax.all_gather(both, GRP)
-    packed = jnp.concatenate([pack_small(s, place) for s in (small_0, small_1)], axis=1)
-    low, packed = beside(
-        low, lambda v: inner_y(v, y_lo, y_hi), packed, lambda v: small_z(v, z)
-    )
-    low, (packed, gradient) = beside(
-        low,
-        lambda v: inner_z(v, z),
-        (packed, gradient),
-        lambda v: (small_y(v[0], y_hi), regroup(v[1], core, y_hi)),
-    )
-    low, packed = beside(low, lambda v: jnp.stack([v, swap(v, "y_lo")]), packed, small_x)
-    low, packed = beside(low, gather_x, packed, lambda v: v + swap(v, "core"))
-    g_input, g_project = unpack_inner(corner, low, swap(low, "core"), full)
+        (grads, lambda v: core_sum(pack_outer(*v), core), with_project, to_xy),
+        tail_pack,
+    )
+
+    def to_all(value):
+        return lax.all_to_all(value, GRP + CTX, split_axis=0, concat_axis=0, tiled=True)
+
+    def outer_rows(given):
+        crossed, inner_1 = given
+        both = jnp.sum(crossed.astype(f32), axis=0).astype(bf16)
+        both = y_rows(jnp.concatenate([both, inner_1], axis=1), y_hi)
+        at = 2 * D + 512
+        spread = spread_z(jnp.concatenate([both[:, D : 2 * D], both[:, at:]], axis=1), z)
+        return [both[:, :D], spread[:, :D], both[:, 2 * D : at], spread[:, D:]]
+
+    low, (both, wide_grads) = beside(
+        low, to_all, (crossed, inner_1, wide_grads), lambda v: (outer_rows(v[:2]), v[2])
+    )
+    left, _ = scatter(lambda: None)
+    gradient = regroup(finish(left)[0], core, y_hi)
+    low = low.reshape(32, 32, 896).astype(f32)
+    vector = jnp.sum(low[:, :, 768:].reshape(128, 8, 128), axis=0)
+    vector = jnp.pad(vector, ((0, 24), (0, 0)))
+    low = jnp.sum(low[:, :, :768], axis=0)
+    low = jnp.concatenate([low, vector], axis=1).astype(bf16)
+    full = lax.all_gather(jnp.concatenate(both + [low], axis=1), GRP)
+    vector = full[0:12, 0:2, 4096:4224].astype(f32)
+    g_input, g_project = unpack_inner(full)
     g_down, g_up = unpack_outer(full, wide_grads)
+    packed = vector.reshape(LAYERS * 1536)
     vector = packed.reshape(LAYERS, -1)
     parts = [vector[:, i * 128 : (i + 1) * 128] for i in range(6)]
     return (

time: 682 us -> 657 us (0.963)
  starting transfers between devices: 166 us -> 134 us
  other arithmetic: 68.1 us -> 53.4 us
  local copies, waits for them, and re-layouts: 39.4 us -> 53.1 us
  waiting for transfers between devices: 267 us -> 274 us
    ppermute x21 -> x6, waiting for transfers between devices: 28.1 us -> 0.02 us  [shift_x(): return lax.ppermute(value, 'x', [(i, (i + step) % 4) for i in range(4)])]
    ppermute x5, waiting for transfers between devices: 0.52 us -> 18.2 us  [regroup(): got = lax.ppermute(value, ('core', 'y_hi'), [(1, 2), (2, 1)])]
    ppermute x21 -> x6, starting transfers between devices: 22.6 us -> 7.99 us  [shift_x(): return lax.ppermute(value, 'x', [(i, (i + step) % 4) for i in range(4)])]
    unnamed x250 -> x211, local copies, waits for them, and re-layouts: 23.8 us -> 37.5 us
    all_to_all x1, waiting for transfers between devices: 0.01 us -> 12.9 us  [to_xy(): lax.all_to_all(value, ('x', 'y_lo'), split_axis=0, concat_axis=0, tiled=T...]
    ppermute x6 -> x0, starting transfers between devices: 8.92 us -> none  [across_y(): total = total + lax.ppermute(value, axes, list(enumerate(to))).astype(f32)]
    all_gather x1, waiting for transfers between devices: 0.01 us -> 8.31 us  [on_device(): lax.all_gather(jnp.sum(wide_grads.astype(f32), axis=0).astype(bf16), GRP)]
    ppermute x5, starting transfers between devices: 31.9 us -> 24.1 us  [regroup(): got = lax.ppermute(value, ('core', 'y_hi'), [(1, 2), (2, 1)])]
  transfers between devices with their start and end apart: 111 -> 83, of which waited for: 59 -> 47; matrix products, arithmetic and copies ran while one was open for 17% -> 16% of each run, Pallas kernels for 7% -> 8%
where the time goes in v6:
time: 657 us; the launch traced here: 648 us
  waiting for transfers between devices  274 us (42%)
  starting transfers between devices  134 us (20%)
  Pallas kernels  74.3 us (11%)
  other arithmetic  53.4 us (8%)
  local copies, waits for them, and re-layouts  53.1 us (8%)
  matrix products  44.2 us (7%)
  between operations  16 us (2%)
    ppermute x39, waiting for transfers between devices, shift_z(): return lax.ppermute(value, 'z', [(i, (i + step) % 4) for i in range(4)])  199 us
    ppermute x39, starting transfers between devices, shift_z(): return lax.ppermute(value, 'z', [(i, (i + step) % 4) for i in range(4)])  46.4 us
    unnamed x211, local copies, waits for them, and re-layouts  37.5 us
    ppermute x5, starting transfers between devices, regroup(): got = lax.ppermute(value, ('core', 'y_hi'), [(1, 2), (2, 1)])  24.1 us
    pallas_call x2, Pallas kernels, attend_back(): pl.pallas_call(attend_back_kernel, out_shape=(jax.ShapeDtypeStruct((HALF,...  22.1 us
    ppermute x21, starting transfers between devices, swap(): return lax.ppermute(value, axis, [(0, 1), (1, 0)])  21.5 us
    all_to_all x4, starting transfers between devices, to_ctx(): return lax.all_to_all(value, CTX, split_axis=0, concat_axis=0, tiled=True)  21 us
    dot_general x9, matrix products, dot_t(): lax.dot_general(left, right, (((1,), (1,)), ((), ())), preferred_element_...  19.3 us
  transfers between devices with their start and end apart: 83, of which 47 were waited for; matrix products, arithmetic and copies ran while one was open for 16% of the time, Pallas kernels for 8%

profile of v6, /device:TPU:1, one launch (start us, length us, event | category | flops | bytes accessed | tf_op | source)
XLA Modules:
  0.0 648.5 jit_solution(13013245547762674903)
XLA Ops:
  7.2 6.3 collective-permute-start
  24.1 3.3 collective-permute-start.2
  28.1 3.5 all-to-all-start
  36.7 8.3 %collective-permute-done.2 = bf16[192,1024]{1,0:T(8,128)(2,1)} collective-permute-done((bf16[192,1024]{1,0:T(8,128)(2,1)S(1)}, bf16[192,1024]{1,0:T(8,128)(2,1)}, u32[]{:S(2)}, u32[]{:S(2)}) %collective-permute-start.2) | collective-permute-done | bytes 393248 | tf_op jit(solution)/shard_map/ppermute | solution.py:31
  46.4 2.8 collective-permute-start.5
  52.3 6.1 all-to-all-start.1
  68.5 6.8 %all-to-all-done.1.mine = bf16[8,64,1024]{2,1,0:T(8,128)(2,1)S(1)} async-done(((bf16[8,64,1024]{2,1,0:T(8,128)(2,1)}), bf16[8,64,1024]{2,1,0:T(8,128)(2,1)S(1)}, u32[]{:S(2)}, u32[]{:S(2)}) %all-to-all-start.1) | async-done | bytes 1048608 | tf_op jit(solution)/shard_map/all_to_all | solution.py:597
  75.9 2.8 add_convert_fusion.1
  79.7 2.7 collective-permute-start.13
  83.7 3.0 collective-permute-start.12
  86.8 4.3 all-to-all-start.2
  91.4 3.0 collective-permute-start.10
  95.6 9.5 %attend.2 = (bf16[768,128]{1,0:T(8,128)(2,1)S(1)}, bf16[768,128]{1,0:T(8,128)(2,1)}, f32[2,1536]{1,0:T(2,128)S(1)}, bf16[1536,384]{1,0:T(8,128)(2,1)S(1)}) custom-call(s32[4]{0:T(128)S(1)} %pad_add_fusion.info, f32[2]{0:T(128)S(1)} %multiply_exponential_fusion.slopes, bf16[768,384]{1,0:T(8,128)(2,1)S(1)} %get-tuple-element.421.mine, ...), custom_call_target="tpu_custom_call" | custom-call | flops 1000000 | bytes 36000000 | tf_op jit(solution)/shard_map/attend/pallas_call | solution.py:208
  121.2 3.0 collective-permute-start.16
  129.2 11.4 %collective-permute-done.16 = bf16[192,1024]{1,0:T(8,128)(2,1)S(1)} collective-permute-done((bf16[192,1024]{1,0:T(8,128)(2,1)S(1)}, bf16[192,1024]{1,0:T(8,128)(2,1)S(1)}, u32[]{:S(2)}, u32[]{:S(2)}) %collective-permute-start.16) | collective-permute-done | bytes 393248 | tf_op jit(solution)/shard_map/ppermute | solution.py:31
  140.6 4.6 collective-permute-done.18
  153.3 15.5 %collective-permute-done.20 = bf16[192,1024]{1,0:T(8,128)(2,1)S(1)} collective-permute-done((bf16[192,1024]{1,0:T(8,128)(2,1)}, bf16[192,1024]{1,0:T(8,128)(2,1)S(1)}, u32[]{:S(2)}, u32[]{:S(2)}) %collective-permute-start.20) | collective-permute-done | bytes 393248 | tf_op jit(solution)/shard_map/ppermute | solution.py:31
  171.7 4.1 fusion.24
  177.3 2.9 collective-permute-start.24
  180.8 5.5 collective-permute-start.27
  187.0 9.4 %collective-permute-done.24 = bf16[192,1024]{1,0:T(8,128)(2,1)S(1)} collective-permute-done((bf16[192,1024]{1,0:T(8,128)(2,1)S(1)}, bf16[192,1024]{1,0:T(8,128)(2,1)S(1)}, u32[]{:S(2)}, u32[]{:S(2)}) %collective-permute-start.24) | collective-permute-done | bytes 393248 | tf_op jit(solution)/shard_map/ppermute | solution.py:31
  196.4 4.2 collective-permute-done.26
  204.3 16.8 %collective-permute-done.28 = bf16[192,1024]{1,0:T(8,128)(2,1)S(1)} collective-permute-done((bf16[192,1024]{1,0:T(8,128)(2,1)S(1)}, bf16[192,1024]{1,0:T(8,128)(2,1)S(1)}, u32[]{:S(2)}, u32[]{:S(2)}) %collective-permute-start.28) | collective-permute-done | bytes 393248 | tf_op jit(solution)/shard_map/ppermute | solution.py:31
  227.3 8.3 %attend.3 = (bf16[768,128]{1,0:T(8,128)(2,1)S(1)}, bf16[768,128]{1,0:T(8,128)(2,1)S(1)}, f32[2,1536]{1,0:T(2,128)S(1)}, bf16[1536,384]{1,0:T(8,128)(2,1)S(1)}) custom-call(s32[4]{0:T(128)S(1)} %pad_add_fusion.info, f32[2]{0:T(128)S(1)} %multiply_exponential_fusion.slopes, bf16[768,384]{1,0:T(8,128)(2,1)S(1)} %get-tuple-element.413.mine, ...), custom_call_target="tpu_custom_call" | custom-call | flops 1000000 | bytes 36000000 | tf_op jit(solution)/shard_map/attend/pallas_call | solution.py:208
  241.8 7.6 %collective-permute-done.34 = bf16[192,1024]{1,0:T(8,128)(2,1)S(1)} collective-permute-done((bf16[192,1024]{1,0:T(8,128)(2,1)S(1)}, bf16[192,1024]{1,0:T(8,128)(2,1)S(1)}, u32[]{:S(2)}, u32[]{:S(2)}) %collective-permute-start.34) | collective-permute-done | bytes 393248 | tf_op jit(solution)/shard_map/ppermute | solution.py:31
  249.4 3.1 collective-permute-done.35
  252.4 8.8 %collective-permute-done.36 = bf16[192,1024]{1,0:T(8,128)(2,1)S(1)} collective-permute-done((bf16[192,1024]{1,0:T(8,128)(2,1)S(1)}, bf16[192,1024]{1,0:T(8,128)(2,1)S(1)}, u32[]{:S(2)}, u32[]{:S(2)}) %collective-permute-start.36) | collective-permute-done | bytes 393248 | tf_op jit(solution)/shard_map/ppermute | solution.py:31
  266.1 18.2 %wide_part.1 = (f32[192,1024]{1,0:T(8,128)}, bf16[192,1024]{1,0:T(8,128)(2,1)}, f32[192,1024]{1,0:T(8,128)}, bf16[192,1024]{1,0:T(8,128)(2,1)}, f32[4,1,512]{2,1...) custom-call(bf16[192,1024]{1,0:T(8,128)(2,1)} %add_convert_fusion.2.rows_own, ...), custom_call_target="tpu_custom_call" | custom-call | flops 11274289152 | bytes 50000000 | tf_op jit(solution)/shard_map/wide_part/pallas_call | solution.py:357
  288.3 2.9 fusion.64
  295.0 8.8 %collective-permute-done.41 = bf16[192,1024]{1,0:T(8,128)(2,1)} collective-permute-done((bf16[192,1024]{1,0:T(8,128)(2,1)}, bf16[192,1024]{1,0:T(8,128)(2,1)}, u32[]{:S(2)}, u32[]{:S(2)}) %collective-permute-start.41) | collective-permute-done | bytes 393248 | tf_op jit(solution)/shard_map/ppermute | solution.py:31
  303.9 6.8 %collective-permute-done.42 = bf16[192,1024]{1,0:T(8,128)(2,1)} collective-permute-done((bf16[192,1024]{1,0:T(8,128)(2,1)}, bf16[192,1024]{1,0:T(8,128)(2,1)}, u32[]{:S(2)}, u32[]{:S(2)}) %collective-permute-start.42) | collective-permute-done | bytes 393248 | tf_op jit(solution)/shard_map/ppermute | solution.py:31
  317.1 11.4 %attend_back.2 = (bf16[768,384]{1,0:T(8,128)(2,1)S(1)}, bf16[768,384]{1,0:T(8,128)(2,1)}, f32[1,384]{1,0:T(1,128)S(1)}) custom-call(s32[4]{0:T(128)S(1)} %pad_add_fusion.info, f32[2]{0:T(128)S(1)} %multiply_exponential_fusion.slopes, bf16[1536,384]{1,0:T(8,128)(2,1)S(1)} %copy-done.26, bf16[768,128]{1,0:T(8,128)(2,1)S(1)} %get-tuple-element.427.mine, ...), custom_call_target="tpu_custom_call" | custom-call | flops 1000000 | bytes 48000000 | tf_op jit(solution)/shard_map/attend_back/pallas_call | solution.py:232
  343.9 13.3 %collective-permute-done.46 = bf16[192,1024]{1,0:T(8,128)(2,1)} collective-permute-done((bf16[192,1024]{1,0:T(8,128)(2,1)}, bf16[192,1024]{1,0:T(8,128)(2,1)}, u32[]{:S(2)}, u32[]{:S(2)}) %collective-permute-start.46) | collective-permute-done | bytes 393248 | tf_op jit(solution)/shard_map/ppermute | solution.py:31
  357.2 3.5 collective-permute-done.48
  368.4 2.6 collective-permute-start.50
  372.1 6.1 collective-permute-done.49
  378.2 9.5 %collective-permute-done.50 = bf16[192,1024]{1,0:T(8,128)(2,1)S(1)} collective-permute-done((bf16[192,1024]{1,0:T(8,128)(2,1)S(1)}, bf16[192,1024]{1,0:T(8,128)(2,1)S(1)}, u32[]{:S(2)}, u32[]{:S(2)}) %collective-permute-start.50) | collective-permute-done | bytes 393248 | tf_op jit(solution)/shard_map/ppermute | solution.py:31
  390.3 2.6 fusion.29
  392.9 7.1 %all-to-all-start.3 = ((bf16[8,64,1024]{2,1,0:T(8,128)(2,1)}), bf16[8,64,1024]{2,1,0:T(8,128)(2,1)}, u32[]{:S(2)}, u32[]{:S(2)}) async-start(bf16[8,64,1024]{2,1,0:T(8,128)(2,1)} %fusion.29), calls=%async_computation.4 | async-start | bytes 2097152 | tf_op jit(solution)/shard_map/all_to_all | solution.py:597
  400.9 7.6 %fusion.16 = bf16[768,1024]{1,0:T(8,128)(2,1)} fusion(f32[768,1024]{1,0:T(8,128)} %get-tuple-element.304, bf16[768,1024]{1,0:T(8,128)(2,1)} %pad_maximum_fusion.6, bf16[1024,1024]{1,0:T(8,128)(2,1)} %copy-done.4), kind=kOutput, calls=%fused_computation.28 | convolution fusion | flops 1626341376 | bytes 8388608 | tf_op jit(solution)/shard_map/dot_general | solution.py:65
  408.5 5.5 all-to-all-done.3
  414.0 3.5 convolution_convert_fusion.5
  425.9 2.6 collective-permute-done.53
  430.6 11.3 %collective-permute-done.55 = bf16[192,1024]{1,0:T(8,128)(2,1)S(1)} collective-permute-done((bf16[192,1024]{1,0:T(8,128)(2,1)S(1)}, bf16[192,1024]{1,0:T(8,128)(2,1)S(1)}, u32[]{:S(2)}, u32[]{:S(2)}) %collective-permute-start.55) | collective-permute-done | bytes 393248 | tf_op jit(solution)/shard_map/ppermute | solution.py:31
  452.7 15.5 %collective-permute-done.56 = bf16[192,1024]{1,0:T(8,128)(2,1)S(1)} collective-permute-done((bf16[192,1024]{1,0:T(8,128)(2,1)S(1)}, bf16[192,1024]{1,0:T(8,128)(2,1)S(1)}, u32[]{:S(2)}, u32[]{:S(2)}) %collective-permute-start.56) | collective-permute-done | bytes 393248 | tf_op jit(solution)/shard_map/ppermute | solution.py:31
  468.6 3.3 fusion
  476.7 4.5 all-to-all-start.4
  485.4 10.7 %attend_back.3 = (bf16[768,384]{1,0:T(8,128)(2,1)S(1)}, bf16[768,384]{1,0:T(8,128)(2,1)S(1)}, f32[1,384]{1,0:T(1,128)S(1)}) custom-call(s32[4]{0:T(128)S(1)} %pad_add_fusion.info, f32[2]{0:T(128)S(1)} %multiply_exponential_fusion.slopes, bf16[1536,384]{1,0:T(8,128)(2,1)S(1)} %copy-done.24, bf16[768,128]{1,0:T(8,128)(2,1)S(1)} %get-tuple-element.424.mine, ...), custom_call_target="tpu_custom_call" | custom-call | flops 1000000 | bytes 48000000 | tf_op jit(solution)/shard_map/attend_back/pallas_call | solution.py:232
  504.2 12.9 %all-to-all-done.4 = bf16[8,64,2304]{2,1,0:T(8,128)(2,1)} async-done(((bf16[8,64,2304]{2,1,0:T(8,128)(2,1)}), bf16[8,64,2304]{2,1,0:T(8,128)(2,1)}, u32[]{:S(2)}, u32[]{:S(2)}) %all-to-all-start.4) | async-done | bytes 2359328 | tf_op jit(solution)/shard_map/all_to_all | solution.py:749
  517.1 8.3 %all-gather.12.cloned.1.call-done = bf16[1024,1024]{1,0:T(8,128)(2,1)} async-done(((bf16[64,1024]{1,0:T(8,128)(2,1)}), bf16[1024,1024]{1,0:T(8,128)(2,1)}) %all-gather.12.cloned.1.call-update) | async-done | bytes 2097168 | tf_op jit(solution)/shard_map/all_gather | solution.py:1129
  527.5 3.5 collective-permute-start.67
  531.0 5.4 collective-permute-done.67
  539.4 7.9 %all-to-all-start.5 = ((bf16[128,8,896]{2,1,0:T(8,128)(2,1)}), bf16[128,8,896]{2,1,0:T(8,128)(2,1)S(1)}, u32[]{:S(2)}, u32[]{:S(2)}) async-start(bf16[128,8,896]{2,1,0:T(8,128)(2,1)} %bitcast.75), calls=%async_computation.7 | async-start | bytes 3670016 | tf_op jit(solution)/shard_map/all_to_all | solution.py:1158
  547.3 3.4 collective-permute-start.69
  551.8 9.7 %collective-permute-done.69 = bf16[8,1792]{1,0:T(8,128)(2,1)S(1)} collective-permute-done((bf16[8,1792]{1,0:T(8,128)(2,1)}, bf16[8,1792]{1,0:T(8,128)(2,1)S(1)}, u32[]{:S(2)}, u32[]{:S(2)}) %collective-permute-start.69) | collective-permute-done | bytes 28704 | tf_op jit(solution)/shard_map/ppermute | solution.py:31
  562.1 4.6 collective-permute-done.70
  570.7 3.8 all-to-all-done.5
  584.4 4.7 collective-permute-start.39
  590.9 2.8 collective-permute-done.64
  593.8 9.7 %collective-permute-done.65 = bf16[192,1024]{1,0:T(8,128)(2,1)S(1)} collective-permute-done((bf16[192,1024]{1,0:T(8,128)(2,1)S(1)}, bf16[192,1024]{1,0:T(8,128)(2,1)S(1)}, u32[]{:S(2)}, u32[]{:S(2)}) %collective-permute-start.65) | collective-permute-done | bytes 393248 | tf_op jit(solution)/shard_map/ppermute | solution.py:31
  604.2 4.4 collective-permute-start.66
  608.7 5.0 collective-permute-done.39
  614.6 13.2 %collective-permute-done.66 = f32[192,1024]{1,0:T(8,128)S(1)} collective-permute-done((f32[192,1024]{1,0:T(8,128)S(1)}, f32[192,1024]{1,0:T(8,128)S(1)}, u32[]{:S(2)}, u32[]{:S(2)}) %collective-permute-start.66) | collective-permute-done | bytes 786464 | tf_op jit(solution)/shard_map/ppermute | solution.py:43
  637.4 4.1 unpack_outer.1
  (494 shorter events, 204.3 us)
Async XLA Ops:
  7.2 14.0 %collective-permute-start = (bf16[192,1024]{1,0:T(8,128)(2,1)}, bf16[192,1024]{1,0:T(8,128)(2,1)S(1)}, u32[]{:S(2)}, u32[]{:S(2)}) collective-permute-start(bf16[192,1024]{1,0:T(8,128)(2,1)} %bitcast.221), channel_id=1, source_target_pairs={{4,8},{8,4},{5,9},{9,5},{6,10},{10,6},{7,11},{11,7},{20,24},{24,20... | collective-permute-start | bytes 1179656 | tf_op jit(solution)/shard_map/ppermute | solution.py:43
  22.4 14.3 %collective-permute-start.1 = (bf16[192,1024]{1,0:T(8,128)(2,1)S(1)}, bf16[192,1024]{1,0:T(8,128)(2,1)}, u32[]{:S(2)}, u32[]{:S(2)}) collective-permute-start(bf16[192,1024]{1,0:T(8,128)(2,1)S(1)} %get-tuple-element.187), channel_id=1, source_target_pairs={{0,1},{1,2},{2,3},{3,0},{4,5},{5,6},{6,7},{7,4},{8,9},{9,10},{10,1... | collective-permute-start | bytes 1179656 | tf_op jit(solution)/shard_map/ppermute | solution.py:31
  24.1 20.8 %collective-permute-start.2 = (bf16[192,1024]{1,0:T(8,128)(2,1)S(1)}, bf16[192,1024]{1,0:T(8,128)(2,1)}, u32[]{:S(2)}, u32[]{:S(2)}) collective-permute-start(bf16[192,1024]{1,0:T(8,128)(2,1)S(1)} %get-tuple-element.187), channel_id=1, source_target_pairs={{0,2},{1,3},{2,0},{3,1},{4,6},{5,7},{6,4},{7,5},{8,10},{9,11},{10,... | collective-permute-start | bytes 1179656 | tf_op jit(solution)/shard_map/ppermute | solution.py:31
  27.4 17.5 %collective-permute-start.3 = (bf16[192,1024]{1,0:T(8,128)(2,1)S(1)}, bf16[192,1024]{1,0:T(8,128)(2,1)}, u32[]{:S(2)}, u32[]{:S(2)}) collective-permute-start(bf16[192,1024]{1,0:T(8,128)(2,1)S(1)} %get-tuple-element.187), channel_id=1, source_target_pairs={{0,3},{1,0},{2,1},{3,2},{4,7},{5,4},{6,5},{7,6},{8,11},{9,8},{10,9... | collective-permute-start | bytes 1179656 | tf_op jit(solution)/shard_map/ppermute | solution.py:31
  28.1 18.2 %all-to-all-start = ((bf16[8,32,768]{2,1,0:T(8,128)(2,1)}), bf16[8,32,768]{2,1,0:T(8,128)(2,1)S(1)}, u32[]{:S(2)}, u32[]{:S(2)}) async-start(bf16[8,32,768]{2,1,0:T(8,128)(2,1)} %pack_first.1), calls=%async_computation | async-start | bytes 786432 | tf_op jit(solution)/shard_map/all_to_all | solution.py:597
  31.6 87.6 %all-gather.8.cloned.1.call-start = ((), (), s32[]{:S(2)}) async-start(), calls=%async_computation.8 | async-start | bytes 2359296 | tf_op jit(solution)/shard_map/all_gather | solution.py:1017
  46.4 14.4 %collective-permute-start.5 = (bf16[128,768]{1,0:T(8,128)(2,1)S(1)}, bf16[128,768]{1,0:T(8,128)(2,1)S(1)}, u32[]{:S(2)}, u32[]{:S(2)}) collective-permute-start(bf16[128,768]{1,0:T(8,128)(2,1)S(1)} %bitcast.215), channel_id=1, source_target_pairs={{0,64},{32,96},{64,0},{96,32},{1,65},{33,97},{65,1},{97,33},{2,66}... | collective-permute-start | bytes 589832 | tf_op jit(solution)/shard_map/ppermute | solution.py:35
  49.2 11.6 %collective-permute-start.6 = (bf16[128,768]{1,0:T(8,128)(2,1)S(1)}, bf16[128,768]{1,0:T(8,128)(2,1)}, u32[]{:S(2)}, u32[]{:S(2)}) collective-permute-start(bf16[128,768]{1,0:T(8,128)(2,1)S(1)} %bitcast.216), channel_id=1, source_target_pairs={{0,96},{32,0},{64,32},{96,64},{1,97},{33,1},{65,33},{97,65},{2,98}... | collective-permute-start | bytes 589832 | tf_op jit(solution)/shard_map/ppermute | solution.py:35
  50.1 10.7 %collective-permute-start.4 = (bf16[128,768]{1,0:T(8,128)(2,1)S(1)}, bf16[128,768]{1,0:T(8,128)(2,1)}, u32[]{:S(2)}, u32[]{:S(2)}) collective-permute-start(bf16[128,768]{1,0:T(8,128)(2,1)S(1)} %bitcast.217), channel_id=1, source_target_pairs={{0,32},{32,64},{64,96},{96,0},{1,33},{33,65},{65,97},{97,1},{2,34}... | collective-permute-start | bytes 589832 | tf_op jit(solution)/shard_map/ppermute | solution.py:35
  52.3 23.1 %all-to-all-start.1 = ((bf16[8,64,1024]{2,1,0:T(8,128)(2,1)}), bf16[8,64,1024]{2,1,0:T(8,128)(2,1)S(1)}, u32[]{:S(2)}, u32[]{:S(2)}) async-start(bf16[8,64,1024]{2,1,0:T(8,128)(2,1)} %get-tuple-element.198), calls=%async_computation.1 | async-start | bytes 2097152 | tf_op jit(solution)/shard_map/all_to_all | solution.py:597
  79.7 15.9 %collective-permute-start.13 = (bf16[768,384]{1,0:T(8,128)(2,1)}, bf16[768,384]{1,0:T(8,128)(2,1)}, u32[]{:S(2)}, u32[]{:S(2)}) collective-permute-start(bf16[768,384]{1,0:T(8,128)(2,1)} %get-tuple-element.420), channel_id=1, source_target_pairs={{0,8},{8,0},{1,9},{9,1},{2,10},{10,2},{3,11},{11,3},{4,12},{12,4},... | collective-permute-start | bytes 1769480 | tf_op jit(solution)/shard_map/ppermute | solution.py:39
  83.7 11.1 %collective-permute-start.12 = (s32[1,128]{1,0:T(1,128)S(1)}, s32[1,128]{1,0:T(1,128)S(1)}, u32[]{:S(2)}, u32[]{:S(2)}) collective-permute-start(s32[1,128]{1,0:T(1,128)S(1)} %broadcast_in_dim.12), channel_id=1, source_target_pairs={{4,8},{8,4},{5,9},{9,5},{6,10},{10,6},{7,11},{11,7},{20,24},{24,20... | collective-permute-start | bytes 1544 | tf_op jit(solution)/shard_map/ppermute | solution.py:43
  86.8 26.0 %all-to-all-start.2 = ((bf16[8,64,768]{2,1,0:T(8,128)(2,1)}), bf16[8,64,768]{2,1,0:T(8,128)(2,1)}, u32[]{:S(2)}, u32[]{:S(2)}) async-start(bf16[8,64,768]{2,1,0:T(8,128)(2,1)} %copy-done.27), calls=%async_computation.2 | async-start | bytes 1572864 | tf_op jit(solution)/shard_map/all_to_all | solution.py:597
  91.1 175.1 %all-gather.10.cloned.1.call-start = ((), (), s32[]{:S(2)}) async-start(), calls=%async_computation.11 | async-start | bytes 10485760 | tf_op jit(solution)/shard_map/all_gather | solution.py:1053
  91.1 17.6 %collective-permute-start.9 = (bf16[96,1024]{1,0:T(8,128)(2,1)}, bf16[96,1024]{1,0:T(8,128)(2,1)S(1)}, u32[]{:S(2)}, u32[]{:S(2)}) collective-permute-start(bf16[96,1024]{1,0:T(8,128)(2,1)} %collective-permute-done.7), channel_id=1, source_target_pairs={{0,32},{32,64},{64,96},{96,0},{1,33},{33,65},{65,97},{97,1},{2,34}... | collective-permute-start | bytes 589832 | tf_op jit(solution)/shard_map/ppermute | solution.py:35
  91.4 17.3 %collective-permute-start.10 = (bf16[96,1024]{1,0:T(8,128)(2,1)}, bf16[96,1024]{1,0:T(8,128)(2,1)}, u32[]{:S(2)}, u32[]{:S(2)}) collective-permute-start(bf16[96,1024]{1,0:T(8,128)(2,1)} %collective-permute-done.7), channel_id=1, source_target_pairs={{0,64},{32,96},{64,0},{96,32},{1,65},{33,97},{65,1},{97,33},{2,66}... | collective-permute-start | bytes 589832 | tf_op jit(solution)/shard_map/ppermute | solution.py:35
  94.4 14.3 %collective-permute-start.11 = (bf16[96,1024]{1,0:T(8,128)(2,1)}, bf16[96,1024]{1,0:T(8,128)(2,1)}, u32[]{:S(2)}, u32[]{:S(2)}) collective-permute-start(bf16[96,1024]{1,0:T(8,128)(2,1)} %collective-permute-done.7), channel_id=1, source_target_pairs={{0,96},{32,0},{64,32},{96,64},{1,97},{33,1},{65,33},{97,65},{2,98}... | collective-permute-start | bytes 589832 | tf_op jit(solution)/shard_map/ppermute | solution.py:35
  121.2 19.4 %collective-permute-start.16 = (bf16[192,1024]{1,0:T(8,128)(2,1)S(1)}, bf16[192,1024]{1,0:T(8,128)(2,1)S(1)}, u32[]{:S(2)}, u32[]{:S(2)}) collective-permute-start(bf16[192,1024]{1,0:T(8,128)(2,1)S(1)} %get-tuple-element.419), channel_id=1, source_target_pairs={{0,3},{1,0},{2,1},{3,2},{4,7},{5,4},{6,5},{7,6},{8,11},{9,8},{10,9... | collective-permute-start | bytes 1179656 | tf_op jit(solution)/shard_map/ppermute | solution.py:31
  124.2 16.4 %collective-permute-start.17 = (bf16[192,1024]{1,0:T(8,128)(2,1)S(1)}, bf16[192,1024]{1,0:T(8,128)(2,1)S(1)}, u32[]{:S(2)}, u32[]{:S(2)}) collective-permute-start(bf16[192,1024]{1,0:T(8,128)(2,1)S(1)} %get-tuple-element.418), channel_id=1, source_target_pairs={{0,2},{1,3},{2,0},{3,1},{4,6},{5,7},{6,4},{7,5},{8,10},{9,11},{10,... | collective-permute-start | bytes 1179656 | tf_op jit(solution)/shard_map/ppermute | solution.py:31
  124.8 20.3 %collective-permute-start.18 = (bf16[192,1024]{1,0:T(8,128)(2,1)S(1)}, bf16[192,1024]{1,0:T(8,128)(2,1)S(1)}, u32[]{:S(2)}, u32[]{:S(2)}) collective-permute-start(bf16[192,1024]{1,0:T(8,128)(2,1)S(1)} %get-tuple-element.417), channel_id=1, source_target_pairs={{0,1},{1,2},{2,3},{3,0},{4,5},{5,6},{6,7},{7,4},{8,9},{9,10},{10,1... | collective-permute-start | bytes 1179656 | tf_op jit(solution)/shard_map/ppermute | solution.py:31
  147.5 216.3 %reduce-scatter.3.cloned.1.call-start = ((), (), s32[]{:S(2)}) async-start(), calls=%async_computation.9 | async-start | bytes 10485760 | tf_op jit(solution)/shard_map/reduce_scatter | solution.py:1091
  147.6 21.7 %collective-permute-start.23 = (bf16[8,64,768]{2,1,0:T(8,128)(2,1)}, bf16[8,64,768]{2,1,0:T(8,128)(2,1)S(1)}, u32[]{:S(2)}, u32[]{:S(2)}) collective-permute-start(bf16[8,64,768]{2,1,0:T(8,128)(2,1)} %all-to-all-done.2.mine), channel_id=1, source_target_pairs={{0,8},{8,0},{1,9},{9,1},{2,10},{10,2},{3,11},{11,3},{4,12},{12,4},... | collective-permute-start | bytes 2359304 | tf_op jit(solution)/shard_map/ppermute | solution.py:39
  148.1 20.6 %collective-permute-start.20 = (bf16[192,1024]{1,0:T(8,128)(2,1)}, bf16[192,1024]{1,0:T(8,128)(2,1)S(1)}, u32[]{:S(2)}, u32[]{:S(2)}) collective-permute-start(bf16[192,1024]{1,0:T(8,128)(2,1)} %add_convert_fusion.4), channel_id=1, source_target_pairs={{0,1},{1,2},{2,3},{3,0},{4,5},{5,6},{6,7},{7,4},{8,9},{9,10},{10,1... | collective-permute-start | bytes 1179656 | tf_op jit(solution)/shard_map/ppermute | solution.py:31
  148.1 20.6 %collective-permute-start.21 = (bf16[192,1024]{1,0:T(8,128)(2,1)}, bf16[192,1024]{1,0:T(8,128)(2,1)S(1)}, u32[]{:S(2)}, u32[]{:S(2)}) collective-permute-start(bf16[192,1024]{1,0:T(8,128)(2,1)} %add_convert_fusion.4), channel_id=1, source_target_pairs={{0,2},{1,3},{2,0},{3,1},{4,6},{5,7},{6,4},{7,5},{8,10},{9,11},{10,... | collective-permute-start | bytes 1179656 | tf_op jit(solution)/shard_map/ppermute | solution.py:31
  149.7 19.4 %collective-permute-start.22 = (bf16[192,1024]{1,0:T(8,128)(2,1)}, bf16[192,1024]{1,0:T(8,128)(2,1)S(1)}, u32[]{:S(2)}, u32[]{:S(2)}) collective-permute-start(bf16[192,1024]{1,0:T(8,128)(2,1)} %add_convert_fusion.4), channel_id=1, source_target_pairs={{0,3},{1,0},{2,1},{3,2},{4,7},{5,4},{6,5},{7,6},{8,11},{9,8},{10,9... | collective-permute-start | bytes 1179656 | tf_op jit(solution)/shard_map/ppermute | solution.py:31
  177.3 19.1 %collective-permute-start.24 = (bf16[192,1024]{1,0:T(8,128)(2,1)S(1)}, bf16[192,1024]{1,0:T(8,128)(2,1)S(1)}, u32[]{:S(2)}, u32[]{:S(2)}) collective-permute-start(bf16[192,1024]{1,0:T(8,128)(2,1)S(1)} %get-tuple-element.416), channel_id=1, source_target_pairs={{0,3},{1,0},{2,1},{3,2},{4,7},{5,4},{6,5},{7,6},{8,11},{9,8},{10,9... | collective-permute-start | bytes 1179656 | tf_op jit(solution)/shard_map/ppermute | solution.py:31
  180.2 16.3 %collective-permute-start.25 = (bf16[192,1024]{1,0:T(8,128)(2,1)S(1)}, bf16[192,1024]{1,0:T(8,128)(2,1)S(1)}, u32[]{:S(2)}, u32[]{:S(2)}) collective-permute-start(bf16[192,1024]{1,0:T(8,128)(2,1)S(1)} %get-tuple-element.415), channel_id=1, source_target_pairs={{0,2},{1,3},{2,0},{3,1},{4,6},{5,7},{6,4},{7,5},{8,10},{9,11},{10,... | collective-permute-start | bytes 1179656 | tf_op jit(solution)/shard_map/ppermute | solution.py:31
  180.2 20.5 %collective-permute-start.26 = (bf16[192,1024]{1,0:T(8,128)(2,1)S(1)}, bf16[192,1024]{1,0:T(8,128)(2,1)S(1)}, u32[]{:S(2)}, u32[]{:S(2)}) collective-permute-start(bf16[192,1024]{1,0:T(8,128)(2,1)S(1)} %get-tuple-element.414), channel_id=1, source_target_pairs={{0,1},{1,2},{2,3},{3,0},{4,5},{5,6},{6,7},{7,4},{8,9},{9,10},{10,1... | collective-permute-start | bytes 1179656 | tf_op jit(solution)/shard_map/ppermute | solution.py:31
  180.8 23.3 %collective-permute-start.27 = (bf16[192,1024]{1,0:T(8,128)(2,1)S(1)}, bf16[192,1024]{1,0:T(8,128)(2,1)S(1)}, u32[]{:S(2)}, u32[]{:S(2)}) collective-permute-start(bf16[192,1024]{1,0:T(8,128)(2,1)S(1)} %bitcast.222), channel_id=1, source_target_pairs={{4,8},{8,4},{5,9},{9,5},{6,10},{10,6},{7,11},{11,7},{20,24},{24,20... | collective-permute-start | bytes 1179656 | tf_op jit(solution)/shard_map/ppermute | solution.py:43
  201.4 19.8 %collective-permute-start.28 = (bf16[192,1024]{1,0:T(8,128)(2,1)S(1)}, bf16[192,1024]{1,0:T(8,128)(2,1)S(1)}, u32[]{:S(2)}, u32[]{:S(2)}) collective-permute-start(bf16[192,1024]{1,0:T(8,128)(2,1)S(1)} %add_convert_fusion.3), channel_id=1, source_target_pairs={{0,1},{1,2},{2,3},{3,0},{4,5},{5,6},{6,7},{7,4},{8,9},{9,10},{10,1... | collective-permute-start | bytes 1179656 | tf_op jit(solution)/shard_map/ppermute | solution.py:31
  201.5 19.7 %collective-permute-start.29 = (bf16[192,1024]{1,0:T(8,128)(2,1)S(1)}, bf16[192,1024]{1,0:T(8,128)(2,1)S(1)}, u32[]{:S(2)}, u32[]{:S(2)}) collective-permute-start(bf16[192,1024]{1,0:T(8,128)(2,1)S(1)} %add_convert_fusion.3), channel_id=1, source_target_pairs={{0,2},{1,3},{2,0},{3,1},{4,6},{5,7},{6,4},{7,5},{8,10},{9,11},{10,... | collective-permute-start | bytes 1179656 | tf_op jit(solution)/shard_map/ppermute | solution.py:31
  202.4 19.1 %collective-permute-start.30 = (bf16[192,1024]{1,0:T(8,128)(2,1)S(1)}, bf16[192,1024]{1,0:T(8,128)(2,1)S(1)}, u32[]{:S(2)}, u32[]{:S(2)}) collective-permute-start(bf16[192,1024]{1,0:T(8,128)(2,1)S(1)} %add_convert_fusion.3), channel_id=1, source_target_pairs={{0,3},{1,0},{2,1},{3,2},{4,7},{5,4},{6,5},{7,6},{8,11},{9,8},{10,9... | collective-permute-start | bytes 1179656 | tf_op jit(solution)/shard_map/ppermute | solution.py:31
  225.7 11.6 %collective-permute-start.31 = (bf16[192,1024]{1,0:T(8,128)(2,1)S(1)}, bf16[192,1024]{1,0:T(8,128)(2,1)S(1)}, u32[]{:S(2)}, u32[]{:S(2)}) collective-permute-start(bf16[192,1024]{1,0:T(8,128)(2,1)S(1)} %get-tuple-element.258.grads_own), channel_id=1, source_target_pairs={{0,8},{8,0},{1,9},{9,1},{2,10},{10,2},{3,11},{11,3},{4,12},{12,4},... | collective-permute-start | bytes 1179656 | tf_op jit(solution)/shard_map/ppermute | solution.py:39
  238.7 10.7 %collective-permute-start.34 = (bf16[192,1024]{1,0:T(8,128)(2,1)S(1)}, bf16[192,1024]{1,0:T(8,128)(2,1)S(1)}, u32[]{:S(2)}, u32[]{:S(2)}) collective-permute-start(bf16[192,1024]{1,0:T(8,128)(2,1)S(1)} %get-tuple-element.411), channel_id=1, source_target_pairs={{0,3},{1,0},{2,1},{3,2},{4,7},{5,4},{6,5},{7,6},{8,11},{9,8},{10,9... | collective-permute-start | bytes 1179656 | tf_op jit(solution)/shard_map/ppermute | solution.py:31
  240.8 11.6 %collective-permute-start.35 = (bf16[192,1024]{1,0:T(8,128)(2,1)S(1)}, bf16[192,1024]{1,0:T(8,128)(2,1)S(1)}, u32[]{:S(2)}, u32[]{:S(2)}) collective-permute-start(bf16[192,1024]{1,0:T(8,128)(2,1)S(1)} %get-tuple-element.410), channel_id=1, source_target_pairs={{0,2},{1,3},{2,0},{3,1},{4,6},{5,7},{6,4},{7,5},{8,10},{9,11},{10,... | collective-permute-start | bytes 1179656 | tf_op jit(solution)/shard_map/ppermute | solution.py:31
  240.8 20.4 %collective-permute-start.36 = (bf16[192,1024]{1,0:T(8,128)(2,1)S(1)}, bf16[192,1024]{1,0:T(8,128)(2,1)S(1)}, u32[]{:S(2)}, u32[]{:S(2)}) collective-permute-start(bf16[192,1024]{1,0:T(8,128)(2,1)S(1)} %get-tuple-element.409), channel_id=1, source_target_pairs={{0,1},{1,2},{2,3},{3,0},{4,5},{5,6},{6,7},{7,4},{8,9},{9,10},{10,1... | collective-permute-start | bytes 1179656 | tf_op jit(solution)/shard_map/ppermute | solution.py:31
  291.2 12.7 %collective-permute-start.41 = (bf16[192,1024]{1,0:T(8,128)(2,1)}, bf16[192,1024]{1,0:T(8,128)(2,1)}, u32[]{:S(2)}, u32[]{:S(2)}) collective-permute-start(bf16[192,1024]{1,0:T(8,128)(2,1)} %get-tuple-element.282), channel_id=1, source_target_pairs={{0,1},{1,2},{2,3},{3,0},{4,5},{5,6},{6,7},{7,4},{8,9},{9,10},{10,1... | collective-permute-start | bytes 1179656 | tf_op jit(solution)/shard_map/ppermute | solution.py:31
  291.2 19.4 %collective-permute-start.42 = (bf16[192,1024]{1,0:T(8,128)(2,1)}, bf16[192,1024]{1,0:T(8,128)(2,1)}, u32[]{:S(2)}, u32[]{:S(2)}) collective-permute-start(bf16[192,1024]{1,0:T(8,128)(2,1)} %get-tuple-element.282), channel_id=1, source_target_pairs={{0,2},{1,3},{2,0},{3,1},{4,6},{5,7},{6,4},{7,5},{8,10},{9,11},{10,... | collective-permute-start | bytes 1179656 | tf_op jit(solution)/shard_map/ppermute | solution.py:31
  293.0 18.8 %collective-permute-start.43 = (bf16[192,1024]{1,0:T(8,128)(2,1)}, bf16[192,1024]{1,0:T(8,128)(2,1)}, u32[]{:S(2)}, u32[]{:S(2)}) collective-permute-start(bf16[192,1024]{1,0:T(8,128)(2,1)} %get-tuple-element.282), channel_id=1, source_target_pairs={{0,3},{1,0},{2,1},{3,2},{4,7},{5,4},{6,5},{7,6},{8,11},{9,8},{10,9... | collective-permute-start | bytes 1179656 | tf_op jit(solution)/shard_map/ppermute | solution.py:31
  337.8 19.4 %collective-permute-start.46 = (bf16[192,1024]{1,0:T(8,128)(2,1)}, bf16[192,1024]{1,0:T(8,128)(2,1)}, u32[]{:S(2)}, u32[]{:S(2)}) collective-permute-start(bf16[192,1024]{1,0:T(8,128)(2,1)} %get-tuple-element.408), channel_id=1, source_target_pairs={{0,3},{1,0},{2,1},{3,2},{4,7},{5,4},{6,5},{7,6},{8,11},{9,8},{10,9... | collective-permute-start | bytes 1179656 | tf_op jit(solution)/shard_map/ppermute | solution.py:31
  340.0 17.2 %collective-permute-start.47 = (bf16[192,1024]{1,0:T(8,128)(2,1)}, bf16[192,1024]{1,0:T(8,128)(2,1)}, u32[]{:S(2)}, u32[]{:S(2)}) collective-permute-start(bf16[192,1024]{1,0:T(8,128)(2,1)} %get-tuple-element.407), channel_id=1, source_target_pairs={{0,2},{1,3},{2,0},{3,1},{4,6},{5,7},{6,4},{7,5},{8,10},{9,11},{10,... | collective-permute-start | bytes 1179656 | tf_op jit(solution)/shard_map/ppermute | solution.py:31
  340.0 20.7 %collective-permute-start.48 = (bf16[192,1024]{1,0:T(8,128)(2,1)}, bf16[192,1024]{1,0:T(8,128)(2,1)}, u32[]{:S(2)}, u32[]{:S(2)}) collective-permute-start(bf16[192,1024]{1,0:T(8,128)(2,1)} %get-tuple-element.406), channel_id=1, source_target_pairs={{0,1},{1,2},{2,3},{3,0},{4,5},{5,6},{6,7},{7,4},{8,9},{9,10},{10,1... | collective-permute-start | bytes 1179656 | tf_op jit(solution)/shard_map/ppermute | solution.py:31
  366.0 24.3 %collective-permute-start.52 = (bf16[8,64,1024]{2,1,0:T(8,128)(2,1)}, bf16[8,64,1024]{2,1,0:T(8,128)(2,1)}, u32[]{:S(2)}, u32[]{:S(2)}) collective-permute-start(bf16[8,64,1024]{2,1,0:T(8,128)(2,1)} %dynamic-slice_bitcast_fusion), channel_id=1, source_target_pairs={{0,16},{16,0},{1,17},{17,1},{2,18},{18,2},{3,19},{19,3},{4,20},{20... | collective-permute-start | bytes 3145736 | tf_op jit(solution)/shard_map/ppermute | solution.py:39
  367.4 10.8 %collective-permute-start.49 = (bf16[192,1024]{1,0:T(8,128)(2,1)S(1)}, bf16[192,1024]{1,0:T(8,128)(2,1)S(1)}, u32[]{:S(2)}, u32[]{:S(2)}) collective-permute-start(bf16[192,1024]{1,0:T(8,128)(2,1)S(1)} %get-tuple-element.297), channel_id=1, source_target_pairs={{0,1},{1,2},{2,3},{3,0},{4,5},{5,6},{6,7},{7,4},{8,9},{9,10},{10,1... | collective-permute-start | bytes 1179656 | tf_op jit(solution)/shard_map/ppermute | solution.py:31
  368.4 19.2 %collective-permute-start.50 = (bf16[192,1024]{1,0:T(8,128)(2,1)S(1)}, bf16[192,1024]{1,0:T(8,128)(2,1)S(1)}, u32[]{:S(2)}, u32[]{:S(2)}) collective-permute-start(bf16[192,1024]{1,0:T(8,128)(2,1)S(1)} %get-tuple-element.297), channel_id=1, source_target_pairs={{0,2},{1,3},{2,0},{3,1},{4,6},{5,7},{6,4},{7,5},{8,10},{9,11},{10,... | collective-permute-start | bytes 1179656 | tf_op jit(solution)/shard_map/ppermute | solution.py:31
  371.0 16.7 %collective-permute-start.51 = (bf16[192,1024]{1,0:T(8,128)(2,1)S(1)}, bf16[192,1024]{1,0:T(8,128)(2,1)}, u32[]{:S(2)}, u32[]{:S(2)}) collective-permute-start(bf16[192,1024]{1,0:T(8,128)(2,1)S(1)} %get-tuple-element.297), channel_id=1, source_target_pairs={{0,3},{1,0},{2,1},{3,2},{4,7},{5,4},{6,5},{7,6},{8,11},{9,8},{10,9... | collective-permute-start | bytes 1179656 | tf_op jit(solution)/shard_map/ppermute | solution.py:31
  392.9 21.1 %all-to-all-start.3 = ((bf16[8,64,1024]{2,1,0:T(8,128)(2,1)}), bf16[8,64,1024]{2,1,0:T(8,128)(2,1)}, u32[]{:S(2)}, u32[]{:S(2)}) async-start(bf16[8,64,1024]{2,1,0:T(8,128)(2,1)} %fusion.29), calls=%async_computation.4 | async-start | bytes 2097152 | tf_op jit(solution)/shard_map/all_to_all | solution.py:597
  400.0 117.1 %reduce-scatter.5.cloned.1.call-start = ((), (), s32[]{:S(2)}) async-start(), calls=%async_computation.10 | async-start | bytes 2228224 | tf_op jit(solution)/shard_map/reduce_scatter | solution.py:1121
  400.6 124.8 %all-gather.12.cloned.1.call-start = ((), (), s32[]{:S(2)}) async-start(), calls=%async_computation.12 | async-start | bytes 2228224 | tf_op jit(solution)/shard_map/all_gather | solution.py:1129
  421.5 20.4 %collective-permute-start.55 = (bf16[192,1024]{1,0:T(8,128)(2,1)S(1)}, bf16[192,1024]{1,0:T(8,128)(2,1)S(1)}, u32[]{:S(2)}, u32[]{:S(2)}) collective-permute-start(bf16[192,1024]{1,0:T(8,128)(2,1)S(1)} %get-tuple-element.403), channel_id=1, source_target_pairs={{0,1},{1,2},{2,3},{3,0},{4,5},{5,6},{6,7},{7,4},{8,9},{9,10},{10,1... | collective-permute-start | bytes 1179656 | tf_op jit(solution)/shard_map/ppermute | solution.py:31
  446.8 21.8 %collective-permute-start.59 = (bf16[8,64,2048]{2,1,0:T(8,128)(2,1)}, bf16[8,64,2048]{2,1,0:T(8,128)(2,1)}, u32[]{:S(2)}, u32[]{:S(2)}) collective-permute-start(bf16[8,64,2048]{2,1,0:T(8,128)(2,1)} %fusion.26), channel_id=1, source_target_pairs={{0,8},{8,0},{1,9},{9,1},{2,10},{10,2},{3,11},{11,3},{4,12},{12,4},... | collective-permute-start | bytes 6291464 | tf_op jit(solution)/shard_map/ppermute | solution.py:39
  447.7 20.4 %collective-permute-start.56 = (bf16[192,1024]{1,0:T(8,128)(2,1)S(1)}, bf16[192,1024]{1,0:T(8,128)(2,1)S(1)}, u32[]{:S(2)}, u32[]{:S(2)}) collective-permute-start(bf16[192,1024]{1,0:T(8,128)(2,1)S(1)} %get-tuple-element.318), channel_id=1, source_target_pairs={{0,1},{1,2},{2,3},{3,0},{4,5},{5,6},{6,7},{7,4},{8,9},{9,10},{10,1... | collective-permute-start | bytes 1179656 | tf_op jit(solution)/shard_map/ppermute | solution.py:31
  447.8 20.4 %collective-permute-start.57 = (bf16[192,1024]{1,0:T(8,128)(2,1)S(1)}, bf16[192,1024]{1,0:T(8,128)(2,1)S(1)}, u32[]{:S(2)}, u32[]{:S(2)}) collective-permute-start(bf16[192,1024]{1,0:T(8,128)(2,1)S(1)} %get-tuple-element.318), channel_id=1, source_target_pairs={{0,2},{1,3},{2,0},{3,1},{4,6},{5,7},{6,4},{7,5},{8,10},{9,11},{10,... | collective-permute-start | bytes 1179656 | tf_op jit(solution)/shard_map/ppermute | solution.py:31
  449.3 19.2 %collective-permute-start.58 = (bf16[192,1024]{1,0:T(8,128)(2,1)S(1)}, bf16[192,1024]{1,0:T(8,128)(2,1)S(1)}, u32[]{:S(2)}, u32[]{:S(2)}) collective-permute-start(bf16[192,1024]{1,0:T(8,128)(2,1)S(1)} %get-tuple-element.318), channel_id=1, source_target_pairs={{0,3},{1,0},{2,1},{3,2},{4,7},{5,4},{6,5},{7,6},{8,11},{9,8},{10,9... | collective-permute-start | bytes 1179656 | tf_op jit(solution)/shard_map/ppermute | solution.py:31
  476.7 40.4 %all-to-all-start.4 = ((bf16[8,64,2304]{2,1,0:T(8,128)(2,1)}), bf16[8,64,2304]{2,1,0:T(8,128)(2,1)}, u32[]{:S(2)}, u32[]{:S(2)}) async-start(bf16[8,64,2304]{2,1,0:T(8,128)(2,1)} %pad_maximum_fusion), calls=%async_computation.5 | async-start | bytes 4718592 | tf_op jit(solution)/shard_map/all_to_all | solution.py:749
  537.8 13.4 %collective-permute-start.68 = (bf16[8,1792]{1,0:T(8,128)(2,1)}, bf16[8,1792]{1,0:T(8,128)(2,1)S(1)}, u32[]{:S(2)}, u32[]{:S(2)}) collective-permute-start(bf16[8,1792]{1,0:T(8,128)(2,1)} %get-tuple-element.433), channel_id=1, source_target_pairs={{0,3},{1,0},{2,1},{3,2},{4,7},{5,4},{6,5},{7,6},{8,11},{9,8},{10,9... | collective-permute-start | bytes 86024 | tf_op jit(solution)/shard_map/ppermute | solution.py:31
  539.4 35.1 %all-to-all-start.5 = ((bf16[128,8,896]{2,1,0:T(8,128)(2,1)}), bf16[128,8,896]{2,1,0:T(8,128)(2,1)S(1)}, u32[]{:S(2)}, u32[]{:S(2)}) async-start(bf16[128,8,896]{2,1,0:T(8,128)(2,1)} %bitcast.75), calls=%async_computation.7 | async-start | bytes 3670016 | tf_op jit(solution)/shard_map/all_to_all | solution.py:1158
  547.3 81.6 %all-gather.14.cloned.1.call-start = ((), (), s32[]{:S(2)}) async-start(), calls=%async_computation.13 | async-start | bytes 4595712 | tf_op jit(solution)/shard_map/all_gather | solution.py:1178
  547.3 14.2 %collective-permute-start.69 = (bf16[8,1792]{1,0:T(8,128)(2,1)}, bf16[8,1792]{1,0:T(8,128)(2,1)S(1)}, u32[]{:S(2)}, u32[]{:S(2)}) collective-permute-start(bf16[8,1792]{1,0:T(8,128)(2,1)} %get-tuple-element.432), channel_id=1, source_target_pairs={{0,2},{1,3},{2,0},{3,1},{4,6},{5,7},{6,4},{7,5},{8,10},{9,11},{10,... | collective-permute-start | bytes 86024 | tf_op jit(solution)/shard_map/ppermute | solution.py:31
  550.7 16.0 %collective-permute-start.70 = (bf16[8,1792]{1,0:T(8,128)(2,1)}, bf16[8,1792]{1,0:T(8,128)(2,1)S(1)}, u32[]{:S(2)}, u32[]{:S(2)}) collective-permute-start(bf16[8,1792]{1,0:T(8,128)(2,1)} %get-tuple-element.430), channel_id=1, source_target_pairs={{0,1},{1,2},{2,3},{3,0},{4,5},{5,6},{6,7},{7,4},{8,9},{9,10},{10,1... | collective-permute-start | bytes 86024 | tf_op jit(solution)/shard_map/ppermute | solution.py:31
  582.5 11.3 %collective-permute-start.64 = (bf16[192,1024]{1,0:T(8,128)(2,1)S(1)}, bf16[192,1024]{1,0:T(8,128)(2,1)S(1)}, u32[]{:S(2)}, u32[]{:S(2)}) collective-permute-start(bf16[192,1024]{1,0:T(8,128)(2,1)S(1)} %get-tuple-element.401), channel_id=1, source_target_pairs={{0,2},{1,3},{2,0},{3,1},{4,6},{5,7},{6,4},{7,5},{8,10},{9,11},{10,... | collective-permute-start | bytes 1179656 | tf_op jit(solution)/shard_map/ppermute | solution.py:31
  584.1 19.3 %collective-permute-start.65 = (bf16[192,1024]{1,0:T(8,128)(2,1)S(1)}, bf16[192,1024]{1,0:T(8,128)(2,1)S(1)}, u32[]{:S(2)}, u32[]{:S(2)}) collective-permute-start(bf16[192,1024]{1,0:T(8,128)(2,1)S(1)} %get-tuple-element.400), channel_id=1, source_target_pairs={{0,1},{1,2},{2,3},{3,0},{4,5},{5,6},{6,7},{7,4},{8,9},{9,10},{10,1... | collective-permute-start | bytes 1179656 | tf_op jit(solution)/shard_map/ppermute | solution.py:31
  584.4 29.3 %collective-permute-start.39 = (f32[192,1024]{1,0:T(8,128)S(1)}, f32[192,1024]{1,0:T(8,128)S(1)}, u32[]{:S(2)}, u32[]{:S(2)}) collective-permute-start(f32[192,1024]{1,0:T(8,128)S(1)} %copy-done.46), channel_id=1, source_target_pairs={{4,8},{8,4},{5,9},{9,5},{6,10},{10,6},{7,11},{11,7},{20,24},{24,20... | collective-permute-start | bytes 2359304 | tf_op jit(solution)/shard_map/ppermute | solution.py:43
  604.2 23.6 %collective-permute-start.66 = (f32[192,1024]{1,0:T(8,128)S(1)}, f32[192,1024]{1,0:T(8,128)S(1)}, u32[]{:S(2)}, u32[]{:S(2)}) collective-permute-start(f32[192,1024]{1,0:T(8,128)S(1)} %fusion.42), channel_id=1, source_target_pairs={{4,8},{8,4},{5,9},{9,5},{6,10},{10,6},{7,11},{11,7},{20,24},{24,20... | collective-permute-start | bytes 2359304 | tf_op jit(solution)/shard_map/ppermute | solution.py:43
  (113 other events, 778.9 us)
Sparse Core Ops, SparseCore 0:
  52.3 65.1 all-gather.7
  147.6 82.0 all-gather.9
  284.4 79.2 reduce-scatter.2
  403.0 61.3 reduce-scatter.4
  466.5 58.8 all-gather.11
  580.6 44.0 all-gather.13

commit v7 on v6

--- a/solution.py
+++ b/solution.py
@@ -54,7 +54,15 @@
 
 
 def gather_z(rows):
-    return jnp.concatenate([rows] + [shift_z(rows, k) for k in (1, 2, 3)], axis=0)
+    half = rows.shape[0] // 2
+    first, second = rows[:half], rows[half:]
+    first_left, second_right = shift_z(first, 1), shift_z(second, 3)
+    second_left, first_right = shift_z(second, 1), shift_z(first, 3)
+    first_left, second_right = lax.optimization_barrier((first_left, second_right))
+    first_far, second_far = shift_z(first_left, 1), shift_z(second_right, 3)
+    return jnp.concatenate(
+        [rows, first_left, second_left, first_far, second_far, first_right, second_right], axis=0
+    )
 
 
 def dot(left, right):
@@ -609,16 +617,19 @@
     return lax.dynamic_slice_in_dim(value, at * width, width, 1)
 
 
-def forward_attention(normed_all, w_in, in_bias, info, slopes, core, side):
-    def attention(normed_all):
-        projected = (dot(normed_all, w_in) + in_bias).astype(bf16)
-        received = swap(columns_at(projected, 1 - core, 384), "core")
-        mine = columns_at(projected, core, 384)
-        ctx_mine, ctx_other, logsum, rows = attend(info, slopes, mine, received)
-        return in_order(ctx_mine, swap(ctx_other, "core"), core), logsum, rows
-
-    side_done, (context, logsum, rows) = beside(side[0], side[1], normed_all, attention)
-    return context, logsum, rows, side_done
+def forward_project(normed_all, w_in, in_bias, core):
+    projected = (dot(normed_all, w_in) + in_bias).astype(bf16)
+    received = swap(columns_at(projected, 1 - core, 384), "core")
+    return columns_at(projected, core, 384), received
+
+
+def forward_attention(rows, info, slopes, core, side):
+    def attention(rows):
+        ctx_mine, ctx_other, logsum, kept = attend(info, slopes, *rows)
+        return in_order(ctx_mine, swap(ctx_other, "core"), core), logsum, kept
+
+    side_done, (context, logsum, kept) = beside(side[0], side[1], rows, attention)
+    return context, logsum, kept, side_done
 
 
 def forward_middle(hidden, context, params, given=None, work=lambda v: None):
@@ -641,22 +652,22 @@
     return last[0] + dot_own(last[1], params[10], dot) + params[11]
 
 
-def backward_two(grad_down, d_before, params, kept, core):
+def backward_two(grad_down, d_before, params, kept, core, more):
     up = params[8]
     normed_two, _, activated = kept[6:]
     sum_up = jnp.sum(d_before.astype(f32), axis=0)
 
     def work_two(given):
-        activated, grad_down, normed_two, d_before = given
+        activated, grad_down, normed_two, d_before, value = given
         own = dot_own(d_before, up, dot_t)
         g_down = outer(activated, grad_down).astype(bf16)
         g_up = outer(normed_two, d_before).astype(bf16)
-        return own, (g_down, g_up)
+        return own, (more[1](value), g_down, g_up)
 
     parts, (own, grads) = beside(
         dot_others(d_before, up, dot_t),
         scatter_parts,
-        (activated, grad_down, normed_two, d_before),
+        (activated, grad_down, normed_two, d_before, more[0]),
         work_two,
     )
     return sum_parts(own, parts), grads, sum_up
@@ -686,8 +697,9 @@
 
     def attention_more(grad_out_all):
         d_joined, sums = attention(grad_out_all)
-        return d_joined, sums, more(d_joined, sums, (sum_project, sum_gain_two, sum_offset_two, sum_down, sums, sum_up))
-
+        return d_joined, sums, more(held, d_joined, sums, (sum_project, sum_gain_two, sum_offset_two, sum_down, sums, sum_up))
+
+    crossed, grad_out_all, held = lax.optimization_barrier((crossed, grad_out_all, across[4]))
     crossed, (d_joined, sums, done_more) = beside(
         across[2](crossed, context, grad_out_all), across[3], grad_out_all, attention_more
     )
@@ -753,11 +765,24 @@
     return take(value, at).astype(f32) + swap(take(value, 1 - at), axis).astype(f32)
 
 
+def sum_z(value, z):
+    split = value.reshape(2, 4, *value.shape[1:])
+    total = take(split, z, 1).astype(f32)
+    for k in (1, 2, 3):
+        total = total + shift_z(take(split, (z + k) % 4, 1), k).astype(f32)
+    return total.astype(bf16)
+
+
 def spread_z(both, z):
     columns = both.reshape(4, 8, -1)
     blocks = [take(columns, z)] + [shift_z(take(columns, (z + 4 - k) % 4), 4 - k) for k in (1, 2, 3)]
-    blocks = jnp.stack(blocks + blocks)
-    return lax.dynamic_slice_in_dim(blocks, (4 - z) % 4, 4, 0).reshape(32, -1)
+    out = []
+    for four in range(4):
+        at = (four + 4 - z) % 4
+        low = jnp.where(at == 0, blocks[0], blocks[1])
+        high = jnp.where(at == 2, blocks[2], blocks[3])
+        out.append(jnp.where(at < 2, low, high))
+    return jnp.concatenate(out)
 
 
 def y_rows(summed, y_hi):
@@ -817,14 +842,7 @@
     return total + shift_x(total, 1) + shift_x(total, 2) + shift_x(total, 3)
 
 
-def unpack_outer_kernel(first, second, down, up):
-    for g in range(16):
-        down[0, g * 32 : (g + 1) * 32, :] = first[g, :, 0:D].astype(f32)
-        for four in range(4):
-            rows = first[g, four * 8 : (four + 1) * 8, D : 2 * D].astype(f32)
-            for side in range(2):
-                at = side * 2048 + four * 512
-                up[0, g * 8 : (g + 1) * 8, at : at + 512] = rows[:, side * 512 : (side + 1) * 512]
+def unpack_wide_kernel(second, down, up):
     for pair in range(2):
         for y_lo in range(2):
             for core in range(2):
@@ -832,13 +850,31 @@
                 high = second[(pair * 2 + 1) * 4 + y_lo * 2 + core].astype(f32)
                 for x, block in ((pair * 2, low), (pair * 2 + 1, high)):
                     at = core * 256 + x * 64
-                    down[1, at : at + 64, y_lo * 512 : (y_lo + 1) * 512] = block[:, 512:1024]
+                    down[0, at : at + 64, y_lo * 512 : (y_lo + 1) * 512] = block[:, 512:1024]
                 for place in range(8):
                     lanes = slice(place * 64, (place + 1) * 64)
                     at = place * 512 + core * 256 + pair * 128
-                    up[1, y_lo * 64 : (y_lo + 1) * 64, at : at + 128] = jnp.concatenate(
+                    up[0, y_lo * 64 : (y_lo + 1) * 64, at : at + 128] = jnp.concatenate(
                         [low[:, lanes], high[:, lanes]], axis=1
                     )
+
+
+def unpack_wide(second):
+    return pl.pallas_call(
+        unpack_wide_kernel,
+        grid=(1,),
+        out_shape=(
+            jax.ShapeDtypeStruct((LAYERS, 512, D), f32),
+            jax.ShapeDtypeStruct((LAYERS, 128, FF), f32),
+        ),
+        in_specs=[whole],
+        out_specs=(
+            pl.BlockSpec((1, 512, D), lambda i: (1, 0, 0)),
+            pl.BlockSpec((1, 128, FF), lambda i: (1, 0, 0)),
+        ),
+        compiler_params=params_one,
+        name="unpack_wide",
+    )(second)
 
 
 def place_input(block, layer, row, inputs):
@@ -852,44 +888,47 @@
                 inputs[layer, rows, to : to + 128] = part_rows[:, at : at + 128]
 
 
-def unpack_inner_kernel(full, inputs, project):
-    for g in range(16):
+def unpack_full_kernel(full, old_down, old_up, down, up, inputs, project):
+    for g in range(2):
+        rows = slice(g * 8, (g + 1) * 8)
+        down[0, g * 32 : (g + 1) * 32, :] = full[g, :, 0:D].astype(f32)
+        for four in range(4):
+            found = full[g, four * 8 : (four + 1) * 8, D : 2 * D].astype(f32)
+            for side in range(2):
+                at = side * 2048 + four * 512
+                up[0, rows, at : at + 512] = found[:, side * 512 : (side + 1) * 512]
         place_input(full[g, :, 3328:4096], 0, g * 8, inputs)
         place_input(full[g, :, 2560:3328], 1, g * 8, inputs)
         for layer, at in ((0, 2048), (1, 2304)):
             block = full[g, :, at : at + 256].astype(f32)
             for four in range(4):
-                project[layer, g * 8 : (g + 1) * 8, four * 256 : (four + 1) * 256] = block[
+                project[layer, rows, four * 256 : (four + 1) * 256] = block[
                     four * 8 : (four + 1) * 8, :
                 ]
 
 
-def unpack_outer(first, second):
+def unpack_full(full, down, up):
+    old = pl.BlockSpec(memory_space=pl.ANY)
     return pl.pallas_call(
-        unpack_outer_kernel,
+        unpack_full_kernel,
+        grid=(8,),
         out_shape=(
             jax.ShapeDtypeStruct((LAYERS, 512, D), f32),
             jax.ShapeDtypeStruct((LAYERS, 128, FF), f32),
-        ),
-        in_specs=[whole, whole],
-        out_specs=(whole, whole),
-        compiler_params=params_one,
-        name="unpack_outer",
-    )(first, second)
-
-
-def unpack_inner(full):
-    return pl.pallas_call(
-        unpack_inner_kernel,
-        out_shape=(
             jax.ShapeDtypeStruct((LAYERS, 128, 3072), f32),
             jax.ShapeDtypeStruct((LAYERS, 128, D), f32),
         ),
-        in_specs=[whole],
-        out_specs=(whole, whole),
-        compiler_params=params_one,
-        name="unpack_inner",
-    )(full)
+        in_specs=[pl.BlockSpec((2, 32, 4224), lambda i: (i, 0, 0)), old, old],
+        out_specs=(
+            pl.BlockSpec((1, 64, D), lambda i: (0, i, 0)),
+            pl.BlockSpec((1, 16, FF), lambda i: (0, i, 0)),
+            pl.BlockSpec((LAYERS, 16, 3072), lambda i: (0, i, 0)),
+            pl.BlockSpec((LAYERS, 16, D), lambda i: (0, i, 0)),
+        ),
+        input_output_aliases={1: 0, 2: 1},
+        compiler_params=pltpu.CompilerParams(vmem_limit_bytes=58 * 2**20),
+        name="unpack_full",
+    )(full, down, up)
 
 
 def pack_tail_kernel(
@@ -1009,26 +1048,22 @@
             (first, raw_all),
             first_norm,
         )
-        return join_columns(corner, w_first, swap(w_first, "core")), rows, parts
-
-    up_zero, (w_first, rows, (vectors, in_bias, unit_bias, normed_all, unit_all)) = beside(
+        w_first = join_columns(corner, w_first, swap(w_first, "core"))
+        return w_first, rows, parts, forward_project(parts[3], w_first, parts[1][0], core)
+
+    up_zero, (w_first, rows, first_parts, projected) = beside(
         up_zero, to_ctx, (first, raw_all, rows), first_weight
     )
+    vectors, in_bias, unit_bias, normed_all, unit_all = first_parts
     wide = lax.all_gather(wide, CTX, axis=0, tiled=True)
     vector = [vectors[i] for i in range(12)]
-    nothing = (jnp.zeros((8, 128), f32), lambda v: v, lambda v, *more: v, lambda v: v)
+    nothing = (jnp.zeros((8, 128), f32), lambda v: v, lambda v, *more: v, lambda v: v, None)
     unit_wide = first[:, 19:20, 256:768].reshape(8, 2, 4, 64)
     unit_wide = lax.dynamic_index_in_dim(unit_wide, core, 1, keepdims=False)
     unit_wide = unit_wide.transpose(1, 0, 2).reshape(4, 1, 512).astype(f32)
     hidden = rows_in.astype(f32)
     context, logsum, rows_kept, (pieces, second) = forward_attention(
-        normed_all,
-        w_first,
-        in_bias[0],
-        info,
-        slopes,
-        core,
-        ((rows, second), lambda v: (gather_x(v[0]), to_ctx(v[1]))),
+        projected, info, slopes, core, ((rows, second), lambda v: (gather_x(v[0]), to_ctx(v[1])))
     )
     other = swap(pieces, "core")
     project_zero, project_one = join_project(corner, project_weight, pieces, other)
@@ -1079,7 +1114,11 @@
     )
     gradient = regroup(cotangent[0], core, y_hi)
     context, logsum, rows_kept, grad_other = forward_attention(
-        normed_all, w_second, in_bias[1], info, slopes, core, (gradient, lambda v: swap(v, "core"))
+        forward_project(normed_all, w_second, in_bias[1], core),
+        info,
+        slopes,
+        core,
+        (gradient, lambda v: swap(v, "core")),
     )
     middle, normed_two, _ = forward_middle(hidden, context, params_1)
     own, other, d_own, d_other, sum_up, wide_grads = wide_part(
@@ -1121,27 +1160,35 @@
     inner_1 = lax.psum_scatter(inner_1, GRP, scatter_dimension=0, tiled=True)[0]
     wide_grads, d_before = beside(
         wide_grads,
-        to_ctx,
+        lambda v: sum_z(v, z),
         (grad_down, kept_0[7]),
         lambda v: jax.vjp(gelu, v[1])[1](dot_t(v[0], params_0[10]))[0].astype(bf16),
     )
-    d_normed, grads, sum_up = backward_two(grad_down, d_before, params_0, kept_0, core)
-    wide_grads = lax.all_gather(jnp.sum(wide_grads.astype(f32), axis=0).astype(bf16), GRP)
+    d_normed, (wide_grads, *grads), sum_up = backward_two(
+        grad_down,
+        d_before,
+        params_0,
+        kept_0,
+        core,
+        (wide_grads, lambda v: sum_pairs(v, y_hi, "y_hi").astype(bf16)),
+    )
+    wide_grads = lax.all_gather(wide_grads, GRP)
 
     def with_project(summed, context, grad_out_all):
         g_project = outer(context, grad_out_all).astype(bf16)
         rows = g_project.reshape(2, 16, 8, 4, 256).transpose(1, 0, 3, 2, 4).reshape(16, 64, 256)
         return jnp.concatenate([summed, core_sum(rows, core)], axis=-1)
 
-    def tail_pack(d_joined, sums, vectors):
+    def tail_pack(inner_sum, d_joined, sums, vectors):
         w_in = params_0[2].astype(f32)
         gain = jnp.sum(outer(unit_all, d_joined) * w_in, axis=1)
         offset = jnp.sum(d_joined.astype(f32), axis=0, keepdims=True)
         offset = jnp.sum(offset * w_in, axis=1)
         g_input = outer(kept_0[1], d_joined).astype(bf16)
-        return pack_tail(info, g_input, (gain, offset), vectors, packed_1)
-
-    crossed, _, low, _, _, scatter, finish = backward(
+        packed = pack_tail(info, g_input, (gain, offset), vectors, packed_1)
+        return packed, inner_sum
+
+    crossed, _, (low, inner_1), _, _, scatter, finish = backward(
         gradient,
         d_normed,
         sum_up,
@@ -1150,7 +1197,7 @@
         info,
         slopes,
         core,
-        (grads, lambda v: core_sum(pack_outer(*v), core), with_project, to_xy),
+        (grads, lambda v: core_sum(pack_outer(*v), core), with_project, to_xy, inner_1),
         tail_pack,
     )
 
@@ -1165,9 +1212,8 @@
         spread = spread_z(jnp.concatenate([both[:, D : 2 * D], both[:, at:]], axis=1), z)
         return [both[:, :D], spread[:, :D], both[:, 2 * D : at], spread[:, D:]]
 
-    low, (both, wide_grads) = beside(
-        low, to_all, (crossed, inner_1, wide_grads), lambda v: (outer_rows(v[:2]), v[2])
-    )
+    low, both = beside(low, to_all, (crossed, inner_1), outer_rows)
+    low, wide_grads = lax.optimization_barrier((low, wide_grads))
     left, _ = scatter(lambda: None)
     gradient = regroup(finish(left)[0], core, y_hi)
     low = low.reshape(32, 32, 896).astype(f32)
@@ -1177,8 +1223,7 @@
     low = jnp.concatenate([low, vector], axis=1).astype(bf16)
     full = lax.all_gather(jnp.concatenate(both + [low], axis=1), GRP)
     vector = full[0:12, 0:2, 4096:4224].astype(f32)
-    g_input, g_project = unpack_inner(full)
-    g_down, g_up = unpack_outer(full, wide_grads)
+    g_down, g_up, g_input, g_project = unpack_full(full, *unpack_wide(wide_grads))
     packed = vector.reshape(LAYERS * 1536)
     vector = packed.reshape(LAYERS, -1)
     parts = [vector[:, i * 128 : (i + 1) * 128] for i in range(6)]

time: 657 us -> 642 us (0.977)
  waiting for transfers between devices: 274 us -> 226 us
  starting transfers between devices: 134 us -> 160 us
    ppermute x39 -> x60, waiting for transfers between devices: 199 us -> 159 us  [shift_z(): return lax.ppermute(value, 'z', [(i, (i + step) % 4) for i in range(4)])]
    ppermute x39 -> x60, starting transfers between devices: 46.4 us -> 77.9 us  [shift_z(): return lax.ppermute(value, 'z', [(i, (i + step) % 4) for i in range(4)])]
    ppermute x6, waiting for transfers between devices: 0.02 us -> 9.01 us  [shift_x(): return lax.ppermute(value, 'x', [(i, (i + step) % 4) for i in range(4)])]
    all_to_all x4 -> x3, waiting for transfers between devices: 12.3 us -> 3.56 us  [to_ctx(): return lax.all_to_all(value, CTX, split_axis=0, concat_axis=0, tiled=True)]
    all_gather x1, waiting for transfers between devices: 8.31 us -> 0.01 us  [on_device(): wide_grads = lax.all_gather(wide_grads, GRP)]
    all_to_all x4 -> x3, starting transfers between devices: 21 us -> 14.8 us  [to_ctx(): return lax.all_to_all(value, CTX, split_axis=0, concat_axis=0, tiled=True)]
    unnamed x211 -> x250, local copies, waits for them, and re-layouts: 37.5 us -> 40.6 us
    ppermute x21 -> x22, waiting for transfers between devices: 18.5 us -> 17.4 us  [swap(): return lax.ppermute(value, axis, [(0, 1), (1, 0)])]
  transfers between devices with their start and end apart: 83 -> 104, of which waited for: 47 -> 46; matrix products, arithmetic and copies ran while one was open for 16% -> 16% of each run, Pallas kernels for 8% -> 8%
where the time goes in v7:
time: 642 us; the launch traced here: 633 us
  waiting for transfers between devices  226 us (35%)
  starting transfers between devices  160 us (25%)
  Pallas kernels  78.4 us (12%)
  local copies, waits for them, and re-layouts  58.2 us (9%)
  other arithmetic  51.1 us (8%)
  matrix products  42.3 us (7%)
  between operations  16.6 us (3%)
    ppermute x60, waiting for transfers between devices, shift_z(): return lax.ppermute(value, 'z', [(i, (i + step) % 4) for i in range(4)])  159 us
    ppermute x60, starting transfers between devices, shift_z(): return lax.ppermute(value, 'z', [(i, (i + step) % 4) for i in range(4)])  77.9 us
    unnamed x250, local copies, waits for them, and re-layouts  40.6 us
    ppermute x5, starting transfers between devices, regroup(): got = lax.ppermute(value, ('core', 'y_hi'), [(1, 2), (2, 1)])  24.1 us
    pallas_call x2, Pallas kernels, attend_back(): pl.pallas_call(attend_back_kernel, out_shape=(jax.ShapeDtypeStruct((HALF,...  22.7 us
    ppermute x22, starting transfers between devices, swap(): return lax.ppermute(value, axis, [(0, 1), (1, 0)])  20.5 us
    ppermute x5, waiting for transfers between devices, regroup(): got = lax.ppermute(value, ('core', 'y_hi'), [(1, 2), (2, 1)])  18.5 us
    pallas_call x1, Pallas kernels, wide_part(): pl.pallas_call(wide_kernel, grid=(4,), out_shape=(jax.ShapeDtypeStruct((P...  18.2 us
  transfers between devices with their start and end apart: 104, of which 46 were waited for; matrix products, arithmetic and copies ran while one was open for 16% of the time, Pallas kernels for 8%

profile of v7, /device:TPU:1, one launch (start us, length us, event | category | flops | bytes accessed | tf_op | source)
XLA Modules:
  0.0 632.5 jit_solution(11179520468921079969)
XLA Ops:
  7.2 6.2 collective-permute-start
  27.3 2.7 collective-permute-start.6
  30.0 3.5 all-to-all-start
  43.2 4.2 collective-permute-done.4
  48.4 2.8 collective-permute-start.8
  63.5 5.1 all-to-all-start.1
  76.7 5.1 collective-permute-start.16
  81.8 3.6 all-to-all-done.1.mine
  85.3 6.2 all-to-all-start.2
  92.6 9.5 %attend.2 = (bf16[768,128]{1,0:T(8,128)(2,1)S(1)}, bf16[768,128]{1,0:T(8,128)(2,1)}, f32[2,1536]{1,0:T(2,128)S(1)}, bf16[1536,384]{1,0:T(8,128)(2,1)S(1)}) custom-call(s32[4]{0:T(128)S(1)} %pad_add_fusion.info, f32[2]{0:T(128)S(1)} %multiply_exponential_fusion.slopes, bf16[768,384]{1,0:T(8,128)(2,1)S(1)} %get-tuple-element.249.mine, ...), custom_call_target="tpu_custom_call" | custom-call | flops 1000000 | bytes 36000000 | tf_op jit(solution)/shard_map/attend/pallas_call | solution.py:216
  104.4 2.7 collective-permute-start.14
  111.9 4.7 collective-permute-done.14
  127.7 3.0 collective-permute-start.19
  134.4 13.0 %collective-permute-done.19 = bf16[192,1024]{1,0:T(8,128)(2,1)S(1)} collective-permute-done((bf16[192,1024]{1,0:T(8,128)(2,1)S(1)}, bf16[192,1024]{1,0:T(8,128)(2,1)S(1)}, u32[]{:S(2)}, u32[]{:S(2)}) %collective-permute-start.19) | collective-permute-done | bytes 393248 | tf_op jit(solution)/shard_map/ppermute | solution.py:31
  147.4 4.3 collective-permute-done.21
  158.4 2.7 collective-permute-start.28
  168.4 5.2 collective-permute-done.26
  176.1 4.1 fusion.24
  185.4 6.5 %collective-permute-done.30 = bf16[192,1024]{1,0:T(8,128)(2,1)S(1)} collective-permute-done((bf16[192,1024]{1,0:T(8,128)(2,1)S(1)}, bf16[192,1024]{1,0:T(8,128)(2,1)S(1)}, u32[]{:S(2)}, u32[]{:S(2)}) %collective-permute-start.30) | collective-permute-done | bytes 393248 | tf_op jit(solution)/shard_map/ppermute | solution.py:31
  192.0 3.2 collective-permute-done.31
  195.1 9.5 %collective-permute-done.32 = bf16[192,1024]{1,0:T(8,128)(2,1)S(1)} collective-permute-done((bf16[192,1024]{1,0:T(8,128)(2,1)S(1)}, bf16[192,1024]{1,0:T(8,128)(2,1)S(1)}, u32[]{:S(2)}, u32[]{:S(2)}) %collective-permute-start.32) | collective-permute-done | bytes 393248 | tf_op jit(solution)/shard_map/ppermute | solution.py:31
  208.1 5.7 collective-permute-start.33
  214.0 2.7 collective-permute-start.39
  216.7 2.7 collective-permute-start.38
  229.6 8.3 %attend.3 = (bf16[768,128]{1,0:T(8,128)(2,1)S(1)}, bf16[768,128]{1,0:T(8,128)(2,1)S(1)}, f32[2,1536]{1,0:T(2,128)S(1)}, bf16[1536,384]{1,0:T(8,128)(2,1)S(1)}) custom-call(s32[4]{0:T(128)S(1)} %pad_add_fusion.info, f32[2]{0:T(128)S(1)} %multiply_exponential_fusion.slopes, bf16[768,384]{1,0:T(8,128)(2,1)S(1)} %get-tuple-element.292.mine, ...), custom_call_target="tpu_custom_call" | custom-call | flops 1000000 | bytes 36000000 | tf_op jit(solution)/shard_map/attend/pallas_call | solution.py:216
  241.0 2.8 collective-permute-start.43
  244.7 15.5 %collective-permute-done.43 = bf16[192,1024]{1,0:T(8,128)(2,1)S(1)} collective-permute-done((bf16[192,1024]{1,0:T(8,128)(2,1)S(1)}, bf16[192,1024]{1,0:T(8,128)(2,1)S(1)}, u32[]{:S(2)}, u32[]{:S(2)}) %collective-permute-start.43) | collective-permute-done | bytes 393248 | tf_op jit(solution)/shard_map/ppermute | solution.py:31
  260.2 4.0 collective-permute-done.45
  269.0 18.2 %wide_part.1 = (f32[192,1024]{1,0:T(8,128)}, bf16[192,1024]{1,0:T(8,128)(2,1)}, f32[192,1024]{1,0:T(8,128)}, bf16[192,1024]{1,0:T(8,128)(2,1)}, f32[4,1,512]{2,1...) custom-call(bf16[192,1024]{1,0:T(8,128)(2,1)} %add_convert_fusion.2.rows_own, ...), custom_call_target="tpu_custom_call" | custom-call | flops 11274289152 | bytes 50000000 | tf_op jit(solution)/shard_map/wide_part/pallas_call | solution.py:365
  291.4 2.8 fusion.72
  298.6 7.7 %collective-permute-done.50 = bf16[96,1024]{1,0:T(8,128)(2,1)S(1)} collective-permute-done((bf16[96,1024]{1,0:T(8,128)(2,1)S(1)}, bf16[96,1024]{1,0:T(8,128)(2,1)S(1)}, u32[]{:S(2)}, u32[]{:S(2)}) %collective-permute-start.50) | collective-permute-done | bytes 196640 | tf_op jit(solution)/shard_map/ppermute | solution.py:31
  306.2 2.7 collective-permute-start.54
  309.0 3.6 collective-permute-done.53
  317.5 11.4 %attend_back.2 = (bf16[768,384]{1,0:T(8,128)(2,1)S(1)}, bf16[768,384]{1,0:T(8,128)(2,1)}, f32[1,384]{1,0:T(1,128)S(1)}) custom-call(s32[4]{0:T(128)S(1)} %pad_add_fusion.info, f32[2]{0:T(128)S(1)} %multiply_exponential_fusion.slopes, bf16[1536,384]{1,0:T(8,128)(2,1)S(1)} %copy-done.24, bf16[768,128]{1,0:T(8,128)(2,1)S(1)} %get-tuple-element.483.mine, ...), custom_call_target="tpu_custom_call" | custom-call | flops 1000000 | bytes 48000000 | tf_op jit(solution)/shard_map/attend_back/pallas_call | solution.py:240
  338.2 2.7 collective-permute-start.58
  344.9 13.2 %collective-permute-done.58 = bf16[192,1024]{1,0:T(8,128)(2,1)} collective-permute-done((bf16[192,1024]{1,0:T(8,128)(2,1)}, bf16[192,1024]{1,0:T(8,128)(2,1)}, u32[]{:S(2)}, u32[]{:S(2)}) %collective-permute-start.58) | collective-permute-done | bytes 393248 | tf_op jit(solution)/shard_map/ppermute | solution.py:31
  358.1 3.6 collective-permute-done.60
  379.2 3.1 collective-permute-done.64
  384.0 6.2 collective-permute-done.67
  398.0 6.6 %fusion.16 = bf16[768,1024]{1,0:T(8,128)(2,1)S(1)} fusion(f32[768,1024]{1,0:T(8,128)} %get-tuple-element.341, bf16[768,1024]{1,0:T(8,128)(2,1)} %copy-done.87, bf16[1024,1024]{1,0:T(8,128)(2,1)} %copy-done.2), kind=kOutput, calls=%fused_computation.28 | convolution fusion | flops 1626341376 | bytes 8388608 | tf_op jit(solution)/shard_map/dot_general | solution.py:73
  404.6 2.7 collective-permute-done.69
  410.0 2.8 collective-permute-start.74
  413.8 3.2 collective-permute-start.71
  418.0 3.2 convolution_convert_fusion
  421.1 3.2 convolution_convert_fusion.1
  427.8 10.5 %collective-permute-done.73 = bf16[192,1024]{1,0:T(8,128)(2,1)} collective-permute-done((bf16[192,1024]{1,0:T(8,128)(2,1)}, bf16[192,1024]{1,0:T(8,128)(2,1)}, u32[]{:S(2)}, u32[]{:S(2)}) %collective-permute-start.73) | collective-permute-done | bytes 393248 | tf_op jit(solution)/shard_map/ppermute | solution.py:31
  451.9 7.8 %collective-permute-done.75 = bf16[96,1024]{1,0:T(8,128)(2,1)S(1)} collective-permute-done((bf16[96,1024]{1,0:T(8,128)(2,1)S(1)}, bf16[96,1024]{1,0:T(8,128)(2,1)S(1)}, u32[]{:S(2)}, u32[]{:S(2)}) %collective-permute-start.75) | collective-permute-done | bytes 196640 | tf_op jit(solution)/shard_map/ppermute | solution.py:31
  459.7 2.7 collective-permute-start.79
  462.5 3.9 collective-permute-done.78
  467.6 3.8 fusion
  479.8 4.5 all-to-all-start.3
  486.0 11.3 %attend_back.3 = (bf16[768,384]{1,0:T(8,128)(2,1)S(1)}, bf16[768,384]{1,0:T(8,128)(2,1)}, f32[1,384]{1,0:T(1,128)S(1)}) custom-call(s32[4]{0:T(128)S(1)} %pad_add_fusion.info, f32[2]{0:T(128)S(1)} %multiply_exponential_fusion.slopes, bf16[1536,384]{1,0:T(8,128)(2,1)S(1)} %copy-done.22, bf16[768,128]{1,0:T(8,128)(2,1)S(1)} %get-tuple-element.476.mine, ...), custom_call_target="tpu_custom_call" | custom-call | flops 1000000 | bytes 48000000 | tf_op jit(solution)/shard_map/attend_back/pallas_call | solution.py:240
  508.7 13.5 %all-to-all-done.3 = bf16[8,64,2304]{2,1,0:T(8,128)(2,1)} async-done(((bf16[8,64,2304]{2,1,0:T(8,128)(2,1)}), bf16[8,64,2304]{2,1,0:T(8,128)(2,1)}, u32[]{:S(2)}, u32[]{:S(2)}) %all-to-all-start.3) | async-done | bytes 2359328 | tf_op jit(solution)/shard_map/all_to_all | solution.py:761
  525.7 9.5 %all-to-all-start.4 = ((bf16[128,8,896]{2,1,0:T(8,128)(2,1)}), bf16[128,8,896]{2,1,0:T(8,128)(2,1)S(1)}, u32[]{:S(2)}, u32[]{:S(2)}) async-start(bf16[128,8,896]{2,1,0:T(8,128)(2,1)} %bitcast.83), calls=%async_computation.6 | async-start | bytes 3670016 | tf_op jit(solution)/shard_map/all_to_all | solution.py:1205
  538.3 3.3 collective-permute-start.90
  542.5 14.1 %collective-permute-done.90 = bf16[8,1792]{1,0:T(8,128)(2,1)S(1)} collective-permute-done((bf16[8,1792]{1,0:T(8,128)(2,1)}, bf16[8,1792]{1,0:T(8,128)(2,1)S(1)}, u32[]{:S(2)}, u32[]{:S(2)}) %collective-permute-start.90) | collective-permute-done | bytes 28704 | tf_op jit(solution)/shard_map/ppermute | solution.py:31
  558.1 4.3 all-to-all-done.4
  568.5 3.7 collective-permute-start.48
  575.2 2.7 collective-permute-done.86
  577.9 9.7 %collective-permute-done.87 = bf16[192,1024]{1,0:T(8,128)(2,1)S(1)} collective-permute-done((bf16[192,1024]{1,0:T(8,128)(2,1)S(1)}, bf16[192,1024]{1,0:T(8,128)(2,1)S(1)}, u32[]{:S(2)}, u32[]{:S(2)}) %collective-permute-start.87) | collective-permute-done | bytes 393248 | tf_op jit(solution)/shard_map/ppermute | solution.py:31
  589.0 3.4 collective-permute-start.88
  592.5 7.1 %collective-permute-done.48 = f32[192,1024]{1,0:T(8,128)S(1)} collective-permute-done((f32[192,1024]{1,0:T(8,128)S(1)}, f32[192,1024]{1,0:T(8,128)S(1)}, u32[]{:S(2)}, u32[]{:S(2)}) %collective-permute-start.48) | collective-permute-done | bytes 786464 | tf_op jit(solution)/shard_map/ppermute | solution.py:43
  600.5 11.5 %collective-permute-done.88 = f32[192,1024]{1,0:T(8,128)S(1)} collective-permute-done((f32[192,1024]{1,0:T(8,128)S(1)}, f32[192,1024]{1,0:T(8,128)S(1)}, u32[]{:S(2)}, u32[]{:S(2)}) %collective-permute-start.88) | collective-permute-done | bytes 786464 | tf_op jit(solution)/shard_map/ppermute | solution.py:43
  618.0 7.3 %unpack_full.1 = (f32[2,512,1024]{2,1,0:T(8,128)}, f32[2,128,4096]{2,1,0:T(8,128)}, f32[2,128,3072]{2,1,0:T(8,128)}, f32[2,128,1024]{2,1,0:T(8,128)}) custom-call(bf16[16,32,4224]{2,1,0:T(8,128)(2,1)} %bitcast.222, f32[2,512,1024]{2,1,0:T(8,128)} %get-tuple-element.403.old_down, ...), custom_call_target="tpu_custom_call", output_to_operand_aliasing={{0}: (1, {}), {1}: (2, {})} | custom-call | tf_op jit(solution)/shard_map/unpack_full/pallas_call | solution.py:912
  (586 shorter events, 235.6 us)
Async XLA Ops:
  7.2 13.9 %collective-permute-start = (bf16[192,1024]{1,0:T(8,128)(2,1)}, bf16[192,1024]{1,0:T(8,128)(2,1)}, u32[]{:S(2)}, u32[]{:S(2)}) collective-permute-start(bf16[192,1024]{1,0:T(8,128)(2,1)} %bitcast.242), channel_id=1, source_target_pairs={{4,8},{8,4},{5,9},{9,5},{6,10},{10,6},{7,11},{11,7},{20,24},{24,20... | collective-permute-start | bytes 1179656 | tf_op jit(solution)/shard_map/ppermute | solution.py:43
  23.5 15.0 %collective-permute-start.1 = (bf16[96,1024]{1,0:T(8,128)(2,1)}, bf16[96,1024]{1,0:T(8,128)(2,1)}, u32[]{:S(2)}, u32[]{:S(2)}) collective-permute-start(bf16[96,1024]{1,0:T(8,128)(2,1)} %get-tuple-element.491), channel_id=1, source_target_pairs={{0,1},{1,2},{2,3},{3,0},{4,5},{5,6},{6,7},{7,4},{8,9},{9,10},{10,1... | collective-permute-start | bytes 589832 | tf_op jit(solution)/shard_map/ppermute | solution.py:31
  25.2 13.4 %collective-permute-start.2 = (bf16[96,1024]{1,0:T(8,128)(2,1)}, bf16[96,1024]{1,0:T(8,128)(2,1)S(1)}, u32[]{:S(2)}, u32[]{:S(2)}) collective-permute-start(bf16[96,1024]{1,0:T(8,128)(2,1)} %get-tuple-element.490), channel_id=1, source_target_pairs={{0,3},{1,0},{2,1},{3,2},{4,7},{5,4},{6,5},{7,6},{8,11},{9,8},{10,9... | collective-permute-start | bytes 589832 | tf_op jit(solution)/shard_map/ppermute | solution.py:31
  27.3 15.0 %collective-permute-start.3 = (bf16[96,1024]{1,0:T(8,128)(2,1)}, bf16[96,1024]{1,0:T(8,128)(2,1)}, u32[]{:S(2)}, u32[]{:S(2)}) collective-permute-start(bf16[96,1024]{1,0:T(8,128)(2,1)} %get-tuple-element.490), channel_id=1, source_target_pairs={{0,1},{1,2},{2,3},{3,0},{4,5},{5,6},{6,7},{7,4},{8,9},{9,10},{10,1... | collective-permute-start | bytes 589832 | tf_op jit(solution)/shard_map/ppermute | solution.py:31
  27.3 20.1 %collective-permute-start.6 = (bf16[96,1024]{1,0:T(8,128)(2,1)}, bf16[96,1024]{1,0:T(8,128)(2,1)}, u32[]{:S(2)}, u32[]{:S(2)}) collective-permute-start(bf16[96,1024]{1,0:T(8,128)(2,1)} %get-tuple-element.491), channel_id=1, source_target_pairs={{0,3},{1,0},{2,1},{3,2},{4,7},{5,4},{6,5},{7,6},{8,11},{9,8},{10,9... | collective-permute-start | bytes 589832 | tf_op jit(solution)/shard_map/ppermute | solution.py:31
  30.0 18.4 %all-to-all-start = ((bf16[8,32,768]{2,1,0:T(8,128)(2,1)}), bf16[8,32,768]{2,1,0:T(8,128)(2,1)S(1)}, u32[]{:S(2)}, u32[]{:S(2)}) async-start(bf16[8,32,768]{2,1,0:T(8,128)(2,1)} %pack_first.1), calls=%async_computation | async-start | bytes 786432 | tf_op jit(solution)/shard_map/all_to_all | solution.py:605
  33.4 92.1 %all-gather.8.cloned.1.call-start = ((), (), s32[]{:S(2)}) async-start(), calls=%async_computation.7 | async-start | bytes 2359296 | tf_op jit(solution)/shard_map/all_gather | solution.py:1058
  63.5 21.8 %all-to-all-start.1 = ((bf16[8,64,1024]{2,1,0:T(8,128)(2,1)}), bf16[8,64,1024]{2,1,0:T(8,128)(2,1)S(1)}, u32[]{:S(2)}, u32[]{:S(2)}) async-start(bf16[8,64,1024]{2,1,0:T(8,128)(2,1)} %get-tuple-element.225), calls=%async_computation.1 | async-start | bytes 2097152 | tf_op jit(solution)/shard_map/all_to_all | solution.py:605
  74.4 10.9 %collective-permute-start.12 = (bf16[768,384]{1,0:T(8,128)(2,1)}, bf16[768,384]{1,0:T(8,128)(2,1)}, u32[]{:S(2)}, u32[]{:S(2)}) collective-permute-start(bf16[768,384]{1,0:T(8,128)(2,1)} %get-tuple-element.469), channel_id=1, source_target_pairs={{0,8},{8,0},{1,9},{9,1},{2,10},{10,2},{3,11},{11,3},{4,12},{12,4},... | collective-permute-start | bytes 1769480 | tf_op jit(solution)/shard_map/ppermute | solution.py:39
  76.7 15.1 %collective-permute-start.16 = (s32[1,128]{1,0:T(1,128)S(1)}, s32[1,128]{1,0:T(1,128)S(1)}, u32[]{:S(2)}, u32[]{:S(2)}) collective-permute-start(s32[1,128]{1,0:T(1,128)S(1)} %broadcast_in_dim.12), channel_id=1, source_target_pairs={{4,8},{8,4},{5,9},{9,5},{6,10},{10,6},{7,11},{11,7},{20,24},{24,20... | collective-permute-start | bytes 1544 | tf_op jit(solution)/shard_map/ppermute | solution.py:43
  85.3 33.3 %all-to-all-start.2 = ((bf16[8,64,768]{2,1,0:T(8,128)(2,1)}), bf16[8,64,768]{2,1,0:T(8,128)(2,1)}, u32[]{:S(2)}, u32[]{:S(2)}) async-start(bf16[8,64,768]{2,1,0:T(8,128)(2,1)} %copy-done.25), calls=%async_computation.2 | async-start | bytes 1572864 | tf_op jit(solution)/shard_map/all_to_all | solution.py:605
  91.6 177.5 %all-gather.10.cloned.1.call-start = ((), (), s32[]{:S(2)}) async-start(), calls=%async_computation.10 | async-start | bytes 10485760 | tf_op jit(solution)/shard_map/all_gather | solution.py:1088
  104.4 12.2 %collective-permute-start.14 = (bf16[96,1024]{1,0:T(8,128)(2,1)}, bf16[96,1024]{1,0:T(8,128)(2,1)S(1)}, u32[]{:S(2)}, u32[]{:S(2)}) collective-permute-start(bf16[96,1024]{1,0:T(8,128)(2,1)} %copy-done.75), channel_id=1, source_target_pairs={{0,64},{32,96},{64,0},{96,32},{1,65},{33,97},{65,1},{97,33},{2,66}... | collective-permute-start | bytes 589832 | tf_op jit(solution)/shard_map/ppermute | solution.py:35
  127.7 19.6 %collective-permute-start.19 = (bf16[192,1024]{1,0:T(8,128)(2,1)S(1)}, bf16[192,1024]{1,0:T(8,128)(2,1)S(1)}, u32[]{:S(2)}, u32[]{:S(2)}) collective-permute-start(bf16[192,1024]{1,0:T(8,128)(2,1)S(1)} %get-tuple-element.468), channel_id=1, source_target_pairs={{0,3},{1,0},{2,1},{3,2},{4,7},{5,4},{6,5},{7,6},{8,11},{9,8},{10,9... | collective-permute-start | bytes 1179656 | tf_op jit(solution)/shard_map/ppermute | solution.py:31
  130.7 16.7 %collective-permute-start.20 = (bf16[192,1024]{1,0:T(8,128)(2,1)S(1)}, bf16[192,1024]{1,0:T(8,128)(2,1)S(1)}, u32[]{:S(2)}, u32[]{:S(2)}) collective-permute-start(bf16[192,1024]{1,0:T(8,128)(2,1)S(1)} %get-tuple-element.467), channel_id=1, source_target_pairs={{0,2},{1,3},{2,0},{3,1},{4,6},{5,7},{6,4},{7,5},{8,10},{9,11},{10,... | collective-permute-start | bytes 1179656 | tf_op jit(solution)/shard_map/ppermute | solution.py:31
  131.3 20.4 %collective-permute-start.21 = (bf16[192,1024]{1,0:T(8,128)(2,1)S(1)}, bf16[192,1024]{1,0:T(8,128)(2,1)S(1)}, u32[]{:S(2)}, u32[]{:S(2)}) collective-permute-start(bf16[192,1024]{1,0:T(8,128)(2,1)S(1)} %get-tuple-element.466), channel_id=1, source_target_pairs={{0,1},{1,2},{2,3},{3,0},{4,5},{5,6},{6,7},{7,4},{8,9},{9,10},{10,1... | collective-permute-start | bytes 1179656 | tf_op jit(solution)/shard_map/ppermute | solution.py:31
  154.0 210.7 %reduce-scatter.3.cloned.1.call-start = ((), (), s32[]{:S(2)}) async-start(), calls=%async_computation.8 | async-start | bytes 10485760 | tf_op jit(solution)/shard_map/reduce_scatter | solution.py:1130
  155.2 10.4 %collective-permute-start.23 = (bf16[96,1024]{1,0:T(8,128)(2,1)S(1)}, bf16[96,1024]{1,0:T(8,128)(2,1)S(1)}, u32[]{:S(2)}, u32[]{:S(2)}) collective-permute-start(bf16[96,1024]{1,0:T(8,128)(2,1)S(1)} %get-tuple-element.489), channel_id=1, source_target_pairs={{0,1},{1,2},{2,3},{3,0},{4,5},{5,6},{6,7},{7,4},{8,9},{9,10},{10,1... | collective-permute-start | bytes 589832 | tf_op jit(solution)/shard_map/ppermute | solution.py:31
  158.4 15.3 %collective-permute-start.28 = (bf16[96,1024]{1,0:T(8,128)(2,1)S(1)}, bf16[96,1024]{1,0:T(8,128)(2,1)S(1)}, u32[]{:S(2)}, u32[]{:S(2)}) collective-permute-start(bf16[96,1024]{1,0:T(8,128)(2,1)S(1)} %get-tuple-element.489), channel_id=1, source_target_pairs={{0,3},{1,0},{2,1},{3,2},{4,7},{5,4},{6,5},{7,6},{8,11},{9,8},{10,9... | collective-permute-start | bytes 589832 | tf_op jit(solution)/shard_map/ppermute | solution.py:31
  161.0 12.7 %collective-permute-start.29 = (bf16[8,64,768]{2,1,0:T(8,128)(2,1)}, bf16[8,64,768]{2,1,0:T(8,128)(2,1)S(1)}, u32[]{:S(2)}, u32[]{:S(2)}) collective-permute-start(bf16[8,64,768]{2,1,0:T(8,128)(2,1)} %all-to-all-done.2.mine), channel_id=1, source_target_pairs={{0,8},{8,0},{1,9},{9,1},{2,10},{10,2},{3,11},{11,3},{4,12},{12,4},... | collective-permute-start | bytes 2359304 | tf_op jit(solution)/shard_map/ppermute | solution.py:39
  181.8 10.2 %collective-permute-start.30 = (bf16[192,1024]{1,0:T(8,128)(2,1)S(1)}, bf16[192,1024]{1,0:T(8,128)(2,1)S(1)}, u32[]{:S(2)}, u32[]{:S(2)}) collective-permute-start(bf16[192,1024]{1,0:T(8,128)(2,1)S(1)} %get-tuple-element.465), channel_id=1, source_target_pairs={{0,3},{1,0},{2,1},{3,2},{4,7},{5,4},{6,5},{7,6},{8,11},{9,8},{10,9... | collective-permute-start | bytes 1179656 | tf_op jit(solution)/shard_map/ppermute | solution.py:31
  184.2 11.0 %collective-permute-start.31 = (bf16[192,1024]{1,0:T(8,128)(2,1)S(1)}, bf16[192,1024]{1,0:T(8,128)(2,1)S(1)}, u32[]{:S(2)}, u32[]{:S(2)}) collective-permute-start(bf16[192,1024]{1,0:T(8,128)(2,1)S(1)} %get-tuple-element.464), channel_id=1, source_target_pairs={{0,2},{1,3},{2,0},{3,1},{4,6},{5,7},{6,4},{7,5},{8,10},{9,11},{10,... | collective-permute-start | bytes 1179656 | tf_op jit(solution)/shard_map/ppermute | solution.py:31
  184.2 20.4 %collective-permute-start.32 = (bf16[192,1024]{1,0:T(8,128)(2,1)S(1)}, bf16[192,1024]{1,0:T(8,128)(2,1)S(1)}, u32[]{:S(2)}, u32[]{:S(2)}) collective-permute-start(bf16[192,1024]{1,0:T(8,128)(2,1)S(1)} %get-tuple-element.463), channel_id=1, source_target_pairs={{0,1},{1,2},{2,3},{3,0},{4,5},{5,6},{6,7},{7,4},{8,9},{9,10},{10,1... | collective-permute-start | bytes 1179656 | tf_op jit(solution)/shard_map/ppermute | solution.py:31
  205.4 11.3 %collective-permute-start.34 = (bf16[96,1024]{1,0:T(8,128)(2,1)S(1)}, bf16[96,1024]{1,0:T(8,128)(2,1)S(1)}, u32[]{:S(2)}, u32[]{:S(2)}) collective-permute-start(bf16[96,1024]{1,0:T(8,128)(2,1)S(1)} %get-tuple-element.487), channel_id=1, source_target_pairs={{0,1},{1,2},{2,3},{3,0},{4,5},{5,6},{6,7},{7,4},{8,9},{9,10},{10,1... | collective-permute-start | bytes 589832 | tf_op jit(solution)/shard_map/ppermute | solution.py:31
  205.5 11.2 %collective-permute-start.35 = (bf16[96,1024]{1,0:T(8,128)(2,1)S(1)}, bf16[96,1024]{1,0:T(8,128)(2,1)S(1)}, u32[]{:S(2)}, u32[]{:S(2)}) collective-permute-start(bf16[96,1024]{1,0:T(8,128)(2,1)S(1)} %get-tuple-element.486), channel_id=1, source_target_pairs={{0,3},{1,0},{2,1},{3,2},{4,7},{5,4},{6,5},{7,6},{8,11},{9,8},{10,9... | collective-permute-start | bytes 589832 | tf_op jit(solution)/shard_map/ppermute | solution.py:31
  208.1 19.3 %collective-permute-start.33 = (bf16[192,1024]{1,0:T(8,128)(2,1)S(1)}, bf16[192,1024]{1,0:T(8,128)(2,1)S(1)}, u32[]{:S(2)}, u32[]{:S(2)}) collective-permute-start(bf16[192,1024]{1,0:T(8,128)(2,1)S(1)} %bitcast.243), channel_id=1, source_target_pairs={{4,8},{8,4},{5,9},{9,5},{6,10},{10,6},{7,11},{11,7},{20,24},{24,20... | collective-permute-start | bytes 1179656 | tf_op jit(solution)/shard_map/ppermute | solution.py:43
  214.0 10.4 %collective-permute-start.39 = (bf16[96,1024]{1,0:T(8,128)(2,1)S(1)}, bf16[96,1024]{1,0:T(8,128)(2,1)S(1)}, u32[]{:S(2)}, u32[]{:S(2)}) collective-permute-start(bf16[96,1024]{1,0:T(8,128)(2,1)S(1)} %get-tuple-element.487), channel_id=1, source_target_pairs={{0,3},{1,0},{2,1},{3,2},{4,7},{5,4},{6,5},{7,6},{8,11},{9,8},{10,9... | collective-permute-start | bytes 589832 | tf_op jit(solution)/shard_map/ppermute | solution.py:31
  229.4 10.1 %collective-permute-start.41 = (bf16[192,1024]{1,0:T(8,128)(2,1)S(1)}, bf16[192,1024]{1,0:T(8,128)(2,1)S(1)}, u32[]{:S(2)}, u32[]{:S(2)}) collective-permute-start(bf16[192,1024]{1,0:T(8,128)(2,1)S(1)} %get-tuple-element.291.grads_own), channel_id=1, source_target_pairs={{0,8},{8,0},{1,9},{9,1},{2,10},{10,2},{3,11},{11,3},{4,12},{12,4},... | collective-permute-start | bytes 1179656 | tf_op jit(solution)/shard_map/ppermute | solution.py:39
  241.0 19.2 %collective-permute-start.43 = (bf16[192,1024]{1,0:T(8,128)(2,1)S(1)}, bf16[192,1024]{1,0:T(8,128)(2,1)S(1)}, u32[]{:S(2)}, u32[]{:S(2)}) collective-permute-start(bf16[192,1024]{1,0:T(8,128)(2,1)S(1)} %get-tuple-element.460), channel_id=1, source_target_pairs={{0,3},{1,0},{2,1},{3,2},{4,7},{5,4},{6,5},{7,6},{8,11},{9,8},{10,9... | collective-permute-start | bytes 1179656 | tf_op jit(solution)/shard_map/ppermute | solution.py:31
  243.8 16.4 %collective-permute-start.44 = (bf16[192,1024]{1,0:T(8,128)(2,1)S(1)}, bf16[192,1024]{1,0:T(8,128)(2,1)S(1)}, u32[]{:S(2)}, u32[]{:S(2)}) collective-permute-start(bf16[192,1024]{1,0:T(8,128)(2,1)S(1)} %get-tuple-element.459), channel_id=1, source_target_pairs={{0,2},{1,3},{2,0},{3,1},{4,6},{5,7},{6,4},{7,5},{8,10},{9,11},{10,... | collective-permute-start | bytes 1179656 | tf_op jit(solution)/shard_map/ppermute | solution.py:31
  243.8 20.4 %collective-permute-start.45 = (bf16[192,1024]{1,0:T(8,128)(2,1)S(1)}, bf16[192,1024]{1,0:T(8,128)(2,1)S(1)}, u32[]{:S(2)}, u32[]{:S(2)}) collective-permute-start(bf16[192,1024]{1,0:T(8,128)(2,1)S(1)} %get-tuple-element.458), channel_id=1, source_target_pairs={{0,1},{1,2},{2,3},{3,0},{4,5},{5,6},{6,7},{7,4},{8,9},{9,10},{10,1... | collective-permute-start | bytes 1179656 | tf_op jit(solution)/shard_map/ppermute | solution.py:31
  287.2 184.2 %reduce-scatter.5.cloned.1.call-start = ((), (), s32[]{:S(2)}) async-start(), calls=%async_computation.9 | async-start | bytes 2228224 | tf_op jit(solution)/shard_map/reduce_scatter | solution.py:1160
  294.2 12.0 %collective-permute-start.51 = (bf16[96,1024]{1,0:T(8,128)(2,1)S(1)}, bf16[96,1024]{1,0:T(8,128)(2,1)S(1)}, u32[]{:S(2)}, u32[]{:S(2)}) collective-permute-start(bf16[96,1024]{1,0:T(8,128)(2,1)S(1)} %get-tuple-element.484), channel_id=1, source_target_pairs={{0,3},{1,0},{2,1},{3,2},{4,7},{5,4},{6,5},{7,6},{8,11},{9,8},{10,9... | collective-permute-start | bytes 589832 | tf_op jit(solution)/shard_map/ppermute | solution.py:31
  294.9 14.0 %collective-permute-start.52 = (bf16[96,1024]{1,0:T(8,128)(2,1)S(1)}, bf16[96,1024]{1,0:T(8,128)(2,1)S(1)}, u32[]{:S(2)}, u32[]{:S(2)}) collective-permute-start(bf16[96,1024]{1,0:T(8,128)(2,1)S(1)} %get-tuple-element.484), channel_id=1, source_target_pairs={{0,1},{1,2},{2,3},{3,0},{4,5},{5,6},{6,7},{7,4},{8,9},{9,10},{10,1... | collective-permute-start | bytes 589832 | tf_op jit(solution)/shard_map/ppermute | solution.py:31
  295.8 10.5 %collective-permute-start.50 = (bf16[96,1024]{1,0:T(8,128)(2,1)S(1)}, bf16[96,1024]{1,0:T(8,128)(2,1)S(1)}, u32[]{:S(2)}, u32[]{:S(2)}) collective-permute-start(bf16[96,1024]{1,0:T(8,128)(2,1)S(1)} %get-tuple-element.485), channel_id=1, source_target_pairs={{0,1},{1,2},{2,3},{3,0},{4,5},{5,6},{6,7},{7,4},{8,9},{9,10},{10,1... | collective-permute-start | bytes 589832 | tf_op jit(solution)/shard_map/ppermute | solution.py:31
  295.8 16.8 %collective-permute-start.55 = (bf16[96,1024]{1,0:T(8,128)(2,1)S(1)}, bf16[96,1024]{1,0:T(8,128)(2,1)S(1)}, u32[]{:S(2)}, u32[]{:S(2)}) collective-permute-start(bf16[96,1024]{1,0:T(8,128)(2,1)S(1)} %get-tuple-element.485), channel_id=1, source_target_pairs={{0,3},{1,0},{2,1},{3,2},{4,7},{5,4},{6,5},{7,6},{8,11},{9,8},{10,9... | collective-permute-start | bytes 589832 | tf_op jit(solution)/shard_map/ppermute | solution.py:31
  338.2 19.9 %collective-permute-start.58 = (bf16[192,1024]{1,0:T(8,128)(2,1)}, bf16[192,1024]{1,0:T(8,128)(2,1)}, u32[]{:S(2)}, u32[]{:S(2)}) collective-permute-start(bf16[192,1024]{1,0:T(8,128)(2,1)} %get-tuple-element.457), channel_id=1, source_target_pairs={{0,3},{1,0},{2,1},{3,2},{4,7},{5,4},{6,5},{7,6},{8,11},{9,8},{10,9... | collective-permute-start | bytes 1179656 | tf_op jit(solution)/shard_map/ppermute | solution.py:31
  340.9 17.2 %collective-permute-start.59 = (bf16[192,1024]{1,0:T(8,128)(2,1)}, bf16[192,1024]{1,0:T(8,128)(2,1)}, u32[]{:S(2)}, u32[]{:S(2)}) collective-permute-start(bf16[192,1024]{1,0:T(8,128)(2,1)} %get-tuple-element.456), channel_id=1, source_target_pairs={{0,2},{1,3},{2,0},{3,1},{4,6},{5,7},{6,4},{7,5},{8,10},{9,11},{10,... | collective-permute-start | bytes 1179656 | tf_op jit(solution)/shard_map/ppermute | solution.py:31
  340.9 20.7 %collective-permute-start.60 = (bf16[192,1024]{1,0:T(8,128)(2,1)}, bf16[192,1024]{1,0:T(8,128)(2,1)}, u32[]{:S(2)}, u32[]{:S(2)}) collective-permute-start(bf16[192,1024]{1,0:T(8,128)(2,1)} %get-tuple-element.455), channel_id=1, source_target_pairs={{0,1},{1,2},{2,3},{3,0},{4,5},{5,6},{6,7},{7,4},{8,9},{9,10},{10,1... | collective-permute-start | bytes 1179656 | tf_op jit(solution)/shard_map/ppermute | solution.py:31
  366.1 24.1 %collective-permute-start.67 = (bf16[8,64,1024]{2,1,0:T(8,128)(2,1)S(1)}, bf16[8,64,1024]{2,1,0:T(8,128)(2,1)}, u32[]{:S(2)}, u32[]{:S(2)}) collective-permute-start(bf16[8,64,1024]{2,1,0:T(8,128)(2,1)S(1)} %dynamic-slice_bitcast_fusion), channel_id=1, source_target_pairs={{0,16},{16,0},{1,17},{17,1},{2,18},{18,2},{3,19},{19,3},{4,20},{20... | collective-permute-start | bytes 3145736 | tf_op jit(solution)/shard_map/ppermute | solution.py:39
  370.8 12.0 %collective-permute-start.66 = (bf16[96,1024]{1,0:T(8,128)(2,1)}, bf16[96,1024]{1,0:T(8,128)(2,1)S(1)}, u32[]{:S(2)}, u32[]{:S(2)}) collective-permute-start(bf16[96,1024]{1,0:T(8,128)(2,1)} %get-tuple-element.481), channel_id=1, source_target_pairs={{0,3},{1,0},{2,1},{3,2},{4,7},{5,4},{6,5},{7,6},{8,11},{9,8},{10,9... | collective-permute-start | bytes 589832 | tf_op jit(solution)/shard_map/ppermute | solution.py:31
  392.7 11.9 %collective-permute-start.68 = (bf16[2,64,1024]{2,1,0:T(8,128)(2,1)}, bf16[2,64,1024]{2,1,0:T(8,128)(2,1)S(1)}, u32[]{:S(2)}, u32[]{:S(2)}) collective-permute-start(bf16[2,64,1024]{2,1,0:T(8,128)(2,1)} %get-tuple-element.471), channel_id=1, source_target_pairs={{0,1},{1,2},{2,3},{3,0},{4,5},{5,6},{6,7},{7,4},{8,9},{9,10},{10,1... | collective-permute-start | bytes 786440 | tf_op jit(solution)/shard_map/ppermute | solution.py:31
  393.9 13.4 %collective-permute-start.69 = (bf16[2,64,1024]{2,1,0:T(8,128)(2,1)}, bf16[2,64,1024]{2,1,0:T(8,128)(2,1)}, u32[]{:S(2)}, u32[]{:S(2)}) collective-permute-start(bf16[2,64,1024]{2,1,0:T(8,128)(2,1)} %get-tuple-element.473), channel_id=1, source_target_pairs={{0,2},{1,3},{2,0},{3,1},{4,6},{5,7},{6,4},{7,5},{8,10},{9,11},{10,... | collective-permute-start | bytes 786440 | tf_op jit(solution)/shard_map/ppermute | solution.py:31
  396.5 10.8 %collective-permute-start.70 = (bf16[2,64,1024]{2,1,0:T(8,128)(2,1)S(1)}, bf16[2,64,1024]{2,1,0:T(8,128)(2,1)}, u32[]{:S(2)}, u32[]{:S(2)}) collective-permute-start(bf16[2,64,1024]{2,1,0:T(8,128)(2,1)S(1)} %get-tuple-element.472), channel_id=1, source_target_pairs={{0,3},{1,0},{2,1},{3,2},{4,7},{5,4},{6,5},{7,6},{8,11},{9,8},{10,9... | collective-permute-start | bytes 786440 | tf_op jit(solution)/shard_map/ppermute | solution.py:31
  410.0 15.2 %collective-permute-start.74 = (bf16[64,1024]{1,0:T(8,128)(2,1)S(1)}, bf16[64,1024]{1,0:T(8,128)(2,1)S(1)}, u32[]{:S(2)}, u32[]{:S(2)}) collective-permute-start(bf16[64,1024]{1,0:T(8,128)(2,1)S(1)} %dynamic-slice_bitcast_fusion.6), channel_id=1, source_target_pairs={{0,4},{4,0},{1,5},{5,1},{2,6},{6,2},{3,7},{7,3},{8,12},{12,8},{9,1... | collective-permute-start | bytes 393224 | tf_op jit(solution)/shard_map/ppermute | solution.py:39
  413.8 12.0 %collective-permute-start.71 = (bf16[192,1024]{1,0:T(8,128)(2,1)}, bf16[192,1024]{1,0:T(8,128)(2,1)}, u32[]{:S(2)}, u32[]{:S(2)}) collective-permute-start(bf16[192,1024]{1,0:T(8,128)(2,1)} %get-tuple-element.454), channel_id=1, source_target_pairs={{0,3},{1,0},{2,1},{3,2},{4,7},{5,4},{6,5},{7,6},{8,11},{9,8},{10,9... | collective-permute-start | bytes 1179656 | tf_op jit(solution)/shard_map/ppermute | solution.py:31
  417.0 10.8 %collective-permute-start.72 = (bf16[192,1024]{1,0:T(8,128)(2,1)}, bf16[192,1024]{1,0:T(8,128)(2,1)}, u32[]{:S(2)}, u32[]{:S(2)}) collective-permute-start(bf16[192,1024]{1,0:T(8,128)(2,1)} %get-tuple-element.453), channel_id=1, source_target_pairs={{0,2},{1,3},{2,0},{3,1},{4,6},{5,7},{6,4},{7,5},{8,10},{9,11},{10,... | collective-permute-start | bytes 1179656 | tf_op jit(solution)/shard_map/ppermute | solution.py:31
  417.9 20.3 %collective-permute-start.73 = (bf16[192,1024]{1,0:T(8,128)(2,1)}, bf16[192,1024]{1,0:T(8,128)(2,1)}, u32[]{:S(2)}, u32[]{:S(2)}) collective-permute-start(bf16[192,1024]{1,0:T(8,128)(2,1)} %get-tuple-element.452), channel_id=1, source_target_pairs={{0,1},{1,2},{2,3},{3,0},{4,5},{5,6},{6,7},{7,4},{8,9},{9,10},{10,1... | collective-permute-start | bytes 1179656 | tf_op jit(solution)/shard_map/ppermute | solution.py:31
  446.6 21.0 %collective-permute-start.81 = (bf16[8,64,2048]{2,1,0:T(8,128)(2,1)}, bf16[8,64,2048]{2,1,0:T(8,128)(2,1)}, u32[]{:S(2)}, u32[]{:S(2)}) collective-permute-start(bf16[8,64,2048]{2,1,0:T(8,128)(2,1)} %fusion.26), channel_id=1, source_target_pairs={{0,8},{8,0},{1,9},{9,1},{2,10},{10,2},{3,11},{11,3},{4,12},{12,4},... | collective-permute-start | bytes 6291464 | tf_op jit(solution)/shard_map/ppermute | solution.py:39
  447.6 12.1 %collective-permute-start.76 = (bf16[96,1024]{1,0:T(8,128)(2,1)S(1)}, bf16[96,1024]{1,0:T(8,128)(2,1)S(1)}, u32[]{:S(2)}, u32[]{:S(2)}) collective-permute-start(bf16[96,1024]{1,0:T(8,128)(2,1)S(1)} %get-tuple-element.477), channel_id=1, source_target_pairs={{0,3},{1,0},{2,1},{3,2},{4,7},{5,4},{6,5},{7,6},{8,11},{9,8},{10,9... | collective-permute-start | bytes 589832 | tf_op jit(solution)/shard_map/ppermute | solution.py:31
  448.0 14.4 %collective-permute-start.77 = (bf16[96,1024]{1,0:T(8,128)(2,1)S(1)}, bf16[96,1024]{1,0:T(8,128)(2,1)S(1)}, u32[]{:S(2)}, u32[]{:S(2)}) collective-permute-start(bf16[96,1024]{1,0:T(8,128)(2,1)S(1)} %get-tuple-element.477), channel_id=1, source_target_pairs={{0,1},{1,2},{2,3},{3,0},{4,5},{5,6},{6,7},{7,4},{8,9},{9,10},{10,1... | collective-permute-start | bytes 589832 | tf_op jit(solution)/shard_map/ppermute | solution.py:31
  449.1 10.6 %collective-permute-start.75 = (bf16[96,1024]{1,0:T(8,128)(2,1)S(1)}, bf16[96,1024]{1,0:T(8,128)(2,1)S(1)}, u32[]{:S(2)}, u32[]{:S(2)}) collective-permute-start(bf16[96,1024]{1,0:T(8,128)(2,1)S(1)} %get-tuple-element.478), channel_id=1, source_target_pairs={{0,1},{1,2},{2,3},{3,0},{4,5},{5,6},{6,7},{7,4},{8,9},{9,10},{10,1... | collective-permute-start | bytes 589832 | tf_op jit(solution)/shard_map/ppermute | solution.py:31
  449.2 17.2 %collective-permute-start.80 = (bf16[96,1024]{1,0:T(8,128)(2,1)S(1)}, bf16[96,1024]{1,0:T(8,128)(2,1)S(1)}, u32[]{:S(2)}, u32[]{:S(2)}) collective-permute-start(bf16[96,1024]{1,0:T(8,128)(2,1)S(1)} %get-tuple-element.478), channel_id=1, source_target_pairs={{0,3},{1,0},{2,1},{3,2},{4,7},{5,4},{6,5},{7,6},{8,11},{9,8},{10,9... | collective-permute-start | bytes 589832 | tf_op jit(solution)/shard_map/ppermute | solution.py:31
  479.8 42.4 %all-to-all-start.3 = ((bf16[8,64,2304]{2,1,0:T(8,128)(2,1)}), bf16[8,64,2304]{2,1,0:T(8,128)(2,1)}, u32[]{:S(2)}, u32[]{:S(2)}) async-start(bf16[8,64,2304]{2,1,0:T(8,128)(2,1)} %pad_maximum_fusion), calls=%async_computation.5 | async-start | bytes 4718592 | tf_op jit(solution)/shard_map/all_to_all | solution.py:761
  484.3 78.1 %all-gather.12.cloned.1.call-start = ((), (), s32[]{:S(2)}) async-start(), calls=%async_computation.11 | async-start | bytes 2228224 | tf_op jit(solution)/shard_map/all_gather | solution.py:1175
  525.7 36.7 %all-to-all-start.4 = ((bf16[128,8,896]{2,1,0:T(8,128)(2,1)}), bf16[128,8,896]{2,1,0:T(8,128)(2,1)S(1)}, u32[]{:S(2)}, u32[]{:S(2)}) async-start(bf16[128,8,896]{2,1,0:T(8,128)(2,1)} %bitcast.83), calls=%async_computation.6 | async-start | bytes 3670016 | tf_op jit(solution)/shard_map/all_to_all | solution.py:1205
  535.2 80.3 %all-gather.14.cloned.1.call-start = ((), (), s32[]{:S(2)}) async-start(), calls=%async_computation.12 | async-start | bytes 4595712 | tf_op jit(solution)/shard_map/all_gather | solution.py:1224
  538.3 18.3 %collective-permute-start.90 = (bf16[8,1792]{1,0:T(8,128)(2,1)}, bf16[8,1792]{1,0:T(8,128)(2,1)S(1)}, u32[]{:S(2)}, u32[]{:S(2)}) collective-permute-start(bf16[8,1792]{1,0:T(8,128)(2,1)} %get-tuple-element.500), channel_id=1, source_target_pairs={{0,3},{1,0},{2,1},{3,2},{4,7},{5,4},{6,5},{7,6},{8,11},{9,8},{10,9... | collective-permute-start | bytes 86024 | tf_op jit(solution)/shard_map/ppermute | solution.py:31
  541.6 15.0 %collective-permute-start.91 = (bf16[8,1792]{1,0:T(8,128)(2,1)}, bf16[8,1792]{1,0:T(8,128)(2,1)}, u32[]{:S(2)}, u32[]{:S(2)}) collective-permute-start(bf16[8,1792]{1,0:T(8,128)(2,1)} %get-tuple-element.499), channel_id=1, source_target_pairs={{0,2},{1,3},{2,0},{3,1},{4,6},{5,7},{6,4},{7,5},{8,10},{9,11},{10,... | collective-permute-start | bytes 86024 | tf_op jit(solution)/shard_map/ppermute | solution.py:31
  541.6 15.0 %collective-permute-start.92 = (bf16[8,1792]{1,0:T(8,128)(2,1)}, bf16[8,1792]{1,0:T(8,128)(2,1)}, u32[]{:S(2)}, u32[]{:S(2)}) collective-permute-start(bf16[8,1792]{1,0:T(8,128)(2,1)} %get-tuple-element.498), channel_id=1, source_target_pairs={{0,1},{1,2},{2,3},{3,0},{4,5},{5,6},{6,7},{7,4},{8,9},{9,10},{10,1... | collective-permute-start | bytes 86024 | tf_op jit(solution)/shard_map/ppermute | solution.py:31
  566.6 11.3 %collective-permute-start.86 = (bf16[192,1024]{1,0:T(8,128)(2,1)S(1)}, bf16[192,1024]{1,0:T(8,128)(2,1)S(1)}, u32[]{:S(2)}, u32[]{:S(2)}) collective-permute-start(bf16[192,1024]{1,0:T(8,128)(2,1)S(1)} %get-tuple-element.450), channel_id=1, source_target_pairs={{0,2},{1,3},{2,0},{3,1},{4,6},{5,7},{6,4},{7,5},{8,10},{9,11},{10,... | collective-permute-start | bytes 1179656 | tf_op jit(solution)/shard_map/ppermute | solution.py:31
  568.3 19.3 %collective-permute-start.87 = (bf16[192,1024]{1,0:T(8,128)(2,1)S(1)}, bf16[192,1024]{1,0:T(8,128)(2,1)S(1)}, u32[]{:S(2)}, u32[]{:S(2)}) collective-permute-start(bf16[192,1024]{1,0:T(8,128)(2,1)S(1)} %get-tuple-element.449), channel_id=1, source_target_pairs={{0,1},{1,2},{2,3},{3,0},{4,5},{5,6},{6,7},{7,4},{8,9},{9,10},{10,1... | collective-permute-start | bytes 1179656 | tf_op jit(solution)/shard_map/ppermute | solution.py:31
  568.5 31.0 %collective-permute-start.48 = (f32[192,1024]{1,0:T(8,128)S(1)}, f32[192,1024]{1,0:T(8,128)S(1)}, u32[]{:S(2)}, u32[]{:S(2)}) collective-permute-start(f32[192,1024]{1,0:T(8,128)S(1)} %copy-done.47), channel_id=1, source_target_pairs={{4,8},{8,4},{5,9},{9,5},{6,10},{10,6},{7,11},{11,7},{20,24},{24,20... | collective-permute-start | bytes 2359304 | tf_op jit(solution)/shard_map/ppermute | solution.py:43
  589.0 23.0 %collective-permute-start.88 = (f32[192,1024]{1,0:T(8,128)S(1)}, f32[192,1024]{1,0:T(8,128)S(1)}, u32[]{:S(2)}, u32[]{:S(2)}) collective-permute-start(f32[192,1024]{1,0:T(8,128)S(1)} %fusion.42), channel_id=1, source_target_pairs={{4,8},{8,4},{5,9},{9,5},{6,10},{10,6},{7,11},{11,7},{20,24},{24,20... | collective-permute-start | bytes 2359304 | tf_op jit(solution)/shard_map/ppermute | solution.py:43
  (140 other events, 879.3 us)
Sparse Core Ops, SparseCore 0:
  55.8 66.6 all-gather.7
  154.2 81.4 all-gather.9
  287.4 77.1 reduce-scatter.2
  398.1 59.9 reduce-scatter.4
  498.3 38.9 all-gather.11
  564.7 41.4 all-gather.13

commit v8 on v7

--- a/solution.py
+++ b/solution.py
@@ -1179,6 +1179,8 @@
         rows = g_project.reshape(2, 16, 8, 4, 256).transpose(1, 0, 3, 2, 4).reshape(16, 64, 256)
         return jnp.concatenate([summed, core_sum(rows, core)], axis=-1)
 
+    wide_all = wide_grads
+
     def tail_pack(inner_sum, d_joined, sums, vectors):
         w_in = params_0[2].astype(f32)
         gain = jnp.sum(outer(unit_all, d_joined) * w_in, axis=1)
@@ -1186,9 +1188,9 @@
         offset = jnp.sum(offset * w_in, axis=1)
         g_input = outer(kept_0[1], d_joined).astype(bf16)
         packed = pack_tail(info, g_input, (gain, offset), vectors, packed_1)
-        return packed, inner_sum
-
-    crossed, _, (low, inner_1), _, _, scatter, finish = backward(
+        return packed, inner_sum, wide_all
+
+    crossed, _, (low, inner_1, wide_grads), _, _, scatter, finish = backward(
         gradient,
         d_normed,
         sum_up,
@@ -1213,7 +1215,6 @@
         return [both[:, :D], spread[:, :D], both[:, 2 * D : at], spread[:, D:]]
 
     low, both = beside(low, to_all, (crossed, inner_1), outer_rows)
-    low, wide_grads = lax.optimization_barrier((low, wide_grads))
     left, _ = scatter(lambda: None)
     gradient = regroup(finish(left)[0], core, y_hi)
     low = low.reshape(32, 32, 896).astype(f32)

time: 642 us -> 641 us (level)
    all_to_all x1, waiting for transfers between devices: 13.5 us -> 2.22 us  [to_xy(): lax.all_to_all(value, ('x', 'y_lo'), split_axis=0, concat_axis=0, tiled=T...]
    all_gather x1, waiting for transfers between devices: 0.01 us -> 9.52 us  [on_device(): wide_grads = lax.all_gather(wide_grads, GRP)]
    unnamed x250 -> x246, local copies, waits for them, and re-layouts: 40.6 us -> 40.7 us
  transfers between devices with their start and end apart: 104 -> 104, of which waited for: 46 -> 47; matrix products, arithmetic and copies ran while one was open for 16% -> 17% of each run, Pallas kernels for 8% -> 8%
where the time goes in v8:
time: 641 us; the launch traced here: 632 us
  waiting for transfers between devices  221 us (34%)
  starting transfers between devices  162 us (25%)
  Pallas kernels  77.7 us (12%)
  local copies, waits for them, and re-layouts  58.9 us (9%)
  other arithmetic  50.8 us (8%)
  matrix products  44.7 us (7%)
  between operations  16.6 us (3%)
    ppermute x60, waiting for transfers between devices, shift_z(): return lax.ppermute(value, 'z', [(i, (i + step) % 4) for i in range(4)])  159 us
    ppermute x60, starting transfers between devices, shift_z(): return lax.ppermute(value, 'z', [(i, (i + step) % 4) for i in range(4)])  77.2 us
    unnamed x246, local copies, waits for them, and re-layouts  40.7 us
    ppermute x5, starting transfers between devices, regroup(): got = lax.ppermute(value, ('core', 'y_hi'), [(1, 2), (2, 1)])  24.2 us
    ppermute x22, starting transfers between devices, swap(): return lax.ppermute(value, axis, [(0, 1), (1, 0)])  24.1 us
    pallas_call x2, Pallas kernels, attend_back(): pl.pallas_call(attend_back_kernel, out_shape=(jax.ShapeDtypeStruct((HALF,...  22.1 us
    pallas_call x1, Pallas kernels, wide_part(): pl.pallas_call(wide_kernel, grid=(4,), out_shape=(jax.ShapeDtypeStruct((P...  18.2 us
    pallas_call x2, Pallas kernels, attend(): pl.pallas_call(attend_kernel, out_shape=(jax.ShapeDtypeStruct((HALF, 128)...  17.8 us
  transfers between devices with their start and end apart: 104, of which 47 were waited for; matrix products, arithmetic and copies ran while one was open for 17% of the time, Pallas kernels for 8%

profile of v8, /device:TPU:1, one launch (start us, length us, event | category | flops | bytes accessed | tf_op | source)
XLA Modules:
  0.0 631.8 jit_solution(8820701448399358286)
XLA Ops:
  7.2 6.2 collective-permute-start
  27.3 2.7 collective-permute-start.6
  30.0 3.5 all-to-all-start
  43.2 4.2 collective-permute-done.4
  48.4 2.8 collective-permute-start.8
  63.5 5.1 all-to-all-start.1
  76.7 5.1 collective-permute-start.16
  81.8 3.6 all-to-all-done.1.mine
  85.3 6.2 all-to-all-start.2
  92.8 9.5 %attend.2 = (bf16[768,128]{1,0:T(8,128)(2,1)S(1)}, bf16[768,128]{1,0:T(8,128)(2,1)}, f32[2,1536]{1,0:T(2,128)S(1)}, bf16[1536,384]{1,0:T(8,128)(2,1)S(1)}) custom-call(s32[4]{0:T(128)S(1)} %pad_add_fusion.info, f32[2]{0:T(128)S(1)} %multiply_exponential_fusion.slopes, bf16[768,384]{1,0:T(8,128)(2,1)S(1)} %get-tuple-element.248.mine, ...), custom_call_target="tpu_custom_call" | custom-call | flops 1000000 | bytes 36000000 | tf_op jit(solution)/shard_map/attend/pallas_call | solution.py:216
  104.6 2.7 collective-permute-start.14
  112.1 4.7 collective-permute-done.14
  128.0 3.0 collective-permute-start.19
  134.6 13.0 %collective-permute-done.19 = bf16[192,1024]{1,0:T(8,128)(2,1)S(1)} collective-permute-done((bf16[192,1024]{1,0:T(8,128)(2,1)S(1)}, bf16[192,1024]{1,0:T(8,128)(2,1)S(1)}, u32[]{:S(2)}, u32[]{:S(2)}) %collective-permute-start.19) | collective-permute-done | bytes 393248 | tf_op jit(solution)/shard_map/ppermute | solution.py:31
  147.6 4.3 collective-permute-done.21
  158.4 2.7 collective-permute-start.28
  168.5 5.1 collective-permute-done.26
  176.1 4.1 fusion.24
  185.4 6.5 %collective-permute-done.30 = bf16[192,1024]{1,0:T(8,128)(2,1)S(1)} collective-permute-done((bf16[192,1024]{1,0:T(8,128)(2,1)S(1)}, bf16[192,1024]{1,0:T(8,128)(2,1)S(1)}, u32[]{:S(2)}, u32[]{:S(2)}) %collective-permute-start.30) | collective-permute-done | bytes 393248 | tf_op jit(solution)/shard_map/ppermute | solution.py:31
  191.9 3.1 collective-permute-done.31
  195.0 9.5 %collective-permute-done.32 = bf16[192,1024]{1,0:T(8,128)(2,1)S(1)} collective-permute-done((bf16[192,1024]{1,0:T(8,128)(2,1)S(1)}, bf16[192,1024]{1,0:T(8,128)(2,1)S(1)}, u32[]{:S(2)}, u32[]{:S(2)}) %collective-permute-start.32) | collective-permute-done | bytes 393248 | tf_op jit(solution)/shard_map/ppermute | solution.py:31
  208.1 5.7 collective-permute-start.33
  214.0 2.7 collective-permute-start.39
  216.7 2.7 collective-permute-start.38
  229.6 8.3 %attend.3 = (bf16[768,128]{1,0:T(8,128)(2,1)S(1)}, bf16[768,128]{1,0:T(8,128)(2,1)S(1)}, f32[2,1536]{1,0:T(2,128)S(1)}, bf16[1536,384]{1,0:T(8,128)(2,1)S(1)}) custom-call(s32[4]{0:T(128)S(1)} %pad_add_fusion.info, f32[2]{0:T(128)S(1)} %multiply_exponential_fusion.slopes, bf16[768,384]{1,0:T(8,128)(2,1)S(1)} %get-tuple-element.291.mine, ...), custom_call_target="tpu_custom_call" | custom-call | flops 1000000 | bytes 36000000 | tf_op jit(solution)/shard_map/attend/pallas_call | solution.py:216
  241.0 2.8 collective-permute-start.43
  244.7 15.5 %collective-permute-done.43 = bf16[192,1024]{1,0:T(8,128)(2,1)S(1)} collective-permute-done((bf16[192,1024]{1,0:T(8,128)(2,1)S(1)}, bf16[192,1024]{1,0:T(8,128)(2,1)S(1)}, u32[]{:S(2)}, u32[]{:S(2)}) %collective-permute-start.43) | collective-permute-done | bytes 393248 | tf_op jit(solution)/shard_map/ppermute | solution.py:31
  260.2 4.0 collective-permute-done.45
  269.2 18.2 %wide_part.1 = (f32[192,1024]{1,0:T(8,128)}, bf16[192,1024]{1,0:T(8,128)(2,1)}, f32[192,1024]{1,0:T(8,128)}, bf16[192,1024]{1,0:T(8,128)(2,1)}, f32[4,1,512]{2,1...) custom-call(bf16[192,1024]{1,0:T(8,128)(2,1)} %add_convert_fusion.2.rows_own, ...), custom_call_target="tpu_custom_call" | custom-call | flops 11274289152 | bytes 50000000 | tf_op jit(solution)/shard_map/wide_part/pallas_call | solution.py:365
  291.6 2.8 fusion.72
  298.8 7.7 %collective-permute-done.50 = bf16[96,1024]{1,0:T(8,128)(2,1)S(1)} collective-permute-done((bf16[96,1024]{1,0:T(8,128)(2,1)S(1)}, bf16[96,1024]{1,0:T(8,128)(2,1)S(1)}, u32[]{:S(2)}, u32[]{:S(2)}) %collective-permute-start.50) | collective-permute-done | bytes 196640 | tf_op jit(solution)/shard_map/ppermute | solution.py:31
  306.4 2.7 collective-permute-start.54
  309.2 3.6 collective-permute-done.53
  317.5 11.4 %attend_back.2 = (bf16[768,384]{1,0:T(8,128)(2,1)S(1)}, bf16[768,384]{1,0:T(8,128)(2,1)}, f32[1,384]{1,0:T(1,128)S(1)}) custom-call(s32[4]{0:T(128)S(1)} %pad_add_fusion.info, f32[2]{0:T(128)S(1)} %multiply_exponential_fusion.slopes, bf16[1536,384]{1,0:T(8,128)(2,1)S(1)} %copy-done.24, bf16[768,128]{1,0:T(8,128)(2,1)S(1)} %get-tuple-element.481.mine, ...), custom_call_target="tpu_custom_call" | custom-call | flops 1000000 | bytes 48000000 | tf_op jit(solution)/shard_map/attend_back/pallas_call | solution.py:240
  338.4 2.7 collective-permute-start.58
  344.9 13.3 %collective-permute-done.58 = bf16[192,1024]{1,0:T(8,128)(2,1)} collective-permute-done((bf16[192,1024]{1,0:T(8,128)(2,1)}, bf16[192,1024]{1,0:T(8,128)(2,1)}, u32[]{:S(2)}, u32[]{:S(2)}) %collective-permute-start.58) | collective-permute-done | bytes 393248 | tf_op jit(solution)/shard_map/ppermute | solution.py:31
  358.2 3.5 collective-permute-done.60
  380.3 3.1 collective-permute-done.64
  385.1 6.3 collective-permute-done.67
  399.7 6.6 %fusion.16 = bf16[768,1024]{1,0:T(8,128)(2,1)S(1)} fusion(f32[768,1024]{1,0:T(8,128)} %get-tuple-element.340, bf16[768,1024]{1,0:T(8,128)(2,1)} %copy-done.86, bf16[1024,1024]{1,0:T(8,128)(2,1)} %copy-done.2), kind=kOutput, calls=%fused_computation.28 | convolution fusion | flops 1626341376 | bytes 8388608 | tf_op jit(solution)/shard_map/dot_general | solution.py:73
  411.2 2.8 collective-permute-start.74
  415.0 3.3 collective-permute-start.71
  418.9 3.2 convolution_convert_fusion
  422.1 3.2 convolution_convert_fusion.1
  429.3 10.3 %collective-permute-done.73 = bf16[192,1024]{1,0:T(8,128)(2,1)} collective-permute-done((bf16[192,1024]{1,0:T(8,128)(2,1)}, bf16[192,1024]{1,0:T(8,128)(2,1)}, u32[]{:S(2)}, u32[]{:S(2)}) %collective-permute-start.73) | collective-permute-done | bytes 393248 | tf_op jit(solution)/shard_map/ppermute | solution.py:31
  453.4 7.8 %collective-permute-done.75 = bf16[96,1024]{1,0:T(8,128)(2,1)S(1)} collective-permute-done((bf16[96,1024]{1,0:T(8,128)(2,1)S(1)}, bf16[96,1024]{1,0:T(8,128)(2,1)S(1)}, u32[]{:S(2)}, u32[]{:S(2)}) %collective-permute-start.75) | collective-permute-done | bytes 196640 | tf_op jit(solution)/shard_map/ppermute | solution.py:31
  461.1 2.7 collective-permute-start.79
  463.9 3.9 collective-permute-done.78
  469.0 4.1 fusion
  480.2 4.5 all-to-all-start.3
  488.6 10.7 %attend_back.3 = (bf16[768,384]{1,0:T(8,128)(2,1)S(1)}, bf16[768,384]{1,0:T(8,128)(2,1)S(1)}, f32[1,384]{1,0:T(1,128)S(1)}) custom-call(s32[4]{0:T(128)S(1)} %pad_add_fusion.info, f32[2]{0:T(128)S(1)} %multiply_exponential_fusion.slopes, bf16[1536,384]{1,0:T(8,128)(2,1)S(1)} %copy-done.22, bf16[768,128]{1,0:T(8,128)(2,1)S(1)} %get-tuple-element.474.mine, ...), custom_call_target="tpu_custom_call" | custom-call | flops 1000000 | bytes 48000000 | tf_op jit(solution)/shard_map/attend_back/pallas_call | solution.py:240
  508.2 9.5 %all-gather.12.cloned.1.call-done = bf16[1024,1024]{1,0:T(8,128)(2,1)} async-done(((bf16[64,1024]{1,0:T(8,128)(2,1)}), bf16[1024,1024]{1,0:T(8,128)(2,1)}) %all-gather.12.cloned.1.call-update) | async-done | bytes 2097168 | tf_op jit(solution)/shard_map/all_gather | solution.py:1175
  523.4 3.0 collective-permute-start.89
  526.4 7.4 %all-to-all-start.4 = ((bf16[128,8,896]{2,1,0:T(8,128)(2,1)}), bf16[128,8,896]{2,1,0:T(8,128)(2,1)S(1)}, u32[]{:S(2)}, u32[]{:S(2)}) async-start(bf16[128,8,896]{2,1,0:T(8,128)(2,1)} %bitcast.83), calls=%async_computation.6 | async-start | bytes 3670016 | tf_op jit(solution)/shard_map/all_to_all | solution.py:1207
  537.0 3.3 collective-permute-start.90
  541.1 14.1 %collective-permute-done.90 = bf16[8,1792]{1,0:T(8,128)(2,1)S(1)} collective-permute-done((bf16[8,1792]{1,0:T(8,128)(2,1)}, bf16[8,1792]{1,0:T(8,128)(2,1)S(1)}, u32[]{:S(2)}, u32[]{:S(2)}) %collective-permute-start.90) | collective-permute-done | bytes 28704 | tf_op jit(solution)/shard_map/ppermute | solution.py:31
  556.7 4.3 all-to-all-done.4
  570.2 3.7 collective-permute-start.48
  576.8 2.7 collective-permute-done.86
  579.6 9.7 %collective-permute-done.87 = bf16[192,1024]{1,0:T(8,128)(2,1)S(1)} collective-permute-done((bf16[192,1024]{1,0:T(8,128)(2,1)S(1)}, bf16[192,1024]{1,0:T(8,128)(2,1)S(1)}, u32[]{:S(2)}, u32[]{:S(2)}) %collective-permute-start.87) | collective-permute-done | bytes 393248 | tf_op jit(solution)/shard_map/ppermute | solution.py:31
  590.7 3.6 collective-permute-start.88
  594.3 6.9 %collective-permute-done.48 = f32[192,1024]{1,0:T(8,128)S(1)} collective-permute-done((f32[192,1024]{1,0:T(8,128)S(1)}, f32[192,1024]{1,0:T(8,128)S(1)}, u32[]{:S(2)}, u32[]{:S(2)}) %collective-permute-start.48) | collective-permute-done | bytes 786464 | tf_op jit(solution)/shard_map/ppermute | solution.py:43
  604.7 9.0 %collective-permute-done.88 = f32[192,1024]{1,0:T(8,128)S(1)} collective-permute-done((f32[192,1024]{1,0:T(8,128)S(1)}, f32[192,1024]{1,0:T(8,128)S(1)}, u32[]{:S(2)}, u32[]{:S(2)}) %collective-permute-start.88) | collective-permute-done | bytes 786464 | tf_op jit(solution)/shard_map/ppermute | solution.py:43
  617.2 7.3 %unpack_full.1 = (f32[2,512,1024]{2,1,0:T(8,128)}, f32[2,128,4096]{2,1,0:T(8,128)}, f32[2,128,3072]{2,1,0:T(8,128)}, f32[2,128,1024]{2,1,0:T(8,128)}) custom-call(bf16[16,32,4224]{2,1,0:T(8,128)(2,1)} %bitcast.222, f32[2,512,1024]{2,1,0:T(8,128)} %get-tuple-element.401.old_down, ...), custom_call_target="tpu_custom_call", output_to_operand_aliasing={{0}: (1, {}), {1}: (2, {})} | custom-call | tf_op jit(solution)/shard_map/unpack_full/pallas_call | solution.py:912
  (582 shorter events, 243.5 us)
Async XLA Ops:
  7.2 13.9 %collective-permute-start = (bf16[192,1024]{1,0:T(8,128)(2,1)}, bf16[192,1024]{1,0:T(8,128)(2,1)}, u32[]{:S(2)}, u32[]{:S(2)}) collective-permute-start(bf16[192,1024]{1,0:T(8,128)(2,1)} %bitcast.242), channel_id=1, source_target_pairs={{4,8},{8,4},{5,9},{9,5},{6,10},{10,6},{7,11},{11,7},{20,24},{24,20... | collective-permute-start | bytes 1179656 | tf_op jit(solution)/shard_map/ppermute | solution.py:43
  23.5 15.0 %collective-permute-start.1 = (bf16[96,1024]{1,0:T(8,128)(2,1)}, bf16[96,1024]{1,0:T(8,128)(2,1)}, u32[]{:S(2)}, u32[]{:S(2)}) collective-permute-start(bf16[96,1024]{1,0:T(8,128)(2,1)} %get-tuple-element.489), channel_id=1, source_target_pairs={{0,1},{1,2},{2,3},{3,0},{4,5},{5,6},{6,7},{7,4},{8,9},{9,10},{10,1... | collective-permute-start | bytes 589832 | tf_op jit(solution)/shard_map/ppermute | solution.py:31
  25.2 13.4 %collective-permute-start.2 = (bf16[96,1024]{1,0:T(8,128)(2,1)}, bf16[96,1024]{1,0:T(8,128)(2,1)S(1)}, u32[]{:S(2)}, u32[]{:S(2)}) collective-permute-start(bf16[96,1024]{1,0:T(8,128)(2,1)} %get-tuple-element.488), channel_id=1, source_target_pairs={{0,3},{1,0},{2,1},{3,2},{4,7},{5,4},{6,5},{7,6},{8,11},{9,8},{10,9... | collective-permute-start | bytes 589832 | tf_op jit(solution)/shard_map/ppermute | solution.py:31
  27.3 15.0 %collective-permute-start.3 = (bf16[96,1024]{1,0:T(8,128)(2,1)}, bf16[96,1024]{1,0:T(8,128)(2,1)}, u32[]{:S(2)}, u32[]{:S(2)}) collective-permute-start(bf16[96,1024]{1,0:T(8,128)(2,1)} %get-tuple-element.488), channel_id=1, source_target_pairs={{0,1},{1,2},{2,3},{3,0},{4,5},{5,6},{6,7},{7,4},{8,9},{9,10},{10,1... | collective-permute-start | bytes 589832 | tf_op jit(solution)/shard_map/ppermute | solution.py:31
  27.3 20.1 %collective-permute-start.6 = (bf16[96,1024]{1,0:T(8,128)(2,1)}, bf16[96,1024]{1,0:T(8,128)(2,1)}, u32[]{:S(2)}, u32[]{:S(2)}) collective-permute-start(bf16[96,1024]{1,0:T(8,128)(2,1)} %get-tuple-element.489), channel_id=1, source_target_pairs={{0,3},{1,0},{2,1},{3,2},{4,7},{5,4},{6,5},{7,6},{8,11},{9,8},{10,9... | collective-permute-start | bytes 589832 | tf_op jit(solution)/shard_map/ppermute | solution.py:31
  30.0 18.4 %all-to-all-start = ((bf16[8,32,768]{2,1,0:T(8,128)(2,1)}), bf16[8,32,768]{2,1,0:T(8,128)(2,1)S(1)}, u32[]{:S(2)}, u32[]{:S(2)}) async-start(bf16[8,32,768]{2,1,0:T(8,128)(2,1)} %pack_first.1), calls=%async_computation | async-start | bytes 786432 | tf_op jit(solution)/shard_map/all_to_all | solution.py:605
  33.4 92.4 %all-gather.8.cloned.1.call-start = ((), (), s32[]{:S(2)}) async-start(), calls=%async_computation.7 | async-start | bytes 2359296 | tf_op jit(solution)/shard_map/all_gather | solution.py:1058
  63.5 21.8 %all-to-all-start.1 = ((bf16[8,64,1024]{2,1,0:T(8,128)(2,1)}), bf16[8,64,1024]{2,1,0:T(8,128)(2,1)S(1)}, u32[]{:S(2)}, u32[]{:S(2)}) async-start(bf16[8,64,1024]{2,1,0:T(8,128)(2,1)} %get-tuple-element.224), calls=%async_computation.1 | async-start | bytes 2097152 | tf_op jit(solution)/shard_map/all_to_all | solution.py:605
  74.4 10.9 %collective-permute-start.12 = (bf16[768,384]{1,0:T(8,128)(2,1)}, bf16[768,384]{1,0:T(8,128)(2,1)}, u32[]{:S(2)}, u32[]{:S(2)}) collective-permute-start(bf16[768,384]{1,0:T(8,128)(2,1)} %get-tuple-element.467), channel_id=1, source_target_pairs={{0,8},{8,0},{1,9},{9,1},{2,10},{10,2},{3,11},{11,3},{4,12},{12,4},... | collective-permute-start | bytes 1769480 | tf_op jit(solution)/shard_map/ppermute | solution.py:39
  76.7 15.4 %collective-permute-start.16 = (s32[1,128]{1,0:T(1,128)S(1)}, s32[1,128]{1,0:T(1,128)S(1)}, u32[]{:S(2)}, u32[]{:S(2)}) collective-permute-start(s32[1,128]{1,0:T(1,128)S(1)} %broadcast_in_dim.12), channel_id=1, source_target_pairs={{4,8},{8,4},{5,9},{9,5},{6,10},{10,6},{7,11},{11,7},{20,24},{24,20... | collective-permute-start | bytes 1544 | tf_op jit(solution)/shard_map/ppermute | solution.py:43
  85.3 33.6 %all-to-all-start.2 = ((bf16[8,64,768]{2,1,0:T(8,128)(2,1)}), bf16[8,64,768]{2,1,0:T(8,128)(2,1)}, u32[]{:S(2)}, u32[]{:S(2)}) async-start(bf16[8,64,768]{2,1,0:T(8,128)(2,1)} %copy-done.25), calls=%async_computation.2 | async-start | bytes 1572864 | tf_op jit(solution)/shard_map/all_to_all | solution.py:605
  91.5 177.7 %all-gather.10.cloned.1.call-start = ((), (), s32[]{:S(2)}) async-start(), calls=%async_computation.10 | async-start | bytes 10485760 | tf_op jit(solution)/shard_map/all_gather | solution.py:1088
  104.6 12.2 %collective-permute-start.14 = (bf16[96,1024]{1,0:T(8,128)(2,1)}, bf16[96,1024]{1,0:T(8,128)(2,1)S(1)}, u32[]{:S(2)}, u32[]{:S(2)}) collective-permute-start(bf16[96,1024]{1,0:T(8,128)(2,1)} %copy-done.73), channel_id=1, source_target_pairs={{0,64},{32,96},{64,0},{96,32},{1,65},{33,97},{65,1},{97,33},{2,66}... | collective-permute-start | bytes 589832 | tf_op jit(solution)/shard_map/ppermute | solution.py:35
  128.0 19.6 %collective-permute-start.19 = (bf16[192,1024]{1,0:T(8,128)(2,1)S(1)}, bf16[192,1024]{1,0:T(8,128)(2,1)S(1)}, u32[]{:S(2)}, u32[]{:S(2)}) collective-permute-start(bf16[192,1024]{1,0:T(8,128)(2,1)S(1)} %get-tuple-element.466), channel_id=1, source_target_pairs={{0,3},{1,0},{2,1},{3,2},{4,7},{5,4},{6,5},{7,6},{8,11},{9,8},{10,9... | collective-permute-start | bytes 1179656 | tf_op jit(solution)/shard_map/ppermute | solution.py:31
  131.0 16.7 %collective-permute-start.20 = (bf16[192,1024]{1,0:T(8,128)(2,1)S(1)}, bf16[192,1024]{1,0:T(8,128)(2,1)S(1)}, u32[]{:S(2)}, u32[]{:S(2)}) collective-permute-start(bf16[192,1024]{1,0:T(8,128)(2,1)S(1)} %get-tuple-element.465), channel_id=1, source_target_pairs={{0,2},{1,3},{2,0},{3,1},{4,6},{5,7},{6,4},{7,5},{8,10},{9,11},{10,... | collective-permute-start | bytes 1179656 | tf_op jit(solution)/shard_map/ppermute | solution.py:31
  131.6 20.4 %collective-permute-start.21 = (bf16[192,1024]{1,0:T(8,128)(2,1)S(1)}, bf16[192,1024]{1,0:T(8,128)(2,1)S(1)}, u32[]{:S(2)}, u32[]{:S(2)}) collective-permute-start(bf16[192,1024]{1,0:T(8,128)(2,1)S(1)} %get-tuple-element.464), channel_id=1, source_target_pairs={{0,1},{1,2},{2,3},{3,0},{4,5},{5,6},{6,7},{7,4},{8,9},{9,10},{10,1... | collective-permute-start | bytes 1179656 | tf_op jit(solution)/shard_map/ppermute | solution.py:31
  154.3 210.6 %reduce-scatter.3.cloned.1.call-start = ((), (), s32[]{:S(2)}) async-start(), calls=%async_computation.8 | async-start | bytes 10485760 | tf_op jit(solution)/shard_map/reduce_scatter | solution.py:1130
  155.5 10.2 %collective-permute-start.23 = (bf16[96,1024]{1,0:T(8,128)(2,1)S(1)}, bf16[96,1024]{1,0:T(8,128)(2,1)S(1)}, u32[]{:S(2)}, u32[]{:S(2)}) collective-permute-start(bf16[96,1024]{1,0:T(8,128)(2,1)S(1)} %get-tuple-element.487), channel_id=1, source_target_pairs={{0,1},{1,2},{2,3},{3,0},{4,5},{5,6},{6,7},{7,4},{8,9},{9,10},{10,1... | collective-permute-start | bytes 589832 | tf_op jit(solution)/shard_map/ppermute | solution.py:31
  158.4 15.2 %collective-permute-start.28 = (bf16[96,1024]{1,0:T(8,128)(2,1)S(1)}, bf16[96,1024]{1,0:T(8,128)(2,1)S(1)}, u32[]{:S(2)}, u32[]{:S(2)}) collective-permute-start(bf16[96,1024]{1,0:T(8,128)(2,1)S(1)} %get-tuple-element.487), channel_id=1, source_target_pairs={{0,3},{1,0},{2,1},{3,2},{4,7},{5,4},{6,5},{7,6},{8,11},{9,8},{10,9... | collective-permute-start | bytes 589832 | tf_op jit(solution)/shard_map/ppermute | solution.py:31
  161.1 12.6 %collective-permute-start.29 = (bf16[8,64,768]{2,1,0:T(8,128)(2,1)}, bf16[8,64,768]{2,1,0:T(8,128)(2,1)S(1)}, u32[]{:S(2)}, u32[]{:S(2)}) collective-permute-start(bf16[8,64,768]{2,1,0:T(8,128)(2,1)} %all-to-all-done.2.mine), channel_id=1, source_target_pairs={{0,8},{8,0},{1,9},{9,1},{2,10},{10,2},{3,11},{11,3},{4,12},{12,4},... | collective-permute-start | bytes 2359304 | tf_op jit(solution)/shard_map/ppermute | solution.py:39
  181.7 10.1 %collective-permute-start.30 = (bf16[192,1024]{1,0:T(8,128)(2,1)S(1)}, bf16[192,1024]{1,0:T(8,128)(2,1)S(1)}, u32[]{:S(2)}, u32[]{:S(2)}) collective-permute-start(bf16[192,1024]{1,0:T(8,128)(2,1)S(1)} %get-tuple-element.463), channel_id=1, source_target_pairs={{0,3},{1,0},{2,1},{3,2},{4,7},{5,4},{6,5},{7,6},{8,11},{9,8},{10,9... | collective-permute-start | bytes 1179656 | tf_op jit(solution)/shard_map/ppermute | solution.py:31
  184.1 10.9 %collective-permute-start.31 = (bf16[192,1024]{1,0:T(8,128)(2,1)S(1)}, bf16[192,1024]{1,0:T(8,128)(2,1)S(1)}, u32[]{:S(2)}, u32[]{:S(2)}) collective-permute-start(bf16[192,1024]{1,0:T(8,128)(2,1)S(1)} %get-tuple-element.462), channel_id=1, source_target_pairs={{0,2},{1,3},{2,0},{3,1},{4,6},{5,7},{6,4},{7,5},{8,10},{9,11},{10,... | collective-permute-start | bytes 1179656 | tf_op jit(solution)/shard_map/ppermute | solution.py:31
  184.1 20.4 %collective-permute-start.32 = (bf16[192,1024]{1,0:T(8,128)(2,1)S(1)}, bf16[192,1024]{1,0:T(8,128)(2,1)S(1)}, u32[]{:S(2)}, u32[]{:S(2)}) collective-permute-start(bf16[192,1024]{1,0:T(8,128)(2,1)S(1)} %get-tuple-element.461), channel_id=1, source_target_pairs={{0,1},{1,2},{2,3},{3,0},{4,5},{5,6},{6,7},{7,4},{8,9},{9,10},{10,1... | collective-permute-start | bytes 1179656 | tf_op jit(solution)/shard_map/ppermute | solution.py:31
  205.4 11.3 %collective-permute-start.34 = (bf16[96,1024]{1,0:T(8,128)(2,1)S(1)}, bf16[96,1024]{1,0:T(8,128)(2,1)S(1)}, u32[]{:S(2)}, u32[]{:S(2)}) collective-permute-start(bf16[96,1024]{1,0:T(8,128)(2,1)S(1)} %get-tuple-element.485), channel_id=1, source_target_pairs={{0,1},{1,2},{2,3},{3,0},{4,5},{5,6},{6,7},{7,4},{8,9},{9,10},{10,1... | collective-permute-start | bytes 589832 | tf_op jit(solution)/shard_map/ppermute | solution.py:31
  205.4 11.2 %collective-permute-start.35 = (bf16[96,1024]{1,0:T(8,128)(2,1)S(1)}, bf16[96,1024]{1,0:T(8,128)(2,1)S(1)}, u32[]{:S(2)}, u32[]{:S(2)}) collective-permute-start(bf16[96,1024]{1,0:T(8,128)(2,1)S(1)} %get-tuple-element.484), channel_id=1, source_target_pairs={{0,3},{1,0},{2,1},{3,2},{4,7},{5,4},{6,5},{7,6},{8,11},{9,8},{10,9... | collective-permute-start | bytes 589832 | tf_op jit(solution)/shard_map/ppermute | solution.py:31
  208.1 19.3 %collective-permute-start.33 = (bf16[192,1024]{1,0:T(8,128)(2,1)S(1)}, bf16[192,1024]{1,0:T(8,128)(2,1)S(1)}, u32[]{:S(2)}, u32[]{:S(2)}) collective-permute-start(bf16[192,1024]{1,0:T(8,128)(2,1)S(1)} %bitcast.243), channel_id=1, source_target_pairs={{4,8},{8,4},{5,9},{9,5},{6,10},{10,6},{7,11},{11,7},{20,24},{24,20... | collective-permute-start | bytes 1179656 | tf_op jit(solution)/shard_map/ppermute | solution.py:43
  214.0 10.4 %collective-permute-start.39 = (bf16[96,1024]{1,0:T(8,128)(2,1)S(1)}, bf16[96,1024]{1,0:T(8,128)(2,1)S(1)}, u32[]{:S(2)}, u32[]{:S(2)}) collective-permute-start(bf16[96,1024]{1,0:T(8,128)(2,1)S(1)} %get-tuple-element.485), channel_id=1, source_target_pairs={{0,3},{1,0},{2,1},{3,2},{4,7},{5,4},{6,5},{7,6},{8,11},{9,8},{10,9... | collective-permute-start | bytes 589832 | tf_op jit(solution)/shard_map/ppermute | solution.py:31
  241.0 19.2 %collective-permute-start.43 = (bf16[192,1024]{1,0:T(8,128)(2,1)S(1)}, bf16[192,1024]{1,0:T(8,128)(2,1)S(1)}, u32[]{:S(2)}, u32[]{:S(2)}) collective-permute-start(bf16[192,1024]{1,0:T(8,128)(2,1)S(1)} %get-tuple-element.458), channel_id=1, source_target_pairs={{0,3},{1,0},{2,1},{3,2},{4,7},{5,4},{6,5},{7,6},{8,11},{9,8},{10,9... | collective-permute-start | bytes 1179656 | tf_op jit(solution)/shard_map/ppermute | solution.py:31
  243.8 16.4 %collective-permute-start.44 = (bf16[192,1024]{1,0:T(8,128)(2,1)S(1)}, bf16[192,1024]{1,0:T(8,128)(2,1)S(1)}, u32[]{:S(2)}, u32[]{:S(2)}) collective-permute-start(bf16[192,1024]{1,0:T(8,128)(2,1)S(1)} %get-tuple-element.457), channel_id=1, source_target_pairs={{0,2},{1,3},{2,0},{3,1},{4,6},{5,7},{6,4},{7,5},{8,10},{9,11},{10,... | collective-permute-start | bytes 1179656 | tf_op jit(solution)/shard_map/ppermute | solution.py:31
  243.8 20.4 %collective-permute-start.45 = (bf16[192,1024]{1,0:T(8,128)(2,1)S(1)}, bf16[192,1024]{1,0:T(8,128)(2,1)S(1)}, u32[]{:S(2)}, u32[]{:S(2)}) collective-permute-start(bf16[192,1024]{1,0:T(8,128)(2,1)S(1)} %get-tuple-element.456), channel_id=1, source_target_pairs={{0,1},{1,2},{2,3},{3,0},{4,5},{5,6},{6,7},{7,4},{8,9},{9,10},{10,1... | collective-permute-start | bytes 1179656 | tf_op jit(solution)/shard_map/ppermute | solution.py:31
  287.4 185.6 %reduce-scatter.5.cloned.1.call-start = ((), (), s32[]{:S(2)}) async-start(), calls=%async_computation.9 | async-start | bytes 2228224 | tf_op jit(solution)/shard_map/reduce_scatter | solution.py:1160
  294.4 12.0 %collective-permute-start.51 = (bf16[96,1024]{1,0:T(8,128)(2,1)S(1)}, bf16[96,1024]{1,0:T(8,128)(2,1)S(1)}, u32[]{:S(2)}, u32[]{:S(2)}) collective-permute-start(bf16[96,1024]{1,0:T(8,128)(2,1)S(1)} %get-tuple-element.482), channel_id=1, source_target_pairs={{0,3},{1,0},{2,1},{3,2},{4,7},{5,4},{6,5},{7,6},{8,11},{9,8},{10,9... | collective-permute-start | bytes 589832 | tf_op jit(solution)/shard_map/ppermute | solution.py:31
  295.1 14.0 %collective-permute-start.52 = (bf16[96,1024]{1,0:T(8,128)(2,1)S(1)}, bf16[96,1024]{1,0:T(8,128)(2,1)S(1)}, u32[]{:S(2)}, u32[]{:S(2)}) collective-permute-start(bf16[96,1024]{1,0:T(8,128)(2,1)S(1)} %get-tuple-element.482), channel_id=1, source_target_pairs={{0,1},{1,2},{2,3},{3,0},{4,5},{5,6},{6,7},{7,4},{8,9},{9,10},{10,1... | collective-permute-start | bytes 589832 | tf_op jit(solution)/shard_map/ppermute | solution.py:31
  296.0 10.5 %collective-permute-start.50 = (bf16[96,1024]{1,0:T(8,128)(2,1)S(1)}, bf16[96,1024]{1,0:T(8,128)(2,1)S(1)}, u32[]{:S(2)}, u32[]{:S(2)}) collective-permute-start(bf16[96,1024]{1,0:T(8,128)(2,1)S(1)} %get-tuple-element.483), channel_id=1, source_target_pairs={{0,1},{1,2},{2,3},{3,0},{4,5},{5,6},{6,7},{7,4},{8,9},{9,10},{10,1... | collective-permute-start | bytes 589832 | tf_op jit(solution)/shard_map/ppermute | solution.py:31
  296.0 16.8 %collective-permute-start.55 = (bf16[96,1024]{1,0:T(8,128)(2,1)S(1)}, bf16[96,1024]{1,0:T(8,128)(2,1)S(1)}, u32[]{:S(2)}, u32[]{:S(2)}) collective-permute-start(bf16[96,1024]{1,0:T(8,128)(2,1)S(1)} %get-tuple-element.483), channel_id=1, source_target_pairs={{0,3},{1,0},{2,1},{3,2},{4,7},{5,4},{6,5},{7,6},{8,11},{9,8},{10,9... | collective-permute-start | bytes 589832 | tf_op jit(solution)/shard_map/ppermute | solution.py:31
  338.4 19.9 %collective-permute-start.58 = (bf16[192,1024]{1,0:T(8,128)(2,1)}, bf16[192,1024]{1,0:T(8,128)(2,1)}, u32[]{:S(2)}, u32[]{:S(2)}) collective-permute-start(bf16[192,1024]{1,0:T(8,128)(2,1)} %get-tuple-element.455), channel_id=1, source_target_pairs={{0,3},{1,0},{2,1},{3,2},{4,7},{5,4},{6,5},{7,6},{8,11},{9,8},{10,9... | collective-permute-start | bytes 1179656 | tf_op jit(solution)/shard_map/ppermute | solution.py:31
  341.0 17.2 %collective-permute-start.59 = (bf16[192,1024]{1,0:T(8,128)(2,1)}, bf16[192,1024]{1,0:T(8,128)(2,1)}, u32[]{:S(2)}, u32[]{:S(2)}) collective-permute-start(bf16[192,1024]{1,0:T(8,128)(2,1)} %get-tuple-element.454), channel_id=1, source_target_pairs={{0,2},{1,3},{2,0},{3,1},{4,6},{5,7},{6,4},{7,5},{8,10},{9,11},{10,... | collective-permute-start | bytes 1179656 | tf_op jit(solution)/shard_map/ppermute | solution.py:31
  341.0 20.8 %collective-permute-start.60 = (bf16[192,1024]{1,0:T(8,128)(2,1)}, bf16[192,1024]{1,0:T(8,128)(2,1)}, u32[]{:S(2)}, u32[]{:S(2)}) collective-permute-start(bf16[192,1024]{1,0:T(8,128)(2,1)} %get-tuple-element.453), channel_id=1, source_target_pairs={{0,1},{1,2},{2,3},{3,0},{4,5},{5,6},{6,7},{7,4},{8,9},{9,10},{10,1... | collective-permute-start | bytes 1179656 | tf_op jit(solution)/shard_map/ppermute | solution.py:31
  367.1 24.3 %collective-permute-start.67 = (bf16[8,64,1024]{2,1,0:T(8,128)(2,1)}, bf16[8,64,1024]{2,1,0:T(8,128)(2,1)}, u32[]{:S(2)}, u32[]{:S(2)}) collective-permute-start(bf16[8,64,1024]{2,1,0:T(8,128)(2,1)} %dynamic-slice_bitcast_fusion), channel_id=1, source_target_pairs={{0,16},{16,0},{1,17},{17,1},{2,18},{18,2},{3,19},{19,3},{4,20},{20... | collective-permute-start | bytes 3145736 | tf_op jit(solution)/shard_map/ppermute | solution.py:39
  371.9 12.0 %collective-permute-start.66 = (bf16[96,1024]{1,0:T(8,128)(2,1)}, bf16[96,1024]{1,0:T(8,128)(2,1)S(1)}, u32[]{:S(2)}, u32[]{:S(2)}) collective-permute-start(bf16[96,1024]{1,0:T(8,128)(2,1)} %get-tuple-element.479), channel_id=1, source_target_pairs={{0,3},{1,0},{2,1},{3,2},{4,7},{5,4},{6,5},{7,6},{8,11},{9,8},{10,9... | collective-permute-start | bytes 589832 | tf_op jit(solution)/shard_map/ppermute | solution.py:31
  394.1 12.2 %collective-permute-start.68 = (bf16[2,64,1024]{2,1,0:T(8,128)(2,1)S(1)}, bf16[2,64,1024]{2,1,0:T(8,128)(2,1)S(1)}, u32[]{:S(2)}, u32[]{:S(2)}) collective-permute-start(bf16[2,64,1024]{2,1,0:T(8,128)(2,1)S(1)} %get-tuple-element.469), channel_id=1, source_target_pairs={{0,1},{1,2},{2,3},{3,0},{4,5},{5,6},{6,7},{7,4},{8,9},{9,10},{10,1... | collective-permute-start | bytes 786440 | tf_op jit(solution)/shard_map/ppermute | solution.py:31
  395.5 13.0 %collective-permute-start.69 = (bf16[2,64,1024]{2,1,0:T(8,128)(2,1)S(1)}, bf16[2,64,1024]{2,1,0:T(8,128)(2,1)S(1)}, u32[]{:S(2)}, u32[]{:S(2)}) collective-permute-start(bf16[2,64,1024]{2,1,0:T(8,128)(2,1)S(1)} %get-tuple-element.471), channel_id=1, source_target_pairs={{0,2},{1,3},{2,0},{3,1},{4,6},{5,7},{6,4},{7,5},{8,10},{9,11},{10,... | collective-permute-start | bytes 786440 | tf_op jit(solution)/shard_map/ppermute | solution.py:31
  398.1 10.5 %collective-permute-start.70 = (bf16[2,64,1024]{2,1,0:T(8,128)(2,1)S(1)}, bf16[2,64,1024]{2,1,0:T(8,128)(2,1)S(1)}, u32[]{:S(2)}, u32[]{:S(2)}) collective-permute-start(bf16[2,64,1024]{2,1,0:T(8,128)(2,1)S(1)} %get-tuple-element.470), channel_id=1, source_target_pairs={{0,3},{1,0},{2,1},{3,2},{4,7},{5,4},{6,5},{7,6},{8,11},{9,8},{10,9... | collective-permute-start | bytes 786440 | tf_op jit(solution)/shard_map/ppermute | solution.py:31
  399.2 118.5 %all-gather.12.cloned.1.call-start = ((), (), s32[]{:S(2)}) async-start(), calls=%async_computation.11 | async-start | bytes 2228224 | tf_op jit(solution)/shard_map/all_gather | solution.py:1175
  411.2 15.8 %collective-permute-start.74 = (bf16[64,1024]{1,0:T(8,128)(2,1)S(1)}, bf16[64,1024]{1,0:T(8,128)(2,1)S(1)}, u32[]{:S(2)}, u32[]{:S(2)}) collective-permute-start(bf16[64,1024]{1,0:T(8,128)(2,1)S(1)} %dynamic-slice_bitcast_fusion.6), channel_id=1, source_target_pairs={{0,4},{4,0},{1,5},{5,1},{2,6},{6,2},{3,7},{7,3},{8,12},{12,8},{9,1... | collective-permute-start | bytes 393224 | tf_op jit(solution)/shard_map/ppermute | solution.py:39
  415.0 12.7 %collective-permute-start.71 = (bf16[192,1024]{1,0:T(8,128)(2,1)}, bf16[192,1024]{1,0:T(8,128)(2,1)S(1)}, u32[]{:S(2)}, u32[]{:S(2)}) collective-permute-start(bf16[192,1024]{1,0:T(8,128)(2,1)} %get-tuple-element.452), channel_id=1, source_target_pairs={{0,3},{1,0},{2,1},{3,2},{4,7},{5,4},{6,5},{7,6},{8,11},{9,8},{10,9... | collective-permute-start | bytes 1179656 | tf_op jit(solution)/shard_map/ppermute | solution.py:31
  418.3 11.0 %collective-permute-start.72 = (bf16[192,1024]{1,0:T(8,128)(2,1)}, bf16[192,1024]{1,0:T(8,128)(2,1)}, u32[]{:S(2)}, u32[]{:S(2)}) collective-permute-start(bf16[192,1024]{1,0:T(8,128)(2,1)} %get-tuple-element.451), channel_id=1, source_target_pairs={{0,2},{1,3},{2,0},{3,1},{4,6},{5,7},{6,4},{7,5},{8,10},{9,11},{10,... | collective-permute-start | bytes 1179656 | tf_op jit(solution)/shard_map/ppermute | solution.py:31
  418.9 20.7 %collective-permute-start.73 = (bf16[192,1024]{1,0:T(8,128)(2,1)}, bf16[192,1024]{1,0:T(8,128)(2,1)}, u32[]{:S(2)}, u32[]{:S(2)}) collective-permute-start(bf16[192,1024]{1,0:T(8,128)(2,1)} %get-tuple-element.450), channel_id=1, source_target_pairs={{0,1},{1,2},{2,3},{3,0},{4,5},{5,6},{6,7},{7,4},{8,9},{9,10},{10,1... | collective-permute-start | bytes 1179656 | tf_op jit(solution)/shard_map/ppermute | solution.py:31
  448.0 20.9 %collective-permute-start.81 = (bf16[8,64,2048]{2,1,0:T(8,128)(2,1)}, bf16[8,64,2048]{2,1,0:T(8,128)(2,1)}, u32[]{:S(2)}, u32[]{:S(2)}) collective-permute-start(bf16[8,64,2048]{2,1,0:T(8,128)(2,1)} %fusion.26), channel_id=1, source_target_pairs={{0,8},{8,0},{1,9},{9,1},{2,10},{10,2},{3,11},{11,3},{4,12},{12,4},... | collective-permute-start | bytes 6291464 | tf_op jit(solution)/shard_map/ppermute | solution.py:39
  449.0 12.1 %collective-permute-start.76 = (bf16[96,1024]{1,0:T(8,128)(2,1)S(1)}, bf16[96,1024]{1,0:T(8,128)(2,1)S(1)}, u32[]{:S(2)}, u32[]{:S(2)}) collective-permute-start(bf16[96,1024]{1,0:T(8,128)(2,1)S(1)} %get-tuple-element.475), channel_id=1, source_target_pairs={{0,3},{1,0},{2,1},{3,2},{4,7},{5,4},{6,5},{7,6},{8,11},{9,8},{10,9... | collective-permute-start | bytes 589832 | tf_op jit(solution)/shard_map/ppermute | solution.py:31
  449.4 14.4 %collective-permute-start.77 = (bf16[96,1024]{1,0:T(8,128)(2,1)S(1)}, bf16[96,1024]{1,0:T(8,128)(2,1)S(1)}, u32[]{:S(2)}, u32[]{:S(2)}) collective-permute-start(bf16[96,1024]{1,0:T(8,128)(2,1)S(1)} %get-tuple-element.475), channel_id=1, source_target_pairs={{0,1},{1,2},{2,3},{3,0},{4,5},{5,6},{6,7},{7,4},{8,9},{9,10},{10,1... | collective-permute-start | bytes 589832 | tf_op jit(solution)/shard_map/ppermute | solution.py:31
  450.5 10.6 %collective-permute-start.75 = (bf16[96,1024]{1,0:T(8,128)(2,1)S(1)}, bf16[96,1024]{1,0:T(8,128)(2,1)S(1)}, u32[]{:S(2)}, u32[]{:S(2)}) collective-permute-start(bf16[96,1024]{1,0:T(8,128)(2,1)S(1)} %get-tuple-element.476), channel_id=1, source_target_pairs={{0,1},{1,2},{2,3},{3,0},{4,5},{5,6},{6,7},{7,4},{8,9},{9,10},{10,1... | collective-permute-start | bytes 589832 | tf_op jit(solution)/shard_map/ppermute | solution.py:31
  450.6 17.2 %collective-permute-start.80 = (bf16[96,1024]{1,0:T(8,128)(2,1)S(1)}, bf16[96,1024]{1,0:T(8,128)(2,1)S(1)}, u32[]{:S(2)}, u32[]{:S(2)}) collective-permute-start(bf16[96,1024]{1,0:T(8,128)(2,1)S(1)} %get-tuple-element.476), channel_id=1, source_target_pairs={{0,3},{1,0},{2,1},{3,2},{4,7},{5,4},{6,5},{7,6},{8,11},{9,8},{10,9... | collective-permute-start | bytes 589832 | tf_op jit(solution)/shard_map/ppermute | solution.py:31
  480.2 39.8 %all-to-all-start.3 = ((bf16[8,64,2304]{2,1,0:T(8,128)(2,1)}), bf16[8,64,2304]{2,1,0:T(8,128)(2,1)}, u32[]{:S(2)}, u32[]{:S(2)}) async-start(bf16[8,64,2304]{2,1,0:T(8,128)(2,1)} %pad_maximum_fusion), calls=%async_computation.5 | async-start | bytes 4718592 | tf_op jit(solution)/shard_map/all_to_all | solution.py:761
  523.4 10.5 %collective-permute-start.89 = (bf16[32,3328]{1,0:T(8,128)(2,1)}, bf16[32,3328]{1,0:T(8,128)(2,1)}, u32[]{:S(2)}, u32[]{:S(2)}) collective-permute-start(bf16[32,3328]{1,0:T(8,128)(2,1)} %dynamic-slice_bitcast_fusion.5), channel_id=1, source_target_pairs={{0,4},{4,0},{1,5},{5,1},{2,6},{6,2},{3,7},{7,3},{8,12},{12,8},{9,1... | collective-permute-start | bytes 638984 | tf_op jit(solution)/shard_map/ppermute | solution.py:39
  526.4 34.6 %all-to-all-start.4 = ((bf16[128,8,896]{2,1,0:T(8,128)(2,1)}), bf16[128,8,896]{2,1,0:T(8,128)(2,1)S(1)}, u32[]{:S(2)}, u32[]{:S(2)}) async-start(bf16[128,8,896]{2,1,0:T(8,128)(2,1)} %bitcast.83), calls=%async_computation.6 | async-start | bytes 3670016 | tf_op jit(solution)/shard_map/all_to_all | solution.py:1207
  533.8 80.8 %all-gather.14.cloned.1.call-start = ((), (), s32[]{:S(2)}) async-start(), calls=%async_computation.12 | async-start | bytes 4595712 | tf_op jit(solution)/shard_map/all_gather | solution.py:1225
  537.0 18.3 %collective-permute-start.90 = (bf16[8,1792]{1,0:T(8,128)(2,1)}, bf16[8,1792]{1,0:T(8,128)(2,1)S(1)}, u32[]{:S(2)}, u32[]{:S(2)}) collective-permute-start(bf16[8,1792]{1,0:T(8,128)(2,1)} %get-tuple-element.498), channel_id=1, source_target_pairs={{0,3},{1,0},{2,1},{3,2},{4,7},{5,4},{6,5},{7,6},{8,11},{9,8},{10,9... | collective-permute-start | bytes 86024 | tf_op jit(solution)/shard_map/ppermute | solution.py:31
  540.2 15.0 %collective-permute-start.91 = (bf16[8,1792]{1,0:T(8,128)(2,1)}, bf16[8,1792]{1,0:T(8,128)(2,1)}, u32[]{:S(2)}, u32[]{:S(2)}) collective-permute-start(bf16[8,1792]{1,0:T(8,128)(2,1)} %get-tuple-element.497), channel_id=1, source_target_pairs={{0,2},{1,3},{2,0},{3,1},{4,6},{5,7},{6,4},{7,5},{8,10},{9,11},{10,... | collective-permute-start | bytes 86024 | tf_op jit(solution)/shard_map/ppermute | solution.py:31
  540.3 15.0 %collective-permute-start.92 = (bf16[8,1792]{1,0:T(8,128)(2,1)}, bf16[8,1792]{1,0:T(8,128)(2,1)}, u32[]{:S(2)}, u32[]{:S(2)}) collective-permute-start(bf16[8,1792]{1,0:T(8,128)(2,1)} %get-tuple-element.496), channel_id=1, source_target_pairs={{0,1},{1,2},{2,3},{3,0},{4,5},{5,6},{6,7},{7,4},{8,9},{9,10},{10,1... | collective-permute-start | bytes 86024 | tf_op jit(solution)/shard_map/ppermute | solution.py:31
  568.3 11.3 %collective-permute-start.86 = (bf16[192,1024]{1,0:T(8,128)(2,1)S(1)}, bf16[192,1024]{1,0:T(8,128)(2,1)S(1)}, u32[]{:S(2)}, u32[]{:S(2)}) collective-permute-start(bf16[192,1024]{1,0:T(8,128)(2,1)S(1)} %get-tuple-element.448), channel_id=1, source_target_pairs={{0,2},{1,3},{2,0},{3,1},{4,6},{5,7},{6,4},{7,5},{8,10},{9,11},{10,... | collective-permute-start | bytes 1179656 | tf_op jit(solution)/shard_map/ppermute | solution.py:31
  570.0 19.3 %collective-permute-start.87 = (bf16[192,1024]{1,0:T(8,128)(2,1)S(1)}, bf16[192,1024]{1,0:T(8,128)(2,1)S(1)}, u32[]{:S(2)}, u32[]{:S(2)}) collective-permute-start(bf16[192,1024]{1,0:T(8,128)(2,1)S(1)} %get-tuple-element.447), channel_id=1, source_target_pairs={{0,1},{1,2},{2,3},{3,0},{4,5},{5,6},{6,7},{7,4},{8,9},{9,10},{10,1... | collective-permute-start | bytes 1179656 | tf_op jit(solution)/shard_map/ppermute | solution.py:31
  570.2 31.0 %collective-permute-start.48 = (f32[192,1024]{1,0:T(8,128)S(1)}, f32[192,1024]{1,0:T(8,128)S(1)}, u32[]{:S(2)}, u32[]{:S(2)}) collective-permute-start(f32[192,1024]{1,0:T(8,128)S(1)} %copy-done.47), channel_id=1, source_target_pairs={{4,8},{8,4},{5,9},{9,5},{6,10},{10,6},{7,11},{11,7},{20,24},{24,20... | collective-permute-start | bytes 2359304 | tf_op jit(solution)/shard_map/ppermute | solution.py:43
  590.7 23.0 %collective-permute-start.88 = (f32[192,1024]{1,0:T(8,128)S(1)}, f32[192,1024]{1,0:T(8,128)S(1)}, u32[]{:S(2)}, u32[]{:S(2)}) collective-permute-start(f32[192,1024]{1,0:T(8,128)S(1)} %fusion.42), channel_id=1, source_target_pairs={{4,8},{8,4},{5,9},{9,5},{6,10},{10,6},{7,11},{11,7},{20,24},{24,20... | collective-permute-start | bytes 2359304 | tf_op jit(solution)/shard_map/ppermute | solution.py:43
  (138 other events, 859.5 us)
Sparse Core Ops, SparseCore 0:
  55.8 66.6 all-gather.7
  154.4 81.4 all-gather.9
  287.6 77.2 reduce-scatter.2
  399.3 59.7 reduce-scatter.4
  460.7 56.9 all-gather.11
  566.4 41.4 all-gather.13
